TPU v7x, 128 devices: a whole 4x4x4 slice. The times are simulated.
128 devices in a mesh: dp: 16 (over x_hi, y, core), group: 8 (over z, x_lo).
Axes of the slice: x: 4 (x_hi: 2, x_lo: 2; x = x_hi * 2 + x_lo), y: 4, z: 4, core: 2. Of those that a mesh axis runs over, the one named last changes fastest.
Arguments:
- grad_parts: bfloat16 [16, 8, 4194304], P('dp', 'group'), may hold values from -3 to 3
- master_weights: float32 [8, 4194304], P('group', 'dp'), may hold values from -6 to 6
- first_moment: float32 [8, 4194304], P('group', 'dp'), may hold values from -6 to 6
- second_moment: float32 [8, 4194304], P('group', 'dp'), may hold values from 0.25 to 4
- cauchy_points: int32 [10], replicated, may hold values from 1 to 16, as said below
- parity_holder: int32 [16, 8], P('dp'), may hold values from 0 to 7, each once within a row
Outputs:
- new_master: float32 [8, 4194304], P('group', 'dp')
- new_first: float32 [8, 4194304], P('group', 'dp')
- new_second: float32 [8, 4194304], P('group', 'dp')
- parity_shard: float32 [16, 8, 2, 3, 32768], P('dp', 'group')
Inputs may be any that keep to these rules, and one draw needn't show every extreme that they name: `cauchy_points`: 10 distinct integers; 1 and 16 are always among them. `parity_holder`: each row is a permutation of 0..7.
All inputs are finite; a program needn't handle non-finite values.
Results may differ from a plain program's by a relative error of at most 0.0003.
Values sent between devices are 32-bit elements; how exact they have to be, the bound alone decides.
No kernel may reach another device: no remote copies, remote signals or barrier semaphores. Data moves between devices by JAX's collectives and lax.ppermute only.
A program may use at most 128 MiB of HBM per device.

v0:
```python
import jax
import jax.numpy as jnp
from jax import lax
from jax.sharding import PartitionSpec as P

STEP = 10


def per_device(
    grad_parts, master_weights, first_moment, second_moment, cauchy_points, parity_holder
):
    members = lax.axis_size("group")
    length = master_weights.shape[1]
    piece = length // members
    flat_grad = grad_parts.reshape(grad_parts.shape[2])
    grad = lax.psum_scatter(
        flat_grad.astype(jnp.float32), "dp", scatter_dimension=0, tiled=True
    ).reshape(1, length)
    new_first = 0.9 * first_moment + 0.1 * grad
    new_second = 0.95 * second_moment + 0.05 * grad * grad
    first_hat = new_first / (1.0 - 0.9**STEP)
    second_hat = new_second / (1.0 - 0.95**STEP)
    new_master = master_weights - 0.01 * (
        first_hat / (jnp.sqrt(second_hat) + 1e-08) + 0.1 * master_weights
    )
    points = cauchy_points.astype(jnp.float32)
    coeff = 1.0 / (points[:2][:, None] + points[2:][None, :])
    member_ids = jnp.arange(members, dtype=jnp.int32)
    onehot = (parity_holder[0][:, None] == member_ids[None, :]).astype(jnp.int32)
    inverse = jnp.sum(onehot * member_ids[:, None], axis=0)
    states = jnp.concatenate([new_master, new_first, new_second], axis=0).reshape(3, members, piece)
    ordered = jnp.take(states, inverse, axis=1)
    own_index = lax.axis_index("group")
    own_coeff = lax.dynamic_slice_in_dim(coeff, own_index, 1, 1).reshape(2, 1, 1, 1)
    weighted = own_coeff * ordered[None]
    shard = lax.psum_scatter(weighted, "group", scatter_dimension=2, tiled=True)
    parity_shard = shard.reshape(1, 1, 2, 3, piece)
    return (new_master, new_first, new_second, parity_shard)


def solution(mesh):
    in_specs = (
        P("dp", "group", None),
        P("group", "dp"),
        P("group", "dp"),
        P("group", "dp"),
        P(),
        P("dp", None),
    )
    out_specs = (
        P("group", "dp"),
        P("group", "dp"),
        P("group", "dp"),
        P("dp", "group", None, None, None),
    )
    return jax.shard_map(
        per_device, mesh=mesh, in_specs=in_specs, out_specs=out_specs, check_vma=False
    )
```

profile of v0, /device:TPU:24, one launch (start us, length us, event | category | flops | bytes accessed | tf_op | source)
XLA Modules:
  0.0 528.1 jit_solution(4920792229867141345)
XLA Ops:
  7.2 0.0 all-reduce.5.cloned.1.call-start
  7.2 19.8 %convert_element_type.13 = f32[1,1,4194304]{2,1,0:T(1,128)} convert(bf16[1,1,4194304]{2,1,0:T(2,128)(2,1)} %param.6) | non-fusion elementwise | flops 4194304 | bytes 25165824 | tf_op jit(solution)/shard_map/convert_element_type | solution.py:17
  27.1 0.0 copy-start.3
  27.1 0.0 copy-start.6
  27.1 0.0 copy-start.4
  27.1 0.0 all-reduce.5.cloned.1.call-update
  27.1 0.0 all-reduce.7.cloned.1.call-start
  27.2 0.5 copy-done.3
  27.7 0.1 slice.7
  27.8 0.0 copy-done.6
  27.8 0.6 dynamic-slice
  29.0 0.1 add_divide_fusion
  29.1 0.0 copy-done.4
  29.1 0.1 select_reduce_fusion
  29.2 196.8 %all-reduce.5.cloned.1.call-done = f32[4194304]{0:T(1024)} async-done(((f32[4194304]{0:T(1024)}), f32[4194304]{0:T(1024)}) %all-reduce.5.cloned.1.call-update) | async-done | bytes 16777232
  226.0 1.4 multiply_multiply_fusion
  227.4 7.3 %multiply_subtract_fusion = (f32[1,262144]{1,0:T(1,128)S(1)}, f32[1,262144]{1,0:T(1,128)S(1)}, f32[1,262144]{1,0:T(1,128)S(1)}) fusion(f32[1,262144]{1,0:T(1,128)} %param.7, f32[1,262144]{1,0:T(1,128)S(1)} %bitcast.21, f32[1,262144]{1,0:T(1,128)} %param.8, f32[1,262144]{1,0:T(1,128)S(1)} %bitcast.20, f32[1,262144]{1,0:T(1,128)} %param.9), kind=kLoop, calls=%fused_computation.5 | loop fusion | flops 3145728 | bytes 8388608 | tf_op jit(solution)/shard_map/sub | solution.py:23
  234.8 0.0 copy-start
  234.8 0.0 copy-start.1
  234.8 0.0 copy-start.2
  234.8 4.2 pad_maximum_fusion
  239.1 6.9 %gather_fusion = f32[8,3,32768]{2,1,0:T(4,128)} fusion(f32[3,8,32768]{2,0,1:T(4,128)} %bitcast.19, s32[1024]{0:T(1024)S(1)} %pad_clamp_fusion), kind=kCustom, calls=%fused_computation | custom fusion | bytes 6291488 | tf_op jit(solution)/shard_map/jit(_take)/gather | solution.py:32
  246.0 0.0 copy-done
  246.0 0.0 copy-done.1
  246.0 0.0 copy-done.2
  246.0 3.3 select_bitcast_fusion
  249.3 5.0 broadcast_multiply_fusion
  254.3 0.0 all-reduce.7.cloned.1.call-update
  254.3 0.6 copy-done.5
  255.0 0.7 dynamic-slice.2
  255.6 262.9 %all-reduce.7.cloned.1.call-done = f32[2,3,8,32768]{3,0,1,2:T(2,128)} async-done(((f32[2,3,8,32768]{3,0,1,2:T(2,128)}), f32[2,3,8,32768]{3,0,1,2:T(2,128)}) %all-reduce.7.cloned.1.call-update) | async-done | bytes 6291472
  518.5 2.7 dynamic-slice_bitcast_fusion
  (6 shorter events, 0.0 us)
Async XLA Ops:
  7.2 218.9 %all-reduce.5.cloned.1.call-start = ((), (), s32[]{:S(2)}) async-start(), calls=%async_computation | async-start | bytes 33554432
  27.1 0.7 copy-start.3
  27.1 0.7 copy-start.6
  27.1 2.0 copy-start.4
  27.1 491.4 %all-reduce.7.cloned.1.call-start = ((), (), s32[]{:S(2)}) async-start(), calls=%async_computation.1 | async-start | bytes 12582912
  234.8 11.2 %copy-start = (f32[1,262144]{1,0:T(1,128)}, f32[1,262144]{1,0:T(1,128)S(1)}, u32[]{:S(2)}) copy-start(f32[1,262144]{1,0:T(1,128)S(1)} %get-tuple-element.4) | copy-start | bytes 3145732
  234.8 11.2 %copy-start.1 = (f32[1,262144]{1,0:T(1,128)}, f32[1,262144]{1,0:T(1,128)S(1)}, u32[]{:S(2)}) copy-start(f32[1,262144]{1,0:T(1,128)S(1)} %get-tuple-element.5) | copy-start | bytes 3145732
  234.8 11.2 %copy-start.2 = (f32[1,262144]{1,0:T(1,128)}, f32[1,262144]{1,0:T(1,128)S(1)}, u32[]{:S(2)}) copy-start(f32[1,262144]{1,0:T(1,128)S(1)} %get-tuple-element.6) | copy-start | bytes 3145732
  254.3 0.7 copy-start.5
Sparse Core Ops, SparseCore 0:
  27.2 198.7 all-reduce.4
  254.5 264.0 all-reduce.6
where the time goes:
time: 529 us; the launch traced here: 528 us
  waiting for transfers between devices  460 us (87%)
  other arithmetic  41.3 us (8%)
  between operations  14.8 us (3%)
  local copies, waits for them, and re-layouts  12.2 us (2%)
    unnamed x4, waiting for transfers between devices  460 us
    convert_element_type x1, other arithmetic, per_device(): flat_grad.astype(jnp.float32)  19.8 us
  transfers between devices with their start and end apart: 2, of which 2 were waited for; matrix products, arithmetic and copies ran while one was open for 0% of the time, Pallas kernels for 0%

commit v1 on v0

v1 whole, which is shorter than its diff:
```python
import functools

import jax
import jax.numpy as jnp
from jax import lax
from jax.experimental import pallas as pl
from jax.experimental.pallas import tpu as pltpu
from jax.sharding import PartitionSpec as P

STEP = 10
X, Y, C = 2, 4, 2
G = 8
ROWS = 256
LANES = 128
SHARD = G * ROWS * LANES
CHUNKS = ((0, 64, False), (64, 64, False), (128, 64, False), (192, 64, True))
VMEM = 16 * 2**20


def dp_index(x, y, c):
    return (x * Y + y) * C + c


def dp_perm(move):
    return [
        (dp_index(x, y, c), dp_index(*move(x, y, c)))
        for x in range(X)
        for y in range(Y)
        for c in range(C)
    ]


CORE_SWAP = dp_perm(lambda x, y, c: (x, y, 1 - c))
X_SWAP = dp_perm(lambda x, y, c: (1 - x, y, c))
Y_RING = dp_perm(lambda x, y, c: (x, (y + (1 if c == 0 else -1)) % Y, c))


def params():
    return pltpu.CompilerParams(vmem_limit_bytes=VMEM)


def grad_specs(rows, chunk):
    return [
        pl.BlockSpec(
            (1, 1, rows * LANES),
            lambda i, t, j=j: (0, 0, (t[i] * G + j) * (ROWS // rows) + chunk),
        )
        for j in range(G)
    ]


def widen_kernel(rows, t, *refs):
    out = refs[-1]
    for j in range(G):
        out[0, j] = refs[j][0].astype(jnp.float32).reshape(rows, LANES)


def widen(grad, table, start, rows):
    return pl.pallas_call(
        functools.partial(widen_kernel, rows),
        grid_spec=pltpu.PrefetchScalarGridSpec(
            num_scalar_prefetch=1,
            grid=(X * Y,),
            in_specs=grad_specs(rows, start // rows),
            out_specs=pl.BlockSpec((1, G, rows, LANES), lambda i, t: (i, 0, 0, 0)),
        ),
        out_shape=jax.ShapeDtypeStruct((X * Y, G, rows, LANES), jnp.float32),
        compiler_params=params(),
    )(table, *[grad] * G)


def add_kernel(rows, each, t, *refs):
    got = refs[G]
    outs = refs[G + 1 :]
    step = pl.program_id(0)
    for n, out in enumerate(outs):

        @pl.when(step // each == n)
        def _():
            for j in range(G):
                out[0, j] = refs[j][0].astype(jnp.float32).reshape(rows, LANES) + got[0, j]


def add_core(grad, got, table, start, rows, parts):
    each = X * Y // parts
    return pl.pallas_call(
        functools.partial(add_kernel, rows, each),
        grid_spec=pltpu.PrefetchScalarGridSpec(
            num_scalar_prefetch=1,
            grid=(X * Y,),
            in_specs=grad_specs(rows, start // rows)
            + [pl.BlockSpec((1, G, rows, LANES), lambda i, t: (i, 0, 0, 0))],
            out_specs=[
                pl.BlockSpec(
                    (1, G, rows, LANES),
                    lambda i, t, n=n: (jnp.clip(i - n * each, 0, each - 1), 0, 0, 0),
                )
                for n in range(parts)
            ],
        ),
        out_shape=[jax.ShapeDtypeStruct((each, G, rows, LANES), jnp.float32)] * parts,
        compiler_params=params(),
    )(table, *[grad] * G, got)


def adam_kernel(terms, holder, *refs):
    parts, rest = refs[:terms], refs[terms:]
    master, first, second = rest[:3]
    new_master, new_first, new_second, ordered = rest[-4:]
    for j in range(G):
        grad = parts[0][0, j]
        for part in parts[1:]:
            grad = grad + part[0, j]
        old = master[j]
        m = 0.9 * first[j] + 0.1 * grad
        v = 0.95 * second[j] + 0.05 * grad * grad
        first_hat = m / (1.0 - 0.9**STEP)
        second_hat = v / (1.0 - 0.95**STEP)
        w = old - 0.01 * (first_hat / (jnp.sqrt(second_hat) + 1e-08) + 0.1 * old)
        new_master[j] = w
        new_first[j] = m
        new_second[j] = v
        to = holder[j]
        ordered[to, 0] = w
        ordered[to, 1] = m
        ordered[to, 2] = v


def adam(parts, state, done, holder, start, rows):
    chunk = start // rows
    block = pl.BlockSpec((G, rows, LANES), lambda i, h: (0, chunk, 0))
    term = pl.BlockSpec((1, G, rows, LANES), lambda i, h: (0, 0, 0, 0))
    whole = jax.ShapeDtypeStruct((G, ROWS, LANES), jnp.float32)
    held = list(done or ())
    first_alias = 1 + len(parts) + 3
    return pl.pallas_call(
        functools.partial(adam_kernel, len(parts)),
        grid_spec=pltpu.PrefetchScalarGridSpec(
            num_scalar_prefetch=1,
            grid=(1,),
            in_specs=[term] * len(parts) + [block] * 3 + [pl.BlockSpec(memory_space=pl.ANY)] * len(held),
            out_specs=[block] * 3 + [pl.BlockSpec((G, 3, rows, LANES), lambda i, h: (0, 0, 0, 0))],
        ),
        out_shape=[whole] * 3 + [jax.ShapeDtypeStruct((G, 3, rows, LANES), jnp.float32)],
        input_output_aliases={first_alias + n: n for n in range(len(held))},
        compiler_params=params(),
    )(holder, *parts, *state, *held)


def parity_kernel(coeff, got, *refs):
    out = refs[-1]
    for s in range(3):
        terms = [got[g, s] for g in range(G)]
        for k in range(2):
            total = coeff[k, 0] * terms[0]
            for g in range(1, G):
                total = total + coeff[k, g] * terms[g]
            out[k, s] = total


def parity(got, coeff, done, start, rows):
    chunk = start // rows
    held = [] if done is None else [done]
    return pl.pallas_call(
        parity_kernel,
        grid_spec=pltpu.PrefetchScalarGridSpec(
            num_scalar_prefetch=1,
            grid=(1,),
            in_specs=[pl.BlockSpec((G, 3, rows, LANES), lambda i, c: (0, 0, 0, 0))]
            + [pl.BlockSpec(memory_space=pl.ANY)] * len(held),
            out_specs=pl.BlockSpec((2, 3, rows, LANES), lambda i, c: (0, 0, chunk, 0)),
        ),
        out_shape=jax.ShapeDtypeStruct((2, 3, ROWS, LANES), jnp.float32),
        input_output_aliases={2: 0} if held else {},
        compiler_params=params(),
    )(coeff, got, *held)


def per_device(
    grad_parts, master_weights, first_moment, second_moment, cauchy_points, parity_holder
):
    index = lax.axis_index("dp")
    core, y, x = index % C, (index // C) % Y, index // (C * Y)
    holder = parity_holder.reshape(G)
    state = [a.reshape(G, ROWS, LANES) for a in (master_weights, first_moment, second_moment)]
    points = cauchy_points.astype(jnp.float32)
    coeff = 1.0 / (points[:2][:, None] + points[2:][None, :])

    def table(of_core, x_first):
        way = 1 - 2 * of_core
        steps = jnp.arange(1, Y + 1, dtype=jnp.int32)
        ys = (y - steps * way) % Y
        if x_first:
            xs = jnp.stack([1 - x, x])
            return (((xs[:, None] * Y + ys[None, :]) * C) + of_core).reshape(X * Y)
        xs = jnp.stack([x, 1 - x])
        return (((xs[None, :] * Y + ys[:, None]) * C) + of_core).reshape(X * Y)

    sends = {f: table(1 - core, f).astype(jnp.int32) for f in (False, True)}
    keeps = {f: table(core, f).astype(jnp.int32) for f in (False, True)}

    wide = [widen(grad_parts, sends[f], s, r) for s, r, f in CHUNKS]
    got = [lax.ppermute(w, "dp", CORE_SWAP) for w in wide]
    done, shards = None, None
    for (start, rows, x_first), theirs in zip(CHUNKS, got):
        sums = add_core(grad_parts, theirs, keeps[x_first], start, rows, 2 if x_first else Y)
        if x_first:
            across = lax.ppermute(sums[0], "dp", X_SWAP)
            sums = [sums[1][i : i + 1] + across[i : i + 1] for i in range(Y)]
        running = sums[0]
        for i in range(1, Y):
            running = lax.ppermute(running, "dp", Y_RING)
            if i < Y - 1:
                running = running + sums[i]
        parts = [running, sums[Y - 1]]
        if not x_first:
            parts.append(lax.ppermute(running[1:] + sums[Y - 1][1:], "dp", X_SWAP))
        *done, ordered = adam(parts, state, done, holder, start, rows)
        members = lax.all_to_all(ordered, "group", 0, 0)
        shards = parity(members, coeff, shards, start, rows)
    outs = [a.reshape(1, SHARD) for a in done]
    return (*outs, shards.reshape(1, 1, 2, 3, ROWS * LANES))


def solution(mesh):
    in_specs = (
        P("dp", "group", None),
        P("group", "dp"),
        P("group", "dp"),
        P("group", "dp"),
        P(),
        P("dp", None),
    )
    out_specs = (
        P("group", "dp"),
        P("group", "dp"),
        P("group", "dp"),
        P("dp", "group", None, None, None),
    )
    return jax.shard_map(
        per_device, mesh=mesh, in_specs=in_specs, out_specs=out_specs, check_vma=False
    )
```

time: 529 us -> 206 us (0.39)
  the two profiles are of different devices: /device:TPU:24 before, /device:TPU:8 now
where the time goes in v1:
time: 206 us; the launch traced here: 205 us
  waiting for transfers between devices  66.4 us (32%)
  Pallas kernels  50.4 us (24%)
  starting transfers between devices  43.7 us (21%)
  local copies, waits for them, and re-layouts  30.9 us (15%)
  other arithmetic  12.9 us (6%)
    ppermute x3, waiting for transfers between devices, per_device(): parts.append(lax.ppermute(running[1:] + sums[Y - 1][1:], 'dp', X_SWAP))  29.1 us
    unnamed x44, local copies, waits for them, and re-layouts  29 us
    ppermute x12, waiting for transfers between devices, per_device(): running = lax.ppermute(running, 'dp', Y_RING)  22.7 us
    all_to_all x4, starting transfers between devices, per_device(): members = lax.all_to_all(ordered, 'group', 0, 0)  20.6 us
    pallas_call x4, Pallas kernels, widen(): pl.pallas_call(functools.partial(widen_kernel, rows), grid_spec=pltpu.Pre...  17.5 us
    pallas_call x4, Pallas kernels, add_core(): pl.pallas_call(functools.partial(add_kernel, rows, each), grid_spec=pltpu...  17.5 us
    all_to_all x4, waiting for transfers between devices, per_device(): members = lax.all_to_all(ordered, 'group', 0, 0)  14.5 us
    ppermute x12, starting transfers between devices, per_device(): running = lax.ppermute(running, 'dp', Y_RING)  12.5 us
  transfers between devices with their start and end apart: 24, of which 12 were waited for; matrix products, arithmetic and copies ran while one was open for 6% of the time, Pallas kernels for 22%

profile of v1, /device:TPU:8, one launch (start us, length us, event | category | flops | bytes accessed | tf_op | source)
XLA Modules:
  0.0 205.2 jit_solution(6083608031458765630)
XLA Ops:
  1.5 5.8 %copy-done = bf16[1,1,4194304]{2,1,0:T(2,128)(2,1)S(1)} copy-done((bf16[1,1,4194304]{2,1,0:T(2,128)(2,1)S(1)}, bf16[1,1,4194304]{2,1,0:T(2,128)(2,1)}, u32[]{:S(2)}) %copy-start) | copy-done | bytes 8388632
  7.3 4.3 %shard_map.99 = f32[8,8,64,128]{3,2,1,0:T(8,128)} custom-call(s32[8]{0:T(128)S(1)} %add.247.t, bf16[1,1,4194304]{2,1,0:T(2,128)(2,1)S(1)} %copy-done, bf16[1,1,4194304]{2,1,0:T(2,128)(2,1)S(1)} %copy-done, bf16[1,1,4194304]{2,1,0:T(2,128)(2,1)S(1)} %copy-done, bf16[1,1,4194304]{2,1,0:T(2,128)(2,1)S(1)} %copy-done, bf16[1,1,4194304]{2,1,0:T(2,128)(2,1)S(1)} %copy-done, ...), custom_call_target="tpu_custom_call" | custom-call | tf_op jit(solution)/shard_map/pallas_call | solution.py:59
  11.6 4.4 %shard_map.97 = f32[8,8,64,128]{3,2,1,0:T(8,128)} custom-call(s32[8]{0:T(128)S(1)} %add.247.t, bf16[1,1,4194304]{2,1,0:T(2,128)(2,1)S(1)} %copy-done, bf16[1,1,4194304]{2,1,0:T(2,128)(2,1)S(1)} %copy-done, bf16[1,1,4194304]{2,1,0:T(2,128)(2,1)S(1)} %copy-done, bf16[1,1,4194304]{2,1,0:T(2,128)(2,1)S(1)} %copy-done, bf16[1,1,4194304]{2,1,0:T(2,128)(2,1)S(1)} %copy-done, ...), custom_call_target="tpu_custom_call" | custom-call | tf_op jit(solution)/shard_map/pallas_call | solution.py:59
  16.5 4.4 %shard_map.95 = f32[8,8,64,128]{3,2,1,0:T(8,128)} custom-call(s32[8]{0:T(128)S(1)} %add.247.t, bf16[1,1,4194304]{2,1,0:T(2,128)(2,1)S(1)} %copy-done, bf16[1,1,4194304]{2,1,0:T(2,128)(2,1)S(1)} %copy-done, bf16[1,1,4194304]{2,1,0:T(2,128)(2,1)S(1)} %copy-done, bf16[1,1,4194304]{2,1,0:T(2,128)(2,1)S(1)} %copy-done, bf16[1,1,4194304]{2,1,0:T(2,128)(2,1)S(1)} %copy-done, ...), custom_call_target="tpu_custom_call" | custom-call | tf_op jit(solution)/shard_map/pallas_call | solution.py:59
  21.0 5.8 %copy-done.1 = bf16[1,1,4194304]{2,1,0:T(2,128)(2,1)S(1)} copy-done((bf16[1,1,4194304]{2,1,0:T(2,128)(2,1)S(1)}, bf16[1,1,4194304]{2,1,0:T(2,128)(2,1)}, u32[]{:S(2)}) %copy-start.1) | copy-done | bytes 8388632
  26.8 4.4 %shard_map.93 = f32[8,8,64,128]{3,2,1,0:T(8,128)} custom-call(s32[8]{0:T(128)S(1)} %add.230.t, bf16[1,1,4194304]{2,1,0:T(2,128)(2,1)S(1)} %copy-done.1, bf16[1,1,4194304]{2,1,0:T(2,128)(2,1)S(1)} %copy-done.1, bf16[1,1,4194304]{2,1,0:T(2,128)(2,1)S(1)} %copy-done.1, bf16[1,1,4194304]{2,1,0:T(2,128)(2,1)S(1)} %copy-done.1, ...), custom_call_target="tpu_custom_call" | custom-call | tf_op jit(solution)/shard_map/pallas_call | solution.py:59
  31.8 5.8 %copy-done.2 = bf16[1,1,4194304]{2,1,0:T(2,128)(2,1)S(1)} copy-done((bf16[1,1,4194304]{2,1,0:T(2,128)(2,1)S(1)}, bf16[1,1,4194304]{2,1,0:T(2,128)(2,1)}, u32[]{:S(2)}) %copy-start.2) | copy-done | bytes 8388632
  37.6 4.8 %shard_map.100 = (f32[2,8,64,128]{3,2,1,0:T(8,128)S(1)}, f32[2,8,64,128]{3,2,1,0:T(8,128)S(1)}, f32[2,8,64,128]{3,2,1,0:T(8,128)S(1)}, f32[2,8,64,128]{3,2,1,0:T(8,128)S(1)}) custom-call(s32[8]{0:T(128)S(1)} %add.242.t, bf16[1,1,4194304]{2,1,0:T(2,128)(2,1)S(1)} %copy-done.2, bf16[1,1,4194304]{2,1,0:T(2,128)(2,1)S(1)} %copy-done.2, ...), custom_call_target="tpu_custom_call" | custom-call | tf_op jit(solution)/shard_map/pallas_call | solution.py:86
  44.8 4.8 %shard_map.98 = (f32[2,8,64,128]{3,2,1,0:T(8,128)S(1)}, f32[2,8,64,128]{3,2,1,0:T(8,128)S(1)}, f32[2,8,64,128]{3,2,1,0:T(8,128)S(1)}, f32[2,8,64,128]{3,2,1,0:T(8,128)S(1)}) custom-call(s32[8]{0:T(128)S(1)} %add.242.t, bf16[1,1,4194304]{2,1,0:T(2,128)(2,1)S(1)} %copy-done.2, bf16[1,1,4194304]{2,1,0:T(2,128)(2,1)S(1)} %copy-done.2, ...), custom_call_target="tpu_custom_call" | custom-call | tf_op jit(solution)/shard_map/pallas_call | solution.py:86
  54.1 4.8 %collective-permute-done.11 = f32[2,8,64,128]{3,2,1,0:T(8,128)S(1)} collective-permute-done((f32[2,8,64,128]{3,2,1,0:T(8,128)S(1)}, f32[2,8,64,128]{3,2,1,0:T(8,128)S(1)}, u32[]{:S(2)}, u32[]{:S(2)}) %collective-permute-start.11) | collective-permute-done | bytes 524320 | tf_op jit(solution)/shard_map/ppermute | solution.py:212
  60.3 4.2 %collective-permute-done.17 = f32[2,8,64,128]{3,2,1,0:T(8,128)S(1)} collective-permute-done((f32[2,8,64,128]{3,2,1,0:T(8,128)S(1)}, f32[2,8,64,128]{3,2,1,0:T(8,128)S(1)}, u32[]{:S(2)}, u32[]{:S(2)}) %collective-permute-start.17) | collective-permute-done | bytes 524320 | tf_op jit(solution)/shard_map/ppermute | solution.py:212
  66.7 3.5 %collective-permute-done.12 = f32[2,8,64,128]{3,2,1,0:T(8,128)S(1)} collective-permute-done((f32[2,8,64,128]{3,2,1,0:T(8,128)S(1)}, f32[2,8,64,128]{3,2,1,0:T(8,128)S(1)}, u32[]{:S(2)}, u32[]{:S(2)}) %collective-permute-start.12) | collective-permute-done | bytes 524320 | tf_op jit(solution)/shard_map/ppermute | solution.py:212
  72.4 5.8 %copy-done.3 = bf16[1,1,4194304]{2,1,0:T(2,128)(2,1)S(1)} copy-done((bf16[1,1,4194304]{2,1,0:T(2,128)(2,1)S(1)}, bf16[1,1,4194304]{2,1,0:T(2,128)(2,1)}, u32[]{:S(2)}) %copy-start.3) | copy-done | bytes 8388632
  81.9 6.3 %shard_map.94 = (f32[4,8,64,128]{3,2,1,0:T(8,128)}, f32[4,8,64,128]{3,2,1,0:T(8,128)S(1)}) custom-call(s32[8]{0:T(128)S(1)} %add.224.t, bf16[1,1,4194304]{2,1,0:T(2,128)(2,1)S(1)} %copy-done.3, bf16[1,1,4194304]{2,1,0:T(2,128)(2,1)S(1)} %copy-done.3, bf16[1,1,4194304]{2,1,0:T(2,128)(2,1)S(1)} %copy-done.3, bf16[1,1,4194304]{2,1,0:T(2,128)(2,1)S(1)} %copy-done.3, ...), custom_call_target="tpu_custom_call" | custom-call | tf_op jit(solution)/shard_map/pallas_call | solution.py:86
  88.2 3.1 %collective-permute-start.1 = (f32[4,8,64,128]{3,2,1,0:T(8,128)}, f32[4,8,64,128]{3,2,1,0:T(8,128)}, u32[]{:S(2)}, u32[]{:S(2)}) collective-permute-start(f32[4,8,64,128]{3,2,1,0:T(8,128)} %get-tuple-element.35), channel_id=1, source_target_pairs={{0,64},{8,72},{16,80},{24,88},{32,96},{40,104},{48,112},{56,120},{... | collective-permute-start | bytes 3145736 | tf_op jit(solution)/shard_map/ppermute | solution.py:208
  94.6 2.4 %collective-permute-start.14 = (f32[1,8,64,128]{3,2,1,0:T(8,128)S(1)}, f32[1,8,64,128]{3,2,1,0:T(8,128)S(1)}, u32[]{:S(2)}, u32[]{:S(2)}) collective-permute-start(f32[1,8,64,128]{3,2,1,0:T(8,128)S(1)} %slice_add_fusion.1), channel_id=1, source_target_pairs={{0,64},{8,72},{16,80},{24,88},{32,96},{40,104},{48,112},{56,120},{... | collective-permute-start | bytes 786440 | tf_op jit(solution)/shard_map/ppermute | solution.py:217
  98.0 2.3 %collective-permute-start.7 = (f32[2,8,64,128]{3,2,1,0:T(8,128)}, f32[2,8,64,128]{3,2,1,0:T(8,128)}, u32[]{:S(2)}, u32[]{:S(2)}) collective-permute-start(f32[2,8,64,128]{3,2,1,0:T(8,128)} %add.248), channel_id=1, source_target_pairs={{0,16},{8,56},{16,32},{24,8},{32,48},{40,24},{48,0},{56,40},{64,80... | collective-permute-start | bytes 1572872 | tf_op jit(solution)/shard_map/ppermute | solution.py:212
  100.3 21.4 %collective-permute-done.19.refs_2_ = f32[1,8,64,128]{3,2,1,0:T(8,128)S(1)} collective-permute-done((f32[1,8,64,128]{3,2,1,0:T(8,128)S(1)}, f32[1,8,64,128]{3,2,1,0:T(8,128)S(1)}, u32[]{:S(2)}, u32[]{:S(2)}) %collective-permute-start.19) | collective-permute-done | bytes 262176 | tf_op jit(solution)/shard_map/ppermute | solution.py:217
  121.7 2.6 %shard_map.101 = (f32[8,256,128]{2,1,0:T(8,128)}, f32[8,256,128]{2,1,0:T(8,128)}, f32[8,256,128]{2,1,0:T(8,128)}, f32[8,3,64,128]{3,2,1,0:T(8,128)S(1)}) custom-call(s32[8]{0:T(128)S(1)} %bitcast.26, f32[2,8,64,128]{3,2,1,0:T(8,128)} %collective-permute-done.18.refs_0_, f32[2,8,64,128]{3,2,1,0:T(8,128)S(1)} %copy-done.8, ...), custom_call_target="tpu_custom_call" | custom-call | tf_op jit(solution)/shard_map/pallas_call | solution.py:136
  126.4 2.6 %shard_map.102 = (f32[8,256,128]{2,1,0:T(8,128)}, f32[8,256,128]{2,1,0:T(8,128)}, f32[8,256,128]{2,1,0:T(8,128)}, f32[8,3,64,128]{3,2,1,0:T(8,128)S(1)}) custom-call(s32[8]{0:T(128)S(1)} %bitcast.27, f32[2,8,64,128]{3,2,1,0:T(8,128)} %collective-permute-done.13.refs_0_, ...), custom_call_target="tpu_custom_call", output_to_operand_aliasing={{0}: (7, {}), {1}: (8, {}), {2}: (9, {})} | custom-call | tf_op jit(solution)/shard_map/pallas_call | solution.py:136
  129.9 6.2 %all-to-all-start.2 = ((f32[8,3,64,128]{3,2,1,0:T(8,128)}), f32[8,3,64,128]{3,2,1,0:T(8,128)}, u32[]{:S(2)}, u32[]{:S(2)}) async-start(f32[8,3,64,128]{3,2,1,0:T(8,128)} %copy-done.17), calls=%async_computation.2 | async-start | bytes 1572864 | tf_op jit(solution)/shard_map/all_to_all | solution.py:219
  136.2 2.1 %add.249 = f32[2,8,64,128]{3,2,1,0:T(8,128)} add(f32[2,8,64,128]{3,2,1,0:T(8,128)} %collective-permute-done.7, f32[2,8,64,128]{3,2,1,0:T(8,128)} %copy-done.18) | non-fusion elementwise | flops 131072 | bytes 1572864 | tf_op jit(solution)/shard_map/add | solution.py:214
  139.1 9.5 %all-to-all-done.2.got = f32[8,3,64,128]{3,2,1,0:T(8,128)} async-done(((f32[8,3,64,128]{3,2,1,0:T(8,128)}), f32[8,3,64,128]{3,2,1,0:T(8,128)}, u32[]{:S(2)}, u32[]{:S(2)}) %all-to-all-start.2) | async-done | bytes 786464 | tf_op jit(solution)/shard_map/all_to_all | solution.py:219
  148.6 4.2 %all-to-all-start.3 = ((f32[8,3,64,128]{3,2,1,0:T(8,128)}), f32[8,3,64,128]{3,2,1,0:T(8,128)}, u32[]{:S(2)}, u32[]{:S(2)}) async-start(f32[8,3,64,128]{3,2,1,0:T(8,128)} %copy-done.14), calls=%async_computation.3 | async-start | bytes 1572864 | tf_op jit(solution)/shard_map/all_to_all | solution.py:219
  155.2 2.8 %collective-permute-start.9 = (f32[1,8,64,128]{3,2,1,0:T(8,128)S(1)}, f32[1,8,64,128]{3,2,1,0:T(8,128)S(1)}, u32[]{:S(2)}, u32[]{:S(2)}) collective-permute-start(f32[1,8,64,128]{3,2,1,0:T(8,128)S(1)} %slice_add_fusion.2), channel_id=1, source_target_pairs={{0,64},{8,72},{16,80},{24,88},{32,96},{40,104},{48,112},{56,120},{... | collective-permute-start | bytes 786440 | tf_op jit(solution)/shard_map/ppermute | solution.py:217
  158.0 2.5 %collective-permute-done.2 = f32[1,8,64,128]{3,2,1,0:T(8,128)S(1)} collective-permute-done((f32[1,8,64,128]{3,2,1,0:T(8,128)S(1)}, f32[1,8,64,128]{3,2,1,0:T(8,128)S(1)}, u32[]{:S(2)}, u32[]{:S(2)}) %collective-permute-start.2) | collective-permute-done | bytes 262176 | tf_op jit(solution)/shard_map/ppermute | solution.py:212
  162.2 6.5 %collective-permute-done.9.refs_2_ = f32[1,8,64,128]{3,2,1,0:T(8,128)S(1)} collective-permute-done((f32[1,8,64,128]{3,2,1,0:T(8,128)S(1)}, f32[1,8,64,128]{3,2,1,0:T(8,128)S(1)}, u32[]{:S(2)}, u32[]{:S(2)}) %collective-permute-start.9) | collective-permute-done | bytes 262176 | tf_op jit(solution)/shard_map/ppermute | solution.py:217
  168.8 2.6 %shard_map.103 = (f32[8,256,128]{2,1,0:T(8,128)}, f32[8,256,128]{2,1,0:T(8,128)}, f32[8,256,128]{2,1,0:T(8,128)}, f32[8,3,64,128]{3,2,1,0:T(8,128)S(1)}) custom-call(s32[8]{0:T(128)S(1)} %bitcast.28, f32[2,8,64,128]{3,2,1,0:T(8,128)} %collective-permute-done.8.refs_0_, ...), custom_call_target="tpu_custom_call", output_to_operand_aliasing={{0}: (7, {}), {1}: (8, {}), {2}: (9, {})} | custom-call | tf_op jit(solution)/shard_map/pallas_call | solution.py:136
  172.3 4.8 %all-to-all-start.1 = ((f32[8,3,64,128]{3,2,1,0:T(8,128)}), f32[8,3,64,128]{3,2,1,0:T(8,128)}, u32[]{:S(2)}, u32[]{:S(2)}) async-start(f32[8,3,64,128]{3,2,1,0:T(8,128)} %copy-done.15), calls=%async_computation.1 | async-start | bytes 1572864 | tf_op jit(solution)/shard_map/all_to_all | solution.py:219
  178.4 6.4 %collective-permute-done.4.refs_0_ = f32[1,8,64,128]{3,2,1,0:T(8,128)S(1)} collective-permute-done((f32[1,8,64,128]{3,2,1,0:T(8,128)S(1)}, f32[1,8,64,128]{3,2,1,0:T(8,128)S(1)}, u32[]{:S(2)}, u32[]{:S(2)}) %collective-permute-start.4) | collective-permute-done | bytes 262176 | tf_op jit(solution)/shard_map/ppermute | solution.py:212
  187.7 5.3 %all-to-all-start = ((f32[8,3,64,128]{3,2,1,0:T(8,128)}), f32[8,3,64,128]{3,2,1,0:T(8,128)S(1)}, u32[]{:S(2)}, u32[]{:S(2)}) async-start(f32[8,3,64,128]{3,2,1,0:T(8,128)} %copy-done.16), calls=%async_computation | async-start | bytes 1572864 | tf_op jit(solution)/shard_map/all_to_all | solution.py:219
  198.5 4.6 %all-to-all-done.got = f32[8,3,64,128]{3,2,1,0:T(8,128)S(1)} async-done(((f32[8,3,64,128]{3,2,1,0:T(8,128)}), f32[8,3,64,128]{3,2,1,0:T(8,128)S(1)}, u32[]{:S(2)}, u32[]{:S(2)}) %all-to-all-start) | async-done | bytes 786464 | tf_op jit(solution)/shard_map/all_to_all | solution.py:219
  (101 shorter events, 43.4 us)
Async XLA Ops:
  11.6 20.2 %collective-permute-start.15 = (f32[8,8,64,128]{3,2,1,0:T(8,128)}, f32[8,8,64,128]{3,2,1,0:T(8,128)}, u32[]{:S(2)}, u32[]{:S(2)}) collective-permute-start(f32[8,8,64,128]{3,2,1,0:T(8,128)} %shard_map.99), channel_id=1, source_target_pairs={{0,8},{8,0},{16,24},{24,16},{32,40},{40,32},{48,56},{56,48},{64,72... | collective-permute-start | bytes 6291464 | tf_op jit(solution)/shard_map/ppermute | solution.py:203
  16.0 28.8 %collective-permute-start.10 = (f32[8,8,64,128]{3,2,1,0:T(8,128)}, f32[8,8,64,128]{3,2,1,0:T(8,128)}, u32[]{:S(2)}, u32[]{:S(2)}) collective-permute-start(f32[8,8,64,128]{3,2,1,0:T(8,128)} %shard_map.97), channel_id=1, source_target_pairs={{0,8},{8,0},{16,24},{24,16},{32,40},{40,32},{48,56},{56,48},{64,72... | collective-permute-start | bytes 6291464 | tf_op jit(solution)/shard_map/ppermute | solution.py:203
  20.9 51.5 %collective-permute-start.5 = (f32[8,8,64,128]{3,2,1,0:T(8,128)}, f32[8,8,64,128]{3,2,1,0:T(8,128)S(1)}, u32[]{:S(2)}, u32[]{:S(2)}) collective-permute-start(f32[8,8,64,128]{3,2,1,0:T(8,128)} %shard_map.95), channel_id=1, source_target_pairs={{0,8},{8,0},{16,24},{24,16},{32,40},{40,32},{48,56},{56,48},{64,72... | collective-permute-start | bytes 6291464 | tf_op jit(solution)/shard_map/ppermute | solution.py:203
  31.2 50.7 %collective-permute-start = (f32[8,8,64,128]{3,2,1,0:T(8,128)}, f32[8,8,64,128]{3,2,1,0:T(8,128)}, u32[]{:S(2)}, u32[]{:S(2)}) collective-permute-start(f32[8,8,64,128]{3,2,1,0:T(8,128)} %shard_map.93), channel_id=1, source_target_pairs={{0,8},{8,0},{16,24},{24,16},{32,40},{40,32},{48,56},{56,48},{64,72... | collective-permute-start | bytes 6291464 | tf_op jit(solution)/shard_map/ppermute | solution.py:203
  43.2 9.2 %collective-permute-start.16 = (f32[2,8,64,128]{3,2,1,0:T(8,128)S(1)}, f32[2,8,64,128]{3,2,1,0:T(8,128)S(1)}, u32[]{:S(2)}, u32[]{:S(2)}) collective-permute-start(f32[2,8,64,128]{3,2,1,0:T(8,128)S(1)} %get-tuple-element.44), channel_id=1, source_target_pairs={{0,16},{8,56},{16,32},{24,8},{32,48},{40,24},{48,0},{56,40},{64,80... | collective-permute-start | bytes 1572872 | tf_op jit(solution)/shard_map/ppermute | solution.py:212
  49.6 15.7 %copy-start.11 = (f32[2,8,64,128]{3,2,1,0:T(8,128)}, f32[2,8,64,128]{3,2,1,0:T(8,128)S(1)}, u32[]{:S(2)}) copy-start(f32[2,8,64,128]{3,2,1,0:T(8,128)S(1)} %get-tuple-element.43.refs_1_) | copy-start | bytes 1572868
  49.6 9.2 %collective-permute-start.11 = (f32[2,8,64,128]{3,2,1,0:T(8,128)S(1)}, f32[2,8,64,128]{3,2,1,0:T(8,128)S(1)}, u32[]{:S(2)}, u32[]{:S(2)}) collective-permute-start(f32[2,8,64,128]{3,2,1,0:T(8,128)S(1)} %get-tuple-element.40), channel_id=1, source_target_pairs={{0,16},{8,56},{16,32},{24,8},{32,48},{40,24},{48,0},{56,40},{64,80... | collective-permute-start | bytes 1572872 | tf_op jit(solution)/shard_map/ppermute | solution.py:212
  52.5 12.1 %collective-permute-start.17 = (f32[2,8,64,128]{3,2,1,0:T(8,128)S(1)}, f32[2,8,64,128]{3,2,1,0:T(8,128)S(1)}, u32[]{:S(2)}, u32[]{:S(2)}) collective-permute-start(f32[2,8,64,128]{3,2,1,0:T(8,128)S(1)} %add.254), channel_id=1, source_target_pairs={{0,16},{8,56},{16,32},{24,8},{32,48},{40,24},{48,0},{56,40},{64,80... | collective-permute-start | bytes 1572872 | tf_op jit(solution)/shard_map/ppermute | solution.py:212
  59.0 11.2 %collective-permute-start.12 = (f32[2,8,64,128]{3,2,1,0:T(8,128)S(1)}, f32[2,8,64,128]{3,2,1,0:T(8,128)S(1)}, u32[]{:S(2)}, u32[]{:S(2)}) collective-permute-start(f32[2,8,64,128]{3,2,1,0:T(8,128)S(1)} %add.251), channel_id=1, source_target_pairs={{0,16},{8,56},{16,32},{24,8},{32,48},{40,24},{48,0},{56,40},{64,80... | collective-permute-start | bytes 1572872 | tf_op jit(solution)/shard_map/ppermute | solution.py:212
  65.4 26.0 %collective-permute-start.18 = (f32[2,8,64,128]{3,2,1,0:T(8,128)}, f32[2,8,64,128]{3,2,1,0:T(8,128)}, u32[]{:S(2)}, u32[]{:S(2)}) collective-permute-start(f32[2,8,64,128]{3,2,1,0:T(8,128)} %add.255), channel_id=1, source_target_pairs={{0,16},{8,56},{16,32},{24,8},{32,48},{40,24},{48,0},{56,40},{64,80... | collective-permute-start | bytes 1572872 | tf_op jit(solution)/shard_map/ppermute | solution.py:212
  71.0 22.6 %collective-permute-start.13 = (f32[2,8,64,128]{3,2,1,0:T(8,128)}, f32[2,8,64,128]{3,2,1,0:T(8,128)}, u32[]{:S(2)}, u32[]{:S(2)}) collective-permute-start(f32[2,8,64,128]{3,2,1,0:T(8,128)} %add.252), channel_id=1, source_target_pairs={{0,16},{8,56},{16,32},{24,8},{32,48},{40,24},{48,0},{56,40},{64,80... | collective-permute-start | bytes 1572872 | tf_op jit(solution)/shard_map/ppermute | solution.py:212
  81.2 12.4 %copy-start.12 = (f32[2,8,64,128]{3,2,1,0:T(8,128)S(1)}, f32[2,8,64,128]{3,2,1,0:T(8,128)}, u32[]{:S(2)}) copy-start(f32[2,8,64,128]{3,2,1,0:T(8,128)} %copy-done.11) | copy-start | bytes 1572868
  81.2 15.8 %collective-permute-start.6 = (f32[2,8,64,128]{3,2,1,0:T(8,128)S(1)}, f32[2,8,64,128]{3,2,1,0:T(8,128)S(1)}, u32[]{:S(2)}, u32[]{:S(2)}) collective-permute-start(f32[2,8,64,128]{3,2,1,0:T(8,128)S(1)} %get-tuple-element.36), channel_id=1, source_target_pairs={{0,16},{8,56},{16,32},{24,8},{32,48},{40,24},{48,0},{56,40},{64,80... | collective-permute-start | bytes 1572872 | tf_op jit(solution)/shard_map/ppermute | solution.py:212
  88.2 36.1 %copy-start.13 = (f32[4,8,64,128]{3,2,1,0:T(8,128)}, f32[4,8,64,128]{3,2,1,0:T(8,128)S(1)}, u32[]{:S(2)}) copy-start(f32[4,8,64,128]{3,2,1,0:T(8,128)S(1)} %get-tuple-element.34) | copy-start | bytes 3145732
  88.2 33.4 %copy-start.4 = (f32[1,262144]{1,0:T(1,128)S(1)}, f32[1,262144]{1,0:T(1,128)}, u32[]{:S(2)}) copy-start(f32[1,262144]{1,0:T(1,128)} %param.7) | copy-start | bytes 3145732
  88.2 33.4 %copy-start.5 = (f32[1,262144]{1,0:T(1,128)S(1)}, f32[1,262144]{1,0:T(1,128)}, u32[]{:S(2)}) copy-start(f32[1,262144]{1,0:T(1,128)} %param.8) | copy-start | bytes 3145732
  88.2 33.4 %copy-start.6 = (f32[1,262144]{1,0:T(1,128)S(1)}, f32[1,262144]{1,0:T(1,128)}, u32[]{:S(2)}) copy-start(f32[1,262144]{1,0:T(1,128)} %param.9) | copy-start | bytes 3145732
  88.2 33.4 %copy-start.19 = (s32[1,8]{1,0:T(1,128)S(1)}, s32[1,8]{1,0:T(1,128)}, u32[]{:S(2)}) copy-start(s32[1,8]{1,0:T(1,128)} %param.11) | copy-start | bytes 100
  88.2 64.7 %collective-permute-start.1 = (f32[4,8,64,128]{3,2,1,0:T(8,128)}, f32[4,8,64,128]{3,2,1,0:T(8,128)}, u32[]{:S(2)}, u32[]{:S(2)}) collective-permute-start(f32[4,8,64,128]{3,2,1,0:T(8,128)} %get-tuple-element.35), channel_id=1, source_target_pairs={{0,64},{8,72},{16,80},{24,88},{32,96},{40,104},{48,112},{56,120},{... | collective-permute-start | bytes 3145736 | tf_op jit(solution)/shard_map/ppermute | solution.py:208
  92.3 29.3 %collective-permute-start.19 = (f32[1,8,64,128]{3,2,1,0:T(8,128)S(1)}, f32[1,8,64,128]{3,2,1,0:T(8,128)S(1)}, u32[]{:S(2)}, u32[]{:S(2)}) collective-permute-start(f32[1,8,64,128]{3,2,1,0:T(8,128)S(1)} %slice_add_fusion), channel_id=1, source_target_pairs={{0,64},{8,72},{16,80},{24,88},{32,96},{40,104},{48,112},{56,120},{... | collective-permute-start | bytes 786440 | tf_op jit(solution)/shard_map/ppermute | solution.py:217
  94.6 31.9 %collective-permute-start.14 = (f32[1,8,64,128]{3,2,1,0:T(8,128)S(1)}, f32[1,8,64,128]{3,2,1,0:T(8,128)S(1)}, u32[]{:S(2)}, u32[]{:S(2)}) collective-permute-start(f32[1,8,64,128]{3,2,1,0:T(8,128)S(1)} %slice_add_fusion.1), channel_id=1, source_target_pairs={{0,64},{8,72},{16,80},{24,88},{32,96},{40,104},{48,112},{56,120},{... | collective-permute-start | bytes 786440 | tf_op jit(solution)/shard_map/ppermute | solution.py:217
  98.0 38.2 %collective-permute-start.7 = (f32[2,8,64,128]{3,2,1,0:T(8,128)}, f32[2,8,64,128]{3,2,1,0:T(8,128)}, u32[]{:S(2)}, u32[]{:S(2)}) collective-permute-start(f32[2,8,64,128]{3,2,1,0:T(8,128)} %add.248), channel_id=1, source_target_pairs={{0,16},{8,56},{16,32},{24,8},{32,48},{40,24},{48,0},{56,40},{64,80... | collective-permute-start | bytes 1572872 | tf_op jit(solution)/shard_map/ppermute | solution.py:212
  129.9 18.7 %all-to-all-start.2 = ((f32[8,3,64,128]{3,2,1,0:T(8,128)}), f32[8,3,64,128]{3,2,1,0:T(8,128)}, u32[]{:S(2)}, u32[]{:S(2)}) async-start(f32[8,3,64,128]{3,2,1,0:T(8,128)} %copy-done.17), calls=%async_computation.2 | async-start | bytes 1572864 | tf_op jit(solution)/shard_map/all_to_all | solution.py:219
  138.2 15.9 %collective-permute-start.8 = (f32[2,8,64,128]{3,2,1,0:T(8,128)}, f32[2,8,64,128]{3,2,1,0:T(8,128)}, u32[]{:S(2)}, u32[]{:S(2)}) collective-permute-start(f32[2,8,64,128]{3,2,1,0:T(8,128)} %add.249), channel_id=1, source_target_pairs={{0,16},{8,56},{16,32},{24,8},{32,48},{40,24},{48,0},{56,40},{64,80... | collective-permute-start | bytes 1572872 | tf_op jit(solution)/shard_map/ppermute | solution.py:212
  148.6 23.6 %all-to-all-start.3 = ((f32[8,3,64,128]{3,2,1,0:T(8,128)}), f32[8,3,64,128]{3,2,1,0:T(8,128)}, u32[]{:S(2)}, u32[]{:S(2)}) async-start(f32[8,3,64,128]{3,2,1,0:T(8,128)} %copy-done.14), calls=%async_computation.3 | async-start | bytes 1572864 | tf_op jit(solution)/shard_map/all_to_all | solution.py:219
  152.9 15.9 %copy-start.10 = (f32[2,8,64,128]{3,2,1,0:T(8,128)S(1)}, f32[2,8,64,128]{3,2,1,0:T(8,128)}, u32[]{:S(2)}) copy-start(f32[2,8,64,128]{3,2,1,0:T(8,128)} %copy-done.9) | copy-start | bytes 1572868
  154.0 6.4 %collective-permute-start.2 = (f32[1,8,64,128]{3,2,1,0:T(8,128)S(1)}, f32[1,8,64,128]{3,2,1,0:T(8,128)S(1)}, u32[]{:S(2)}, u32[]{:S(2)}) collective-permute-start(f32[1,8,64,128]{3,2,1,0:T(8,128)S(1)} %slice_add_fusion.6), channel_id=1, source_target_pairs={{0,16},{8,56},{16,32},{24,8},{32,48},{40,24},{48,0},{56,40},{64,80... | collective-permute-start | bytes 786440 | tf_op jit(solution)/shard_map/ppermute | solution.py:212
  155.2 13.6 %collective-permute-start.9 = (f32[1,8,64,128]{3,2,1,0:T(8,128)S(1)}, f32[1,8,64,128]{3,2,1,0:T(8,128)S(1)}, u32[]{:S(2)}, u32[]{:S(2)}) collective-permute-start(f32[1,8,64,128]{3,2,1,0:T(8,128)S(1)} %slice_add_fusion.2), channel_id=1, source_target_pairs={{0,64},{8,72},{16,80},{24,88},{32,96},{40,104},{48,112},{56,120},{... | collective-permute-start | bytes 786440 | tf_op jit(solution)/shard_map/ppermute | solution.py:217
  162.2 14.8 %collective-permute-start.3 = (f32[1,8,64,128]{3,2,1,0:T(8,128)}, f32[1,8,64,128]{3,2,1,0:T(8,128)S(1)}, u32[]{:S(2)}, u32[]{:S(2)}) collective-permute-start(f32[1,8,64,128]{3,2,1,0:T(8,128)} %fusion.1), channel_id=1, source_target_pairs={{0,16},{8,56},{16,32},{24,8},{32,48},{40,24},{48,0},{56,40},{64,80... | collective-permute-start | bytes 786440 | tf_op jit(solution)/shard_map/ppermute | solution.py:212
  172.3 15.4 %all-to-all-start.1 = ((f32[8,3,64,128]{3,2,1,0:T(8,128)}), f32[8,3,64,128]{3,2,1,0:T(8,128)}, u32[]{:S(2)}, u32[]{:S(2)}) async-start(f32[8,3,64,128]{3,2,1,0:T(8,128)} %copy-done.15), calls=%async_computation.1 | async-start | bytes 1572864 | tf_op jit(solution)/shard_map/all_to_all | solution.py:219
  178.3 6.4 %collective-permute-start.4 = (f32[1,8,64,128]{3,2,1,0:T(8,128)S(1)}, f32[1,8,64,128]{3,2,1,0:T(8,128)S(1)}, u32[]{:S(2)}, u32[]{:S(2)}) collective-permute-start(f32[1,8,64,128]{3,2,1,0:T(8,128)S(1)} %get-tuple-element.69), channel_id=1, source_target_pairs={{0,16},{8,56},{16,32},{24,8},{32,48},{40,24},{48,0},{56,40},{64,80... | collective-permute-start | bytes 786440 | tf_op jit(solution)/shard_map/ppermute | solution.py:212
  187.7 15.4 %all-to-all-start = ((f32[8,3,64,128]{3,2,1,0:T(8,128)}), f32[8,3,64,128]{3,2,1,0:T(8,128)S(1)}, u32[]{:S(2)}, u32[]{:S(2)}) async-start(f32[8,3,64,128]{3,2,1,0:T(8,128)} %copy-done.16), calls=%async_computation | async-start | bytes 1572864 | tf_op jit(solution)/shard_map/all_to_all | solution.py:219
  (14 other events, 52.3 us)

commit v2 on v1

v2 whole, which is shorter than its diff:
```python
import functools

import jax
import jax.numpy as jnp
from jax import lax
from jax.experimental import pallas as pl
from jax.experimental.pallas import tpu as pltpu
from jax.sharding import PartitionSpec as P

STEP = 10
X, Y, C = 2, 4, 2
G = 8
ROWS = 256
LANES = 128
SHARD = G * ROWS * LANES
CHUNKS = ((0, 96, False), (96, 96, False), (192, 64, True))
VMEM = 16 * 2**20


def dp_index(x, y, c):
    return (x * Y + y) * C + c


def dp_perm(move):
    return [
        (dp_index(x, y, c), dp_index(*move(x, y, c)))
        for x in range(X)
        for y in range(Y)
        for c in range(C)
    ]


CORE_SWAP = dp_perm(lambda x, y, c: (x, y, 1 - c))
X_SWAP = dp_perm(lambda x, y, c: (1 - x, y, c))
Y_RING = dp_perm(lambda x, y, c: (x, (y + (1 if c == 0 else -1)) % Y, c))


def params():
    return pltpu.CompilerParams(vmem_limit_bytes=VMEM)


def cost(size):
    return pl.CostEstimate(flops=0, transcendentals=0, bytes_accessed=size // 4096)


def in_hbm(value):
    return pltpu.with_memory_space_constraint(value, pltpu.HBM)


def in_vmem(value):
    return pltpu.with_memory_space_constraint(value, pltpu.VMEM)


def after(value, *others):
    return lax.optimization_barrier((value, *others))[0]


def combine_kernel(rows, start, first, count, offsets, splits, table, grad, *refs):
    terms, refs = refs[: len(offsets)], refs[len(offsets) :]
    outs, (held, sems) = refs[: len(splits)], refs[len(splits) :]
    size = rows * LANES
    copies = [
        pltpu.make_async_copy(
            grad.at[pl.ds(pl.multiple_of(table[first + i] * G, G), G), :, pl.ds(start * LANES, size)],
            held.at[pl.ds(i * G, G)],
            sems.at[i],
        )
        for i in range(count)
    ]
    for copy in copies:
        copy.start()
    places = [(out, i) for out, n in zip(outs, splits) for i in range(n)]
    for i, (copy, (out, at)) in enumerate(zip(copies, places)):
        copy.wait()
        for j in range(G):
            total = held[i * G + j].astype(jnp.float32).reshape(rows, LANES)
            for term, offset in zip(terms, offsets):
                total = total + term[offset + i, j]
            out[at, j] = total


def combine(grad, table, first, splits, terms, start, rows):
    count = sum(splits)
    arrays, offsets = [a for a, _ in terms], tuple(o for _, o in terms)
    return pl.pallas_call(
        functools.partial(combine_kernel, rows, start, first, count, offsets, splits),
        grid_spec=pltpu.PrefetchScalarGridSpec(
            num_scalar_prefetch=1,
            grid=(),
            in_specs=[pl.BlockSpec(memory_space=pl.ANY)]
            + [pl.BlockSpec(memory_space=pltpu.VMEM)] * len(arrays),
            out_specs=[pl.BlockSpec(memory_space=pltpu.VMEM)] * len(splits),
            scratch_shapes=[
                pltpu.VMEM((count * G, 1, rows * LANES), jnp.bfloat16),
                pltpu.SemaphoreType.DMA((count,)),
            ],
        ),
        out_shape=[pltpu.VMEM((n, G, rows, LANES), jnp.float32) for n in splits],
        compiler_params=params(),
        cost_estimate=cost(count * G * rows * LANES * (8 + 4 * len(arrays))),
    )(table, in_hbm(grad), *[in_vmem(a) for a in arrays])


def adam_kernel(terms, rows, start, holder, *refs):
    parts, (master, first, second) = refs[:terms], refs[terms : terms + 3]
    *outs, ordered, fresh, sems = refs[-6:]
    copies = []
    for j in range(G):
        grad = parts[0][0, j]
        for part in parts[1:]:
            grad = grad + part[0, j]
        here = pl.ds(start, rows)
        old = master[j, here]
        m = 0.9 * first[j, here] + 0.1 * grad
        v = 0.95 * second[j, here] + 0.05 * grad * grad
        first_hat = m / (1.0 - 0.9**STEP)
        second_hat = v / (1.0 - 0.95**STEP)
        fresh[j, 0] = old - 0.01 * (first_hat / (jnp.sqrt(second_hat) + 1e-08) + 0.1 * old)
        fresh[j, 1] = m
        fresh[j, 2] = v
        copies.append(pltpu.make_async_copy(fresh.at[j], ordered.at[holder[j]], sems.at[j, 3]))
        for s in range(3):
            copies.append(pltpu.make_async_copy(fresh.at[j, s], outs[s].at[j, here], sems.at[j, s]))
        for copy in copies[-4:]:
            copy.start()
    for copy in copies:
        copy.wait()


def adam(parts, state, done, holder, start, rows):
    whole = jax.ShapeDtypeStruct((G, ROWS, LANES), jnp.float32)
    held = list(done or ())
    first_alias = 1 + len(parts) + 3
    return pl.pallas_call(
        functools.partial(adam_kernel, len(parts), rows, start),
        grid_spec=pltpu.PrefetchScalarGridSpec(
            num_scalar_prefetch=1,
            grid=(),
            in_specs=[pl.BlockSpec(memory_space=pltpu.VMEM)] * (len(parts) + 3)
            + [pl.BlockSpec(memory_space=pl.ANY)] * len(held),
            out_specs=[pl.BlockSpec(memory_space=pl.ANY)] * 4,
            scratch_shapes=[
                pltpu.VMEM((G, 3, rows, LANES), jnp.float32),
                pltpu.SemaphoreType.DMA((G, 4)),
            ],
        ),
        out_shape=[pltpu.HBM(whole.shape, whole.dtype)] * 3
        + [pltpu.HBM((G, 3, rows, LANES), jnp.float32)],
        input_output_aliases={first_alias + n: n for n in range(len(held))},
        compiler_params=params(),
        cost_estimate=cost(G * rows * LANES * 4 * (len(parts) + 9)),
    )(holder, *[in_vmem(a) for a in (*parts, *state)], *[in_hbm(a) for a in held])


def parity_kernel(coeff, got, *refs):
    out = refs[-1]
    for s in range(3):
        terms = [got[g, s] for g in range(G)]
        for k in range(2):
            total = coeff[k, 0] * terms[0]
            for g in range(1, G):
                total = total + coeff[k, g] * terms[g]
            out[s, :, k, :] = total


def parity(got, coeff, done, start, rows):
    chunk = start // rows
    held = [] if done is None else [done]
    return pl.pallas_call(
        parity_kernel,
        grid_spec=pltpu.PrefetchScalarGridSpec(
            num_scalar_prefetch=1,
            grid=(1,),
            in_specs=[pl.BlockSpec((G, 3, rows, LANES), lambda i, c: (0, 0, 0, 0))]
            + [pl.BlockSpec(memory_space=pl.ANY)] * len(held),
            out_specs=pl.BlockSpec((3, rows, 2, LANES), lambda i, c: (0, chunk, 0, 0)),
        ),
        out_shape=jax.ShapeDtypeStruct((3, ROWS, 2, LANES), jnp.float32),
        input_output_aliases={2: 0} if held else {},
        compiler_params=params(),
        cost_estimate=cost(G * 3 * rows * LANES * 6),
    )(coeff, got, *held)


def per_device(
    grad_parts, master_weights, first_moment, second_moment, cauchy_points, parity_holder
):
    index = lax.axis_index("dp")
    core, y, x = index % C, (index // C) % Y, index // (C * Y)
    holder = parity_holder.reshape(G)
    state = [a.reshape(G, ROWS, LANES) for a in (master_weights, first_moment, second_moment)]
    points = cauchy_points.astype(jnp.float32)
    coeff = 1.0 / (points[:2][:, None] + points[2:][None, :])

    def table(of_core, x_first):
        way = 1 - 2 * of_core
        steps = jnp.arange(1, Y + 1, dtype=jnp.int32)
        ys = (y - steps * way) % Y
        if x_first:
            xs = jnp.stack([1 - x, x])
            return (((xs[:, None] * Y + ys[None, :]) * C) + of_core).reshape(X * Y)
        xs = jnp.stack([x, 1 - x])
        return (((xs[None, :] * Y + ys[:, None]) * C) + of_core).reshape(X * Y)

    grad = grad_parts.reshape(X * Y * C * G, 1, ROWS * LANES)
    sends = {f: table(1 - core, f).astype(jnp.int32) for f in (False, True)}
    keeps = {f: table(core, f).astype(jnp.int32) for f in (False, True)}
    got, runs, done, shards = {}, {}, None, None

    def swap_core(n, parts, *earlier):
        start, rows, x_first = CHUNKS[n]
        got.setdefault(n, [])
        first = sum(g.shape[0] for g in got[n])
        wide = combine(grad, after(sends[x_first], *earlier), first, parts, [], start, rows)
        got[n] += [lax.ppermute(w, "dp", CORE_SWAP) for w in wide]
        return wide[-1]

    def ring(n, i, *earlier):
        start, rows, x_first = CHUNKS[n]
        held = after(keeps[x_first], *earlier)
        running = [(runs[n], 0)] if i else []
        if x_first:
            terms = [(got[n][1], i), (across, i), *running]
            (block,) = combine(grad, held, Y + i, (1,), terms, start, rows)
        elif i < Y - 1:
            (block,) = combine(grad, held, X * i, (X,), [(got[n][i], 0), *running], start, rows)
        else:
            own, block = combine(grad, held, X * i, (1, 1), [(got[n][i], 0), *running], start, rows)
            return own, lax.ppermute(block, "dp", X_SWAP)
        if i == Y - 1:
            return [block]
        runs[n] = lax.ppermute(block, "dp", Y_RING)
        return block

    def update(n, parts):
        nonlocal done
        start, rows, _ = CHUNKS[n]
        *done, ordered = adam(parts, state, done, holder, start, rows)
        return lax.all_to_all(ordered, "group", 0, 0)

    def parities(n, members):
        nonlocal shards
        start, rows, _ = CHUNKS[n]
        shards = parity(members, coeff, shards, start, rows)

    w = swap_core(0, (2,))
    w = swap_core(0, (2, 2, 2), w)
    r = ring(0, 0, w)
    w = swap_core(1, (2, 2, 2, 2), r)
    r = ring(1, 0, w)
    r = ring(0, 1, r)
    w = swap_core(2, (4, 4), r)
    r = ring(1, 1, w)
    start, rows, x_first = CHUNKS[2]
    (theirs,) = combine(grad, after(keeps[True], r), 0, (4,), [(got[2][0], 0)], start, rows)
    across = lax.ppermute(theirs, "dp", X_SWAP)
    r = ring(0, 2, theirs)
    r = ring(1, 2, r)
    p0 = ring(0, 3, r)
    r = ring(2, 0, p0[0])
    m0 = update(0, p0)
    r = ring(2, 1, done[0])
    p1 = ring(1, 3, r)
    r = ring(2, 2, p1[0])
    m1 = update(1, p1)
    parities(0, m0)
    p2 = ring(2, 3, shards, done[0])
    m2 = update(2, p2)
    parities(1, m1)
    parities(2, m2)
    outs = [a.reshape(1, SHARD) for a in done]
    return (*outs, shards.transpose(2, 0, 1, 3).reshape(1, 1, 2, 3, ROWS * LANES))


def solution(mesh):
    in_specs = (
        P("dp", "group", None),
        P("group", "dp"),
        P("group", "dp"),
        P("group", "dp"),
        P(),
        P("dp", None),
    )
    out_specs = (
        P("group", "dp"),
        P("group", "dp"),
        P("group", "dp"),
        P("dp", "group", None, None, None),
    )
    return jax.shard_map(
        per_device, mesh=mesh, in_specs=in_specs, out_specs=out_specs, check_vma=False
    )
```

time: 206 us -> 176 us (0.85)
  the two profiles are of different devices: /device:TPU:8 before, /device:TPU:24 now
where the time goes in v2:
time: 176 us; the launch traced here: 175 us
  waiting for transfers between devices  72.7 us (41%)
  Pallas kernels  59.2 us (34%)
  starting transfers between devices  40 us (23%)
    pallas_call x17, Pallas kernels, combine(): pl.pallas_call(functools.partial(combine_kernel, rows, start, first, coun...  45.6 us
    ppermute x9, waiting for transfers between devices, ring(): runs[n] = lax.ppermute(block, 'dp', Y_RING)  35.6 us
    ppermute x2, waiting for transfers between devices, ring(): return (own, lax.ppermute(block, 'dp', X_SWAP))  26.9 us
    all_to_all x3, starting transfers between devices, update(): return lax.all_to_all(ordered, 'group', 0, 0)  17.3 us
    ppermute x9, starting transfers between devices, ring(): runs[n] = lax.ppermute(block, 'dp', Y_RING)  11.5 us
    all_to_all x3, waiting for transfers between devices, update(): return lax.all_to_all(ordered, 'group', 0, 0)  8.93 us
    pallas_call x3, Pallas kernels, parity(): pl.pallas_call(parity_kernel, grid_spec=pltpu.PrefetchScalarGridSpec(num_...  7.11 us
    pallas_call x3, Pallas kernels, adam(): pl.pallas_call(functools.partial(adam_kernel, len(parts), rows, start), g...  6.49 us
  transfers between devices with their start and end apart: 25, of which 11 were waited for; matrix products, arithmetic and copies ran while one was open for 0% of the time, Pallas kernels for 28%

profile of v2, /device:TPU:24, one launch (start us, length us, event | category | flops | bytes accessed | tf_op | source)
XLA Modules:
  0.0 174.7 jit_solution(8333658083222137638)
XLA Ops:
  0.9 2.1 %shard_map.93 = f32[2,8,96,128]{3,2,1,0:T(8,128)S(1)} custom-call(s32[8]{0:T(128)S(1)} %add.199.table, bf16[128,1,32768]{2,1,0:T(2,128)(2,1)} %bitcast.26), custom_call_target="tpu_custom_call" | custom-call | bytes 384 | tf_op jit(solution)/shard_map/pallas_call | solution.py:85
  3.2 4.1 %shard_map.94 = (f32[2,8,96,128]{3,2,1,0:T(8,128)}, f32[2,8,96,128]{3,2,1,0:T(8,128)}, f32[2,8,96,128]{3,2,1,0:T(8,128)S(1)}) custom-call(s32[8]{0:T(128)S(1)} %add.199.table, bf16[128,1,32768]{2,1,0:T(2,128)(2,1)} %bitcast.27), custom_call_target="tpu_custom_call" | custom-call | bytes 1152 | tf_op jit(solution)/shard_map/pallas_call | solution.py:85
  10.0 5.2 %shard_map.96 = (f32[2,8,96,128]{3,2,1,0:T(8,128)}, f32[2,8,96,128]{3,2,1,0:T(8,128)}, f32[2,8,96,128]{3,2,1,0:T(8,128)}, f32[2,8,96,128]{3,2,1,0:T(8,128)}) custom-call(s32[8]{0:T(128)S(1)} %add.199.table, bf16[128,1,32768]{2,1,0:T(2,128)(2,1)} %bitcast.29), custom_call_target="tpu_custom_call" | custom-call | bytes 1536 | tf_op jit(solution)/shard_map/pallas_call | solution.py:85
  18.2 3.8 %shard_map.97 = f32[2,8,96,128]{3,2,1,0:T(8,128)} custom-call(s32[8]{0:T(128)S(1)} %add.188.table, bf16[128,1,32768]{2,1,0:T(2,128)(2,1)} %bitcast.30, f32[2,8,96,128]{3,2,1,0:T(8,128)} %collective-permute-done.1.refs_0_), custom_call_target="tpu_custom_call" | custom-call | bytes 576 | tf_op jit(solution)/shard_map/pallas_call | solution.py:85
  22.0 5.9 %collective-permute-done.3.refs_1_ = f32[2,8,96,128]{3,2,1,0:T(8,128)S(1)} collective-permute-done((f32[2,8,96,128]{3,2,1,0:T(8,128)S(1)}, f32[2,8,96,128]{3,2,1,0:T(8,128)S(1)}, u32[]{:S(2)}, u32[]{:S(2)}) %collective-permute-start.3) | collective-permute-done | bytes 786464 | tf_op jit(solution)/shard_map/ppermute | solution.py:232
  29.6 4.2 %shard_map.99 = (f32[4,8,64,128]{3,2,1,0:T(8,128)}, f32[4,8,64,128]{3,2,1,0:T(8,128)}) custom-call(s32[8]{0:T(128)S(1)} %add.194.table, bf16[128,1,32768]{2,1,0:T(2,128)(2,1)} %bitcast.32), custom_call_target="tpu_custom_call" | custom-call | bytes 1024 | tf_op jit(solution)/shard_map/pallas_call | solution.py:85
  37.5 9.2 %collective-permute-done.5.refs_1_ = f32[2,8,96,128]{3,2,1,0:T(8,128)} collective-permute-done((f32[2,8,96,128]{3,2,1,0:T(8,128)}, f32[2,8,96,128]{3,2,1,0:T(8,128)}, u32[]{:S(2)}, u32[]{:S(2)}) %collective-permute-start.5) | collective-permute-done | bytes 786464 | tf_op jit(solution)/shard_map/ppermute | solution.py:232
  46.8 2.9 %shard_map.100 = f32[2,8,96,128]{3,2,1,0:T(8,128)S(1)} custom-call(s32[8]{0:T(128)S(1)} %add.188.table, bf16[128,1,32768]{2,1,0:T(2,128)(2,1)} %bitcast.33, f32[2,8,96,128]{3,2,1,0:T(8,128)S(1)} %collective-permute-done.4.refs_0_, f32[2,8,96,128]{3,2,1,0:T(8,128)} %collective-permute-done.5.refs_1_), custom_call_target="tpu_custom_call" | custom-call | bytes 768 | tf_op jit(solution)/shard_map/pallas_call | solution.py:85
  49.7 2.1 %collective-permute-start.10 = (f32[2,8,96,128]{3,2,1,0:T(8,128)S(1)}, f32[2,8,96,128]{3,2,1,0:T(8,128)S(1)}, u32[]{:S(2)}, u32[]{:S(2)}) collective-permute-start(f32[2,8,96,128]{3,2,1,0:T(8,128)S(1)} %shard_map.100), channel_id=1, source_target_pairs={{0,16},{8,56},{16,32},{24,8},{32,48},{40,24},{48,0},{56,40},{64,80... | collective-permute-start | bytes 2359304 | tf_op jit(solution)/shard_map/ppermute | solution.py:232
  51.8 2.8 %shard_map.101 = f32[4,8,64,128]{3,2,1,0:T(8,128)} custom-call(s32[8]{0:T(128)S(1)} %add.179.table, bf16[128,1,32768]{2,1,0:T(2,128)(2,1)} %bitcast.34, f32[4,8,64,128]{3,2,1,0:T(8,128)S(1)} %collective-permute-done.6.refs_0_), custom_call_target="tpu_custom_call" | custom-call | bytes 768 | tf_op jit(solution)/shard_map/pallas_call | solution.py:85
  55.1 3.1 %shard_map.102 = f32[2,8,96,128]{3,2,1,0:T(8,128)S(1)} custom-call(s32[8]{0:T(128)S(1)} %add.188.table, bf16[128,1,32768]{2,1,0:T(2,128)(2,1)} %bitcast.35, f32[2,8,96,128]{3,2,1,0:T(8,128)} %collective-permute-done.7.refs_0_, f32[2,8,96,128]{3,2,1,0:T(8,128)} %collective-permute-done.8.refs_1_), custom_call_target="tpu_custom_call" | custom-call | bytes 768 | tf_op jit(solution)/shard_map/pallas_call | solution.py:85
  58.2 2.2 %collective-permute-start.12 = (f32[2,8,96,128]{3,2,1,0:T(8,128)S(1)}, f32[2,8,96,128]{3,2,1,0:T(8,128)S(1)}, u32[]{:S(2)}, u32[]{:S(2)}) collective-permute-start(f32[2,8,96,128]{3,2,1,0:T(8,128)S(1)} %shard_map.102), channel_id=1, source_target_pairs={{0,16},{8,56},{16,32},{24,8},{32,48},{40,24},{48,0},{56,40},{64,80... | collective-permute-start | bytes 2359304 | tf_op jit(solution)/shard_map/ppermute | solution.py:232
  60.5 3.1 %collective-permute-start.15 = (f32[4,8,64,128]{3,2,1,0:T(8,128)}, f32[4,8,64,128]{3,2,1,0:T(8,128)S(1)}, u32[]{:S(2)}, u32[]{:S(2)}) collective-permute-start(f32[4,8,64,128]{3,2,1,0:T(8,128)} %shard_map.101), channel_id=1, source_target_pairs={{0,64},{8,72},{16,80},{24,88},{32,96},{40,104},{48,112},{56,120},{... | collective-permute-start | bytes 3145736 | tf_op jit(solution)/shard_map/ppermute | solution.py:256
  63.6 2.7 %shard_map.103 = f32[2,8,96,128]{3,2,1,0:T(8,128)} custom-call(s32[8]{0:T(128)S(1)} %add.188.table, bf16[128,1,32768]{2,1,0:T(2,128)(2,1)} %bitcast.36, f32[2,8,96,128]{3,2,1,0:T(8,128)S(1)} %collective-permute-done.9.refs_0_, f32[2,8,96,128]{3,2,1,0:T(8,128)S(1)} %collective-permute-done.10.refs_1_), custom_call_target="tpu_custom_call" | custom-call | bytes 768 | tf_op jit(solution)/shard_map/pallas_call | solution.py:85
  66.3 5.5 %collective-permute-done.12.refs_1_ = f32[2,8,96,128]{3,2,1,0:T(8,128)S(1)} collective-permute-done((f32[2,8,96,128]{3,2,1,0:T(8,128)S(1)}, f32[2,8,96,128]{3,2,1,0:T(8,128)S(1)}, u32[]{:S(2)}, u32[]{:S(2)}) %collective-permute-start.12) | collective-permute-done | bytes 786464 | tf_op jit(solution)/shard_map/ppermute | solution.py:232
  73.6 3.1 %collective-permute-start.13 = (f32[1,8,96,128]{3,2,1,0:T(8,128)S(1)}, f32[1,8,96,128]{3,2,1,0:T(8,128)S(1)}, u32[]{:S(2)}, u32[]{:S(2)}) collective-permute-start(f32[1,8,96,128]{3,2,1,0:T(8,128)S(1)} %get-tuple-element.66), channel_id=1, source_target_pairs={{0,64},{8,72},{16,80},{24,88},{32,96},{40,104},{48,112},{56,120},{... | collective-permute-start | bytes 1179656 | tf_op jit(solution)/shard_map/ppermute | solution.py:229
  76.7 2.2 %collective-permute-start.18 = (f32[2,8,96,128]{3,2,1,0:T(8,128)}, f32[2,8,96,128]{3,2,1,0:T(8,128)}, u32[]{:S(2)}, u32[]{:S(2)}) collective-permute-start(f32[2,8,96,128]{3,2,1,0:T(8,128)} %shard_map.103), channel_id=1, source_target_pairs={{0,16},{8,56},{16,32},{24,8},{32,48},{40,24},{48,0},{56,40},{64,80... | collective-permute-start | bytes 2359304 | tf_op jit(solution)/shard_map/ppermute | solution.py:232
  79.0 17.2 %collective-permute-done.13.refs_1_ = f32[1,8,96,128]{3,2,1,0:T(8,128)S(1)} collective-permute-done((f32[1,8,96,128]{3,2,1,0:T(8,128)S(1)}, f32[1,8,96,128]{3,2,1,0:T(8,128)S(1)}, u32[]{:S(2)}, u32[]{:S(2)}) %collective-permute-start.13) | collective-permute-done | bytes 393248 | tf_op jit(solution)/shard_map/ppermute | solution.py:229
  96.2 2.3 %shard_map.105 = (f32[8,256,128]{2,1,0:T(8,128)}, f32[8,256,128]{2,1,0:T(8,128)}, f32[8,256,128]{2,1,0:T(8,128)}, f32[8,3,96,128]{3,2,1,0:T(8,128)}) custom-call(s32[8]{0:T(128)S(1)} %bitcast.23, f32[1,8,96,128]{3,2,1,0:T(8,128)S(1)} %get-tuple-element.65.refs_0_, f32[1,8,96,128]{3,2,1,0:T(8,128)S(1)} %collective-permute-done.13.refs_1_, ...), custom_call_target="tpu_custom_call" | custom-call | bytes 1056 | tf_op jit(solution)/shard_map/pallas_call | solution.py:134
  98.5 6.3 %all-to-all-start = ((f32[8,3,96,128]{3,2,1,0:T(8,128)}), f32[8,3,96,128]{3,2,1,0:T(8,128)}, u32[]{:S(2)}, u32[]{:S(2)}) async-start(f32[8,3,96,128]{3,2,1,0:T(8,128)} %get-tuple-element.67), calls=%async_computation | async-start | bytes 2359296 | tf_op jit(solution)/shard_map/all_to_all | solution.py:239
  106.8 6.0 %collective-permute-done.16.refs_2_ = f32[1,8,64,128]{3,2,1,0:T(8,128)S(1)} collective-permute-done((f32[1,8,64,128]{3,2,1,0:T(8,128)S(1)}, f32[1,8,64,128]{3,2,1,0:T(8,128)S(1)}, u32[]{:S(2)}, u32[]{:S(2)}) %collective-permute-start.16) | collective-permute-done | bytes 262176 | tf_op jit(solution)/shard_map/ppermute | solution.py:232
  114.5 3.2 %shard_map.109 = (f32[1,8,96,128]{3,2,1,0:T(8,128)S(1)}, f32[1,8,96,128]{3,2,1,0:T(8,128)S(1)}) custom-call(s32[8]{0:T(128)S(1)} %add.188.table, bf16[128,1,32768]{2,1,0:T(2,128)(2,1)} %bitcast.40, f32[2,8,96,128]{3,2,1,0:T(8,128)} %collective-permute-done.17.refs_0_, f32[2,8,96,128]{3,2,1,0:T(8,128)} %collective-permute-done.18.refs_1_), custom_call_target="tpu_custom_call" | custom-call | bytes 768 | tf_op jit(solution)/shard_map/pallas_call | solution.py:85
  117.7 2.8 %collective-permute-start.19 = (f32[1,8,96,128]{3,2,1,0:T(8,128)S(1)}, f32[1,8,96,128]{3,2,1,0:T(8,128)S(1)}, u32[]{:S(2)}, u32[]{:S(2)}) collective-permute-start(f32[1,8,96,128]{3,2,1,0:T(8,128)S(1)} %get-tuple-element.73), channel_id=1, source_target_pairs={{0,64},{8,72},{16,80},{24,88},{32,96},{40,104},{48,112},{56,120},{... | collective-permute-start | bytes 1179656 | tf_op jit(solution)/shard_map/ppermute | solution.py:229
  120.5 9.7 %collective-permute-done.19.refs_1_ = f32[1,8,96,128]{3,2,1,0:T(8,128)S(1)} collective-permute-done((f32[1,8,96,128]{3,2,1,0:T(8,128)S(1)}, f32[1,8,96,128]{3,2,1,0:T(8,128)S(1)}, u32[]{:S(2)}, u32[]{:S(2)}) %collective-permute-start.19) | collective-permute-done | bytes 393248 | tf_op jit(solution)/shard_map/ppermute | solution.py:229
  130.2 2.3 %shard_map.110 = (f32[8,256,128]{2,1,0:T(8,128)}, f32[8,256,128]{2,1,0:T(8,128)}, f32[8,256,128]{2,1,0:T(8,128)}, f32[8,3,96,128]{3,2,1,0:T(8,128)}) custom-call(s32[8]{0:T(128)S(1)} %bitcast.24, f32[1,8,96,128]{3,2,1,0:T(8,128)S(1)} %get-tuple-element.72.refs_0_, ...), custom_call_target="tpu_custom_call", output_to_operand_aliasing={{0}: (6, {}), {1}: (7, {}), {2}: (8, {})} | custom-call | bytes 1056 | tf_op jit(solution)/shard_map/pallas_call | solution.py:134
  132.5 5.3 %all-to-all-start.2 = ((f32[8,3,96,128]{3,2,1,0:T(8,128)}), f32[8,3,96,128]{3,2,1,0:T(8,128)}, u32[]{:S(2)}, u32[]{:S(2)}) async-start(f32[8,3,96,128]{3,2,1,0:T(8,128)} %get-tuple-element.85), calls=%async_computation.2 | async-start | bytes 2359296 | tf_op jit(solution)/shard_map/all_to_all | solution.py:239
  137.8 6.4 %collective-permute-done.20.refs_2_ = f32[1,8,64,128]{3,2,1,0:T(8,128)S(1)} collective-permute-done((f32[1,8,64,128]{3,2,1,0:T(8,128)S(1)}, f32[1,8,64,128]{3,2,1,0:T(8,128)S(1)}, u32[]{:S(2)}, u32[]{:S(2)}) %collective-permute-start.20) | collective-permute-done | bytes 262176 | tf_op jit(solution)/shard_map/ppermute | solution.py:232
  147.2 2.8 %shard_map.106.refs_0_ = f32[3,256,2,128]{3,2,1,0:T(2,128)} custom-call(f32[2,8]{1,0:T(2,128)S(1)} %add_divide_fusion.coeff, f32[8,3,96,128]{3,2,1,0:T(8,128)} %all-to-all-done.got), custom_call_target="tpu_custom_call" | custom-call | bytes 432 | tf_op jit(solution)/shard_map/pallas_call | solution.py:169
  150.1 2.2 %collective-permute-done.21.refs_2_ = f32[1,8,64,128]{3,2,1,0:T(8,128)S(1)} collective-permute-done((f32[1,8,64,128]{3,2,1,0:T(8,128)S(1)}, f32[1,8,64,128]{3,2,1,0:T(8,128)S(1)}, u32[]{:S(2)}, u32[]{:S(2)}) %collective-permute-start.21) | collective-permute-done | bytes 262176 | tf_op jit(solution)/shard_map/ppermute | solution.py:232
  155.9 5.6 %all-to-all-start.1 = ((f32[8,3,64,128]{3,2,1,0:T(8,128)}), f32[8,3,64,128]{3,2,1,0:T(8,128)S(1)}, u32[]{:S(2)}, u32[]{:S(2)}) async-start(f32[8,3,64,128]{3,2,1,0:T(8,128)} %get-tuple-element.84), calls=%async_computation.1 | async-start | bytes 1572864 | tf_op jit(solution)/shard_map/all_to_all | solution.py:239
  161.5 2.8 %shard_map.114.refs_0_ = f32[3,256,2,128]{3,2,1,0:T(2,128)} custom-call(f32[2,8]{1,0:T(2,128)S(1)} %add_divide_fusion.coeff, f32[8,3,96,128]{3,2,1,0:T(8,128)} %all-to-all-done.2.got, f32[3,256,2,128]{3,2,1,0:T(2,128)} %shard_map.106.refs_0_), custom_call_target="tpu_custom_call", output_to_operand_aliasing={{}: (2, {})} | custom-call | bytes 432 | tf_op jit(solution)/shard_map/pallas_call | solution.py:169
  164.3 8.9 %all-to-all-done.1.got = f32[8,3,64,128]{3,2,1,0:T(8,128)S(1)} async-done(((f32[8,3,64,128]{3,2,1,0:T(8,128)}), f32[8,3,64,128]{3,2,1,0:T(8,128)S(1)}, u32[]{:S(2)}, u32[]{:S(2)}) %all-to-all-start.1) | async-done | bytes 786464 | tf_op jit(solution)/shard_map/all_to_all | solution.py:239
  (72 shorter events, 25.7 us)
Async XLA Ops:
  3.0 5.2 %collective-permute-start = (f32[2,8,96,128]{3,2,1,0:T(8,128)S(1)}, f32[2,8,96,128]{3,2,1,0:T(8,128)S(1)}, u32[]{:S(2)}, u32[]{:S(2)}) collective-permute-start(f32[2,8,96,128]{3,2,1,0:T(8,128)S(1)} %shard_map.93), channel_id=1, source_target_pairs={{0,8},{8,0},{16,24},{24,16},{32,40},{40,32},{48,56},{56,48},{64,72... | collective-permute-start | bytes 2359304 | tf_op jit(solution)/shard_map/ppermute | solution.py:215
  15.2 3.0 %collective-permute-start.1 = (f32[2,8,96,128]{3,2,1,0:T(8,128)}, f32[2,8,96,128]{3,2,1,0:T(8,128)}, u32[]{:S(2)}, u32[]{:S(2)}) collective-permute-start(f32[2,8,96,128]{3,2,1,0:T(8,128)} %get-tuple-element.51), channel_id=1, source_target_pairs={{0,8},{8,0},{16,24},{24,16},{32,40},{40,32},{48,56},{56,48},{64,72... | collective-permute-start | bytes 2359304 | tf_op jit(solution)/shard_map/ppermute | solution.py:215
  15.8 6.2 %collective-permute-start.2 = (f32[2,8,96,128]{3,2,1,0:T(8,128)}, f32[2,8,96,128]{3,2,1,0:T(8,128)S(1)}, u32[]{:S(2)}, u32[]{:S(2)}) collective-permute-start(f32[2,8,96,128]{3,2,1,0:T(8,128)} %get-tuple-element.53), channel_id=1, source_target_pairs={{0,8},{8,0},{16,24},{24,16},{32,40},{40,32},{48,56},{56,48},{64,72... | collective-permute-start | bytes 2359304 | tf_op jit(solution)/shard_map/ppermute | solution.py:215
  15.9 12.0 %collective-permute-start.3 = (f32[2,8,96,128]{3,2,1,0:T(8,128)S(1)}, f32[2,8,96,128]{3,2,1,0:T(8,128)S(1)}, u32[]{:S(2)}, u32[]{:S(2)}) collective-permute-start(f32[2,8,96,128]{3,2,1,0:T(8,128)S(1)} %shard_map.95), channel_id=1, source_target_pairs={{0,16},{8,56},{16,32},{24,8},{32,48},{40,24},{48,0},{56,40},{64,80... | collective-permute-start | bytes 2359304 | tf_op jit(solution)/shard_map/ppermute | solution.py:232
  16.0 21.4 %collective-permute-start.4 = (f32[2,8,96,128]{3,2,1,0:T(8,128)}, f32[2,8,96,128]{3,2,1,0:T(8,128)S(1)}, u32[]{:S(2)}, u32[]{:S(2)}) collective-permute-start(f32[2,8,96,128]{3,2,1,0:T(8,128)} %get-tuple-element.57), channel_id=1, source_target_pairs={{0,8},{8,0},{16,24},{24,16},{32,40},{40,32},{48,56},{56,48},{64,72... | collective-permute-start | bytes 2359304 | tf_op jit(solution)/shard_map/ppermute | solution.py:215
  33.8 15.9 %collective-permute-start.6 = (f32[4,8,64,128]{3,2,1,0:T(8,128)}, f32[4,8,64,128]{3,2,1,0:T(8,128)S(1)}, u32[]{:S(2)}, u32[]{:S(2)}) collective-permute-start(f32[4,8,64,128]{3,2,1,0:T(8,128)} %get-tuple-element.59), channel_id=1, source_target_pairs={{0,8},{8,0},{16,24},{24,16},{32,40},{40,32},{48,56},{56,48},{64,72... | collective-permute-start | bytes 3145736 | tf_op jit(solution)/shard_map/ppermute | solution.py:215
  34.4 12.3 %collective-permute-start.5 = (f32[2,8,96,128]{3,2,1,0:T(8,128)}, f32[2,8,96,128]{3,2,1,0:T(8,128)}, u32[]{:S(2)}, u32[]{:S(2)}) collective-permute-start(f32[2,8,96,128]{3,2,1,0:T(8,128)} %shard_map.97), channel_id=1, source_target_pairs={{0,16},{8,56},{16,32},{24,8},{32,48},{40,24},{48,0},{56,40},{64,80... | collective-permute-start | bytes 2359304 | tf_op jit(solution)/shard_map/ppermute | solution.py:232
  35.3 19.3 %collective-permute-start.7 = (f32[2,8,96,128]{3,2,1,0:T(8,128)}, f32[2,8,96,128]{3,2,1,0:T(8,128)}, u32[]{:S(2)}, u32[]{:S(2)}) collective-permute-start(f32[2,8,96,128]{3,2,1,0:T(8,128)} %get-tuple-element.61), channel_id=1, source_target_pairs={{0,8},{8,0},{16,24},{24,16},{32,40},{40,32},{48,56},{56,48},{64,72... | collective-permute-start | bytes 2359304 | tf_op jit(solution)/shard_map/ppermute | solution.py:215
  35.3 19.8 %collective-permute-start.8 = (f32[2,8,96,128]{3,2,1,0:T(8,128)S(1)}, f32[2,8,96,128]{3,2,1,0:T(8,128)}, u32[]{:S(2)}, u32[]{:S(2)}) collective-permute-start(f32[2,8,96,128]{3,2,1,0:T(8,128)S(1)} %shard_map.98), channel_id=1, source_target_pairs={{0,16},{8,56},{16,32},{24,8},{32,48},{40,24},{48,0},{56,40},{64,80... | collective-permute-start | bytes 2359304 | tf_op jit(solution)/shard_map/ppermute | solution.py:232
  37.4 23.1 %collective-permute-start.9 = (f32[2,8,96,128]{3,2,1,0:T(8,128)}, f32[2,8,96,128]{3,2,1,0:T(8,128)S(1)}, u32[]{:S(2)}, u32[]{:S(2)}) collective-permute-start(f32[2,8,96,128]{3,2,1,0:T(8,128)} %get-tuple-element.63), channel_id=1, source_target_pairs={{0,8},{8,0},{16,24},{24,16},{32,40},{40,32},{48,56},{56,48},{64,72... | collective-permute-start | bytes 2359304 | tf_op jit(solution)/shard_map/ppermute | solution.py:215
  46.7 19.7 %collective-permute-start.11 = (f32[2,8,96,128]{3,2,1,0:T(8,128)}, f32[2,8,96,128]{3,2,1,0:T(8,128)S(1)}, u32[]{:S(2)}, u32[]{:S(2)}) collective-permute-start(f32[2,8,96,128]{3,2,1,0:T(8,128)} %copy-done.8), channel_id=1, source_target_pairs={{0,8},{8,0},{16,24},{24,16},{32,40},{40,32},{48,56},{56,48},{64,72... | collective-permute-start | bytes 2359304 | tf_op jit(solution)/shard_map/ppermute | solution.py:215
  49.7 13.9 %collective-permute-start.10 = (f32[2,8,96,128]{3,2,1,0:T(8,128)S(1)}, f32[2,8,96,128]{3,2,1,0:T(8,128)S(1)}, u32[]{:S(2)}, u32[]{:S(2)}) collective-permute-start(f32[2,8,96,128]{3,2,1,0:T(8,128)S(1)} %shard_map.100), channel_id=1, source_target_pairs={{0,16},{8,56},{16,32},{24,8},{32,48},{40,24},{48,0},{56,40},{64,80... | collective-permute-start | bytes 2359304 | tf_op jit(solution)/shard_map/ppermute | solution.py:232
  58.2 13.6 %collective-permute-start.12 = (f32[2,8,96,128]{3,2,1,0:T(8,128)S(1)}, f32[2,8,96,128]{3,2,1,0:T(8,128)S(1)}, u32[]{:S(2)}, u32[]{:S(2)}) collective-permute-start(f32[2,8,96,128]{3,2,1,0:T(8,128)S(1)} %shard_map.102), channel_id=1, source_target_pairs={{0,16},{8,56},{16,32},{24,8},{32,48},{40,24},{48,0},{56,40},{64,80... | collective-permute-start | bytes 2359304 | tf_op jit(solution)/shard_map/ppermute | solution.py:232
  60.5 44.3 %collective-permute-start.14 = (f32[4,8,64,128]{3,2,1,0:T(8,128)}, f32[4,8,64,128]{3,2,1,0:T(8,128)S(1)}, u32[]{:S(2)}, u32[]{:S(2)}) collective-permute-start(f32[4,8,64,128]{3,2,1,0:T(8,128)} %get-tuple-element.55), channel_id=1, source_target_pairs={{0,8},{8,0},{16,24},{24,16},{32,40},{40,32},{48,56},{56,48},{64,72... | collective-permute-start | bytes 3145736 | tf_op jit(solution)/shard_map/ppermute | solution.py:215
  60.5 44.3 %collective-permute-start.15 = (f32[4,8,64,128]{3,2,1,0:T(8,128)}, f32[4,8,64,128]{3,2,1,0:T(8,128)S(1)}, u32[]{:S(2)}, u32[]{:S(2)}) collective-permute-start(f32[4,8,64,128]{3,2,1,0:T(8,128)} %shard_map.101), channel_id=1, source_target_pairs={{0,64},{8,72},{16,80},{24,88},{32,96},{40,104},{48,112},{56,120},{... | collective-permute-start | bytes 3145736 | tf_op jit(solution)/shard_map/ppermute | solution.py:256
  66.3 29.9 %copy-start = (f32[1,262144]{1,0:T(1,128)S(1)}, f32[1,262144]{1,0:T(1,128)}, u32[]{:S(2)}) copy-start(f32[1,262144]{1,0:T(1,128)} %param.7) | copy-start | bytes 3145732
  66.3 29.9 %copy-start.1 = (f32[1,262144]{1,0:T(1,128)S(1)}, f32[1,262144]{1,0:T(1,128)}, u32[]{:S(2)}) copy-start(f32[1,262144]{1,0:T(1,128)} %param.8) | copy-start | bytes 3145732
  66.3 29.9 %copy-start.4 = (f32[1,262144]{1,0:T(1,128)S(1)}, f32[1,262144]{1,0:T(1,128)}, u32[]{:S(2)}) copy-start(f32[1,262144]{1,0:T(1,128)} %param.9) | copy-start | bytes 3145732
  66.3 29.9 %copy-start.7 = (s32[1,8]{1,0:T(1,128)S(1)}, s32[1,8]{1,0:T(1,128)}, u32[]{:S(2)}) copy-start(s32[1,8]{1,0:T(1,128)} %param.11) | copy-start | bytes 100
  73.6 22.6 %collective-permute-start.13 = (f32[1,8,96,128]{3,2,1,0:T(8,128)S(1)}, f32[1,8,96,128]{3,2,1,0:T(8,128)S(1)}, u32[]{:S(2)}, u32[]{:S(2)}) collective-permute-start(f32[1,8,96,128]{3,2,1,0:T(8,128)S(1)} %get-tuple-element.66), channel_id=1, source_target_pairs={{0,64},{8,72},{16,80},{24,88},{32,96},{40,104},{48,112},{56,120},{... | collective-permute-start | bytes 1179656 | tf_op jit(solution)/shard_map/ppermute | solution.py:229
  76.7 37.7 %collective-permute-start.17 = (f32[2,8,96,128]{3,2,1,0:T(8,128)}, f32[2,8,96,128]{3,2,1,0:T(8,128)}, u32[]{:S(2)}, u32[]{:S(2)}) collective-permute-start(f32[2,8,96,128]{3,2,1,0:T(8,128)} %get-tuple-element.49), channel_id=1, source_target_pairs={{0,8},{8,0},{16,24},{24,16},{32,40},{40,32},{48,56},{56,48},{64,72... | collective-permute-start | bytes 2359304 | tf_op jit(solution)/shard_map/ppermute | solution.py:215
  76.7 37.7 %collective-permute-start.18 = (f32[2,8,96,128]{3,2,1,0:T(8,128)}, f32[2,8,96,128]{3,2,1,0:T(8,128)}, u32[]{:S(2)}, u32[]{:S(2)}) collective-permute-start(f32[2,8,96,128]{3,2,1,0:T(8,128)} %shard_map.103), channel_id=1, source_target_pairs={{0,16},{8,56},{16,32},{24,8},{32,48},{40,24},{48,0},{56,40},{64,80... | collective-permute-start | bytes 2359304 | tf_op jit(solution)/shard_map/ppermute | solution.py:232
  98.5 34.0 %all-to-all-start = ((f32[8,3,96,128]{3,2,1,0:T(8,128)}), f32[8,3,96,128]{3,2,1,0:T(8,128)}, u32[]{:S(2)}, u32[]{:S(2)}) async-start(f32[8,3,96,128]{3,2,1,0:T(8,128)} %get-tuple-element.67), calls=%async_computation | async-start | bytes 2359296 | tf_op jit(solution)/shard_map/all_to_all | solution.py:239
  106.4 6.4 %collective-permute-start.16 = (f32[1,8,64,128]{3,2,1,0:T(8,128)S(1)}, f32[1,8,64,128]{3,2,1,0:T(8,128)S(1)}, u32[]{:S(2)}, u32[]{:S(2)}) collective-permute-start(f32[1,8,64,128]{3,2,1,0:T(8,128)S(1)} %shard_map.107), channel_id=1, source_target_pairs={{0,16},{8,56},{16,32},{24,8},{32,48},{40,24},{48,0},{56,40},{64,80... | collective-permute-start | bytes 786440 | tf_op jit(solution)/shard_map/ppermute | solution.py:232
  114.5 15.7 %copy-start.2 = (f32[1,262144]{1,0:T(1,128)S(1)}, f32[1,262144]{1,0:T(1,128)}, u32[]{:S(2)}) copy-start(f32[1,262144]{1,0:T(1,128)} %param.8) | copy-start | bytes 3145732
  114.5 15.7 %copy-start.5 = (f32[1,262144]{1,0:T(1,128)S(1)}, f32[1,262144]{1,0:T(1,128)}, u32[]{:S(2)}) copy-start(f32[1,262144]{1,0:T(1,128)} %param.9) | copy-start | bytes 3145732
  117.7 12.5 %collective-permute-start.19 = (f32[1,8,96,128]{3,2,1,0:T(8,128)S(1)}, f32[1,8,96,128]{3,2,1,0:T(8,128)S(1)}, u32[]{:S(2)}, u32[]{:S(2)}) collective-permute-start(f32[1,8,96,128]{3,2,1,0:T(8,128)S(1)} %get-tuple-element.73), channel_id=1, source_target_pairs={{0,64},{8,72},{16,80},{24,88},{32,96},{40,104},{48,112},{56,120},{... | collective-permute-start | bytes 1179656 | tf_op jit(solution)/shard_map/ppermute | solution.py:229
  132.5 23.4 %all-to-all-start.2 = ((f32[8,3,96,128]{3,2,1,0:T(8,128)}), f32[8,3,96,128]{3,2,1,0:T(8,128)}, u32[]{:S(2)}, u32[]{:S(2)}) async-start(f32[8,3,96,128]{3,2,1,0:T(8,128)} %get-tuple-element.85), calls=%async_computation.2 | async-start | bytes 2359296 | tf_op jit(solution)/shard_map/all_to_all | solution.py:239
  137.7 9.3 %copy-start.9 = (s32[10]{0:T(128)S(1)}, s32[10]{0:T(128)}, u32[]{:S(2)}) copy-start(s32[10]{0:T(128)} %param.10) | copy-start | bytes 124
  137.8 6.4 %collective-permute-start.20 = (f32[1,8,64,128]{3,2,1,0:T(8,128)S(1)}, f32[1,8,64,128]{3,2,1,0:T(8,128)S(1)}, u32[]{:S(2)}, u32[]{:S(2)}) collective-permute-start(f32[1,8,64,128]{3,2,1,0:T(8,128)S(1)} %shard_map.108), channel_id=1, source_target_pairs={{0,16},{8,56},{16,32},{24,8},{32,48},{40,24},{48,0},{56,40},{64,80... | collective-permute-start | bytes 786440 | tf_op jit(solution)/shard_map/ppermute | solution.py:232
  145.8 6.4 %collective-permute-start.21 = (f32[1,8,64,128]{3,2,1,0:T(8,128)S(1)}, f32[1,8,64,128]{3,2,1,0:T(8,128)S(1)}, u32[]{:S(2)}, u32[]{:S(2)}) collective-permute-start(f32[1,8,64,128]{3,2,1,0:T(8,128)S(1)} %shard_map.111), channel_id=1, source_target_pairs={{0,16},{8,56},{16,32},{24,8},{32,48},{40,24},{48,0},{56,40},{64,80... | collective-permute-start | bytes 786440 | tf_op jit(solution)/shard_map/ppermute | solution.py:232
  155.9 17.4 %all-to-all-start.1 = ((f32[8,3,64,128]{3,2,1,0:T(8,128)}), f32[8,3,64,128]{3,2,1,0:T(8,128)S(1)}, u32[]{:S(2)}, u32[]{:S(2)}) async-start(f32[8,3,64,128]{3,2,1,0:T(8,128)} %get-tuple-element.84), calls=%async_computation.1 | async-start | bytes 1572864 | tf_op jit(solution)/shard_map/all_to_all | solution.py:239
  (3 other events, 8.4 us)

commit v3 on v0

v3 whole, which is shorter than its diff:
```python
import functools

import jax
import jax.numpy as jnp
from jax import lax
from jax.experimental import pallas as pl
from jax.experimental.pallas import tpu as pltpu
from jax.sharding import PartitionSpec as P

STEP = 10
X, Y, C = 2, 4, 2
G = 8
ROWS = 256
LANES = 128
SHARD = G * ROWS * LANES
CHUNKS = ((0, 96, False), (96, 96, False), (192, 64, True))
GROUPS = ((0,), (1, 2))
TILE = 32
VMEM = 8 * 2**20


def dp_index(x, y, c):
    return (x * Y + y) * C + c


def dp_perm(move):
    return [
        (dp_index(x, y, c), dp_index(*move(x, y, c)))
        for x in range(X)
        for y in range(Y)
        for c in range(C)
    ]


CORE_SWAP = dp_perm(lambda x, y, c: (x, y, 1 - c))
X_SWAP = dp_perm(lambda x, y, c: (1 - x, y, c))
Y_ON = dp_perm(lambda x, y, c: (x, (y + (1 if c == 0 else -1)) % Y, c))
Y_BACK = dp_perm(lambda x, y, c: (x, (y - (1 if c == 0 else -1)) % Y, c))


def params():
    return pltpu.CompilerParams(vmem_limit_bytes=VMEM)


def cost(size):
    return pl.CostEstimate(flops=0, transcendentals=0, bytes_accessed=size // 4096)


def in_hbm(value):
    return pltpu.with_memory_space_constraint(value, pltpu.HBM)


def in_vmem(value):
    return pltpu.with_memory_space_constraint(value, pltpu.VMEM)


def after(value, *others):
    return lax.optimization_barrier((value, *others))[0]


def combine_kernel(tasks, table, grad, *refs):
    arrays = sum(len(task["offsets"]) for task in tasks)
    pieces = sum(len(task["splits"]) for task in tasks)
    terms, outs, scratch = refs[:arrays], refs[arrays : arrays + pieces], refs[arrays + pieces :]
    work = []
    for n, task in enumerate(tasks):
        held, sems = scratch[2 * n : 2 * n + 2]
        size = task["rows"] * LANES
        copies = [
            pltpu.make_async_copy(
                grad.at[
                    pl.ds(pl.multiple_of(table[task["first"] + i] * G, G), G),
                    :,
                    pl.ds(task["start"] * LANES, size),
                ],
                held.at[pl.ds(i * G, G)],
                sems.at[i],
            )
            for i in range(sum(task["splits"]))
        ]
        for copy in copies:
            copy.start()
        work.append((held, copies))
    for task, (held, copies) in zip(tasks, work):
        mine, terms = terms[: len(task["offsets"])], terms[len(task["offsets"]) :]
        places = [(out, i) for out, n in zip(outs, task["splits"]) for i in range(n)]
        outs = outs[len(task["splits"]) :]
        for i, (copy, (out, at)) in enumerate(zip(copies, places)):
            copy.wait()
            for j in range(G):
                total = held[i * G + j].astype(jnp.float32).reshape(task["rows"], LANES)
                for term, offset in zip(mine, task["offsets"]):
                    if 0 <= offset + i < term.shape[0]:
                        total = total + term[offset + i, j]
                out[at, j] = total


def combine(grad, table, tasks):
    arrays = [a for task in tasks for a, _ in task["terms"]]
    shapes = [(n, task["rows"]) for task in tasks for n in task["splits"]]
    static = [
        {**{k: task[k] for k in ("first", "splits", "start", "rows")}, "offsets": [o for _, o in task["terms"]]}
        for task in tasks
    ]
    scratch = []
    for task in tasks:
        count = sum(task["splits"])
        scratch.append(pltpu.VMEM((count * G, 1, task["rows"] * LANES), jnp.bfloat16))
        scratch.append(pltpu.SemaphoreType.DMA((count,)))
    size = sum(n * G * rows * LANES * 8 for n, rows in shapes) + sum(a.size * 4 for a in arrays)
    outs = pl.pallas_call(
        functools.partial(combine_kernel, static),
        grid_spec=pltpu.PrefetchScalarGridSpec(
            num_scalar_prefetch=1,
            grid=(),
            in_specs=[pl.BlockSpec(memory_space=pl.ANY)]
            + [pl.BlockSpec(memory_space=pltpu.VMEM)] * len(arrays),
            out_specs=[pl.BlockSpec(memory_space=pltpu.VMEM)] * len(shapes),
            scratch_shapes=scratch,
        ),
        out_shape=[pltpu.VMEM((n, G, rows, LANES), jnp.float32) for n, rows in shapes],
        compiler_params=params(),
        cost_estimate=cost(size),
    )(table, in_hbm(grad), *[in_vmem(a) for a in arrays])
    results = []
    for task in tasks:
        results.append(outs[: len(task["splits"])])
        outs = outs[len(task["splits"]) :]
    return results


def order_kernel(holder, *refs):
    (*state, ordered), sems = refs[:-1], refs[-1]
    copies = [
        pltpu.make_async_copy(state[s].at[j], ordered.at[holder[j], s], sems.at[j, s])
        for j in range(G)
        for s in range(3)
    ]
    for copy in copies:
        copy.start()
    for copy in copies:
        copy.wait()


def order_state(state, holder):
    return pl.pallas_call(
        order_kernel,
        grid_spec=pltpu.PrefetchScalarGridSpec(
            num_scalar_prefetch=1,
            grid=(),
            in_specs=[pl.BlockSpec(memory_space=pl.ANY)] * 3,
            out_specs=pl.BlockSpec(memory_space=pl.ANY),
            scratch_shapes=[pltpu.SemaphoreType.DMA((G, 3))],
        ),
        out_shape=pltpu.HBM((G, 3, ROWS, LANES), jnp.float32),
        compiler_params=params(),
        cost_estimate=cost(G * 3 * ROWS * LANES * 8),
    )(holder, *[in_hbm(a) for a in state])


def finish_kernel(terms, first, rows, holder, *refs):
    parts = refs[:terms]
    total, ordered, sems = refs[-3:]
    copies = []
    for j in range(G):
        grad = parts[0][0, j]
        for part in parts[1:]:
            grad = grad + part[0, j]
        total[j] = grad
        copy = pltpu.make_async_copy(
            total.at[j], ordered.at[holder[j], pl.ds(first, rows)], sems.at[j]
        )
        copy.start()
        copies.append(copy)
    for copy in copies:
        copy.wait()


def finish(parts, ordered, holder, first, rows, group_rows):
    held = [] if ordered is None else [in_hbm(ordered)]
    return pl.pallas_call(
        functools.partial(finish_kernel, len(parts), first, rows),
        grid_spec=pltpu.PrefetchScalarGridSpec(
            num_scalar_prefetch=1,
            grid=(),
            in_specs=[pl.BlockSpec(memory_space=pltpu.VMEM)] * len(parts)
            + [pl.BlockSpec(memory_space=pl.ANY)] * len(held),
            out_specs=[
                pl.BlockSpec(memory_space=pltpu.VMEM),
                pl.BlockSpec(memory_space=pl.ANY),
            ],
            scratch_shapes=[pltpu.SemaphoreType.DMA((G,))],
        ),
        out_shape=[
            pltpu.VMEM((G, rows, LANES), jnp.float32),
            pltpu.HBM((G, group_rows, LANES), jnp.float32),
        ],
        input_output_aliases={1 + len(parts): 1} if held else {},
        compiler_params=params(),
        cost_estimate=cost(G * rows * LANES * 4 * (len(parts) + 2)),
    )(holder, *[in_vmem(a) for a in parts], *held)


def adam_step(grad, old, first, second):
    m = 0.9 * first + 0.1 * grad
    v = 0.95 * second + 0.05 * grad * grad
    first_hat = m / (1.0 - 0.9**STEP)
    second_hat = v / (1.0 - 0.95**STEP)
    w = old - 0.01 * (first_hat / (jnp.sqrt(second_hat) + 1e-08) + 0.1 * old)
    return w, m, v


def adam_kernel(rows, start, total, *refs):
    state, refs = refs[:3], refs[3:]
    *outs, fresh, sems = refs[-5:]
    here = pl.ds(start, rows)
    copies = []
    for j in range(G):
        for s, value in enumerate(adam_step(total[j], *[a[j, here] for a in state])):
            fresh[s, j] = value
            copy = pltpu.make_async_copy(fresh.at[s, j], outs[s].at[j, here], sems.at[j, s])
            copy.start()
            copies.append(copy)
    for copy in copies:
        copy.wait()


def adam(total, state, done, start, rows):
    held = [in_hbm(a) for a in done or ()]
    return pl.pallas_call(
        functools.partial(adam_kernel, rows, start),
        grid_spec=pltpu.PrefetchScalarGridSpec(
            num_scalar_prefetch=0,
            grid=(),
            in_specs=[pl.BlockSpec(memory_space=pltpu.VMEM)] * 4
            + [pl.BlockSpec(memory_space=pl.ANY)] * len(held),
            out_specs=[pl.BlockSpec(memory_space=pl.ANY)] * 3,
            scratch_shapes=[
                pltpu.VMEM((3, G, rows, LANES), jnp.float32),
                pltpu.SemaphoreType.DMA((G, 3)),
            ],
        ),
        out_shape=[pltpu.HBM((G, ROWS, LANES), jnp.float32)] * 3,
        input_output_aliases={4 + n: n for n in range(len(held))},
        compiler_params=params(),
        cost_estimate=cost(G * rows * LANES * 4 * 7),
    )(in_vmem(total), *[in_vmem(a) for a in state], *held)


def parity_kernel(coeff, sums, old, *refs):
    out = refs[-1]
    totals = [[None] * 2 for _ in range(3)]
    for g in range(G):
        for s, value in enumerate(adam_step(sums[g], *[old[g, s] for s in range(3)])):
            for k in range(2):
                term = coeff[k, g] * value
                totals[s][k] = term if g == 0 else totals[s][k] + term
    for s in range(3):
        for k in range(2):
            out[s, :, k, :] = totals[s][k]


def parity(sums, old, coeff, done, start, rows):
    first = start // TILE
    held = [] if done is None else [in_hbm(done)]
    return pl.pallas_call(
        parity_kernel,
        grid_spec=pltpu.PrefetchScalarGridSpec(
            num_scalar_prefetch=1,
            grid=(rows // TILE,),
            in_specs=[
                pl.BlockSpec((G, TILE, LANES), lambda i, c: (0, i, 0)),
                pl.BlockSpec((G, 3, TILE, LANES), lambda i, c: (0, 0, first + i, 0)),
            ]
            + [pl.BlockSpec(memory_space=pl.ANY)] * len(held),
            out_specs=pl.BlockSpec((3, TILE, 2, LANES), lambda i, c: (0, first + i, 0, 0)),
        ),
        out_shape=pltpu.HBM((3, ROWS, 2, LANES), jnp.float32),
        input_output_aliases={3: 0} if held else {},
        compiler_params=params(),
        cost_estimate=cost(G * 4 * rows * LANES * 4),
    )(coeff, sums, old, *held)


def per_device(
    grad_parts, master_weights, first_moment, second_moment, cauchy_points, parity_holder
):
    index = lax.axis_index("dp")
    core, y, x = index % C, (index // C) % Y, index // (C * Y)
    holder = parity_holder.reshape(G)
    state = [a.reshape(G, ROWS, LANES) for a in (master_weights, first_moment, second_moment)]
    points = cauchy_points.astype(jnp.float32)
    coeff = 1.0 / (points[:2][:, None] + points[2:][None, :])

    def table(of_core, x_first):
        way = 1 - 2 * of_core
        ys = jnp.stack([y + 2, y - way, y + way, y]) % Y
        if x_first:
            xs = jnp.stack([1 - x, x])
            return (((xs[:, None] * Y + ys[None, :]) * C) + of_core).reshape(X * Y)
        xs = jnp.stack([x, 1 - x])
        return (((xs[None, :] * Y + ys[:, None]) * C) + of_core).reshape(X * Y)

    grad = grad_parts.reshape(X * Y * C * G, 1, ROWS * LANES)
    tables = [table(1 - core, False), table(1 - core, True), table(core, False), table(core, True)]
    blocks = jnp.concatenate(tables).astype(jnp.int32)
    half = X * Y // 2
    got = {n: [] for n in range(len(CHUNKS))}
    across = {n: [] for n in range(len(CHUNKS))}
    hop, totals, ordered, olds, done, shards = {}, {}, {}, None, None, None
    token = ()

    def task(n, own, first, splits, terms):
        start, rows, x_first = CHUNKS[n]
        base = X * Y * (2 * own + x_first)
        return dict(first=base + first, start=start, rows=rows, splits=splits, terms=terms)

    def run(*jobs, wait=()):
        nonlocal token
        table = after(blocks, *token, *wait)
        results = combine(grad, table, [job[0] for job in jobs])
        token = (results[0][0],)
        for (_, use), result in zip(jobs, results):
            use(*result)

    def then(*values):
        nonlocal token
        token = values

    def swap_core(n, part, splits=(2, 2)):
        def use(*sent):
            got[n] += [lax.ppermute(a, "dp", CORE_SWAP) for a in sent]

        return task(n, False, half * part, splits, []), use

    def offsets(arrays, first):
        pairs, at = [], 0
        for a in arrays:
            pairs.append((a, first - at))
            at += a.shape[0]
        return pairs

    def of_core(n, first):
        return offsets(got[n], first)

    def of_x(n, first):
        return offsets(across[n], first - half)

    def x_sum(n):
        def use(*sent):
            across[n] += [lax.ppermute(a, "dp", X_SWAP) for a in sent]

        return task(n, True, 0, (2, 2), of_core(n, 0)), use

    def terms_at(n, first, count):
        terms = of_core(n, first) + (of_x(n, first) if CHUNKS[n][2] else [])
        return [(a, o) for a, o in terms if o < a.shape[0] and o + count > 0]

    def step_1(n):
        first, size = (half, 1) if CHUNKS[n][2] else (0, X)

        def use(far, near):
            hop[n, 0] = lax.ppermute(far, "dp", Y_ON)
            hop[n, 1] = lax.ppermute(near, "dp", Y_BACK)

        return task(n, True, first, (size, size), terms_at(n, first, 2 * size)), use

    def step_2(n):
        first, size = (half + 2, 1) if CHUNKS[n][2] else (half, X)

        def use(block):
            hop[n, 2] = lax.ppermute(block, "dp", Y_ON)

        return task(n, True, first, (size,), terms_at(n, first, size) + [(hop[n, 0], 0)]), use

    def step_3(n):
        first, splits = (half + 3, (1,)) if CHUNKS[n][2] else (half + X, (1, 1))

        def use(own, *block):
            totals[n] = [own] + [lax.ppermute(b, "dp", X_SWAP) for b in block]

        terms = terms_at(n, first, len(splits)) + [(hop[n, 2], 0), (hop[n, 1], 0)]
        return task(n, True, first, splits, terms), use

    def give(n):
        (group,) = [g for g in GROUPS if n in g]
        base = min(CHUNKS[m][0] for m in group)
        start, rows, _ = CHUNKS[n]
        totals[n], ordered[group] = finish(
            totals[n],
            ordered.get(group),
            after(holder, *token),
            start - base,
            rows,
            sum(CHUNKS[m][1] for m in group),
        )
        then(totals[n])

    def to_holders(group):
        ordered[group] = lax.all_to_all(ordered[group], "group", 0, 0)

    def update(n):
        nonlocal done
        start, rows, _ = CHUNKS[n]
        done = adam(after(totals[n], *token), state, done, start, rows)
        then(done[0])

    def parities(group):
        nonlocal shards
        start = min(CHUNKS[m][0] for m in group)
        rows = sum(CHUNKS[m][1] for m in group)
        shards = parity(ordered[group], olds, after(coeff, *token), shards, start, rows)
        then(shards)

    run(swap_core(0, 0))
    run(swap_core(2, 0))
    run(step_1(0))
    run(x_sum(2))
    old = order_state(state, after(holder, *token))
    then(old)
    olds = lax.all_to_all(old, "group", 0, 0)
    run(swap_core(0, 1, (1, 1, 1, 1)), swap_core(1, 0))
    run(step_2(0), swap_core(2, 1), wait=(across[2][0],))
    run(step_1(1), swap_core(1, 1), wait=(hop[0, 1],))
    run(step_3(0), wait=(across[2][1],))
    run(step_2(1))
    then(*token, hop[1, 1])
    give(0)
    to_holders((0,))
    run(step_1(2), wait=(olds,))
    run(step_3(1))
    run(step_2(2))
    update(0)
    run(step_3(2))
    give(2)
    give(1)
    to_holders((1, 2))
    parities((0,))
    update(1)
    update(2)
    parities((1, 2))
    outs = [a.reshape(1, SHARD) for a in done]
    return (*outs, shards.transpose(2, 0, 1, 3).reshape(1, 1, 2, 3, ROWS * LANES))


def solution(mesh):
    in_specs = (
        P("dp", "group", None),
        P("group", "dp"),
        P("group", "dp"),
        P("group", "dp"),
        P(),
        P("dp", None),
    )
    out_specs = (
        P("group", "dp"),
        P("group", "dp"),
        P("group", "dp"),
        P("dp", "group", None, None, None),
    )
    return jax.shard_map(
        per_device, mesh=mesh, in_specs=in_specs, out_specs=out_specs, check_vma=False
    )
```

time: 529 us -> 282 us (0.53)
  waiting for transfers between devices: 460 us -> 75.1 us
  Pallas kernels: 0 us -> 151 us
  starting transfers between devices: 0.08 us -> 41.5 us
  other arithmetic: 41.3 us -> 0.47 us
  between operations: 14.8 us -> 1.16 us
    unnamed x4 -> x0, waiting for transfers between devices: 460 us -> none
    pallas_call x0 -> x22, Pallas kernels: none -> 151 us  [the longest x1 97.1 us: order_state(): pl.pallas_call(order_kernel, grid_spec=pltpu.PrefetchScalarGridSpec(num_s...]
    ppermute x0 -> x27, waiting for transfers between devices: none -> 69 us  [the longest x2 40.7 us: use(): across[n] += [lax.ppermute(a, 'dp', X_SWAP) for a in sent]]
    ppermute x0 -> x27, starting transfers between devices: none -> 24.7 us  [the longest x2 5.98 us: use(): totals[n] = [own] + [lax.ppermute(b, 'dp', X_SWAP) for b in block]]
    convert_element_type x1 -> x0, other arithmetic: 19.8 us -> none  [per_device(): flat_grad.astype(jnp.float32)]
    all_to_all x0 -> x3, starting transfers between devices: none -> 16.8 us  [the longest x2 10.6 us: to_holders(): ordered[group] = lax.all_to_all(ordered[group], 'group', 0, 0)]
    unnamed x16 -> x62, local copies, waits for them, and re-layouts: 2.44 us -> 10.4 us
    sub x1 -> x0, other arithmetic: 7.34 us -> none  [per_device(): master_weights - 0.01 * (first_hat / (jnp.sqrt(second_hat) + 1e-08) + 0.1...]
  transfers between devices with their start and end apart: 2 -> 30, of which waited for: 2 -> 7; matrix products, arithmetic and copies ran while one was open for 0% -> 0% of each run, Pallas kernels for 0% -> 16%
where the time goes in v3:
time: 282 us; the launch traced here: 280 us
  Pallas kernels  151 us (54%)
  waiting for transfers between devices  75.1 us (27%)
  starting transfers between devices  41.5 us (15%)
  local copies, waits for them, and re-layouts  10.8 us (4%)
    pallas_call x1, Pallas kernels, order_state(): pl.pallas_call(order_kernel, grid_spec=pltpu.PrefetchScalarGridSpec(num_s...  97.1 us
    ppermute x2, waiting for transfers between devices, use(): across[n] += [lax.ppermute(a, 'dp', X_SWAP) for a in sent]  40.7 us
    pallas_call x13, Pallas kernels, combine(): pl.pallas_call(functools.partial(combine_kernel, static), grid_spec=pltpu...  37.6 us
    ppermute x3, waiting for transfers between devices, use(): hop[n, 0] = lax.ppermute(far, 'dp', Y_ON)  14.2 us
    all_to_all x2, starting transfers between devices, to_holders(): ordered[group] = lax.all_to_all(ordered[group], 'group', 0, 0)  10.6 us
    unnamed x62, local copies, waits for them, and re-layouts  10.4 us
    ppermute x2, waiting for transfers between devices, use(): totals[n] = [own] + [lax.ppermute(b, 'dp', X_SWAP) for b in block]  9.19 us
    pallas_call x2, Pallas kernels, parity(): pl.pallas_call(parity_kernel, grid_spec=pltpu.PrefetchScalarGridSpec(num_...  7.06 us
  transfers between devices with their start and end apart: 30, of which 7 were waited for; matrix products, arithmetic and copies ran while one was open for 0% of the time, Pallas kernels for 16%

profile of v3, /device:TPU:24, one launch (start us, length us, event | category | flops | bytes accessed | tf_op | source)
XLA Modules:
  0.0 279.6 jit_solution(4746444059934347942)
XLA Ops:
  1.4 2.7 shard_map.93
  4.7 2.3 shard_map.94
  7.6 2.0 shard_map.95
  10.5 1.8 shard_map.96
  13.9 97.1 %shard_map.97 = f32[8,3,256,128]{3,2,1,0:T(8,128)} custom-call(s32[8]{0:T(128)S(1)} %bitcast.32, f32[8,256,128]{2,1,0:T(8,128)} %bitcast.20, f32[8,256,128]{2,1,0:T(8,128)} %bitcast.24, f32[8,256,128]{2,1,0:T(8,128)} %bitcast.28), custom_call_target="tpu_custom_call" | custom-call | bytes 1536 | tf_op jit(solution)/shard_map/pallas_call | solution.py:146
  111.1 6.3 %all-to-all-start = ((f32[8,3,256,128]{3,2,1,0:T(8,128)}), f32[8,3,256,128]{3,2,1,0:T(8,128)S(1)}, u32[]{:S(2)}, u32[]{:S(2)}) async-start(f32[8,3,256,128]{3,2,1,0:T(8,128)} %shard_map.97), calls=%async_computation | async-start | bytes 6291456 | tf_op jit(solution)/shard_map/all_to_all | solution.py:421
  117.4 4.0 %shard_map.98 = (f32[1,8,96,128]{3,2,1,0:T(8,128)S(1)}, f32[1,8,96,128]{3,2,1,0:T(8,128)S(1)}, f32[1,8,96,128]{3,2,1,0:T(8,128)S(1)}, f32[1,8,96,128]{3,2,1,0:T(...) custom-call(s32[32]{0:T(128)S(1)} %pad_add_fusion.table, bf16[128,1,32768]{2,1,0:T(2,128)(2,1)} %bitcast.40), custom_call_target="tpu_custom_call" | custom-call | bytes 1536 | tf_op jit(solution)/shard_map/pallas_call | solution.py:111
  122.2 1.8 collective-permute-start.8
  124.7 2.8 %collective-permute-start.4 = (f32[2,8,64,128]{3,2,1,0:T(8,128)S(1)}, f32[2,8,64,128]{3,2,1,0:T(8,128)S(1)}, u32[]{:S(2)}, u32[]{:S(2)}) collective-permute-start(f32[2,8,64,128]{3,2,1,0:T(8,128)S(1)} %copy-done.28), channel_id=1, source_target_pairs={{0,64},{8,72},{16,80},{24,88},{32,96},{40,104},{48,112},{56,120},{... | collective-permute-start | bytes 1572872 | tf_op jit(solution)/shard_map/ppermute | solution.py:351
  127.6 38.7 %collective-permute-done.4.refs_1_ = f32[2,8,64,128]{3,2,1,0:T(8,128)S(1)} collective-permute-done((f32[2,8,64,128]{3,2,1,0:T(8,128)S(1)}, f32[2,8,64,128]{3,2,1,0:T(8,128)S(1)}, u32[]{:S(2)}, u32[]{:S(2)}) %collective-permute-start.4) | collective-permute-done | bytes 524320 | tf_op jit(solution)/shard_map/ppermute | solution.py:351
  167.9 3.6 %shard_map.99 = (f32[2,8,96,128]{3,2,1,0:T(8,128)S(1)}, f32[2,8,64,128]{3,2,1,0:T(8,128)}, f32[2,8,64,128]{3,2,1,0:T(8,128)}) custom-call(s32[32]{0:T(128)S(1)} %pad_add_fusion.table, bf16[128,1,32768]{2,1,0:T(2,128)(2,1)} %bitcast.41, f32[1,8,96,128]{3,2,1,0:T(8,128)S(1)} %collective-permute-done.5.refs_0_, ...), custom_call_target="tpu_custom_call" | custom-call | bytes 1280 | tf_op jit(solution)/shard_map/pallas_call | solution.py:111
  171.9 4.4 %shard_map.100 = (f32[2,8,96,128]{3,2,1,0:T(8,128)S(1)}, f32[2,8,96,128]{3,2,1,0:T(8,128)S(1)}, f32[2,8,96,128]{3,2,1,0:T(8,128)S(1)}, f32[2,8,96,128]{3,2,1,0:T(8,128)}) custom-call(s32[32]{0:T(128)S(1)} %pad_add_fusion.table, bf16[128,1,32768]{2,1,0:T(2,128)(2,1)} %bitcast.42, f32[2,8,96,128]{3,2,1,0:T(8,128)S(1)} %collective-permute-done.9.refs_0_, ...), custom_call_target="tpu_custom_call" | custom-call | bytes 1920 | tf_op jit(solution)/shard_map/pallas_call | solution.py:111
  177.1 2.5 collective-permute-start.16
  179.6 2.1 collective-permute-done.11.refs_1_
  182.4 2.1 collective-permute-done.14.refs_2_
  186.4 14.2 %collective-permute-done.16.refs_1_ = f32[2,8,96,128]{3,2,1,0:T(8,128)S(1)} collective-permute-done((f32[2,8,96,128]{3,2,1,0:T(8,128)S(1)}, f32[2,8,96,128]{3,2,1,0:T(8,128)S(1)}, u32[]{:S(2)}, u32[]{:S(2)}) %collective-permute-start.16) | collective-permute-done | bytes 786464 | tf_op jit(solution)/shard_map/ppermute | solution.py:363
  200.5 2.6 shard_map.102
  204.7 2.7 collective-permute-start.18
  208.5 9.2 %collective-permute-done.18.refs_1_ = f32[1,8,96,128]{3,2,1,0:T(8,128)S(1)} collective-permute-done((f32[1,8,96,128]{3,2,1,0:T(8,128)S(1)}, f32[1,8,96,128]{3,2,1,0:T(8,128)S(1)}, u32[]{:S(2)}, u32[]{:S(2)}) %collective-permute-start.18) | collective-permute-done | bytes 393248 | tf_op jit(solution)/shard_map/ppermute | solution.py:380
  221.0 3.3 %shard_map.104 = (f32[1,8,64,128]{3,2,1,0:T(8,128)}, f32[1,8,64,128]{3,2,1,0:T(8,128)S(1)}) custom-call(s32[32]{0:T(128)S(1)} %pad_add_fusion.table, bf16[128,1,32768]{2,1,0:T(2,128)(2,1)} %bitcast.45, f32[2,8,64,128]{3,2,1,0:T(8,128)} %collective-permute-done.19.refs_0_, f32[2,8,64,128]{3,2,1,0:T(8,128)S(1)} %copy-done.11), custom_call_target="tpu_custom_call" | custom-call | bytes 512 | tf_op jit(solution)/shard_map/pallas_call | solution.py:111
  226.3 3.9 %shard_map.105 = (f32[1,8,96,128]{3,2,1,0:T(8,128)S(1)}, f32[1,8,96,128]{3,2,1,0:T(8,128)}) custom-call(s32[32]{0:T(128)S(1)} %pad_add_fusion.table, bf16[128,1,32768]{2,1,0:T(2,128)(2,1)} %bitcast.46, f32[2,8,96,128]{3,2,1,0:T(8,128)} %collective-permute-done.20.refs_0_, f32[2,8,96,128]{3,2,1,0:T(8,128)} %collective-permute-done.21.refs_1_, ...), custom_call_target="tpu_custom_call" | custom-call | bytes 960 | tf_op jit(solution)/shard_map/pallas_call | solution.py:111
  231.0 3.2 %collective-permute-start.26 = (f32[1,8,96,128]{3,2,1,0:T(8,128)}, f32[1,8,96,128]{3,2,1,0:T(8,128)}, u32[]{:S(2)}, u32[]{:S(2)}) collective-permute-start(f32[1,8,96,128]{3,2,1,0:T(8,128)} %get-tuple-element.113), channel_id=1, source_target_pairs={{0,64},{8,72},{16,80},{24,88},{32,96},{40,104},{48,112},{56,120},{... | collective-permute-start | bytes 1179656 | tf_op jit(solution)/shard_map/ppermute | solution.py:380
  234.3 4.8 %all-to-all-start.1 = ((f32[8,96,128]{2,1,0:T(8,128)}), f32[8,96,128]{2,1,0:T(8,128)S(1)}, u32[]{:S(2)}, u32[]{:S(2)}) async-start(f32[8,96,128]{2,1,0:T(8,128)} %get-tuple-element.117), calls=%async_computation.1 | async-start | bytes 786432 | tf_op jit(solution)/shard_map/all_to_all | solution.py:400
  241.1 2.7 shard_map.106
  243.8 2.5 collective-permute-start.24
  247.5 2.7 collective-permute-done.24.refs_2_
  250.2 2.6 shard_map.108.refs_0_
  254.9 2.4 shard_map.110
  258.1 5.7 %all-to-all-start.2 = ((f32[8,160,128]{2,1,0:T(8,128)}), f32[8,160,128]{2,1,0:T(8,128)}, u32[]{:S(2)}, u32[]{:S(2)}) async-start(f32[8,160,128]{2,1,0:T(8,128)} %get-tuple-element.129), calls=%async_computation.2 | async-start | bytes 1310720 | tf_op jit(solution)/shard_map/all_to_all | solution.py:400
  264.0 2.4 shard_map.111.refs_0_
  268.8 6.1 %all-to-all-done.2.sums = f32[8,160,128]{2,1,0:T(8,128)} async-done(((f32[8,160,128]{2,1,0:T(8,128)}), f32[8,160,128]{2,1,0:T(8,128)}, u32[]{:S(2)}, u32[]{:S(2)}) %all-to-all-start.2) | async-done | bytes 655392 | tf_op jit(solution)/shard_map/all_to_all | solution.py:400
  274.9 4.7 %shard_map.114 = f32[3,256,2,128]{3,2,1,0:T(2,128)} custom-call(f32[2,8]{1,0:T(2,128)S(1)} %add_divide_fusion.coeff, f32[8,160,128]{2,1,0:T(8,128)} %all-to-all-done.2.sums, f32[8,3,256,128]{3,2,1,0:T(8,128)S(1)} %all-to-all-done.old, f32[3,256,2,128]{3,2,1,0:T(2,128)} %shard_map.111.refs_0_), custom_call_target="tpu_custom_call", output_to_operand_aliasing={{}: (3, {})} | custom-call | bytes 640 | tf_op jit(solution)/shard_map/pallas_call | solution.py:266
  (124 shorter events, 28.6 us)
Async XLA Ops:
  4.1 3.4 %collective-permute-start = (f32[2,8,96,128]{3,2,1,0:T(8,128)S(1)}, f32[2,8,96,128]{3,2,1,0:T(8,128)S(1)}, u32[]{:S(2)}, u32[]{:S(2)}) collective-permute-start(f32[2,8,96,128]{3,2,1,0:T(8,128)S(1)} %get-tuple-element.67), channel_id=1, source_target_pairs={{0,8},{8,0},{16,24},{24,16},{32,40},{40,32},{48,56},{56,48},{64,72... | collective-permute-start | bytes 2359304 | tf_op jit(solution)/shard_map/ppermute | solution.py:332
  4.2 3.4 %collective-permute-start.1 = (f32[2,8,96,128]{3,2,1,0:T(8,128)S(1)}, f32[2,8,96,128]{3,2,1,0:T(8,128)S(1)}, u32[]{:S(2)}, u32[]{:S(2)}) collective-permute-start(f32[2,8,96,128]{3,2,1,0:T(8,128)S(1)} %get-tuple-element.71), channel_id=1, source_target_pairs={{0,8},{8,0},{16,24},{24,16},{32,40},{40,32},{48,56},{56,48},{64,72... | collective-permute-start | bytes 2359304 | tf_op jit(solution)/shard_map/ppermute | solution.py:332
  6.9 3.5 %collective-permute-start.2 = (f32[2,8,64,128]{3,2,1,0:T(8,128)S(1)}, f32[2,8,64,128]{3,2,1,0:T(8,128)S(1)}, u32[]{:S(2)}, u32[]{:S(2)}) collective-permute-start(f32[2,8,64,128]{3,2,1,0:T(8,128)S(1)} %get-tuple-element.69), channel_id=1, source_target_pairs={{0,8},{8,0},{16,24},{24,16},{32,40},{40,32},{48,56},{56,48},{64,72... | collective-permute-start | bytes 1572872 | tf_op jit(solution)/shard_map/ppermute | solution.py:332
  7.1 3.4 %collective-permute-start.3 = (f32[2,8,64,128]{3,2,1,0:T(8,128)S(1)}, f32[2,8,64,128]{3,2,1,0:T(8,128)S(1)}, u32[]{:S(2)}, u32[]{:S(2)}) collective-permute-start(f32[2,8,64,128]{3,2,1,0:T(8,128)S(1)} %get-tuple-element.74), channel_id=1, source_target_pairs={{0,8},{8,0},{16,24},{24,16},{32,40},{40,32},{48,56},{56,48},{64,72... | collective-permute-start | bytes 1572872 | tf_op jit(solution)/shard_map/ppermute | solution.py:332
  111.1 108.8 %all-to-all-start = ((f32[8,3,256,128]{3,2,1,0:T(8,128)}), f32[8,3,256,128]{3,2,1,0:T(8,128)S(1)}, u32[]{:S(2)}, u32[]{:S(2)}) async-start(f32[8,3,256,128]{3,2,1,0:T(8,128)} %shard_map.97), calls=%async_computation | async-start | bytes 6291456 | tf_op jit(solution)/shard_map/all_to_all | solution.py:421
  117.4 49.7 %copy-start.26 = (f32[2,8,64,128]{3,2,1,0:T(8,128)S(1)}, f32[2,8,64,128]{3,2,1,0:T(8,128)}, u32[]{:S(2)}) copy-start(f32[2,8,64,128]{3,2,1,0:T(8,128)} %copy-done.25) | copy-start | bytes 1572868
  121.4 3.4 %collective-permute-start.5 = (f32[1,8,96,128]{3,2,1,0:T(8,128)S(1)}, f32[1,8,96,128]{3,2,1,0:T(8,128)S(1)}, u32[]{:S(2)}, u32[]{:S(2)}) collective-permute-start(f32[1,8,96,128]{3,2,1,0:T(8,128)S(1)} %get-tuple-element.78), channel_id=1, source_target_pairs={{0,8},{8,0},{16,24},{24,16},{32,40},{40,32},{48,56},{56,48},{64,72... | collective-permute-start | bytes 1179656 | tf_op jit(solution)/shard_map/ppermute | solution.py:332
  121.5 3.3 %collective-permute-start.6 = (f32[1,8,96,128]{3,2,1,0:T(8,128)S(1)}, f32[1,8,96,128]{3,2,1,0:T(8,128)S(1)}, u32[]{:S(2)}, u32[]{:S(2)}) collective-permute-start(f32[1,8,96,128]{3,2,1,0:T(8,128)S(1)} %get-tuple-element.80), channel_id=1, source_target_pairs={{0,8},{8,0},{16,24},{24,16},{32,40},{40,32},{48,56},{56,48},{64,72... | collective-permute-start | bytes 1179656 | tf_op jit(solution)/shard_map/ppermute | solution.py:332
  122.0 45.9 %collective-permute-start.7 = (f32[2,8,96,128]{3,2,1,0:T(8,128)S(1)}, f32[2,8,96,128]{3,2,1,0:T(8,128)S(1)}, u32[]{:S(2)}, u32[]{:S(2)}) collective-permute-start(f32[2,8,96,128]{3,2,1,0:T(8,128)S(1)} %copy-done.24), channel_id=1, source_target_pairs={{0,16},{8,56},{16,32},{24,8},{32,48},{40,24},{48,0},{56,40},{64,80... | collective-permute-start | bytes 2359304 | tf_op jit(solution)/shard_map/ppermute | solution.py:363
  122.2 49.3 %collective-permute-start.8 = (f32[2,8,96,128]{3,2,1,0:T(8,128)S(1)}, f32[2,8,96,128]{3,2,1,0:T(8,128)S(1)}, u32[]{:S(2)}, u32[]{:S(2)}) collective-permute-start(f32[2,8,96,128]{3,2,1,0:T(8,128)S(1)} %copy-done.22), channel_id=1, source_target_pairs={{0,48},{8,24},{16,0},{24,40},{32,16},{40,56},{48,32},{56,8},{64,11... | collective-permute-start | bytes 2359304 | tf_op jit(solution)/shard_map/ppermute | solution.py:364
  124.0 47.9 %collective-permute-start.10 = (f32[2,8,96,128]{3,2,1,0:T(8,128)S(1)}, f32[2,8,96,128]{3,2,1,0:T(8,128)S(1)}, u32[]{:S(2)}, u32[]{:S(2)}) collective-permute-start(f32[2,8,96,128]{3,2,1,0:T(8,128)S(1)} %get-tuple-element.85), channel_id=1, source_target_pairs={{0,8},{8,0},{16,24},{24,16},{32,40},{40,32},{48,56},{56,48},{64,72... | collective-permute-start | bytes 2359304 | tf_op jit(solution)/shard_map/ppermute | solution.py:332
  124.7 47.2 %collective-permute-start.9 = (f32[2,8,96,128]{3,2,1,0:T(8,128)S(1)}, f32[2,8,96,128]{3,2,1,0:T(8,128)S(1)}, u32[]{:S(2)}, u32[]{:S(2)}) collective-permute-start(f32[2,8,96,128]{3,2,1,0:T(8,128)S(1)} %get-tuple-element.84), channel_id=1, source_target_pairs={{0,8},{8,0},{16,24},{24,16},{32,40},{40,32},{48,56},{56,48},{64,72... | collective-permute-start | bytes 2359304 | tf_op jit(solution)/shard_map/ppermute | solution.py:332
  124.7 41.5 %collective-permute-start.4 = (f32[2,8,64,128]{3,2,1,0:T(8,128)S(1)}, f32[2,8,64,128]{3,2,1,0:T(8,128)S(1)}, u32[]{:S(2)}, u32[]{:S(2)}) collective-permute-start(f32[2,8,64,128]{3,2,1,0:T(8,128)S(1)} %copy-done.28), channel_id=1, source_target_pairs={{0,64},{8,72},{16,80},{24,88},{32,96},{40,104},{48,112},{56,120},{... | collective-permute-start | bytes 1572872 | tf_op jit(solution)/shard_map/ppermute | solution.py:351
  167.0 14.6 %collective-permute-start.11 = (f32[2,8,64,128]{3,2,1,0:T(8,128)S(1)}, f32[2,8,64,128]{3,2,1,0:T(8,128)S(1)}, u32[]{:S(2)}, u32[]{:S(2)}) collective-permute-start(f32[2,8,64,128]{3,2,1,0:T(8,128)S(1)} %copy-done.26), channel_id=1, source_target_pairs={{0,64},{8,72},{16,80},{24,88},{32,96},{40,104},{48,112},{56,120},{... | collective-permute-start | bytes 1572872 | tf_op jit(solution)/shard_map/ppermute | solution.py:351
  167.9 11.8 %collective-permute-start.12 = (f32[1,8,96,128]{3,2,1,0:T(8,128)S(1)}, f32[1,8,96,128]{3,2,1,0:T(8,128)S(1)}, u32[]{:S(2)}, u32[]{:S(2)}) collective-permute-start(f32[1,8,96,128]{3,2,1,0:T(8,128)S(1)} %get-tuple-element.89), channel_id=1, source_target_pairs={{0,8},{8,0},{16,24},{24,16},{32,40},{40,32},{48,56},{56,48},{64,72... | collective-permute-start | bytes 1179656 | tf_op jit(solution)/shard_map/ppermute | solution.py:332
  171.5 13.1 %collective-permute-start.14 = (f32[2,8,96,128]{3,2,1,0:T(8,128)S(1)}, f32[2,8,96,128]{3,2,1,0:T(8,128)S(1)}, u32[]{:S(2)}, u32[]{:S(2)}) collective-permute-start(f32[2,8,96,128]{3,2,1,0:T(8,128)S(1)} %get-tuple-element.81), channel_id=1, source_target_pairs={{0,16},{8,56},{16,32},{24,8},{32,48},{40,24},{48,0},{56,40},{64,80... | collective-permute-start | bytes 2359304 | tf_op jit(solution)/shard_map/ppermute | solution.py:372
  176.3 10.1 %collective-permute-start.15 = (f32[2,8,96,128]{3,2,1,0:T(8,128)S(1)}, f32[2,8,96,128]{3,2,1,0:T(8,128)S(1)}, u32[]{:S(2)}, u32[]{:S(2)}) collective-permute-start(f32[2,8,96,128]{3,2,1,0:T(8,128)S(1)} %get-tuple-element.93), channel_id=1, source_target_pairs={{0,8},{8,0},{16,24},{24,16},{32,40},{40,32},{48,56},{56,48},{64,72... | collective-permute-start | bytes 2359304 | tf_op jit(solution)/shard_map/ppermute | solution.py:332
  177.1 23.4 %collective-permute-start.16 = (f32[2,8,96,128]{3,2,1,0:T(8,128)S(1)}, f32[2,8,96,128]{3,2,1,0:T(8,128)S(1)}, u32[]{:S(2)}, u32[]{:S(2)}) collective-permute-start(f32[2,8,96,128]{3,2,1,0:T(8,128)S(1)} %get-tuple-element.86), channel_id=1, source_target_pairs={{0,16},{8,56},{16,32},{24,8},{32,48},{40,24},{48,0},{56,40},{64,80... | collective-permute-start | bytes 2359304 | tf_op jit(solution)/shard_map/ppermute | solution.py:363
  179.6 2.8 %collective-permute-start.13 = (f32[1,8,96,128]{3,2,1,0:T(8,128)S(1)}, f32[1,8,96,128]{3,2,1,0:T(8,128)S(1)}, u32[]{:S(2)}, u32[]{:S(2)}) collective-permute-start(f32[1,8,96,128]{3,2,1,0:T(8,128)S(1)} %get-tuple-element.90), channel_id=1, source_target_pairs={{0,8},{8,0},{16,24},{24,16},{32,40},{40,32},{48,56},{56,48},{64,72... | collective-permute-start | bytes 1179656 | tf_op jit(solution)/shard_map/ppermute | solution.py:332
  181.7 25.7 %collective-permute-start.17 = (f32[2,8,96,128]{3,2,1,0:T(8,128)S(1)}, f32[2,8,96,128]{3,2,1,0:T(8,128)S(1)}, u32[]{:S(2)}, u32[]{:S(2)}) collective-permute-start(f32[2,8,96,128]{3,2,1,0:T(8,128)S(1)} %get-tuple-element.94), channel_id=1, source_target_pairs={{0,48},{8,24},{16,0},{24,40},{32,16},{40,56},{48,32},{56,8},{64,11... | collective-permute-start | bytes 2359304 | tf_op jit(solution)/shard_map/ppermute | solution.py:364
  182.4 43.9 %collective-permute-start.20 = (f32[2,8,96,128]{3,2,1,0:T(8,128)}, f32[2,8,96,128]{3,2,1,0:T(8,128)}, u32[]{:S(2)}, u32[]{:S(2)}) collective-permute-start(f32[2,8,96,128]{3,2,1,0:T(8,128)} %get-tuple-element.102), channel_id=1, source_target_pairs={{0,8},{8,0},{16,24},{24,16},{32,40},{40,32},{48,56},{56,48},{64,72... | collective-permute-start | bytes 2359304 | tf_op jit(solution)/shard_map/ppermute | solution.py:332
  203.2 23.1 %collective-permute-start.21 = (f32[2,8,96,128]{3,2,1,0:T(8,128)}, f32[2,8,96,128]{3,2,1,0:T(8,128)}, u32[]{:S(2)}, u32[]{:S(2)}) collective-permute-start(f32[2,8,96,128]{3,2,1,0:T(8,128)} %shard_map.102), channel_id=1, source_target_pairs={{0,16},{8,56},{16,32},{24,8},{32,48},{40,24},{48,0},{56,40},{64,80... | collective-permute-start | bytes 2359304 | tf_op jit(solution)/shard_map/ppermute | solution.py:372
  204.7 15.2 %collective-permute-start.19 = (f32[2,8,64,128]{3,2,1,0:T(8,128)}, f32[2,8,64,128]{3,2,1,0:T(8,128)}, u32[]{:S(2)}, u32[]{:S(2)}) collective-permute-start(f32[2,8,64,128]{3,2,1,0:T(8,128)} %get-tuple-element.99), channel_id=1, source_target_pairs={{0,8},{8,0},{16,24},{24,16},{32,40},{40,32},{48,56},{56,48},{64,72... | collective-permute-start | bytes 1572872 | tf_op jit(solution)/shard_map/ppermute | solution.py:332
  204.7 13.0 %collective-permute-start.18 = (f32[1,8,96,128]{3,2,1,0:T(8,128)S(1)}, f32[1,8,96,128]{3,2,1,0:T(8,128)S(1)}, u32[]{:S(2)}, u32[]{:S(2)}) collective-permute-start(f32[1,8,96,128]{3,2,1,0:T(8,128)S(1)} %get-tuple-element.96), channel_id=1, source_target_pairs={{0,64},{8,72},{16,80},{24,88},{32,96},{40,104},{48,112},{56,120},{... | collective-permute-start | bytes 1179656 | tf_op jit(solution)/shard_map/ppermute | solution.py:380
  208.3 31.5 %collective-permute-start.22 = (f32[2,8,64,128]{3,2,1,0:T(8,128)}, f32[2,8,64,128]{3,2,1,0:T(8,128)}, u32[]{:S(2)}, u32[]{:S(2)}) collective-permute-start(f32[2,8,64,128]{3,2,1,0:T(8,128)} %get-tuple-element.105), channel_id=1, source_target_pairs={{0,8},{8,0},{16,24},{24,16},{32,40},{40,32},{48,56},{56,48},{64,72... | collective-permute-start | bytes 1572872 | tf_op jit(solution)/shard_map/ppermute | solution.py:332
  225.1 14.7 %collective-permute-start.23 = (f32[1,8,64,128]{3,2,1,0:T(8,128)}, f32[1,8,64,128]{3,2,1,0:T(8,128)}, u32[]{:S(2)}, u32[]{:S(2)}) collective-permute-start(f32[1,8,64,128]{3,2,1,0:T(8,128)} %get-tuple-element.100), channel_id=1, source_target_pairs={{0,16},{8,56},{16,32},{24,8},{32,48},{40,24},{48,0},{56,40},{64,80... | collective-permute-start | bytes 786440 | tf_op jit(solution)/shard_map/ppermute | solution.py:363
  231.0 23.9 %collective-permute-start.26 = (f32[1,8,96,128]{3,2,1,0:T(8,128)}, f32[1,8,96,128]{3,2,1,0:T(8,128)}, u32[]{:S(2)}, u32[]{:S(2)}) collective-permute-start(f32[1,8,96,128]{3,2,1,0:T(8,128)} %get-tuple-element.113), channel_id=1, source_target_pairs={{0,64},{8,72},{16,80},{24,88},{32,96},{40,104},{48,112},{56,120},{... | collective-permute-start | bytes 1179656 | tf_op jit(solution)/shard_map/ppermute | solution.py:380
  234.3 23.8 %all-to-all-start.1 = ((f32[8,96,128]{2,1,0:T(8,128)}), f32[8,96,128]{2,1,0:T(8,128)S(1)}, u32[]{:S(2)}, u32[]{:S(2)}) async-start(f32[8,96,128]{2,1,0:T(8,128)} %get-tuple-element.117), calls=%async_computation.1 | async-start | bytes 786432 | tf_op jit(solution)/shard_map/all_to_all | solution.py:400
  239.1 8.4 %collective-permute-start.25 = (f32[1,8,64,128]{3,2,1,0:T(8,128)}, f32[1,8,64,128]{3,2,1,0:T(8,128)S(1)}, u32[]{:S(2)}, u32[]{:S(2)}) collective-permute-start(f32[1,8,64,128]{3,2,1,0:T(8,128)} %copy-done.29), channel_id=1, source_target_pairs={{0,48},{8,24},{16,0},{24,40},{32,16},{40,56},{48,32},{56,8},{64,11... | collective-permute-start | bytes 786440 | tf_op jit(solution)/shard_map/ppermute | solution.py:364
  243.8 6.4 %collective-permute-start.24 = (f32[1,8,64,128]{3,2,1,0:T(8,128)S(1)}, f32[1,8,64,128]{3,2,1,0:T(8,128)S(1)}, u32[]{:S(2)}, u32[]{:S(2)}) collective-permute-start(f32[1,8,64,128]{3,2,1,0:T(8,128)S(1)} %shard_map.106), channel_id=1, source_target_pairs={{0,16},{8,56},{16,32},{24,8},{32,48},{40,24},{48,0},{56,40},{64,80... | collective-permute-start | bytes 786440 | tf_op jit(solution)/shard_map/ppermute | solution.py:372
  247.5 16.3 %copy-start.30 = (s32[10]{0:T(128)S(1)}, s32[10]{0:T(128)}, u32[]{:S(2)}) copy-start(s32[10]{0:T(128)} %param.10) | copy-start | bytes 124
  258.1 16.8 %all-to-all-start.2 = ((f32[8,160,128]{2,1,0:T(8,128)}), f32[8,160,128]{2,1,0:T(8,128)}, u32[]{:S(2)}, u32[]{:S(2)}) async-start(f32[8,160,128]{2,1,0:T(8,128)} %get-tuple-element.129), calls=%async_computation.2 | async-start | bytes 1310720 | tf_op jit(solution)/shard_map/all_to_all | solution.py:400
  (29 other events, 89.1 us)

commit v4 on v3

--- a/solution.py
+++ b/solution.py
@@ -2,6 +2,7 @@
 
 import jax
 import jax.numpy as jnp
+import numpy as np
 from jax import lax
 from jax.experimental import pallas as pl
 from jax.experimental.pallas import tpu as pltpu
@@ -13,8 +14,8 @@
 ROWS = 256
 LANES = 128
 SHARD = G * ROWS * LANES
-CHUNKS = ((0, 96, False), (96, 96, False), (192, 64, True))
-GROUPS = ((0,), (1, 2))
+CHUNKS = ((0, 160, False), (160, 96, False))
+GROUPS = ((0,), (1,))
 TILE = 32
 VMEM = 8 * 2**20
 
@@ -38,12 +39,34 @@
 Y_BACK = dp_perm(lambda x, y, c: (x, (y - (1 if c == 0 else -1)) % Y, c))
 
 
+SHARE = 4096
+
+
 def params():
     return pltpu.CompilerParams(vmem_limit_bytes=VMEM)
 
 
+def block_table(x, y, of_core, x_first):
+    way = 1 - 2 * of_core
+    ys = [(y + step) % Y for step in (2, -way, way, 0)]
+    if x_first:
+        return [dp_index(at, to, of_core) for at in (1 - x, x) for to in ys]
+    return [dp_index(at, to, of_core) for to in ys for at in (x, 1 - x)]
+
+
+TABLES = np.array(
+    [
+        sum((block_table(x, y, of, f) for of in (1 - c, c) for f in (False, True)), [])
+        for x in range(X)
+        for y in range(Y)
+        for c in range(C)
+    ],
+    np.int32,
+)
+
+
 def cost(size):
-    return pl.CostEstimate(flops=0, transcendentals=0, bytes_accessed=size // 4096)
+    return pl.CostEstimate(flops=0, transcendentals=0, bytes_accessed=size // SHARE)
 
 
 def in_hbm(value):
@@ -88,14 +111,14 @@
         for i, (copy, (out, at)) in enumerate(zip(copies, places)):
             copy.wait()
             for j in range(G):
-                total = held[i * G + j].astype(jnp.float32).reshape(task["rows"], LANES)
+                total = held[i * G + j].reshape(task["rows"], LANES).astype(jnp.float32)
                 for term, offset in zip(mine, task["offsets"]):
                     if 0 <= offset + i < term.shape[0]:
                         total = total + term[offset + i, j]
                 out[at, j] = total
 
 
-def combine(grad, table, tasks):
+def combine(grad, table, tasks, name):
     arrays = [a for task in tasks for a, _ in task["terms"]]
     shapes = [(n, task["rows"]) for task in tasks for n in task["splits"]]
     static = [
@@ -119,6 +142,7 @@
             scratch_shapes=scratch,
         ),
         out_shape=[pltpu.VMEM((n, G, rows, LANES), jnp.float32) for n, rows in shapes],
+        name=name,
         compiler_params=params(),
         cost_estimate=cost(size),
     )(table, in_hbm(grad), *[in_vmem(a) for a in arrays])
@@ -148,19 +172,20 @@
         grid_spec=pltpu.PrefetchScalarGridSpec(
             num_scalar_prefetch=1,
             grid=(),
-            in_specs=[pl.BlockSpec(memory_space=pl.ANY)] * 3,
+            in_specs=[pl.BlockSpec(memory_space=pltpu.VMEM)] * 3,
             out_specs=pl.BlockSpec(memory_space=pl.ANY),
             scratch_shapes=[pltpu.SemaphoreType.DMA((G, 3))],
         ),
         out_shape=pltpu.HBM((G, 3, ROWS, LANES), jnp.float32),
+        name="order",
         compiler_params=params(),
         cost_estimate=cost(G * 3 * ROWS * LANES * 8),
-    )(holder, *[in_hbm(a) for a in state])
+    )(holder, *[in_vmem(a) for a in state])
 
 
 def finish_kernel(terms, first, rows, holder, *refs):
     parts = refs[:terms]
-    total, ordered, sems = refs[-3:]
+    ordered, total, sems = refs[-3:]
     copies = []
     for j in range(G):
         grad = parts[0][0, j]
@@ -185,17 +210,15 @@
             grid=(),
             in_specs=[pl.BlockSpec(memory_space=pltpu.VMEM)] * len(parts)
             + [pl.BlockSpec(memory_space=pl.ANY)] * len(held),
-            out_specs=[
-                pl.BlockSpec(memory_space=pltpu.VMEM),
-                pl.BlockSpec(memory_space=pl.ANY),
+            out_specs=pl.BlockSpec(memory_space=pl.ANY),
+            scratch_shapes=[
+                pltpu.VMEM((G, rows, LANES), jnp.float32),
+                pltpu.SemaphoreType.DMA((G,)),
             ],
-            scratch_shapes=[pltpu.SemaphoreType.DMA((G,))],
         ),
-        out_shape=[
-            pltpu.VMEM((G, rows, LANES), jnp.float32),
-            pltpu.HBM((G, group_rows, LANES), jnp.float32),
-        ],
-        input_output_aliases={1 + len(parts): 1} if held else {},
+        out_shape=pltpu.HBM((G, group_rows, LANES), jnp.float32),
+        name="finish",
+        input_output_aliases={1 + len(parts): 0} if held else {},
         compiler_params=params(),
         cost_estimate=cost(G * rows * LANES * 4 * (len(parts) + 2)),
     )(holder, *[in_vmem(a) for a in parts], *held)
@@ -210,41 +233,54 @@
     return w, m, v
 
 
-def adam_kernel(rows, start, total, *refs):
+def adam_kernel(first, rows, start, holder, ordered, *refs):
     state, refs = refs[:3], refs[3:]
-    *outs, fresh, sems = refs[-5:]
+    *outs, grads, old, fresh, in_sems, out_sems = refs[-8:]
     here = pl.ds(start, rows)
-    copies = []
+    loads, stores = [], []
     for j in range(G):
-        for s, value in enumerate(adam_step(total[j], *[a[j, here] for a in state])):
+        pairs = [(ordered.at[holder[j], pl.ds(first, rows)], grads.at[j])]
+        pairs += [(state[s].at[j, here], old.at[s, j]) for s in range(3)]
+        loads.append(
+            [pltpu.make_async_copy(*pair, in_sems.at[j, s]) for s, pair in enumerate(pairs)]
+        )
+        for load in loads[-1]:
+            load.start()
+    for j in range(G):
+        for load in loads[j]:
+            load.wait()
+        for s, value in enumerate(adam_step(grads[j], *[old[s, j] for s in range(3)])):
             fresh[s, j] = value
-            copy = pltpu.make_async_copy(fresh.at[s, j], outs[s].at[j, here], sems.at[j, s])
-            copy.start()
-            copies.append(copy)
-    for copy in copies:
-        copy.wait()
-
-
-def adam(total, state, done, start, rows):
+            store = pltpu.make_async_copy(fresh.at[s, j], outs[s].at[j, here], out_sems.at[j, s])
+            store.start()
+            stores.append(store)
+    for store in stores:
+        store.wait()
+
+
+def adam(ordered, state, done, holder, first, start, rows):
     held = [in_hbm(a) for a in done or ()]
     return pl.pallas_call(
-        functools.partial(adam_kernel, rows, start),
+        functools.partial(adam_kernel, first, rows, start),
         grid_spec=pltpu.PrefetchScalarGridSpec(
-            num_scalar_prefetch=0,
+            num_scalar_prefetch=1,
             grid=(),
-            in_specs=[pl.BlockSpec(memory_space=pltpu.VMEM)] * 4
-            + [pl.BlockSpec(memory_space=pl.ANY)] * len(held),
+            in_specs=[pl.BlockSpec(memory_space=pl.ANY)] * (4 + len(held)),
             out_specs=[pl.BlockSpec(memory_space=pl.ANY)] * 3,
             scratch_shapes=[
+                pltpu.VMEM((G, rows, LANES), jnp.float32),
                 pltpu.VMEM((3, G, rows, LANES), jnp.float32),
+                pltpu.VMEM((3, G, rows, LANES), jnp.float32),
+                pltpu.SemaphoreType.DMA((G, 4)),
                 pltpu.SemaphoreType.DMA((G, 3)),
             ],
         ),
         out_shape=[pltpu.HBM((G, ROWS, LANES), jnp.float32)] * 3,
-        input_output_aliases={4 + n: n for n in range(len(held))},
+        name="adam",
+        input_output_aliases={5 + n: n for n in range(len(held))},
         compiler_params=params(),
         cost_estimate=cost(G * rows * LANES * 4 * 7),
-    )(in_vmem(total), *[in_vmem(a) for a in state], *held)
+    )(holder, in_hbm(ordered), *[in_hbm(a) for a in state], *held)
 
 
 def parity_kernel(coeff, sums, old, *refs):
@@ -276,6 +312,7 @@
             out_specs=pl.BlockSpec((3, TILE, 2, LANES), lambda i, c: (0, first + i, 0, 0)),
         ),
         out_shape=pltpu.HBM((3, ROWS, 2, LANES), jnp.float32),
+        name="parity",
         input_output_aliases={3: 0} if held else {},
         compiler_params=params(),
         cost_estimate=cost(G * 4 * rows * LANES * 4),
@@ -286,28 +323,17 @@
     grad_parts, master_weights, first_moment, second_moment, cauchy_points, parity_holder
 ):
     index = lax.axis_index("dp")
-    core, y, x = index % C, (index // C) % Y, index // (C * Y)
     holder = parity_holder.reshape(G)
     state = [a.reshape(G, ROWS, LANES) for a in (master_weights, first_moment, second_moment)]
     points = cauchy_points.astype(jnp.float32)
     coeff = 1.0 / (points[:2][:, None] + points[2:][None, :])
 
-    def table(of_core, x_first):
-        way = 1 - 2 * of_core
-        ys = jnp.stack([y + 2, y - way, y + way, y]) % Y
-        if x_first:
-            xs = jnp.stack([1 - x, x])
-            return (((xs[:, None] * Y + ys[None, :]) * C) + of_core).reshape(X * Y)
-        xs = jnp.stack([x, 1 - x])
-        return (((xs[None, :] * Y + ys[:, None]) * C) + of_core).reshape(X * Y)
-
     grad = grad_parts.reshape(X * Y * C * G, 1, ROWS * LANES)
-    tables = [table(1 - core, False), table(1 - core, True), table(core, False), table(core, True)]
-    blocks = jnp.concatenate(tables).astype(jnp.int32)
+    blocks = lax.dynamic_index_in_dim(jnp.asarray(TABLES), index, keepdims=False)
     half = X * Y // 2
     got = {n: [] for n in range(len(CHUNKS))}
     across = {n: [] for n in range(len(CHUNKS))}
-    hop, totals, ordered, olds, done, shards = {}, {}, {}, None, None, None
+    hop, totals, ordered, sums, olds, done, shards = {}, {}, {}, {}, None, None, None
     token = ()
 
     def task(n, own, first, splits, terms):
@@ -315,23 +341,28 @@
         base = X * Y * (2 * own + x_first)
         return dict(first=base + first, start=start, rows=rows, splits=splits, terms=terms)
 
+    def send(value, name, n, pairs):
+        with jax.named_scope(f"{name}_{n}"):
+            return lax.ppermute(value, "dp", pairs)
+
     def run(*jobs, wait=()):
         nonlocal token
         table = after(blocks, *token, *wait)
-        results = combine(grad, table, [job[0] for job in jobs])
+        name = "_".join(f"{job[2]}{job[3]}" for job in jobs)
+        results = combine(grad, table, [job[0] for job in jobs], name)
         token = (results[0][0],)
-        for (_, use), result in zip(jobs, results):
+        for (_, use, *_), result in zip(jobs, results):
             use(*result)
 
     def then(*values):
         nonlocal token
         token = values
 
-    def swap_core(n, part, splits=(2, 2)):
+    def swap_core(n, first, splits):
         def use(*sent):
-            got[n] += [lax.ppermute(a, "dp", CORE_SWAP) for a in sent]
-
-        return task(n, False, half * part, splits, []), use
+            got[n] += [send(a, "core", n, CORE_SWAP) for a in sent]
+
+        return task(n, False, first, splits, []), use, "core", n
 
     def offsets(arrays, first):
         pairs, at = [], 0
@@ -348,97 +379,99 @@
 
     def x_sum(n):
         def use(*sent):
-            across[n] += [lax.ppermute(a, "dp", X_SWAP) for a in sent]
-
-        return task(n, True, 0, (2, 2), of_core(n, 0)), use
+            across[n] += [send(a, "cross", n, X_SWAP) for a in sent]
+
+        return task(n, True, 0, (2, 2), of_core(n, 0)), use, "cross", n
 
     def terms_at(n, first, count):
         terms = of_core(n, first) + (of_x(n, first) if CHUNKS[n][2] else [])
         return [(a, o) for a, o in terms if o < a.shape[0] and o + count > 0]
 
-    def step_1(n):
+    def far(n):
         first, size = (half, 1) if CHUNKS[n][2] else (0, X)
 
-        def use(far, near):
-            hop[n, 0] = lax.ppermute(far, "dp", Y_ON)
-            hop[n, 1] = lax.ppermute(near, "dp", Y_BACK)
-
-        return task(n, True, first, (size, size), terms_at(n, first, 2 * size)), use
-
-    def step_2(n):
+        def use(block):
+            hop[n, 0] = send(block, "far", n, Y_ON)
+
+        return task(n, True, first, (size,), terms_at(n, first, size)), use, "far", n
+
+    def near(n):
+        first, size = (half + 1, 1) if CHUNKS[n][2] else (X, X)
+
+        def use(block):
+            hop[n, 1] = send(block, "near", n, Y_BACK)
+
+        return task(n, True, first, (size,), terms_at(n, first, size)), use, "near", n
+
+    def ahead(n):
         first, size = (half + 2, 1) if CHUNKS[n][2] else (half, X)
 
         def use(block):
-            hop[n, 2] = lax.ppermute(block, "dp", Y_ON)
-
-        return task(n, True, first, (size,), terms_at(n, first, size) + [(hop[n, 0], 0)]), use
-
-    def step_3(n):
+            hop[n, 2] = send(block, "ahead", n, Y_ON)
+
+        terms = terms_at(n, first, size) + [(hop[n, 0], 0)]
+        return task(n, True, first, (size,), terms), use, "ahead", n
+
+    def here(n):
         first, splits = (half + 3, (1,)) if CHUNKS[n][2] else (half + X, (1, 1))
 
         def use(own, *block):
-            totals[n] = [own] + [lax.ppermute(b, "dp", X_SWAP) for b in block]
+            totals[n] = [own] + [send(b, "swap", n, X_SWAP) for b in block]
 
         terms = terms_at(n, first, len(splits)) + [(hop[n, 2], 0), (hop[n, 1], 0)]
-        return task(n, True, first, splits, terms), use
-
-    def give(n):
+        return task(n, True, first, splits, terms), use, "here", n
+
+    def place(n):
         (group,) = [g for g in GROUPS if n in g]
         base = min(CHUNKS[m][0] for m in group)
-        start, rows, _ = CHUNKS[n]
-        totals[n], ordered[group] = finish(
-            totals[n],
-            ordered.get(group),
-            after(holder, *token),
-            start - base,
-            rows,
-            sum(CHUNKS[m][1] for m in group),
-        )
-        then(totals[n])
+        return group, CHUNKS[n][0] - base, sum(CHUNKS[m][1] for m in group)
+
+    def give(n):
+        group, first, group_rows = place(n)
+        rows = CHUNKS[n][1]
+        parts, before = totals[n], ordered.get(group)
+        ordered[group] = finish(parts, before, after(holder, *token), first, rows, group_rows)
+        then(ordered[group])
 
     def to_holders(group):
-        ordered[group] = lax.all_to_all(ordered[group], "group", 0, 0)
+        sums[group] = lax.all_to_all(ordered[group], "group", 0, 0)
 
     def update(n):
         nonlocal done
+        group, first, _ = place(n)
         start, rows, _ = CHUNKS[n]
-        done = adam(after(totals[n], *token), state, done, start, rows)
+        done = adam(ordered[group], state, done, after(holder, *token), first, start, rows)
         then(done[0])
 
     def parities(group):
         nonlocal shards
         start = min(CHUNKS[m][0] for m in group)
         rows = sum(CHUNKS[m][1] for m in group)
-        shards = parity(ordered[group], olds, after(coeff, *token), shards, start, rows)
+        shards = parity(sums[group], olds, after(coeff, *token), shards, start, rows)
         then(shards)
 
-    run(swap_core(0, 0))
-    run(swap_core(2, 0))
-    run(step_1(0))
-    run(x_sum(2))
+    run(swap_core(0, 0, (1, 1)))
+    run(swap_core(0, 2, (1, 1)))
+    run(far(0))
     old = order_state(state, after(holder, *token))
     then(old)
-    olds = lax.all_to_all(old, "group", 0, 0)
-    run(swap_core(0, 1, (1, 1, 1, 1)), swap_core(1, 0))
-    run(step_2(0), swap_core(2, 1), wait=(across[2][0],))
-    run(step_1(1), swap_core(1, 1), wait=(hop[0, 1],))
-    run(step_3(0), wait=(across[2][1],))
-    run(step_2(1))
-    then(*token, hop[1, 1])
+    olds = lax.all_to_all(old, 'group', 0, 0)
+    run(near(0), swap_core(0, 4, (1, 1, 1, 1)))
+    run(swap_core(1, 0, (1, 1, 1, 1)), swap_core(1, 4, (1, 1, 1, 1)))
+    run(ahead(0))
+    run(far(1), wait=(hop[0, 1],))
+    run(near(1))
+    run(here(0))
+    run(ahead(1))
     give(0)
     to_holders((0,))
-    run(step_1(2), wait=(olds,))
-    run(step_3(1))
-    run(step_2(2))
+    run(here(1))
     update(0)
-    run(step_3(2))
-    give(2)
+    parities((0,))
     give(1)
-    to_holders((1, 2))
-    parities((0,))
+    to_holders((1,))
     update(1)
-    update(2)
-    parities((1, 2))
+    parities((1,))
     outs = [a.reshape(1, SHARD) for a in done]
     return (*outs, shards.transpose(2, 0, 1, 3).reshape(1, 1, 2, 3, ROWS * LANES))
 

time: 282 us -> 122 us (0.43)
  Pallas kernels: 151 us -> 51.4 us
  waiting for transfers between devices: 75.1 us -> 32.6 us
  local copies, waits for them, and re-layouts: 10.8 us -> 2.52 us
  starting transfers between devices: 41.5 us -> 33.5 us
    pallas_call x1, Pallas kernels: 97.1 us -> 2.41 us  [order_state(): pl.pallas_call(order_kernel, grid_spec=pltpu.PrefetchScalarGridSpec(num_s...]
    ppermute x27 -> x24, waiting for transfers between devices: 69 us -> 27.8 us  [send(): return lax.ppermute(value, 'dp', pairs)]
    unnamed x62 -> x14, local copies, waits for them, and re-layouts: 10.4 us -> 1.75 us
    ppermute x27 -> x24, starting transfers between devices: 24.7 us -> 16.4 us  [send(): return lax.ppermute(value, 'dp', pairs)]
    pallas_call x13 -> x11, Pallas kernels: 37.6 us -> 31.4 us  [combine(): pl.pallas_call(functools.partial(combine_kernel, static), grid_spec=pltpu...]
    pallas_call x3 -> x2, Pallas kernels: 3.62 us -> 6.69 us  [adam(): pl.pallas_call(functools.partial(adam_kernel, first, rows, start), grid_s...]
  transfers between devices with their start and end apart: 30 -> 27, of which waited for: 7 -> 7; matrix products, arithmetic and copies ran while one was open for 0% -> 0% of each run, Pallas kernels for 16% -> 37%
where the time goes in v4:
time: 122 us; the launch traced here: 121 us
  Pallas kernels  51.4 us (42%)
  starting transfers between devices  33.5 us (27%)
  waiting for transfers between devices  32.6 us (27%)
  local copies, waits for them, and re-layouts  2.52 us (2%)
    pallas_call x11, Pallas kernels, combine(): pl.pallas_call(functools.partial(combine_kernel, static), grid_spec=pltpu...  31.4 us
    ppermute x24, waiting for transfers between devices, send(): return lax.ppermute(value, 'dp', pairs)  27.8 us
    ppermute x24, starting transfers between devices, send(): return lax.ppermute(value, 'dp', pairs)  16.4 us
    all_to_all x2, starting transfers between devices, to_holders(): sums[group] = lax.all_to_all(ordered[group], 'group', 0, 0)  10.8 us
    pallas_call x2, Pallas kernels, parity(): pl.pallas_call(parity_kernel, grid_spec=pltpu.PrefetchScalarGridSpec(num_...  7.05 us
    pallas_call x2, Pallas kernels, adam(): pl.pallas_call(functools.partial(adam_kernel, first, rows, start), grid_s...  6.69 us
    all_to_all x1, starting transfers between devices, per_device(): olds = lax.all_to_all(old, 'group', 0, 0)  6.34 us
    all_to_all x2, waiting for transfers between devices, to_holders(): sums[group] = lax.all_to_all(ordered[group], 'group', 0, 0)  4.86 us
  transfers between devices with their start and end apart: 27, of which 7 were waited for; matrix products, arithmetic and copies ran while one was open for 0% of the time, Pallas kernels for 37%

profile of v4, /device:TPU:24, one launch (start us, length us, event | category | flops | bytes accessed | tf_op | source)
XLA Modules:
  0.0 121.0 jit_solution(2684183889340587502)
XLA Ops:
  1.3 1.9 %core0.2 = (f32[1,8,160,128]{3,2,1,0:T(8,128)S(1)}, f32[1,8,160,128]{3,2,1,0:T(8,128)S(1)}) custom-call(s32[32]{0:T(128)S(1)} %dynamic-slice_bitcast_fusion.table, bf16[128,1,32768]{2,1,0:T(2,128)(2,1)} %bitcast.28), custom_call_target="tpu_custom_call" | custom-call | bytes 640 | tf_op jit(solution)/shard_map/core0/pallas_call | solution.py:134
  3.8 2.9 %core0.3 = (f32[1,8,160,128]{3,2,1,0:T(8,128)}, f32[1,8,160,128]{3,2,1,0:T(8,128)}) custom-call(s32[32]{0:T(128)S(1)} %dynamic-slice_bitcast_fusion.table, bf16[128,1,32768]{2,1,0:T(2,128)(2,1)} %bitcast.29), custom_call_target="tpu_custom_call" | custom-call | bytes 640 | tf_op jit(solution)/shard_map/core0/pallas_call | solution.py:134
  7.4 3.0 %far0.1 = f32[2,8,160,128]{3,2,1,0:T(8,128)} custom-call(s32[32]{0:T(128)S(1)} %dynamic-slice_bitcast_fusion.table, bf16[128,1,32768]{2,1,0:T(2,128)(2,1)} %bitcast.30, f32[1,8,160,128]{3,2,1,0:T(8,128)S(1)} %collective-permute-done.refs_0_, f32[1,8,160,128]{3,2,1,0:T(8,128)S(1)} %collective-permute-done.1.refs_1_), custom_call_target="tpu_custom_call" | custom-call | bytes 960 | tf_op jit(solution)/shard_map/far0/pallas_call | solution.py:134
  10.7 2.4 %order.1 = f32[8,3,256,128]{3,2,1,0:T(8,128)} custom-call(s32[8]{0:T(128)S(1)} %bitcast.23, f32[8,256,128]{2,1,0:T(8,128)S(1)} %bitcast.16, f32[8,256,128]{2,1,0:T(8,128)S(1)} %bitcast.19, f32[8,256,128]{2,1,0:T(8,128)S(1)} %bitcast.22), custom_call_target="tpu_custom_call" | custom-call | bytes 1536 | tf_op jit(solution)/shard_map/order/pallas_call | solution.py:170
  13.1 6.3 %all-to-all-start.1 = ((f32[8,3,256,128]{3,2,1,0:T(8,128)}), f32[8,3,256,128]{3,2,1,0:T(8,128)S(1)}, u32[]{:S(2)}, u32[]{:S(2)}) async-start(f32[8,3,256,128]{3,2,1,0:T(8,128)} %order.1), calls=%async_computation.1 | async-start | bytes 6291456 | tf_op jit(solution)/shard_map/all_to_all | solution.py:458
  19.4 4.0 %near0_core0.1 = (f32[2,8,160,128]{3,2,1,0:T(8,128)S(1)}, f32[1,8,160,128]{3,2,1,0:T(8,128)S(1)}, f32[1,8,160,128]{3,2,1,0:T(8,128)S(1)}, f32[1,8,160,128]{3,2,1,0:T(8,128)S(1)}, f32[1,8,160,128]{3,2,1,0:T(8,128)S(1)}) custom-call(s32[32]{0:T(128)S(1)} %dynamic-slice_bitcast_fusion.table, bf16[128,1,32768]{2,1,0:T(2,128)(2,1)} %bitcast.31, ...), custom_call_target="tpu_custom_call" | custom-call | bytes 2240 | tf_op jit(solution)/shard_map/near0_core0/pallas_call | solution.py:134
  23.4 1.9 %collective-permute-start.7 = (f32[2,8,160,128]{3,2,1,0:T(8,128)S(1)}, f32[2,8,160,128]{3,2,1,0:T(8,128)S(1)}, u32[]{:S(2)}, u32[]{:S(2)}) collective-permute-start(f32[2,8,160,128]{3,2,1,0:T(8,128)S(1)} %get-tuple-element.56), channel_id=1, source_target_pairs={{0,48},{8,24},{16,0},{24,40},{32,16},{40,56},{48,32},{56,8},{64,11... | collective-permute-start | bytes 3932168 | tf_op jit(solution)/shard_map/near_0/ppermute | solution.py:346
  26.0 3.3 %core1_core1.1 = (f32[1,8,96,128]{3,2,1,0:T(8,128)S(1)}, f32[1,8,96,128]{3,2,1,0:T(8,128)S(1)}, f32[1,8,96,128]{3,2,1,0:T(8,128)S(1)}, f32[1,8,96,128]{3,2,1,0:T...) custom-call(s32[32]{0:T(128)S(1)} %dynamic-slice_bitcast_fusion.tabl, ...), custom_call_target="tpu_custom_call" | custom-call | bytes 1536 | tf_op jit(solution)/shard_map/core1_core1/pallas_call | solution.py:134
  30.3 3.3 %ahead0.1 = f32[2,8,160,128]{3,2,1,0:T(8,128)S(1)} custom-call(s32[32]{0:T(128)S(1)} %dynamic-slice_bitcast_fusion.table, bf16[128,1,32768]{2,1,0:T(2,128)(2,1)} %bitcast.33, f32[1,8,160,128]{3,2,1,0:T(8,128)S(1)} %collective-permute-done.4.refs_0_, f32[1,8,160,128]{3,2,1,0:T(8,128)S(1)} %collective-permute-done.5.refs_1_, ...), custom_call_target="tpu_custom_call" | custom-call | bytes 1280 | tf_op jit(solution)/shard_map/ahead0/pallas_call | solution.py:134
  34.6 14.0 %collective-permute-done.7.refs_3_ = f32[2,8,160,128]{3,2,1,0:T(8,128)S(1)} collective-permute-done((f32[2,8,160,128]{3,2,1,0:T(8,128)S(1)}, f32[2,8,160,128]{3,2,1,0:T(8,128)S(1)}, u32[]{:S(2)}, u32[]{:S(2)}) %collective-permute-start.7) | collective-permute-done | bytes 1310752 | tf_op jit(solution)/shard_map/near_0/ppermute | solution.py:346
  48.7 1.7 %far1.1 = f32[2,8,96,128]{3,2,1,0:T(8,128)S(1)} custom-call(s32[32]{0:T(128)S(1)} %dynamic-slice_bitcast_fusion.table, bf16[128,1,32768]{2,1,0:T(2,128)(2,1)} %bitcast.34, f32[1,8,96,128]{3,2,1,0:T(8,128)S(1)} %collective-permute-done.8.refs_0_, f32[1,8,96,128]{3,2,1,0:T(8,128)S(1)} %collective-permute-done.9.refs_1_), custom_call_target="tpu_custom_call" | custom-call | bytes 576 | tf_op jit(solution)/shard_map/far1/pallas_call | solution.py:134
  51.9 2.6 %near1.1 = f32[2,8,96,128]{3,2,1,0:T(8,128)} custom-call(s32[32]{0:T(128)S(1)} %dynamic-slice_bitcast_fusion.table, bf16[128,1,32768]{2,1,0:T(2,128)(2,1)} %bitcast.35, f32[1,8,96,128]{3,2,1,0:T(8,128)S(1)} %collective-permute-done.10.refs_0_, f32[1,8,96,128]{3,2,1,0:T(8,128)S(1)} %collective-permute-done.11.refs_1_), custom_call_target="tpu_custom_call" | custom-call | bytes 576 | tf_op jit(solution)/shard_map/near1/pallas_call | solution.py:134
  54.5 1.9 %collective-permute-done.14.refs_2_ = f32[2,8,160,128]{3,2,1,0:T(8,128)S(1)} collective-permute-done((f32[2,8,160,128]{3,2,1,0:T(8,128)S(1)}, f32[2,8,160,128]{3,2,1,0:T(8,128)S(1)}, u32[]{:S(2)}, u32[]{:S(2)}) %collective-permute-start.14) | collective-permute-done | bytes 1310752 | tf_op jit(solution)/shard_map/ahead_0/ppermute | solution.py:346
  56.4 2.0 %here0.1 = (f32[1,8,160,128]{3,2,1,0:T(8,128)S(1)}, f32[1,8,160,128]{3,2,1,0:T(8,128)S(1)}) custom-call(s32[32]{0:T(128)S(1)} %dynamic-slice_bitcast_fusion.table, bf16[128,1,32768]{2,1,0:T(2,128)(2,1)} %bitcast.36, f32[1,8,160,128]{3,2,1,0:T(8,128)S(1)} %collective-permute-done.12.refs_0_, f32[1,8,160,128]{3,2,1,0:T(8,128)S(1)} %collective-permute-done.13.refs_1_, ...), custom_call_target="tpu_custom_call" | custom-call | bytes 1600 | tf_op jit(solution)/shard_map/here0/pallas_call | solution.py:134
  58.4 3.1 %collective-permute-start.18 = (f32[1,8,160,128]{3,2,1,0:T(8,128)S(1)}, f32[1,8,160,128]{3,2,1,0:T(8,128)S(1)}, u32[]{:S(2)}, u32[]{:S(2)}) collective-permute-start(f32[1,8,160,128]{3,2,1,0:T(8,128)S(1)} %get-tuple-element.75), channel_id=1, source_target_pairs={{0,64},{8,72},{16,80},{24,88},{32,96},{40,104},{48,112},{56,120},{... | collective-permute-start | bytes 1966088 | tf_op jit(solution)/shard_map/swap_0/ppermute | solution.py:346
  62.3 2.5 %collective-permute-done.17.refs_2_ = f32[2,8,96,128]{3,2,1,0:T(8,128)S(1)} collective-permute-done((f32[2,8,96,128]{3,2,1,0:T(8,128)S(1)}, f32[2,8,96,128]{3,2,1,0:T(8,128)S(1)}, u32[]{:S(2)}, u32[]{:S(2)}) %collective-permute-start.17) | collective-permute-done | bytes 786464 | tf_op jit(solution)/shard_map/far_1/ppermute | solution.py:346
  64.8 2.6 %ahead1.1 = f32[2,8,96,128]{3,2,1,0:T(8,128)} custom-call(s32[32]{0:T(128)S(1)} %dynamic-slice_bitcast_fusion.table, bf16[128,1,32768]{2,1,0:T(2,128)(2,1)} %bitcast.37, f32[1,8,96,128]{3,2,1,0:T(8,128)S(1)} %collective-permute-done.15.refs_0_, f32[1,8,96,128]{3,2,1,0:T(8,128)S(1)} %collective-permute-done.16.refs_1_, ...), custom_call_target="tpu_custom_call" | custom-call | bytes 768 | tf_op jit(solution)/shard_map/ahead1/pallas_call | solution.py:134
  67.5 2.1 %collective-permute-start.21 = (f32[2,8,96,128]{3,2,1,0:T(8,128)}, f32[2,8,96,128]{3,2,1,0:T(8,128)}, u32[]{:S(2)}, u32[]{:S(2)}) collective-permute-start(f32[2,8,96,128]{3,2,1,0:T(8,128)} %ahead1.1), channel_id=1, source_target_pairs={{0,16},{8,56},{16,32},{24,8},{32,48},{40,24},{48,0},{56,40},{64,80... | collective-permute-start | bytes 2359304 | tf_op jit(solution)/shard_map/ahead_1/ppermute | solution.py:346
  70.1 7.2 %collective-permute-done.18.refs_1_ = f32[1,8,160,128]{3,2,1,0:T(8,128)S(1)} collective-permute-done((f32[1,8,160,128]{3,2,1,0:T(8,128)S(1)}, f32[1,8,160,128]{3,2,1,0:T(8,128)S(1)}, u32[]{:S(2)}, u32[]{:S(2)}) %collective-permute-start.18) | collective-permute-done | bytes 655392 | tf_op jit(solution)/shard_map/swap_0/ppermute | solution.py:346
  77.3 1.5 %finish.2.ordered = f32[8,160,128]{2,1,0:T(8,128)} custom-call(s32[8]{0:T(128)S(1)} %bitcast.24, f32[1,8,160,128]{3,2,1,0:T(8,128)S(1)} %get-tuple-element.70.refs_0_, f32[1,8,160,128]{3,2,1,0:T(8,128)S(1)} %collective-permute-done.18.refs_1_), custom_call_target="tpu_custom_call" | custom-call | bytes 640 | tf_op jit(solution)/shard_map/finish/pallas_call | solution.py:206
  78.9 6.0 %all-to-all-start = ((f32[8,160,128]{2,1,0:T(8,128)}), f32[8,160,128]{2,1,0:T(8,128)}, u32[]{:S(2)}, u32[]{:S(2)}) async-start(f32[8,160,128]{2,1,0:T(8,128)} %finish.2.ordered), calls=%async_computation | async-start | bytes 1310720 | tf_op jit(solution)/shard_map/all_to_all | solution.py:437
  85.6 1.0 copy-done.4
  86.6 4.0 %here1.1 = (f32[1,8,96,128]{3,2,1,0:T(8,128)S(1)}, f32[1,8,96,128]{3,2,1,0:T(8,128)}) custom-call(s32[32]{0:T(128)S(1)} %dynamic-slice_bitcast_fusion.table, bf16[128,1,32768]{2,1,0:T(2,128)(2,1)} %bitcast.38, f32[1,8,96,128]{3,2,1,0:T(8,128)S(1)} %copy-done.4, f32[1,8,96,128]{3,2,1,0:T(8,128)} %collective-permute-done.20.refs_1_, ...), custom_call_target="tpu_custom_call" | custom-call | bytes 960 | tf_op jit(solution)/shard_map/here1/pallas_call | solution.py:134
  90.6 2.8 %collective-permute-start.23 = (f32[1,8,96,128]{3,2,1,0:T(8,128)}, f32[1,8,96,128]{3,2,1,0:T(8,128)}, u32[]{:S(2)}, u32[]{:S(2)}) collective-permute-start(f32[1,8,96,128]{3,2,1,0:T(8,128)} %get-tuple-element.84), channel_id=1, source_target_pairs={{0,64},{8,72},{16,80},{24,88},{32,96},{40,104},{48,112},{56,120},{... | collective-permute-start | bytes 1179656 | tf_op jit(solution)/shard_map/swap_1/ppermute | solution.py:346
  93.6 3.6 %adam.2 = (f32[8,256,128]{2,1,0:T(8,128)}, f32[8,256,128]{2,1,0:T(8,128)}, f32[8,256,128]{2,1,0:T(8,128)}) custom-call(s32[8]{0:T(128)S(1)} %bitcast.25, f32[8,160,128]{2,1,0:T(8,128)} %finish.2.ordered, f32[8,256,128]{2,1,0:T(8,128)} %bitcast.14, f32[8,256,128]{2,1,0:T(8,128)} %bitcast.17, f32[8,256,128]{2,1,0:T(8,128)} %bitcast.20), custom_call_target="tpu_custom_call" | custom-call | bytes 1120 | tf_op jit(solution)/shard_map/adam/pallas_call | solution.py:263
  97.1 4.7 %parity.2.refs_0_ = f32[3,256,2,128]{3,2,1,0:T(2,128)} custom-call(f32[2,8]{1,0:T(2,128)S(1)} %add_divide_fusion.coeff, f32[8,160,128]{2,1,0:T(8,128)} %all-to-all-done.sums, f32[8,3,256,128]{3,2,1,0:T(8,128)S(1)} %all-to-all-done.1.old), custom_call_target="tpu_custom_call" | custom-call | bytes 640 | tf_op jit(solution)/shard_map/parity/pallas_call | solution.py:302
  101.8 1.6 %collective-permute-done.23.refs_1_ = f32[1,8,96,128]{3,2,1,0:T(8,128)} collective-permute-done((f32[1,8,96,128]{3,2,1,0:T(8,128)}, f32[1,8,96,128]{3,2,1,0:T(8,128)}, u32[]{:S(2)}, u32[]{:S(2)}) %collective-permute-start.23) | collective-permute-done | bytes 393248 | tf_op jit(solution)/shard_map/swap_1/ppermute | solution.py:346
  103.4 2.4 %finish.3.ordered = f32[8,96,128]{2,1,0:T(8,128)} custom-call(s32[8]{0:T(128)S(1)} %bitcast.26, f32[1,8,96,128]{3,2,1,0:T(8,128)S(1)} %get-tuple-element.79.refs_0_, f32[1,8,96,128]{3,2,1,0:T(8,128)} %collective-permute-done.23.refs_1_), custom_call_target="tpu_custom_call" | custom-call | bytes 384 | tf_op jit(solution)/shard_map/finish/pallas_call | solution.py:206
  105.8 4.8 %all-to-all-start.2 = ((f32[8,96,128]{2,1,0:T(8,128)}), f32[8,96,128]{2,1,0:T(8,128)S(1)}, u32[]{:S(2)}, u32[]{:S(2)}) async-start(f32[8,96,128]{2,1,0:T(8,128)} %finish.3.ordered), calls=%async_computation.2 | async-start | bytes 786432 | tf_op jit(solution)/shard_map/all_to_all | solution.py:437
  110.7 3.1 %adam.3 = (f32[8,256,128]{2,1,0:T(8,128)}, f32[8,256,128]{2,1,0:T(8,128)}, f32[8,256,128]{2,1,0:T(8,128)}) custom-call(s32[8]{0:T(128)S(1)} %bitcast.27, f32[8,96,128]{2,1,0:T(8,128)} %finish.3.ordered, f32[8,256,128]{2,1,0:T(8,128)} %bitcast.15, f32[8,256,128]{2,1,0:T(8,128)} %bitcast.18, ...), custom_call_target="tpu_custom_call", output_to_operand_aliasing={{0}: (5, {}), {1}: (6, {}), {2}: (7, {})} | custom-call | bytes 672 | tf_op jit(solution)/shard_map/adam/pallas_call | solution.py:263
  113.8 4.9 %all-to-all-done.2.sums = f32[8,96,128]{2,1,0:T(8,128)S(1)} async-done(((f32[8,96,128]{2,1,0:T(8,128)}), f32[8,96,128]{2,1,0:T(8,128)S(1)}, u32[]{:S(2)}, u32[]{:S(2)}) %all-to-all-start.2) | async-done | bytes 393248 | tf_op jit(solution)/shard_map/all_to_all | solution.py:437
  118.6 2.4 %parity.3 = f32[3,256,2,128]{3,2,1,0:T(2,128)} custom-call(f32[2,8]{1,0:T(2,128)S(1)} %add_divide_fusion.coeff, f32[8,96,128]{2,1,0:T(8,128)S(1)} %all-to-all-done.2.sums, f32[8,3,256,128]{3,2,1,0:T(8,128)S(1)} %all-to-all-done.1.old, f32[3,256,2,128]{3,2,1,0:T(2,128)} %parity.2.refs_0_), custom_call_target="tpu_custom_call", output_to_operand_aliasing={{}: (3, {})} | custom-call | bytes 384 | tf_op jit(solution)/shard_map/parity/pallas_call | solution.py:302
  (58 shorter events, 8.5 us)
Async XLA Ops:
  3.2 4.2 %collective-permute-start.1 = (f32[1,8,160,128]{3,2,1,0:T(8,128)S(1)}, f32[1,8,160,128]{3,2,1,0:T(8,128)S(1)}, u32[]{:S(2)}, u32[]{:S(2)}) collective-permute-start(f32[1,8,160,128]{3,2,1,0:T(8,128)S(1)} %get-tuple-element.52), channel_id=1, source_target_pairs={{0,8},{8,0},{16,24},{24,16},{32,40},{40,32},{48,56},{56,48},{64,72... | collective-permute-start | bytes 1966088 | tf_op jit(solution)/shard_map/core_0/ppermute | solution.py:346
  3.3 4.1 %collective-permute-start = (f32[1,8,160,128]{3,2,1,0:T(8,128)S(1)}, f32[1,8,160,128]{3,2,1,0:T(8,128)S(1)}, u32[]{:S(2)}, u32[]{:S(2)}) collective-permute-start(f32[1,8,160,128]{3,2,1,0:T(8,128)S(1)} %get-tuple-element.48), channel_id=1, source_target_pairs={{0,8},{8,0},{16,24},{24,16},{32,40},{40,32},{48,56},{56,48},{64,72... | collective-permute-start | bytes 1966088 | tf_op jit(solution)/shard_map/core_0/ppermute | solution.py:346
  6.7 12.7 %collective-permute-start.3 = (f32[1,8,160,128]{3,2,1,0:T(8,128)}, f32[1,8,160,128]{3,2,1,0:T(8,128)}, u32[]{:S(2)}, u32[]{:S(2)}) collective-permute-start(f32[1,8,160,128]{3,2,1,0:T(8,128)} %get-tuple-element.55), channel_id=1, source_target_pairs={{0,8},{8,0},{16,24},{24,16},{32,40},{40,32},{48,56},{56,48},{64,72... | collective-permute-start | bytes 1966088 | tf_op jit(solution)/shard_map/core_0/ppermute | solution.py:346
  6.9 3.7 %copy-start = (f32[1,262144]{1,0:T(1,128)S(1)}, f32[1,262144]{1,0:T(1,128)}, u32[]{:S(2)}) copy-start(f32[1,262144]{1,0:T(1,128)} %param.8) | copy-start | bytes 3145732
  6.9 3.7 %copy-start.1 = (f32[1,262144]{1,0:T(1,128)S(1)}, f32[1,262144]{1,0:T(1,128)}, u32[]{:S(2)}) copy-start(f32[1,262144]{1,0:T(1,128)} %param.9) | copy-start | bytes 3145732
  6.9 3.7 %copy-start.2 = (f32[1,262144]{1,0:T(1,128)S(1)}, f32[1,262144]{1,0:T(1,128)}, u32[]{:S(2)}) copy-start(f32[1,262144]{1,0:T(1,128)} %param.10) | copy-start | bytes 3145732
  6.9 3.7 %copy-start.5 = (s32[1,8]{1,0:T(1,128)S(1)}, s32[1,8]{1,0:T(1,128)}, u32[]{:S(2)}) copy-start(s32[1,8]{1,0:T(1,128)} %param.12) | copy-start | bytes 100
  6.9 12.5 %collective-permute-start.2 = (f32[1,8,160,128]{3,2,1,0:T(8,128)}, f32[1,8,160,128]{3,2,1,0:T(8,128)}, u32[]{:S(2)}, u32[]{:S(2)}) collective-permute-start(f32[1,8,160,128]{3,2,1,0:T(8,128)} %get-tuple-element.50), channel_id=1, source_target_pairs={{0,8},{8,0},{16,24},{24,16},{32,40},{40,32},{48,56},{56,48},{64,72... | collective-permute-start | bytes 1966088 | tf_op jit(solution)/shard_map/core_0/ppermute | solution.py:346
  10.4 19.9 %collective-permute-start.6 = (f32[2,8,160,128]{3,2,1,0:T(8,128)}, f32[2,8,160,128]{3,2,1,0:T(8,128)}, u32[]{:S(2)}, u32[]{:S(2)}) collective-permute-start(f32[2,8,160,128]{3,2,1,0:T(8,128)} %far0.1), channel_id=1, source_target_pairs={{0,16},{8,56},{16,32},{24,8},{32,48},{40,24},{48,0},{56,40},{64,80... | collective-permute-start | bytes 3932168 | tf_op jit(solution)/shard_map/far_0/ppermute | solution.py:346
  13.1 65.8 %all-to-all-start.1 = ((f32[8,3,256,128]{3,2,1,0:T(8,128)}), f32[8,3,256,128]{3,2,1,0:T(8,128)S(1)}, u32[]{:S(2)}, u32[]{:S(2)}) async-start(f32[8,3,256,128]{3,2,1,0:T(8,128)} %order.1), calls=%async_computation.1 | async-start | bytes 6291456 | tf_op jit(solution)/shard_map/all_to_all | solution.py:458
  23.4 25.2 %collective-permute-start.7 = (f32[2,8,160,128]{3,2,1,0:T(8,128)S(1)}, f32[2,8,160,128]{3,2,1,0:T(8,128)S(1)}, u32[]{:S(2)}, u32[]{:S(2)}) collective-permute-start(f32[2,8,160,128]{3,2,1,0:T(8,128)S(1)} %get-tuple-element.56), channel_id=1, source_target_pairs={{0,48},{8,24},{16,0},{24,40},{32,16},{40,56},{48,32},{56,8},{64,11... | collective-permute-start | bytes 3932168 | tf_op jit(solution)/shard_map/near_0/ppermute | solution.py:346
  25.3 4.6 %collective-permute-start.4 = (f32[1,8,160,128]{3,2,1,0:T(8,128)S(1)}, f32[1,8,160,128]{3,2,1,0:T(8,128)S(1)}, u32[]{:S(2)}, u32[]{:S(2)}) collective-permute-start(f32[1,8,160,128]{3,2,1,0:T(8,128)S(1)} %get-tuple-element.60), channel_id=1, source_target_pairs={{0,8},{8,0},{16,24},{24,16},{32,40},{40,32},{48,56},{56,48},{64,72... | collective-permute-start | bytes 1966088 | tf_op jit(solution)/shard_map/core_0/ppermute | solution.py:346
  26.0 3.9 %collective-permute-start.5 = (f32[1,8,160,128]{3,2,1,0:T(8,128)S(1)}, f32[1,8,160,128]{3,2,1,0:T(8,128)S(1)}, u32[]{:S(2)}, u32[]{:S(2)}) collective-permute-start(f32[1,8,160,128]{3,2,1,0:T(8,128)S(1)} %get-tuple-element.61), channel_id=1, source_target_pairs={{0,8},{8,0},{16,24},{24,16},{32,40},{40,32},{48,56},{56,48},{64,72... | collective-permute-start | bytes 1966088 | tf_op jit(solution)/shard_map/core_0/ppermute | solution.py:346
  29.3 5.3 %collective-permute-start.9 = (f32[1,8,96,128]{3,2,1,0:T(8,128)S(1)}, f32[1,8,96,128]{3,2,1,0:T(8,128)S(1)}, u32[]{:S(2)}, u32[]{:S(2)}) collective-permute-start(f32[1,8,96,128]{3,2,1,0:T(8,128)S(1)} %get-tuple-element.63), channel_id=1, source_target_pairs={{0,8},{8,0},{16,24},{24,16},{32,40},{40,32},{48,56},{56,48},{64,72... | collective-permute-start | bytes 1179656 | tf_op jit(solution)/shard_map/core_1/ppermute | solution.py:346
  33.6 22.8 %collective-permute-start.14 = (f32[2,8,160,128]{3,2,1,0:T(8,128)S(1)}, f32[2,8,160,128]{3,2,1,0:T(8,128)S(1)}, u32[]{:S(2)}, u32[]{:S(2)}) collective-permute-start(f32[2,8,160,128]{3,2,1,0:T(8,128)S(1)} %ahead0.1), channel_id=1, source_target_pairs={{0,16},{8,56},{16,32},{24,8},{32,48},{40,24},{48,0},{56,40},{64,80... | collective-permute-start | bytes 3932168 | tf_op jit(solution)/shard_map/ahead_0/ppermute | solution.py:346
  34.1 14.6 %collective-permute-start.8 = (f32[1,8,96,128]{3,2,1,0:T(8,128)S(1)}, f32[1,8,96,128]{3,2,1,0:T(8,128)S(1)}, u32[]{:S(2)}, u32[]{:S(2)}) collective-permute-start(f32[1,8,96,128]{3,2,1,0:T(8,128)S(1)} %get-tuple-element.58), channel_id=1, source_target_pairs={{0,8},{8,0},{16,24},{24,16},{32,40},{40,32},{48,56},{56,48},{64,72... | collective-permute-start | bytes 1179656 | tf_op jit(solution)/shard_map/core_1/ppermute | solution.py:346
  34.1 17.2 %collective-permute-start.10 = (f32[1,8,96,128]{3,2,1,0:T(8,128)S(1)}, f32[1,8,96,128]{3,2,1,0:T(8,128)S(1)}, u32[]{:S(2)}, u32[]{:S(2)}) collective-permute-start(f32[1,8,96,128]{3,2,1,0:T(8,128)S(1)} %get-tuple-element.65), channel_id=1, source_target_pairs={{0,8},{8,0},{16,24},{24,16},{32,40},{40,32},{48,56},{56,48},{64,72... | collective-permute-start | bytes 1179656 | tf_op jit(solution)/shard_map/core_1/ppermute | solution.py:346
  34.6 17.2 %collective-permute-start.12 = (f32[1,8,160,128]{3,2,1,0:T(8,128)S(1)}, f32[1,8,160,128]{3,2,1,0:T(8,128)S(1)}, u32[]{:S(2)}, u32[]{:S(2)}) collective-permute-start(f32[1,8,160,128]{3,2,1,0:T(8,128)S(1)} %get-tuple-element.68), channel_id=1, source_target_pairs={{0,8},{8,0},{16,24},{24,16},{32,40},{40,32},{48,56},{56,48},{64,72... | collective-permute-start | bytes 1966088 | tf_op jit(solution)/shard_map/core_0/ppermute | solution.py:346
  48.6 2.7 %collective-permute-start.11 = (f32[1,8,96,128]{3,2,1,0:T(8,128)S(1)}, f32[1,8,96,128]{3,2,1,0:T(8,128)S(1)}, u32[]{:S(2)}, u32[]{:S(2)}) collective-permute-start(f32[1,8,96,128]{3,2,1,0:T(8,128)S(1)} %get-tuple-element.66), channel_id=1, source_target_pairs={{0,8},{8,0},{16,24},{24,16},{32,40},{40,32},{48,56},{56,48},{64,72... | collective-permute-start | bytes 1179656 | tf_op jit(solution)/shard_map/core_1/ppermute | solution.py:346
  50.4 14.5 %collective-permute-start.17 = (f32[2,8,96,128]{3,2,1,0:T(8,128)S(1)}, f32[2,8,96,128]{3,2,1,0:T(8,128)S(1)}, u32[]{:S(2)}, u32[]{:S(2)}) collective-permute-start(f32[2,8,96,128]{3,2,1,0:T(8,128)S(1)} %far1.1), channel_id=1, source_target_pairs={{0,16},{8,56},{16,32},{24,8},{32,48},{40,24},{48,0},{56,40},{64,80... | collective-permute-start | bytes 2359304 | tf_op jit(solution)/shard_map/far_1/ppermute | solution.py:346
  51.3 3.2 %collective-permute-start.13 = (f32[1,8,160,128]{3,2,1,0:T(8,128)S(1)}, f32[1,8,160,128]{3,2,1,0:T(8,128)S(1)}, u32[]{:S(2)}, u32[]{:S(2)}) collective-permute-start(f32[1,8,160,128]{3,2,1,0:T(8,128)S(1)} %get-tuple-element.69), channel_id=1, source_target_pairs={{0,8},{8,0},{16,24},{24,16},{32,40},{40,32},{48,56},{56,48},{64,72... | collective-permute-start | bytes 1966088 | tf_op jit(solution)/shard_map/core_0/ppermute | solution.py:346
  51.4 10.9 %collective-permute-start.15 = (f32[1,8,96,128]{3,2,1,0:T(8,128)S(1)}, f32[1,8,96,128]{3,2,1,0:T(8,128)S(1)}, u32[]{:S(2)}, u32[]{:S(2)}) collective-permute-start(f32[1,8,96,128]{3,2,1,0:T(8,128)S(1)} %get-tuple-element.72), channel_id=1, source_target_pairs={{0,8},{8,0},{16,24},{24,16},{32,40},{40,32},{48,56},{56,48},{64,72... | collective-permute-start | bytes 1179656 | tf_op jit(solution)/shard_map/core_1/ppermute | solution.py:346
  51.8 10.5 %collective-permute-start.16 = (f32[1,8,96,128]{3,2,1,0:T(8,128)S(1)}, f32[1,8,96,128]{3,2,1,0:T(8,128)S(1)}, u32[]{:S(2)}, u32[]{:S(2)}) collective-permute-start(f32[1,8,96,128]{3,2,1,0:T(8,128)S(1)} %get-tuple-element.73), channel_id=1, source_target_pairs={{0,8},{8,0},{16,24},{24,16},{32,40},{40,32},{48,56},{56,48},{64,72... | collective-permute-start | bytes 1179656 | tf_op jit(solution)/shard_map/core_1/ppermute | solution.py:346
  58.4 18.9 %collective-permute-start.18 = (f32[1,8,160,128]{3,2,1,0:T(8,128)S(1)}, f32[1,8,160,128]{3,2,1,0:T(8,128)S(1)}, u32[]{:S(2)}, u32[]{:S(2)}) collective-permute-start(f32[1,8,160,128]{3,2,1,0:T(8,128)S(1)} %get-tuple-element.75), channel_id=1, source_target_pairs={{0,64},{8,72},{16,80},{24,88},{32,96},{40,104},{48,112},{56,120},{... | collective-permute-start | bytes 1966088 | tf_op jit(solution)/shard_map/swap_0/ppermute | solution.py:346
  61.6 24.0 %collective-permute-start.22 = (f32[2,8,96,128]{3,2,1,0:T(8,128)}, f32[2,8,96,128]{3,2,1,0:T(8,128)}, u32[]{:S(2)}, u32[]{:S(2)}) collective-permute-start(f32[2,8,96,128]{3,2,1,0:T(8,128)} %near1.1), channel_id=1, source_target_pairs={{0,48},{8,24},{16,0},{24,40},{32,16},{40,56},{48,32},{56,8},{64,11... | collective-permute-start | bytes 2359304 | tf_op jit(solution)/shard_map/near_1/ppermute | solution.py:346
  67.5 18.1 %collective-permute-start.21 = (f32[2,8,96,128]{3,2,1,0:T(8,128)}, f32[2,8,96,128]{3,2,1,0:T(8,128)}, u32[]{:S(2)}, u32[]{:S(2)}) collective-permute-start(f32[2,8,96,128]{3,2,1,0:T(8,128)} %ahead1.1), channel_id=1, source_target_pairs={{0,16},{8,56},{16,32},{24,8},{32,48},{40,24},{48,0},{56,40},{64,80... | collective-permute-start | bytes 2359304 | tf_op jit(solution)/shard_map/ahead_1/ppermute | solution.py:346
  69.6 15.2 %collective-permute-start.19 = (f32[1,8,96,128]{3,2,1,0:T(8,128)}, f32[1,8,96,128]{3,2,1,0:T(8,128)S(1)}, u32[]{:S(2)}, u32[]{:S(2)}) collective-permute-start(f32[1,8,96,128]{3,2,1,0:T(8,128)} %get-tuple-element.77), channel_id=1, source_target_pairs={{0,8},{8,0},{16,24},{24,16},{32,40},{40,32},{48,56},{56,48},{64,72... | collective-permute-start | bytes 1179656 | tf_op jit(solution)/shard_map/core_1/ppermute | solution.py:346
  69.6 16.0 %collective-permute-start.20 = (f32[1,8,96,128]{3,2,1,0:T(8,128)}, f32[1,8,96,128]{3,2,1,0:T(8,128)}, u32[]{:S(2)}, u32[]{:S(2)}) collective-permute-start(f32[1,8,96,128]{3,2,1,0:T(8,128)} %get-tuple-element.78), channel_id=1, source_target_pairs={{0,8},{8,0},{16,24},{24,16},{32,40},{40,32},{48,56},{56,48},{64,72... | collective-permute-start | bytes 1179656 | tf_op jit(solution)/shard_map/core_1/ppermute | solution.py:346
  78.9 14.5 %copy-start.6 = (s32[10]{0:T(128)S(1)}, s32[10]{0:T(128)}, u32[]{:S(2)}) copy-start(s32[10]{0:T(128)} %param.11) | copy-start | bytes 124
  78.9 18.3 %all-to-all-start = ((f32[8,160,128]{2,1,0:T(8,128)}), f32[8,160,128]{2,1,0:T(8,128)}, u32[]{:S(2)}, u32[]{:S(2)}) async-start(f32[8,160,128]{2,1,0:T(8,128)} %finish.2.ordered), calls=%async_computation | async-start | bytes 1310720 | tf_op jit(solution)/shard_map/all_to_all | solution.py:437
  90.6 12.8 %collective-permute-start.23 = (f32[1,8,96,128]{3,2,1,0:T(8,128)}, f32[1,8,96,128]{3,2,1,0:T(8,128)}, u32[]{:S(2)}, u32[]{:S(2)}) collective-permute-start(f32[1,8,96,128]{3,2,1,0:T(8,128)} %get-tuple-element.84), channel_id=1, source_target_pairs={{0,64},{8,72},{16,80},{24,88},{32,96},{40,104},{48,112},{56,120},{... | collective-permute-start | bytes 1179656 | tf_op jit(solution)/shard_map/swap_1/ppermute | solution.py:346
  105.8 12.8 %all-to-all-start.2 = ((f32[8,96,128]{2,1,0:T(8,128)}), f32[8,96,128]{2,1,0:T(8,128)S(1)}, u32[]{:S(2)}, u32[]{:S(2)}) async-start(f32[8,96,128]{2,1,0:T(8,128)} %finish.3.ordered), calls=%async_computation.2 | async-start | bytes 786432 | tf_op jit(solution)/shard_map/all_to_all | solution.py:437
  (2 other events, 1.7 us)

commit v5 on v4

--- a/solution.py
+++ b/solution.py
@@ -16,7 +16,6 @@
 SHARD = G * ROWS * LANES
 CHUNKS = ((0, 160, False), (160, 96, False))
 GROUPS = ((0,), (1,))
-TILE = 32
 VMEM = 8 * 2**20
 
 
@@ -82,62 +81,83 @@
 
 
 def combine_kernel(tasks, table, grad, *refs):
-    arrays = sum(len(task["offsets"]) for task in tasks)
+    arrays = sum(len(term["rows"]) for task in tasks for term in task["terms"])
     pieces = sum(len(task["splits"]) for task in tasks)
-    terms, outs, scratch = refs[:arrays], refs[arrays : arrays + pieces], refs[arrays + pieces :]
+    given, outs, scratch = refs[:arrays], refs[arrays : arrays + pieces], refs[arrays + pieces :]
     work = []
-    for n, task in enumerate(tasks):
-        held, sems = scratch[2 * n : 2 * n + 2]
-        size = task["rows"] * LANES
+    for task in tasks:
+        (held, sems), scratch = scratch[:2], scratch[2:]
+        count, size = sum(task["splits"]), task["rows"] * LANES
         copies = [
-            pltpu.make_async_copy(
-                grad.at[
-                    pl.ds(pl.multiple_of(table[task["first"] + i] * G, G), G),
-                    :,
-                    pl.ds(task["start"] * LANES, size),
-                ],
-                held.at[pl.ds(i * G, G)],
-                sems.at[i],
-            )
-            for i in range(sum(task["splits"]))
+            [
+                pltpu.make_async_copy(
+                    grad.at[
+                        pl.ds(pl.multiple_of(table[task["first"] + i] * G, G), G),
+                        :,
+                        pl.ds(task["start"] * LANES, size),
+                    ],
+                    held.at[pl.ds(i * G, G)],
+                    sems.at[i],
+                )
+            ]
+            for i in range(count)
         ]
-        for copy in copies:
-            copy.start()
-        work.append((held, copies))
-    for task, (held, copies) in zip(tasks, work):
-        mine, terms = terms[: len(task["offsets"])], terms[len(task["offsets"]) :]
+        terms = []
+        for term in task["terms"]:
+            mine, given = given[: len(term["rows"])], given[len(term["rows"]) :]
+            blocks = [i for i in range(count) if 0 <= term["offset"] + i < mine[0].shape[0]]
+            if task["far"]:
+                (near, near_sems), scratch = scratch[:2], scratch[2:]
+                for i in blocks:
+                    copy = pltpu.make_async_copy(
+                        mine[0].at[term["offset"] + i], near.at[i], near_sems.at[i]
+                    )
+                    copies[i].append(copy)
+                terms.append({i: ((near, i),) for i in blocks})
+            else:
+                terms.append({i: tuple((a, term["offset"] + i) for a in mine) for i in blocks})
+        for block in copies:
+            for copy in block:
+                copy.start()
+        work.append((held, copies, terms))
+    for task, (held, copies, terms) in zip(tasks, work):
         places = [(out, i) for out, n in zip(outs, task["splits"]) for i in range(n)]
         outs = outs[len(task["splits"]) :]
-        for i, (copy, (out, at)) in enumerate(zip(copies, places)):
-            copy.wait()
+        for i, (block, (out, at)) in enumerate(zip(copies, places)):
+            for copy in block:
+                copy.wait()
             for j in range(G):
                 total = held[i * G + j].reshape(task["rows"], LANES).astype(jnp.float32)
-                for term, offset in zip(mine, task["offsets"]):
-                    if 0 <= offset + i < term.shape[0]:
-                        total = total + term[offset + i, j]
+                for term in terms:
+                    if i in term:
+                        parts = [a[b, j] for a, b in term[i]]
+                        total = total + (parts[0] if len(parts) == 1 else jnp.concatenate(parts))
                 out[at, j] = total
 
 
 def combine(grad, table, tasks, name):
-    arrays = [a for task in tasks for a, _ in task["terms"]]
+    arrays, places, static, scratch = [], [], [], []
+    for task in tasks:
+        count, rows = sum(task["splits"]), task["rows"]
+        scratch.append(pltpu.VMEM((count * G, 1, rows * LANES), jnp.bfloat16))
+        scratch.append(pltpu.SemaphoreType.DMA((count,)))
+        for held, _ in task["terms"]:
+            for a in held:
+                arrays.append(in_hbm(a) if task["far"] else in_vmem(a))
+                places.append(pl.BlockSpec(memory_space=pl.ANY if task["far"] else pltpu.VMEM))
+            if task["far"]:
+                scratch.append(pltpu.VMEM((count, G, rows, LANES), jnp.float32))
+                scratch.append(pltpu.SemaphoreType.DMA((count,)))
+        terms = [dict(rows=[a.shape[2] for a in held], offset=o) for held, o in task["terms"]]
+        static.append({**task, "terms": terms})
     shapes = [(n, task["rows"]) for task in tasks for n in task["splits"]]
-    static = [
-        {**{k: task[k] for k in ("first", "splits", "start", "rows")}, "offsets": [o for _, o in task["terms"]]}
-        for task in tasks
-    ]
-    scratch = []
-    for task in tasks:
-        count = sum(task["splits"])
-        scratch.append(pltpu.VMEM((count * G, 1, task["rows"] * LANES), jnp.bfloat16))
-        scratch.append(pltpu.SemaphoreType.DMA((count,)))
     size = sum(n * G * rows * LANES * 8 for n, rows in shapes) + sum(a.size * 4 for a in arrays)
     outs = pl.pallas_call(
         functools.partial(combine_kernel, static),
         grid_spec=pltpu.PrefetchScalarGridSpec(
             num_scalar_prefetch=1,
             grid=(),
-            in_specs=[pl.BlockSpec(memory_space=pl.ANY)]
-            + [pl.BlockSpec(memory_space=pltpu.VMEM)] * len(arrays),
+            in_specs=[pl.BlockSpec(memory_space=pl.ANY)] + places,
             out_specs=[pl.BlockSpec(memory_space=pltpu.VMEM)] * len(shapes),
             scratch_shapes=scratch,
         ),
@@ -145,7 +165,7 @@
         name=name,
         compiler_params=params(),
         cost_estimate=cost(size),
-    )(table, in_hbm(grad), *[in_vmem(a) for a in arrays])
+    )(table, in_hbm(grad), *arrays)
     results = []
     for task in tasks:
         results.append(outs[: len(task["splits"])])
@@ -235,25 +255,31 @@
 
 def adam_kernel(first, rows, start, holder, ordered, *refs):
     state, refs = refs[:3], refs[3:]
-    *outs, grads, old, fresh, in_sems, out_sems = refs[-8:]
+    *outs, grads, old, fresh, grad_sems, in_sems, out_sems = refs[-9:]
     here = pl.ds(start, rows)
-    loads, stores = [], []
-    for j in range(G):
-        pairs = [(ordered.at[holder[j], pl.ds(first, rows)], grads.at[j])]
-        pairs += [(state[s].at[j, here], old.at[s, j]) for s in range(3)]
-        loads.append(
-            [pltpu.make_async_copy(*pair, in_sems.at[j, s]) for s, pair in enumerate(pairs)]
-        )
-        for load in loads[-1]:
+    half = G // 2
+    loads, stores = [[], []], []
+    for n in range(2):
+        pieces = pl.ds(n * half, half)
+        for j in range(n * half, (n + 1) * half):
+            source = ordered.at[holder[j], pl.ds(first, rows)]
+            loads[n].append(pltpu.make_async_copy(source, grads.at[j], grad_sems.at[j]))
+        for s in range(3):
+            source = state[s].at[pieces, here]
+            loads[n].append(pltpu.make_async_copy(source, old.at[s, pieces], in_sems.at[n, s]))
+        for load in loads[n]:
             load.start()
-    for j in range(G):
-        for load in loads[j]:
+    for n in range(2):
+        pieces = pl.ds(n * half, half)
+        for load in loads[n]:
             load.wait()
-        for s, value in enumerate(adam_step(grads[j], *[old[s, j] for s in range(3)])):
-            fresh[s, j] = value
-            store = pltpu.make_async_copy(fresh.at[s, j], outs[s].at[j, here], out_sems.at[j, s])
-            store.start()
-            stores.append(store)
+        for j in range(n * half, (n + 1) * half):
+            for s, value in enumerate(adam_step(grads[j], *[old[s, j] for s in range(3)])):
+                fresh[s, j] = value
+        for s in range(3):
+            target = outs[s].at[pieces, here]
+            stores.append(pltpu.make_async_copy(fresh.at[s, pieces], target, out_sems.at[n, s]))
+            stores[-1].start()
     for store in stores:
         store.wait()
 
@@ -271,8 +297,9 @@
                 pltpu.VMEM((G, rows, LANES), jnp.float32),
                 pltpu.VMEM((3, G, rows, LANES), jnp.float32),
                 pltpu.VMEM((3, G, rows, LANES), jnp.float32),
-                pltpu.SemaphoreType.DMA((G, 4)),
-                pltpu.SemaphoreType.DMA((G, 3)),
+                pltpu.SemaphoreType.DMA((G,)),
+                pltpu.SemaphoreType.DMA((2, 3)),
+                pltpu.SemaphoreType.DMA((2, 3)),
             ],
         ),
         out_shape=[pltpu.HBM((G, ROWS, LANES), jnp.float32)] * 3,
@@ -283,33 +310,58 @@
     )(holder, in_hbm(ordered), *[in_hbm(a) for a in state], *held)
 
 
-def parity_kernel(coeff, sums, old, *refs):
-    out = refs[-1]
-    totals = [[None] * 2 for _ in range(3)]
-    for g in range(G):
-        for s, value in enumerate(adam_step(sums[g], *[old[g, s] for s in range(3)])):
+def parity_kernel(start, rows, coeff, sums, old, *refs):
+    out, near_sums, near_old, fresh, in_sems, out_sems = refs[-6:]
+    size = rows // 2
+    loads, stores = [], []
+    for n in range(2):
+        mine, whole = pl.ds(n * size, size), pl.ds(start + n * size, size)
+        loads.append(
+            [
+                pltpu.make_async_copy(sums.at[:, mine], near_sums.at[:, mine], in_sems.at[n, 0]),
+                pltpu.make_async_copy(
+                    old.at[:, :, whole], near_old.at[:, :, mine], in_sems.at[n, 1]
+                ),
+            ]
+        )
+        for load in loads[n]:
+            load.start()
+    for n in range(2):
+        mine, whole = pl.ds(n * size, size), pl.ds(start + n * size, size)
+        for load in loads[n]:
+            load.wait()
+        totals = [[None] * 2 for _ in range(3)]
+        for g in range(G):
+            values = adam_step(near_sums[g, mine], *[near_old[g, s, mine] for s in range(3)])
+            for s, value in enumerate(values):
+                for k in range(2):
+                    term = coeff[k, g] * value
+                    totals[s][k] = term if g == 0 else totals[s][k] + term
+        for s in range(3):
             for k in range(2):
-                term = coeff[k, g] * value
-                totals[s][k] = term if g == 0 else totals[s][k] + term
-    for s in range(3):
-        for k in range(2):
-            out[s, :, k, :] = totals[s][k]
+                fresh[s, mine, k, :] = totals[s][k]
+        stores.append(pltpu.make_async_copy(fresh.at[:, mine], out.at[:, whole], out_sems.at[n]))
+        stores[n].start()
+    for store in stores:
+        store.wait()
 
 
 def parity(sums, old, coeff, done, start, rows):
-    first = start // TILE
     held = [] if done is None else [in_hbm(done)]
     return pl.pallas_call(
-        parity_kernel,
+        functools.partial(parity_kernel, start, rows),
         grid_spec=pltpu.PrefetchScalarGridSpec(
             num_scalar_prefetch=1,
-            grid=(rows // TILE,),
-            in_specs=[
-                pl.BlockSpec((G, TILE, LANES), lambda i, c: (0, i, 0)),
-                pl.BlockSpec((G, 3, TILE, LANES), lambda i, c: (0, 0, first + i, 0)),
-            ]
-            + [pl.BlockSpec(memory_space=pl.ANY)] * len(held),
-            out_specs=pl.BlockSpec((3, TILE, 2, LANES), lambda i, c: (0, first + i, 0, 0)),
+            grid=(),
+            in_specs=[pl.BlockSpec(memory_space=pl.ANY)] * (2 + len(held)),
+            out_specs=pl.BlockSpec(memory_space=pl.ANY),
+            scratch_shapes=[
+                pltpu.VMEM((G, rows, LANES), jnp.float32),
+                pltpu.VMEM((G, 3, rows, LANES), jnp.float32),
+                pltpu.VMEM((3, rows, 2, LANES), jnp.float32),
+                pltpu.SemaphoreType.DMA((2, 2)),
+                pltpu.SemaphoreType.DMA((2,)),
+            ],
         ),
         out_shape=pltpu.HBM((3, ROWS, 2, LANES), jnp.float32),
         name="parity",
@@ -331,15 +383,15 @@
     grad = grad_parts.reshape(X * Y * C * G, 1, ROWS * LANES)
     blocks = lax.dynamic_index_in_dim(jnp.asarray(TABLES), index, keepdims=False)
     half = X * Y // 2
-    got = {n: [] for n in range(len(CHUNKS))}
-    across = {n: [] for n in range(len(CHUNKS))}
-    hop, totals, ordered, sums, olds, done, shards = {}, {}, {}, {}, None, None, None
-    token = ()
-
-    def task(n, own, first, splits, terms):
+    got, across, hop, totals, ordered, sums = {}, {}, {}, {}, {}, {}
+    olds, done, shards, token = None, None, None, ()
+
+    def task(n, own, first, splits, terms, part=None, far=False):
         start, rows, x_first = CHUNKS[n]
+        if part:
+            start, rows = start + part[0], part[1]
         base = X * Y * (2 * own + x_first)
-        return dict(first=base + first, start=start, rows=rows, splits=splits, terms=terms)
+        return dict(first=base + first, start=start, rows=rows, splits=splits, terms=terms, far=far)
 
     def send(value, name, n, pairs):
         with jax.named_scope(f"{name}_{n}"):
@@ -358,48 +410,39 @@
         nonlocal token
         token = values
 
-    def swap_core(n, first, splits):
+    def swap_core(n, first, splits, part=None):
         def use(*sent):
-            got[n] += [send(a, "core", n, CORE_SWAP) for a in sent]
-
-        return task(n, False, first, splits, []), use, "core", n
-
-    def offsets(arrays, first):
-        pairs, at = [], 0
-        for a in arrays:
-            pairs.append((a, first - at))
-            at += a.shape[0]
-        return pairs
-
-    def of_core(n, first):
-        return offsets(got[n], first)
-
-    def of_x(n, first):
-        return offsets(across[n], first - half)
+            at = first
+            for a in sent:
+                got.setdefault((n, part), []).append((at, send(a, "core", n, CORE_SWAP)))
+                at += a.shape[0]
+
+        return task(n, False, first, splits, [], part), use, "core", n
+
+    def terms_at(n, first, count, part=None):
+        held = got[n, part] + (across[n] if CHUNKS[n][2] else [])
+        return [((a,), first - at) for at, a in held if first < at + a.shape[0] and at < first + count]
 
     def x_sum(n):
         def use(*sent):
-            across[n] += [send(a, "cross", n, X_SWAP) for a in sent]
-
-        return task(n, True, 0, (2, 2), of_core(n, 0)), use, "cross", n
-
-    def terms_at(n, first, count):
-        terms = of_core(n, first) + (of_x(n, first) if CHUNKS[n][2] else [])
-        return [(a, o) for a, o in terms if o < a.shape[0] and o + count > 0]
-
-    def far(n):
+            across[n] = [(half + 2 * i, send(a, "cross", n, X_SWAP)) for i, a in enumerate(sent)]
+
+        terms = [((a,), -at) for at, a in got[n, None] if at < half]
+        return task(n, True, 0, (2, 2), terms), use, "cross", n
+
+    def far(n, part=None):
         first, size = (half, 1) if CHUNKS[n][2] else (0, X)
 
         def use(block):
-            hop[n, 0] = send(block, "far", n, Y_ON)
-
-        return task(n, True, first, (size,), terms_at(n, first, size)), use, "far", n
+            hop[n, 0] = hop.get((n, 0), ()) + (send(block, "far", n, Y_ON),)
+
+        return task(n, True, first, (size,), terms_at(n, first, size, part), part), use, "far", n
 
     def near(n):
         first, size = (half + 1, 1) if CHUNKS[n][2] else (X, X)
 
         def use(block):
-            hop[n, 1] = send(block, "near", n, Y_BACK)
+            hop[n, 1] = (send(block, "near", n, Y_BACK),)
 
         return task(n, True, first, (size,), terms_at(n, first, size)), use, "near", n
 
@@ -407,19 +450,19 @@
         first, size = (half + 2, 1) if CHUNKS[n][2] else (half, X)
 
         def use(block):
-            hop[n, 2] = send(block, "ahead", n, Y_ON)
+            hop[n, 2] = (send(block, "ahead", n, Y_ON),)
 
         terms = terms_at(n, first, size) + [(hop[n, 0], 0)]
         return task(n, True, first, (size,), terms), use, "ahead", n
 
-    def here(n):
+    def here(n, from_hbm=False):
         first, splits = (half + 3, (1,)) if CHUNKS[n][2] else (half + X, (1, 1))
 
         def use(own, *block):
             totals[n] = [own] + [send(b, "swap", n, X_SWAP) for b in block]
 
         terms = terms_at(n, first, len(splits)) + [(hop[n, 2], 0), (hop[n, 1], 0)]
-        return task(n, True, first, splits, terms), use, "here", n
+        return task(n, True, first, splits, terms, far=from_hbm), use, "here", n
 
     def place(n):
         (group,) = [g for g in GROUPS if n in g]
@@ -459,17 +502,17 @@
     run(near(0), swap_core(0, 4, (1, 1, 1, 1)))
     run(swap_core(1, 0, (1, 1, 1, 1)), swap_core(1, 4, (1, 1, 1, 1)))
     run(ahead(0))
-    run(far(1), wait=(hop[0, 1],))
+    run(far(1), wait=hop[0, 1])
     run(near(1))
     run(here(0))
     run(ahead(1))
     give(0)
     to_holders((0,))
-    run(here(1))
+    run(here(1, True))
     update(0)
-    parities((0,))
     give(1)
     to_holders((1,))
+    parities((0,))
     update(1)
     parities((1,))
     outs = [a.reshape(1, SHARD) for a in done]

time: 122 us -> 121 us (level)
  Pallas kernels: 51.4 us -> 47.3 us
  waiting for transfers between devices: 32.6 us -> 36.1 us
    ppermute x24, waiting for transfers between devices: 27.8 us -> 34.8 us  [send(): return lax.ppermute(value, 'dp', pairs)]
    all_to_all x2, waiting for transfers between devices: 4.86 us -> 1.34 us  [to_holders(): sums[group] = lax.all_to_all(ordered[group], 'group', 0, 0)]
    pallas_call x2, Pallas kernels: 7.05 us -> 5.37 us  [parity(): pl.pallas_call(functools.partial(parity_kernel, start, rows), grid_spec=p...]
    pallas_call x11, Pallas kernels: 31.4 us -> 29.9 us  [combine(): pl.pallas_call(functools.partial(combine_kernel, static), grid_spec=pltpu...]
  transfers between devices with their start and end apart: 27 -> 27, of which waited for: 7 -> 7; matrix products, arithmetic and copies ran while one was open for 0% -> 0% of each run, Pallas kernels for 37% -> 36%
where the time goes in v5:
time: 121 us; the launch traced here: 120 us
  Pallas kernels  47.3 us (39%)
  waiting for transfers between devices  36.1 us (30%)
  starting transfers between devices  33.7 us (28%)
  local copies, waits for them, and re-layouts  1.5 us (1%)
    ppermute x24, waiting for transfers between devices, send(): return lax.ppermute(value, 'dp', pairs)  34.8 us
    pallas_call x11, Pallas kernels, combine(): pl.pallas_call(functools.partial(combine_kernel, static), grid_spec=pltpu...  29.9 us
    ppermute x24, starting transfers between devices, send(): return lax.ppermute(value, 'dp', pairs)  16.6 us
    all_to_all x2, starting transfers between devices, to_holders(): sums[group] = lax.all_to_all(ordered[group], 'group', 0, 0)  10.8 us
    pallas_call x2, Pallas kernels, adam(): pl.pallas_call(functools.partial(adam_kernel, first, rows, start), grid_s...  6.78 us
    all_to_all x1, starting transfers between devices, per_device(): olds = lax.all_to_all(old, 'group', 0, 0)  6.34 us
    pallas_call x2, Pallas kernels, parity(): pl.pallas_call(functools.partial(parity_kernel, start, rows), grid_spec=p...  5.37 us
    pallas_call x2, Pallas kernels, finish(): pl.pallas_call(functools.partial(finish_kernel, len(parts), first, rows),...  2.88 us
  transfers between devices with their start and end apart: 27, of which 7 were waited for; matrix products, arithmetic and copies ran while one was open for 0% of the time, Pallas kernels for 36%

profile of v5, /device:TPU:24, one launch (start us, length us, event | category | flops | bytes accessed | tf_op | source)
XLA Modules:
  0.0 119.8 jit_solution(8894316906867873797)
XLA Ops:
  1.3 1.9 %core0.2 = (f32[1,8,160,128]{3,2,1,0:T(8,128)S(1)}, f32[1,8,160,128]{3,2,1,0:T(8,128)S(1)}) custom-call(s32[32]{0:T(128)S(1)} %dynamic-slice_bitcast_fusion.table, bf16[128,1,32768]{2,1,0:T(2,128)(2,1)} %bitcast.28), custom_call_target="tpu_custom_call" | custom-call | bytes 640 | tf_op jit(solution)/shard_map/core0/pallas_call | solution.py:155
  3.8 2.9 %core0.3 = (f32[1,8,160,128]{3,2,1,0:T(8,128)}, f32[1,8,160,128]{3,2,1,0:T(8,128)}) custom-call(s32[32]{0:T(128)S(1)} %dynamic-slice_bitcast_fusion.table, bf16[128,1,32768]{2,1,0:T(2,128)(2,1)} %bitcast.29), custom_call_target="tpu_custom_call" | custom-call | bytes 640 | tf_op jit(solution)/shard_map/core0/pallas_call | solution.py:155
  7.4 3.0 %far0.1 = f32[2,8,160,128]{3,2,1,0:T(8,128)} custom-call(s32[32]{0:T(128)S(1)} %dynamic-slice_bitcast_fusion.table, bf16[128,1,32768]{2,1,0:T(2,128)(2,1)} %bitcast.30, f32[1,8,160,128]{3,2,1,0:T(8,128)S(1)} %collective-permute-done.refs_0_, f32[1,8,160,128]{3,2,1,0:T(8,128)S(1)} %collective-permute-done.1.refs_1_), custom_call_target="tpu_custom_call" | custom-call | bytes 960 | tf_op jit(solution)/shard_map/far0/pallas_call | solution.py:155
  10.6 2.4 %order.1 = f32[8,3,256,128]{3,2,1,0:T(8,128)} custom-call(s32[8]{0:T(128)S(1)} %bitcast.23, f32[8,256,128]{2,1,0:T(8,128)S(1)} %bitcast.16, f32[8,256,128]{2,1,0:T(8,128)S(1)} %bitcast.19, f32[8,256,128]{2,1,0:T(8,128)S(1)} %bitcast.22), custom_call_target="tpu_custom_call" | custom-call | bytes 1536 | tf_op jit(solution)/shard_map/order/pallas_call | solution.py:190
  13.0 6.3 %all-to-all-start.1 = ((f32[8,3,256,128]{3,2,1,0:T(8,128)}), f32[8,3,256,128]{3,2,1,0:T(8,128)S(1)}, u32[]{:S(2)}, u32[]{:S(2)}) async-start(f32[8,3,256,128]{3,2,1,0:T(8,128)} %order.1), calls=%async_computation.1 | async-start | bytes 6291456 | tf_op jit(solution)/shard_map/all_to_all | solution.py:501
  19.4 4.0 %near0_core0.1 = (f32[2,8,160,128]{3,2,1,0:T(8,128)S(1)}, f32[1,8,160,128]{3,2,1,0:T(8,128)S(1)}, f32[1,8,160,128]{3,2,1,0:T(8,128)S(1)}, f32[1,8,160,128]{3,2,1,0:T(8,128)S(1)}, f32[1,8,160,128]{3,2,1,0:T(8,128)S(1)}) custom-call(s32[32]{0:T(128)S(1)} %dynamic-slice_bitcast_fusion.table, bf16[128,1,32768]{2,1,0:T(2,128)(2,1)} %bitcast.31, ...), custom_call_target="tpu_custom_call" | custom-call | bytes 2240 | tf_op jit(solution)/shard_map/near0_core0/pallas_call | solution.py:155
  23.4 1.9 %collective-permute-start.7 = (f32[2,8,160,128]{3,2,1,0:T(8,128)S(1)}, f32[2,8,160,128]{3,2,1,0:T(8,128)S(1)}, u32[]{:S(2)}, u32[]{:S(2)}) collective-permute-start(f32[2,8,160,128]{3,2,1,0:T(8,128)S(1)} %get-tuple-element.56), channel_id=1, source_target_pairs={{0,48},{8,24},{16,0},{24,40},{32,16},{40,56},{48,32},{56,8},{64,11... | collective-permute-start | bytes 3932168 | tf_op jit(solution)/shard_map/near_0/ppermute | solution.py:398
  26.0 3.3 %core1_core1.1 = (f32[1,8,96,128]{3,2,1,0:T(8,128)S(1)}, f32[1,8,96,128]{3,2,1,0:T(8,128)S(1)}, f32[1,8,96,128]{3,2,1,0:T(8,128)S(1)}, f32[1,8,96,128]{3,2,1,0:T...) custom-call(s32[32]{0:T(128)S(1)} %dynamic-slice_bitcast_fusion.tabl, ...), custom_call_target="tpu_custom_call" | custom-call | bytes 1536 | tf_op jit(solution)/shard_map/core1_core1/pallas_call | solution.py:155
  30.3 3.3 %ahead0.1 = f32[2,8,160,128]{3,2,1,0:T(8,128)S(1)} custom-call(s32[32]{0:T(128)S(1)} %dynamic-slice_bitcast_fusion.table, bf16[128,1,32768]{2,1,0:T(2,128)(2,1)} %bitcast.33, f32[1,8,160,128]{3,2,1,0:T(8,128)S(1)} %collective-permute-done.4.refs_0_, f32[1,8,160,128]{3,2,1,0:T(8,128)S(1)} %collective-permute-done.5.refs_1_, ...), custom_call_target="tpu_custom_call" | custom-call | bytes 1280 | tf_op jit(solution)/shard_map/ahead0/pallas_call | solution.py:155
  34.6 14.0 %collective-permute-done.7.refs_3_ = f32[2,8,160,128]{3,2,1,0:T(8,128)S(1)} collective-permute-done((f32[2,8,160,128]{3,2,1,0:T(8,128)S(1)}, f32[2,8,160,128]{3,2,1,0:T(8,128)S(1)}, u32[]{:S(2)}, u32[]{:S(2)}) %collective-permute-start.7) | collective-permute-done | bytes 1310752 | tf_op jit(solution)/shard_map/near_0/ppermute | solution.py:398
  48.6 1.7 %far1.1 = f32[2,8,96,128]{3,2,1,0:T(8,128)S(1)} custom-call(s32[32]{0:T(128)S(1)} %dynamic-slice_bitcast_fusion.table, bf16[128,1,32768]{2,1,0:T(2,128)(2,1)} %bitcast.34, f32[1,8,96,128]{3,2,1,0:T(8,128)S(1)} %collective-permute-done.8.refs_0_, f32[1,8,96,128]{3,2,1,0:T(8,128)S(1)} %collective-permute-done.9.refs_1_), custom_call_target="tpu_custom_call" | custom-call | bytes 576 | tf_op jit(solution)/shard_map/far1/pallas_call | solution.py:155
  50.4 0.9 collective-permute-start.17
  52.0 2.6 %near1.1 = f32[2,8,96,128]{3,2,1,0:T(8,128)} custom-call(s32[32]{0:T(128)S(1)} %dynamic-slice_bitcast_fusion.table, bf16[128,1,32768]{2,1,0:T(2,128)(2,1)} %bitcast.35, f32[1,8,96,128]{3,2,1,0:T(8,128)S(1)} %collective-permute-done.10.refs_0_, f32[1,8,96,128]{3,2,1,0:T(8,128)S(1)} %collective-permute-done.11.refs_1_), custom_call_target="tpu_custom_call" | custom-call | bytes 576 | tf_op jit(solution)/shard_map/near1/pallas_call | solution.py:155
  54.6 1.8 %collective-permute-done.14.refs_2_ = f32[2,8,160,128]{3,2,1,0:T(8,128)S(1)} collective-permute-done((f32[2,8,160,128]{3,2,1,0:T(8,128)S(1)}, f32[2,8,160,128]{3,2,1,0:T(8,128)S(1)}, u32[]{:S(2)}, u32[]{:S(2)}) %collective-permute-start.14) | collective-permute-done | bytes 1310752 | tf_op jit(solution)/shard_map/ahead_0/ppermute | solution.py:398
  56.4 2.0 %here0.1 = (f32[1,8,160,128]{3,2,1,0:T(8,128)S(1)}, f32[1,8,160,128]{3,2,1,0:T(8,128)S(1)}) custom-call(s32[32]{0:T(128)S(1)} %dynamic-slice_bitcast_fusion.table, bf16[128,1,32768]{2,1,0:T(2,128)(2,1)} %bitcast.36, f32[1,8,160,128]{3,2,1,0:T(8,128)S(1)} %collective-permute-done.12.refs_0_, f32[1,8,160,128]{3,2,1,0:T(8,128)S(1)} %collective-permute-done.13.refs_1_, ...), custom_call_target="tpu_custom_call" | custom-call | bytes 1600 | tf_op jit(solution)/shard_map/here0/pallas_call | solution.py:155
  58.4 3.1 %collective-permute-start.18 = (f32[1,8,160,128]{3,2,1,0:T(8,128)S(1)}, f32[1,8,160,128]{3,2,1,0:T(8,128)S(1)}, u32[]{:S(2)}, u32[]{:S(2)}) collective-permute-start(f32[1,8,160,128]{3,2,1,0:T(8,128)S(1)} %get-tuple-element.75), channel_id=1, source_target_pairs={{0,64},{8,72},{16,80},{24,88},{32,96},{40,104},{48,112},{56,120},{... | collective-permute-start | bytes 1966088 | tf_op jit(solution)/shard_map/swap_0/ppermute | solution.py:398
  62.3 2.5 %collective-permute-done.17.refs_2_ = f32[2,8,96,128]{3,2,1,0:T(8,128)S(1)} collective-permute-done((f32[2,8,96,128]{3,2,1,0:T(8,128)S(1)}, f32[2,8,96,128]{3,2,1,0:T(8,128)S(1)}, u32[]{:S(2)}, u32[]{:S(2)}) %collective-permute-start.17) | collective-permute-done | bytes 786464 | tf_op jit(solution)/shard_map/far_1/ppermute | solution.py:398
  64.8 2.6 %ahead1.1 = f32[2,8,96,128]{3,2,1,0:T(8,128)} custom-call(s32[32]{0:T(128)S(1)} %dynamic-slice_bitcast_fusion.table, bf16[128,1,32768]{2,1,0:T(2,128)(2,1)} %bitcast.37, f32[1,8,96,128]{3,2,1,0:T(8,128)S(1)} %collective-permute-done.15.refs_0_, f32[1,8,96,128]{3,2,1,0:T(8,128)S(1)} %collective-permute-done.16.refs_1_, ...), custom_call_target="tpu_custom_call" | custom-call | bytes 768 | tf_op jit(solution)/shard_map/ahead1/pallas_call | solution.py:155
  67.5 2.1 %collective-permute-start.21 = (f32[2,8,96,128]{3,2,1,0:T(8,128)}, f32[2,8,96,128]{3,2,1,0:T(8,128)}, u32[]{:S(2)}, u32[]{:S(2)}) collective-permute-start(f32[2,8,96,128]{3,2,1,0:T(8,128)} %ahead1.1), channel_id=1, source_target_pairs={{0,16},{8,56},{16,32},{24,8},{32,48},{40,24},{48,0},{56,40},{64,80... | collective-permute-start | bytes 2359304 | tf_op jit(solution)/shard_map/ahead_1/ppermute | solution.py:398
  70.1 7.2 %collective-permute-done.18.refs_1_ = f32[1,8,160,128]{3,2,1,0:T(8,128)S(1)} collective-permute-done((f32[1,8,160,128]{3,2,1,0:T(8,128)S(1)}, f32[1,8,160,128]{3,2,1,0:T(8,128)S(1)}, u32[]{:S(2)}, u32[]{:S(2)}) %collective-permute-start.18) | collective-permute-done | bytes 655392 | tf_op jit(solution)/shard_map/swap_0/ppermute | solution.py:398
  77.3 1.5 %finish.2.ordered = f32[8,160,128]{2,1,0:T(8,128)} custom-call(s32[8]{0:T(128)S(1)} %bitcast.24, f32[1,8,160,128]{3,2,1,0:T(8,128)S(1)} %get-tuple-element.70.refs_0_, f32[1,8,160,128]{3,2,1,0:T(8,128)S(1)} %collective-permute-done.18.refs_1_), custom_call_target="tpu_custom_call" | custom-call | bytes 640 | tf_op jit(solution)/shard_map/finish/pallas_call | solution.py:226
  78.8 6.0 %all-to-all-start = ((f32[8,160,128]{2,1,0:T(8,128)}), f32[8,160,128]{2,1,0:T(8,128)}, u32[]{:S(2)}, u32[]{:S(2)}) async-start(f32[8,160,128]{2,1,0:T(8,128)} %finish.2.ordered), calls=%async_computation | async-start | bytes 1310720 | tf_op jit(solution)/shard_map/all_to_all | solution.py:480
  85.6 2.5 %here1.1 = (f32[1,8,96,128]{3,2,1,0:T(8,128)S(1)}, f32[1,8,96,128]{3,2,1,0:T(8,128)S(1)}) custom-call(s32[32]{0:T(128)S(1)} %dynamic-slice_bitcast_fusion.table, bf16[128,1,32768]{2,1,0:T(2,128)(2,1)} %bitcast.38, f32[1,8,96,128]{3,2,1,0:T(8,128)} %copy-done.4, f32[1,8,96,128]{3,2,1,0:T(8,128)} %collective-permute-done.20.refs_1_, ...), custom_call_target="tpu_custom_call" | custom-call | bytes 960 | tf_op jit(solution)/shard_map/here1/pallas_call | solution.py:155
  88.1 2.8 %collective-permute-start.23 = (f32[1,8,96,128]{3,2,1,0:T(8,128)S(1)}, f32[1,8,96,128]{3,2,1,0:T(8,128)S(1)}, u32[]{:S(2)}, u32[]{:S(2)}) collective-permute-start(f32[1,8,96,128]{3,2,1,0:T(8,128)S(1)} %get-tuple-element.83), channel_id=1, source_target_pairs={{0,64},{8,72},{16,80},{24,88},{32,96},{40,104},{48,112},{56,120},{... | collective-permute-start | bytes 1179656 | tf_op jit(solution)/shard_map/swap_1/ppermute | solution.py:398
  90.9 3.6 %adam.2 = (f32[8,256,128]{2,1,0:T(8,128)}, f32[8,256,128]{2,1,0:T(8,128)}, f32[8,256,128]{2,1,0:T(8,128)}) custom-call(s32[8]{0:T(128)S(1)} %bitcast.25, f32[8,160,128]{2,1,0:T(8,128)} %finish.2.ordered, f32[8,256,128]{2,1,0:T(8,128)} %bitcast.14, f32[8,256,128]{2,1,0:T(8,128)} %bitcast.17, f32[8,256,128]{2,1,0:T(8,128)} %bitcast.20), custom_call_target="tpu_custom_call" | custom-call | bytes 1120 | tf_op jit(solution)/shard_map/adam/pallas_call | solution.py:289
  94.5 8.8 %collective-permute-done.23.refs_1_ = f32[1,8,96,128]{3,2,1,0:T(8,128)S(1)} collective-permute-done((f32[1,8,96,128]{3,2,1,0:T(8,128)S(1)}, f32[1,8,96,128]{3,2,1,0:T(8,128)S(1)}, u32[]{:S(2)}, u32[]{:S(2)}) %collective-permute-start.23) | collective-permute-done | bytes 393248 | tf_op jit(solution)/shard_map/swap_1/ppermute | solution.py:398
  103.3 1.4 %finish.3.ordered = f32[8,96,128]{2,1,0:T(8,128)} custom-call(s32[8]{0:T(128)S(1)} %bitcast.26, f32[1,8,96,128]{3,2,1,0:T(8,128)S(1)} %get-tuple-element.79.refs_0_, f32[1,8,96,128]{3,2,1,0:T(8,128)S(1)} %collective-permute-done.23.refs_1_), custom_call_target="tpu_custom_call" | custom-call | bytes 384 | tf_op jit(solution)/shard_map/finish/pallas_call | solution.py:226
  104.7 4.8 %all-to-all-start.2 = ((f32[8,96,128]{2,1,0:T(8,128)}), f32[8,96,128]{2,1,0:T(8,128)S(1)}, u32[]{:S(2)}, u32[]{:S(2)}) async-start(f32[8,96,128]{2,1,0:T(8,128)} %finish.3.ordered), calls=%async_computation.2 | async-start | bytes 786432 | tf_op jit(solution)/shard_map/all_to_all | solution.py:480
  109.7 3.3 %parity.2.refs_0_ = f32[3,256,2,128]{3,2,1,0:T(2,128)} custom-call(f32[2,8]{1,0:T(2,128)S(1)} %add_divide_fusion.coeff, f32[8,160,128]{2,1,0:T(8,128)} %all-to-all-done.sums, f32[8,3,256,128]{3,2,1,0:T(8,128)S(1)} %all-to-all-done.1.old), custom_call_target="tpu_custom_call" | custom-call | bytes 640 | tf_op jit(solution)/shard_map/parity/pallas_call | solution.py:351
  113.1 3.1 %adam.3 = (f32[8,256,128]{2,1,0:T(8,128)}, f32[8,256,128]{2,1,0:T(8,128)}, f32[8,256,128]{2,1,0:T(8,128)}) custom-call(s32[8]{0:T(128)S(1)} %bitcast.27, f32[8,96,128]{2,1,0:T(8,128)} %finish.3.ordered, f32[8,256,128]{2,1,0:T(8,128)} %bitcast.15, f32[8,256,128]{2,1,0:T(8,128)} %bitcast.18, ...), custom_call_target="tpu_custom_call", output_to_operand_aliasing={{0}: (5, {}), {1}: (6, {}), {2}: (7, {})} | custom-call | bytes 672 | tf_op jit(solution)/shard_map/adam/pallas_call | solution.py:289
  116.2 1.3 %all-to-all-done.2.sums = f32[8,96,128]{2,1,0:T(8,128)S(1)} async-done(((f32[8,96,128]{2,1,0:T(8,128)}), f32[8,96,128]{2,1,0:T(8,128)S(1)}, u32[]{:S(2)}, u32[]{:S(2)}) %all-to-all-start.2) | async-done | bytes 393248 | tf_op jit(solution)/shard_map/all_to_all | solution.py:480
  117.6 2.0 %parity.3 = f32[3,256,2,128]{3,2,1,0:T(2,128)} custom-call(f32[2,8]{1,0:T(2,128)S(1)} %add_divide_fusion.coeff, f32[8,96,128]{2,1,0:T(8,128)S(1)} %all-to-all-done.2.sums, f32[8,3,256,128]{3,2,1,0:T(8,128)S(1)} %all-to-all-done.1.old, f32[3,256,2,128]{3,2,1,0:T(2,128)} %parity.2.refs_0_), custom_call_target="tpu_custom_call", output_to_operand_aliasing={{}: (3, {})} | custom-call | bytes 384 | tf_op jit(solution)/shard_map/parity/pallas_call | solution.py:351
  (56 shorter events, 7.6 us)
Async XLA Ops:
  3.2 4.2 %collective-permute-start.1 = (f32[1,8,160,128]{3,2,1,0:T(8,128)S(1)}, f32[1,8,160,128]{3,2,1,0:T(8,128)S(1)}, u32[]{:S(2)}, u32[]{:S(2)}) collective-permute-start(f32[1,8,160,128]{3,2,1,0:T(8,128)S(1)} %get-tuple-element.52), channel_id=1, source_target_pairs={{0,8},{8,0},{16,24},{24,16},{32,40},{40,32},{48,56},{56,48},{64,72... | collective-permute-start | bytes 1966088 | tf_op jit(solution)/shard_map/core_0/ppermute | solution.py:398
  3.3 4.1 %collective-permute-start = (f32[1,8,160,128]{3,2,1,0:T(8,128)S(1)}, f32[1,8,160,128]{3,2,1,0:T(8,128)S(1)}, u32[]{:S(2)}, u32[]{:S(2)}) collective-permute-start(f32[1,8,160,128]{3,2,1,0:T(8,128)S(1)} %get-tuple-element.48), channel_id=1, source_target_pairs={{0,8},{8,0},{16,24},{24,16},{32,40},{40,32},{48,56},{56,48},{64,72... | collective-permute-start | bytes 1966088 | tf_op jit(solution)/shard_map/core_0/ppermute | solution.py:398
  6.7 12.7 %collective-permute-start.3 = (f32[1,8,160,128]{3,2,1,0:T(8,128)}, f32[1,8,160,128]{3,2,1,0:T(8,128)}, u32[]{:S(2)}, u32[]{:S(2)}) collective-permute-start(f32[1,8,160,128]{3,2,1,0:T(8,128)} %get-tuple-element.55), channel_id=1, source_target_pairs={{0,8},{8,0},{16,24},{24,16},{32,40},{40,32},{48,56},{56,48},{64,72... | collective-permute-start | bytes 1966088 | tf_op jit(solution)/shard_map/core_0/ppermute | solution.py:398
  6.9 3.7 %copy-start = (f32[1,262144]{1,0:T(1,128)S(1)}, f32[1,262144]{1,0:T(1,128)}, u32[]{:S(2)}) copy-start(f32[1,262144]{1,0:T(1,128)} %param.8) | copy-start | bytes 3145732
  6.9 3.7 %copy-start.1 = (f32[1,262144]{1,0:T(1,128)S(1)}, f32[1,262144]{1,0:T(1,128)}, u32[]{:S(2)}) copy-start(f32[1,262144]{1,0:T(1,128)} %param.9) | copy-start | bytes 3145732
  6.9 3.7 %copy-start.2 = (f32[1,262144]{1,0:T(1,128)S(1)}, f32[1,262144]{1,0:T(1,128)}, u32[]{:S(2)}) copy-start(f32[1,262144]{1,0:T(1,128)} %param.10) | copy-start | bytes 3145732
  6.9 3.7 %copy-start.3 = (s32[1,8]{1,0:T(1,128)S(1)}, s32[1,8]{1,0:T(1,128)}, u32[]{:S(2)}) copy-start(s32[1,8]{1,0:T(1,128)} %param.12) | copy-start | bytes 100
  6.9 12.5 %collective-permute-start.2 = (f32[1,8,160,128]{3,2,1,0:T(8,128)}, f32[1,8,160,128]{3,2,1,0:T(8,128)}, u32[]{:S(2)}, u32[]{:S(2)}) collective-permute-start(f32[1,8,160,128]{3,2,1,0:T(8,128)} %get-tuple-element.50), channel_id=1, source_target_pairs={{0,8},{8,0},{16,24},{24,16},{32,40},{40,32},{48,56},{56,48},{64,72... | collective-permute-start | bytes 1966088 | tf_op jit(solution)/shard_map/core_0/ppermute | solution.py:398
  10.4 19.8 %collective-permute-start.6 = (f32[2,8,160,128]{3,2,1,0:T(8,128)}, f32[2,8,160,128]{3,2,1,0:T(8,128)}, u32[]{:S(2)}, u32[]{:S(2)}) collective-permute-start(f32[2,8,160,128]{3,2,1,0:T(8,128)} %far0.1), channel_id=1, source_target_pairs={{0,16},{8,56},{16,32},{24,8},{32,48},{40,24},{48,0},{56,40},{64,80... | collective-permute-start | bytes 3932168 | tf_op jit(solution)/shard_map/far_0/ppermute | solution.py:398
  13.0 65.8 %all-to-all-start.1 = ((f32[8,3,256,128]{3,2,1,0:T(8,128)}), f32[8,3,256,128]{3,2,1,0:T(8,128)S(1)}, u32[]{:S(2)}, u32[]{:S(2)}) async-start(f32[8,3,256,128]{3,2,1,0:T(8,128)} %order.1), calls=%async_computation.1 | async-start | bytes 6291456 | tf_op jit(solution)/shard_map/all_to_all | solution.py:501
  23.4 25.2 %collective-permute-start.7 = (f32[2,8,160,128]{3,2,1,0:T(8,128)S(1)}, f32[2,8,160,128]{3,2,1,0:T(8,128)S(1)}, u32[]{:S(2)}, u32[]{:S(2)}) collective-permute-start(f32[2,8,160,128]{3,2,1,0:T(8,128)S(1)} %get-tuple-element.56), channel_id=1, source_target_pairs={{0,48},{8,24},{16,0},{24,40},{32,16},{40,56},{48,32},{56,8},{64,11... | collective-permute-start | bytes 3932168 | tf_op jit(solution)/shard_map/near_0/ppermute | solution.py:398
  25.4 4.6 %collective-permute-start.4 = (f32[1,8,160,128]{3,2,1,0:T(8,128)S(1)}, f32[1,8,160,128]{3,2,1,0:T(8,128)S(1)}, u32[]{:S(2)}, u32[]{:S(2)}) collective-permute-start(f32[1,8,160,128]{3,2,1,0:T(8,128)S(1)} %get-tuple-element.60), channel_id=1, source_target_pairs={{0,8},{8,0},{16,24},{24,16},{32,40},{40,32},{48,56},{56,48},{64,72... | collective-permute-start | bytes 1966088 | tf_op jit(solution)/shard_map/core_0/ppermute | solution.py:398
  26.0 3.9 %collective-permute-start.5 = (f32[1,8,160,128]{3,2,1,0:T(8,128)S(1)}, f32[1,8,160,128]{3,2,1,0:T(8,128)S(1)}, u32[]{:S(2)}, u32[]{:S(2)}) collective-permute-start(f32[1,8,160,128]{3,2,1,0:T(8,128)S(1)} %get-tuple-element.61), channel_id=1, source_target_pairs={{0,8},{8,0},{16,24},{24,16},{32,40},{40,32},{48,56},{56,48},{64,72... | collective-permute-start | bytes 1966088 | tf_op jit(solution)/shard_map/core_0/ppermute | solution.py:398
  29.3 5.2 %collective-permute-start.9 = (f32[1,8,96,128]{3,2,1,0:T(8,128)S(1)}, f32[1,8,96,128]{3,2,1,0:T(8,128)S(1)}, u32[]{:S(2)}, u32[]{:S(2)}) collective-permute-start(f32[1,8,96,128]{3,2,1,0:T(8,128)S(1)} %get-tuple-element.63), channel_id=1, source_target_pairs={{0,8},{8,0},{16,24},{24,16},{32,40},{40,32},{48,56},{56,48},{64,72... | collective-permute-start | bytes 1179656 | tf_op jit(solution)/shard_map/core_1/ppermute | solution.py:398
  33.6 22.8 %collective-permute-start.14 = (f32[2,8,160,128]{3,2,1,0:T(8,128)S(1)}, f32[2,8,160,128]{3,2,1,0:T(8,128)S(1)}, u32[]{:S(2)}, u32[]{:S(2)}) collective-permute-start(f32[2,8,160,128]{3,2,1,0:T(8,128)S(1)} %ahead0.1), channel_id=1, source_target_pairs={{0,16},{8,56},{16,32},{24,8},{32,48},{40,24},{48,0},{56,40},{64,80... | collective-permute-start | bytes 3932168 | tf_op jit(solution)/shard_map/ahead_0/ppermute | solution.py:398
  34.1 14.6 %collective-permute-start.8 = (f32[1,8,96,128]{3,2,1,0:T(8,128)S(1)}, f32[1,8,96,128]{3,2,1,0:T(8,128)S(1)}, u32[]{:S(2)}, u32[]{:S(2)}) collective-permute-start(f32[1,8,96,128]{3,2,1,0:T(8,128)S(1)} %get-tuple-element.58), channel_id=1, source_target_pairs={{0,8},{8,0},{16,24},{24,16},{32,40},{40,32},{48,56},{56,48},{64,72... | collective-permute-start | bytes 1179656 | tf_op jit(solution)/shard_map/core_1/ppermute | solution.py:398
  34.1 17.2 %collective-permute-start.10 = (f32[1,8,96,128]{3,2,1,0:T(8,128)S(1)}, f32[1,8,96,128]{3,2,1,0:T(8,128)S(1)}, u32[]{:S(2)}, u32[]{:S(2)}) collective-permute-start(f32[1,8,96,128]{3,2,1,0:T(8,128)S(1)} %get-tuple-element.65), channel_id=1, source_target_pairs={{0,8},{8,0},{16,24},{24,16},{32,40},{40,32},{48,56},{56,48},{64,72... | collective-permute-start | bytes 1179656 | tf_op jit(solution)/shard_map/core_1/ppermute | solution.py:398
  34.6 17.2 %collective-permute-start.12 = (f32[1,8,160,128]{3,2,1,0:T(8,128)S(1)}, f32[1,8,160,128]{3,2,1,0:T(8,128)S(1)}, u32[]{:S(2)}, u32[]{:S(2)}) collective-permute-start(f32[1,8,160,128]{3,2,1,0:T(8,128)S(1)} %get-tuple-element.68), channel_id=1, source_target_pairs={{0,8},{8,0},{16,24},{24,16},{32,40},{40,32},{48,56},{56,48},{64,72... | collective-permute-start | bytes 1966088 | tf_op jit(solution)/shard_map/core_0/ppermute | solution.py:398
  48.6 2.9 %collective-permute-start.11 = (f32[1,8,96,128]{3,2,1,0:T(8,128)S(1)}, f32[1,8,96,128]{3,2,1,0:T(8,128)S(1)}, u32[]{:S(2)}, u32[]{:S(2)}) collective-permute-start(f32[1,8,96,128]{3,2,1,0:T(8,128)S(1)} %get-tuple-element.66), channel_id=1, source_target_pairs={{0,8},{8,0},{16,24},{24,16},{32,40},{40,32},{48,56},{56,48},{64,72... | collective-permute-start | bytes 1179656 | tf_op jit(solution)/shard_map/core_1/ppermute | solution.py:398
  50.4 14.5 %collective-permute-start.17 = (f32[2,8,96,128]{3,2,1,0:T(8,128)S(1)}, f32[2,8,96,128]{3,2,1,0:T(8,128)S(1)}, u32[]{:S(2)}, u32[]{:S(2)}) collective-permute-start(f32[2,8,96,128]{3,2,1,0:T(8,128)S(1)} %far1.1), channel_id=1, source_target_pairs={{0,16},{8,56},{16,32},{24,8},{32,48},{40,24},{48,0},{56,40},{64,80... | collective-permute-start | bytes 2359304 | tf_op jit(solution)/shard_map/far_1/ppermute | solution.py:398
  51.3 3.3 %collective-permute-start.13 = (f32[1,8,160,128]{3,2,1,0:T(8,128)S(1)}, f32[1,8,160,128]{3,2,1,0:T(8,128)S(1)}, u32[]{:S(2)}, u32[]{:S(2)}) collective-permute-start(f32[1,8,160,128]{3,2,1,0:T(8,128)S(1)} %get-tuple-element.69), channel_id=1, source_target_pairs={{0,8},{8,0},{16,24},{24,16},{32,40},{40,32},{48,56},{56,48},{64,72... | collective-permute-start | bytes 1966088 | tf_op jit(solution)/shard_map/core_0/ppermute | solution.py:398
  51.5 10.8 %collective-permute-start.15 = (f32[1,8,96,128]{3,2,1,0:T(8,128)S(1)}, f32[1,8,96,128]{3,2,1,0:T(8,128)S(1)}, u32[]{:S(2)}, u32[]{:S(2)}) collective-permute-start(f32[1,8,96,128]{3,2,1,0:T(8,128)S(1)} %get-tuple-element.72), channel_id=1, source_target_pairs={{0,8},{8,0},{16,24},{24,16},{32,40},{40,32},{48,56},{56,48},{64,72... | collective-permute-start | bytes 1179656 | tf_op jit(solution)/shard_map/core_1/ppermute | solution.py:398
  51.8 10.5 %collective-permute-start.16 = (f32[1,8,96,128]{3,2,1,0:T(8,128)S(1)}, f32[1,8,96,128]{3,2,1,0:T(8,128)S(1)}, u32[]{:S(2)}, u32[]{:S(2)}) collective-permute-start(f32[1,8,96,128]{3,2,1,0:T(8,128)S(1)} %get-tuple-element.73), channel_id=1, source_target_pairs={{0,8},{8,0},{16,24},{24,16},{32,40},{40,32},{48,56},{56,48},{64,72... | collective-permute-start | bytes 1179656 | tf_op jit(solution)/shard_map/core_1/ppermute | solution.py:398
  58.4 18.9 %collective-permute-start.18 = (f32[1,8,160,128]{3,2,1,0:T(8,128)S(1)}, f32[1,8,160,128]{3,2,1,0:T(8,128)S(1)}, u32[]{:S(2)}, u32[]{:S(2)}) collective-permute-start(f32[1,8,160,128]{3,2,1,0:T(8,128)S(1)} %get-tuple-element.75), channel_id=1, source_target_pairs={{0,64},{8,72},{16,80},{24,88},{32,96},{40,104},{48,112},{56,120},{... | collective-permute-start | bytes 1966088 | tf_op jit(solution)/shard_map/swap_0/ppermute | solution.py:398
  61.5 23.3 %collective-permute-start.22 = (f32[2,8,96,128]{3,2,1,0:T(8,128)}, f32[2,8,96,128]{3,2,1,0:T(8,128)}, u32[]{:S(2)}, u32[]{:S(2)}) collective-permute-start(f32[2,8,96,128]{3,2,1,0:T(8,128)} %near1.1), channel_id=1, source_target_pairs={{0,48},{8,24},{16,0},{24,40},{32,16},{40,56},{48,32},{56,8},{64,11... | collective-permute-start | bytes 2359304 | tf_op jit(solution)/shard_map/near_1/ppermute | solution.py:398
  67.5 17.4 %collective-permute-start.21 = (f32[2,8,96,128]{3,2,1,0:T(8,128)}, f32[2,8,96,128]{3,2,1,0:T(8,128)}, u32[]{:S(2)}, u32[]{:S(2)}) collective-permute-start(f32[2,8,96,128]{3,2,1,0:T(8,128)} %ahead1.1), channel_id=1, source_target_pairs={{0,16},{8,56},{16,32},{24,8},{32,48},{40,24},{48,0},{56,40},{64,80... | collective-permute-start | bytes 2359304 | tf_op jit(solution)/shard_map/ahead_1/ppermute | solution.py:398
  69.6 15.2 %collective-permute-start.19 = (f32[1,8,96,128]{3,2,1,0:T(8,128)}, f32[1,8,96,128]{3,2,1,0:T(8,128)S(1)}, u32[]{:S(2)}, u32[]{:S(2)}) collective-permute-start(f32[1,8,96,128]{3,2,1,0:T(8,128)} %get-tuple-element.77), channel_id=1, source_target_pairs={{0,8},{8,0},{16,24},{24,16},{32,40},{40,32},{48,56},{56,48},{64,72... | collective-permute-start | bytes 1179656 | tf_op jit(solution)/shard_map/core_1/ppermute | solution.py:398
  69.6 15.2 %collective-permute-start.20 = (f32[1,8,96,128]{3,2,1,0:T(8,128)}, f32[1,8,96,128]{3,2,1,0:T(8,128)}, u32[]{:S(2)}, u32[]{:S(2)}) collective-permute-start(f32[1,8,96,128]{3,2,1,0:T(8,128)} %get-tuple-element.78), channel_id=1, source_target_pairs={{0,8},{8,0},{16,24},{24,16},{32,40},{40,32},{48,56},{56,48},{64,72... | collective-permute-start | bytes 1179656 | tf_op jit(solution)/shard_map/core_1/ppermute | solution.py:398
  78.8 25.9 %all-to-all-start = ((f32[8,160,128]{2,1,0:T(8,128)}), f32[8,160,128]{2,1,0:T(8,128)}, u32[]{:S(2)}, u32[]{:S(2)}) async-start(f32[8,160,128]{2,1,0:T(8,128)} %finish.2.ordered), calls=%async_computation | async-start | bytes 1310720 | tf_op jit(solution)/shard_map/all_to_all | solution.py:480
  88.1 15.2 %collective-permute-start.23 = (f32[1,8,96,128]{3,2,1,0:T(8,128)S(1)}, f32[1,8,96,128]{3,2,1,0:T(8,128)S(1)}, u32[]{:S(2)}, u32[]{:S(2)}) collective-permute-start(f32[1,8,96,128]{3,2,1,0:T(8,128)S(1)} %get-tuple-element.83), channel_id=1, source_target_pairs={{0,64},{8,72},{16,80},{24,88},{32,96},{40,104},{48,112},{56,120},{... | collective-permute-start | bytes 1179656 | tf_op jit(solution)/shard_map/swap_1/ppermute | solution.py:398
  94.5 15.0 %copy-start.5 = (s32[10]{0:T(128)S(1)}, s32[10]{0:T(128)}, u32[]{:S(2)}) copy-start(s32[10]{0:T(128)} %param.11) | copy-start | bytes 124
  104.7 12.8 %all-to-all-start.2 = ((f32[8,96,128]{2,1,0:T(8,128)}), f32[8,96,128]{2,1,0:T(8,128)S(1)}, u32[]{:S(2)}, u32[]{:S(2)}) async-start(f32[8,96,128]{2,1,0:T(8,128)} %finish.3.ordered), calls=%async_computation.2 | async-start | bytes 786432 | tf_op jit(solution)/shard_map/all_to_all | solution.py:480
  (1 other events, 0.7 us)

commit v6 on v5

--- a/solution.py
+++ b/solution.py
@@ -45,25 +45,6 @@
     return pltpu.CompilerParams(vmem_limit_bytes=VMEM)
 
 
-def block_table(x, y, of_core, x_first):
-    way = 1 - 2 * of_core
-    ys = [(y + step) % Y for step in (2, -way, way, 0)]
-    if x_first:
-        return [dp_index(at, to, of_core) for at in (1 - x, x) for to in ys]
-    return [dp_index(at, to, of_core) for to in ys for at in (x, 1 - x)]
-
-
-TABLES = np.array(
-    [
-        sum((block_table(x, y, of, f) for of in (1 - c, c) for f in (False, True)), [])
-        for x in range(X)
-        for y in range(Y)
-        for c in range(C)
-    ],
-    np.int32,
-)
-
-
 def cost(size):
     return pl.CostEstimate(flops=0, transcendentals=0, bytes_accessed=size // SHARE)
 
@@ -80,7 +61,18 @@
     return lax.optimization_barrier((value, *others))[0]
 
 
-def combine_kernel(tasks, table, grad, *refs):
+def block_at(place, own):
+    index = lax.axis_index("dp")
+    core, y, x = lax.rem(index, C), lax.rem(lax.div(index, C), Y), lax.div(index, C * Y)
+    of_core = core if own else 1 - core
+    way = 1 - 2 * of_core
+    to = lax.rem(y + (2, Y - way, Y + way, 0)[place // X], Y)
+    at = x if place % X == 0 else 1 - x
+    return (at * Y + to) * C + of_core
+
+
+def combine_kernel(tasks, order, grad, *refs):
+    del order
     arrays = sum(len(term["rows"]) for task in tasks for term in task["terms"])
     pieces = sum(len(task["splits"]) for task in tasks)
     given, outs, scratch = refs[:arrays], refs[arrays : arrays + pieces], refs[arrays + pieces :]
@@ -92,7 +84,7 @@
             [
                 pltpu.make_async_copy(
                     grad.at[
-                        pl.ds(pl.multiple_of(table[task["first"] + i] * G, G), G),
+                        pl.ds(pl.multiple_of(block_at(task["first"] + i, task["own"]) * G, G), G),
                         :,
                         pl.ds(task["start"] * LANES, size),
                     ],
@@ -135,7 +127,7 @@
                 out[at, j] = total
 
 
-def combine(grad, table, tasks, name):
+def combine(grad, order, tasks, name):
     arrays, places, static, scratch = [], [], [], []
     for task in tasks:
         count, rows = sum(task["splits"]), task["rows"]
@@ -155,9 +147,9 @@
     outs = pl.pallas_call(
         functools.partial(combine_kernel, static),
         grid_spec=pltpu.PrefetchScalarGridSpec(
-            num_scalar_prefetch=1,
+            num_scalar_prefetch=0,
             grid=(),
-            in_specs=[pl.BlockSpec(memory_space=pl.ANY)] + places,
+            in_specs=[pl.BlockSpec(memory_space=pl.ANY)] * 2 + places,
             out_specs=[pl.BlockSpec(memory_space=pltpu.VMEM)] * len(shapes),
             scratch_shapes=scratch,
         ),
@@ -165,7 +157,7 @@
         name=name,
         compiler_params=params(),
         cost_estimate=cost(size),
-    )(table, in_hbm(grad), *arrays)
+    )(order, in_hbm(grad), *arrays)
     results = []
     for task in tasks:
         results.append(outs[: len(task["splits"])])
@@ -374,24 +366,22 @@
 def per_device(
     grad_parts, master_weights, first_moment, second_moment, cauchy_points, parity_holder
 ):
-    index = lax.axis_index("dp")
     holder = parity_holder.reshape(G)
     state = [a.reshape(G, ROWS, LANES) for a in (master_weights, first_moment, second_moment)]
     points = cauchy_points.astype(jnp.float32)
     coeff = 1.0 / (points[:2][:, None] + points[2:][None, :])
 
     grad = grad_parts.reshape(X * Y * C * G, 1, ROWS * LANES)
-    blocks = lax.dynamic_index_in_dim(jnp.asarray(TABLES), index, keepdims=False)
+    blocks = jnp.zeros((1,), jnp.int32)
     half = X * Y // 2
     got, across, hop, totals, ordered, sums = {}, {}, {}, {}, {}, {}
     olds, done, shards, token = None, None, None, ()
 
     def task(n, own, first, splits, terms, part=None, far=False):
-        start, rows, x_first = CHUNKS[n]
+        start, rows, _ = CHUNKS[n]
         if part:
             start, rows = start + part[0], part[1]
-        base = X * Y * (2 * own + x_first)
-        return dict(first=base + first, start=start, rows=rows, splits=splits, terms=terms, far=far)
+        return dict(own=own, first=first, start=start, rows=rows, splits=splits, terms=terms, far=far)
 
     def send(value, name, n, pairs):
         with jax.named_scope(f"{name}_{n}"):
@@ -399,9 +389,9 @@
 
     def run(*jobs, wait=()):
         nonlocal token
-        table = after(blocks, *token, *wait)
+        order = after(blocks, *token, *wait)
         name = "_".join(f"{job[2]}{job[3]}" for job in jobs)
-        results = combine(grad, table, [job[0] for job in jobs], name)
+        results = combine(grad, order, [job[0] for job in jobs], name)
         token = (results[0][0],)
         for (_, use, *_), result in zip(jobs, results):
             use(*result)

time: 121 us -> 117 us (0.967)
  Pallas kernels: 47.3 us -> 41.5 us
  waiting for transfers between devices: 36.1 us -> 41.8 us
  starting transfers between devices: 33.7 us -> 31.9 us
  local copies, waits for them, and re-layouts: 1.5 us -> 0.09 us
    pallas_call x11, Pallas kernels: 29.9 us -> 24.1 us  [combine(): pl.pallas_call(functools.partial(combine_kernel, static), grid_spec=pltpu...]
    ppermute x24, waiting for transfers between devices: 34.8 us -> 40.5 us  [send(): return lax.ppermute(value, 'dp', pairs)]
    ppermute x24, starting transfers between devices: 16.6 us -> 14.8 us  [send(): return lax.ppermute(value, 'dp', pairs)]
  transfers between devices with their start and end apart: 27 -> 27, of which waited for: 7 -> 7; matrix products, arithmetic and copies ran while one was open for 0% -> 0% of each run, Pallas kernels for 36% -> 33%
where the time goes in v6:
time: 117 us; the launch traced here: 116 us
  waiting for transfers between devices  41.8 us (36%)
  Pallas kernels  41.5 us (35%)
  starting transfers between devices  31.9 us (27%)
    ppermute x24, waiting for transfers between devices, send(): return lax.ppermute(value, 'dp', pairs)  40.5 us
    pallas_call x11, Pallas kernels, combine(): pl.pallas_call(functools.partial(combine_kernel, static), grid_spec=pltpu...  24.1 us
    ppermute x24, starting transfers between devices, send(): return lax.ppermute(value, 'dp', pairs)  14.8 us
    all_to_all x2, starting transfers between devices, to_holders(): sums[group] = lax.all_to_all(ordered[group], 'group', 0, 0)  10.8 us
    pallas_call x2, Pallas kernels, adam(): pl.pallas_call(functools.partial(adam_kernel, first, rows, start), grid_s...  6.78 us
    all_to_all x1, starting transfers between devices, per_device(): olds = lax.all_to_all(old, 'group', 0, 0)  6.34 us
    pallas_call x2, Pallas kernels, parity(): pl.pallas_call(functools.partial(parity_kernel, start, rows), grid_spec=p...  5.37 us
    pallas_call x2, Pallas kernels, finish(): pl.pallas_call(functools.partial(finish_kernel, len(parts), first, rows),...  2.89 us
  transfers between devices with their start and end apart: 27, of which 7 were waited for; matrix products, arithmetic and copies ran while one was open for 0% of the time, Pallas kernels for 33%

profile of v6, /device:TPU:24, one launch (start us, length us, event | category | flops | bytes accessed | tf_op | source)
XLA Modules:
  0.0 116.4 jit_solution(15105668377004763888)
XLA Ops:
  0.6 1.4 %core0.2 = (f32[1,8,160,128]{3,2,1,0:T(8,128)S(1)}, f32[1,8,160,128]{3,2,1,0:T(8,128)S(1)}) custom-call(s32[1]{0:T(128)} %constant.1.clone.1.order, bf16[128,1,32768]{2,1,0:T(2,128)(2,1)} %bitcast.26), custom_call_target="tpu_custom_call" | custom-call | bytes 640 | tf_op jit(solution)/shard_map/core0/pallas_call | solution.py:147
  2.6 2.4 %core0.3 = (f32[1,8,160,128]{3,2,1,0:T(8,128)}, f32[1,8,160,128]{3,2,1,0:T(8,128)}) custom-call(s32[1]{0:T(128)} %constant.1.clone.1.order, bf16[128,1,32768]{2,1,0:T(2,128)(2,1)} %bitcast.27), custom_call_target="tpu_custom_call" | custom-call | bytes 640 | tf_op jit(solution)/shard_map/core0/pallas_call | solution.py:147
  5.6 2.7 %far0.1 = f32[2,8,160,128]{3,2,1,0:T(8,128)} custom-call(s32[1]{0:T(128)} %constant.1.clone.1.order, bf16[128,1,32768]{2,1,0:T(2,128)(2,1)} %bitcast.28, f32[1,8,160,128]{3,2,1,0:T(8,128)S(1)} %collective-permute-done.refs_0_, f32[1,8,160,128]{3,2,1,0:T(8,128)S(1)} %collective-permute-done.1.refs_1_), custom_call_target="tpu_custom_call" | custom-call | bytes 960 | tf_op jit(solution)/shard_map/far0/pallas_call | solution.py:147
  8.6 2.4 %order.1 = f32[8,3,256,128]{3,2,1,0:T(8,128)} custom-call(s32[8]{0:T(128)S(1)} %bitcast.21, f32[8,256,128]{2,1,0:T(8,128)S(1)} %bitcast.14, f32[8,256,128]{2,1,0:T(8,128)S(1)} %bitcast.17, f32[8,256,128]{2,1,0:T(8,128)S(1)} %bitcast.20), custom_call_target="tpu_custom_call" | custom-call | bytes 1536 | tf_op jit(solution)/shard_map/order/pallas_call | solution.py:182
  11.0 6.3 %all-to-all-start.1 = ((f32[8,3,256,128]{3,2,1,0:T(8,128)}), f32[8,3,256,128]{3,2,1,0:T(8,128)S(1)}, u32[]{:S(2)}, u32[]{:S(2)}) async-start(f32[8,3,256,128]{3,2,1,0:T(8,128)} %order.1), calls=%async_computation.1 | async-start | bytes 6291456 | tf_op jit(solution)/shard_map/all_to_all | solution.py:491
  17.4 3.5 %near0_core0.1 = (f32[2,8,160,128]{3,2,1,0:T(8,128)S(1)}, f32[1,8,160,128]{3,2,1,0:T(8,128)S(1)}, f32[1,8,160,128]{3,2,1,0:T(8,128)S(1)}, f32[1,8,160,128]{3,2,1,0:T(8,128)S(1)}, f32[1,8,160,128]{3,2,1,0:T(8,128)S(1)}) custom-call(s32[1]{0:T(128)} %constant.1.clone.1.order, bf16[128,1,32768]{2,1,0:T(2,128)(2,1)} %bitcast.29, ...), custom_call_target="tpu_custom_call" | custom-call | bytes 2240 | tf_op jit(solution)/shard_map/near0_core0/pallas_call | solution.py:147
  20.8 1.9 %collective-permute-start.7 = (f32[2,8,160,128]{3,2,1,0:T(8,128)S(1)}, f32[2,8,160,128]{3,2,1,0:T(8,128)S(1)}, u32[]{:S(2)}, u32[]{:S(2)}) collective-permute-start(f32[2,8,160,128]{3,2,1,0:T(8,128)S(1)} %get-tuple-element.56), channel_id=1, source_target_pairs={{0,48},{8,24},{16,0},{24,40},{32,16},{40,56},{48,32},{56,8},{64,11... | collective-permute-start | bytes 3932168 | tf_op jit(solution)/shard_map/near_0/ppermute | solution.py:388
  23.2 2.6 %core1_core1.1 = (f32[1,8,96,128]{3,2,1,0:T(8,128)S(1)}, f32[1,8,96,128]{3,2,1,0:T(8,128)S(1)}, f32[1,8,96,128]{3,2,1,0:T(8,128)S(1)}, f32[1,8,96,128]{3,2,1,0:T...) custom-call(s32[1]{0:T(128)} %constant.1.clone.1.order, ...), custom_call_target="tpu_custom_call" | custom-call | bytes 1536 | tf_op jit(solution)/shard_map/core1_core1/pallas_call | solution.py:147
  26.3 2.8 %collective-permute-done.6.refs_2_ = f32[2,8,160,128]{3,2,1,0:T(8,128)} collective-permute-done((f32[2,8,160,128]{3,2,1,0:T(8,128)}, f32[2,8,160,128]{3,2,1,0:T(8,128)}, u32[]{:S(2)}, u32[]{:S(2)}) %collective-permute-start.6) | collective-permute-done | bytes 1310752 | tf_op jit(solution)/shard_map/far_0/ppermute | solution.py:388
  29.1 2.8 %ahead0.1 = f32[2,8,160,128]{3,2,1,0:T(8,128)S(1)} custom-call(s32[1]{0:T(128)} %constant.1.clone.1.order, bf16[128,1,32768]{2,1,0:T(2,128)(2,1)} %bitcast.31, f32[1,8,160,128]{3,2,1,0:T(8,128)S(1)} %collective-permute-done.4.refs_0_, f32[1,8,160,128]{3,2,1,0:T(8,128)S(1)} %collective-permute-done.5.refs_1_, f32[2,8,160,128]{3,2,1,0:T(8,128)} %collective-permute-done.6.refs_2_), custom_call_target="tpu_custom_call" | custom-call | bytes 1280 | tf_op jit(solution)/shard_map/ahead0/pallas_call | solution.py:147
  32.6 14.4 %collective-permute-done.7.refs_3_ = f32[2,8,160,128]{3,2,1,0:T(8,128)S(1)} collective-permute-done((f32[2,8,160,128]{3,2,1,0:T(8,128)S(1)}, f32[2,8,160,128]{3,2,1,0:T(8,128)S(1)}, u32[]{:S(2)}, u32[]{:S(2)}) %collective-permute-start.7) | collective-permute-done | bytes 1310752 | tf_op jit(solution)/shard_map/near_0/ppermute | solution.py:388
  47.0 1.2 %far1.1 = f32[2,8,96,128]{3,2,1,0:T(8,128)S(1)} custom-call(s32[1]{0:T(128)} %constant.1.clone.1.order, bf16[128,1,32768]{2,1,0:T(2,128)(2,1)} %bitcast.32, f32[1,8,96,128]{3,2,1,0:T(8,128)S(1)} %collective-permute-done.8.refs_0_, f32[1,8,96,128]{3,2,1,0:T(8,128)S(1)} %collective-permute-done.9.refs_1_), custom_call_target="tpu_custom_call" | custom-call | bytes 576 | tf_op jit(solution)/shard_map/far1/pallas_call | solution.py:147
  49.6 2.1 %near1.1 = f32[2,8,96,128]{3,2,1,0:T(8,128)} custom-call(s32[1]{0:T(128)} %constant.1.clone.1.order, bf16[128,1,32768]{2,1,0:T(2,128)(2,1)} %bitcast.33, f32[1,8,96,128]{3,2,1,0:T(8,128)S(1)} %collective-permute-done.10.refs_0_, f32[1,8,96,128]{3,2,1,0:T(8,128)S(1)} %collective-permute-done.11.refs_1_), custom_call_target="tpu_custom_call" | custom-call | bytes 576 | tf_op jit(solution)/shard_map/near1/pallas_call | solution.py:147
  51.7 2.7 %collective-permute-done.14.refs_2_ = f32[2,8,160,128]{3,2,1,0:T(8,128)S(1)} collective-permute-done((f32[2,8,160,128]{3,2,1,0:T(8,128)S(1)}, f32[2,8,160,128]{3,2,1,0:T(8,128)S(1)}, u32[]{:S(2)}, u32[]{:S(2)}) %collective-permute-start.14) | collective-permute-done | bytes 1310752 | tf_op jit(solution)/shard_map/ahead_0/ppermute | solution.py:388
  54.3 1.5 %here0.1 = (f32[1,8,160,128]{3,2,1,0:T(8,128)S(1)}, f32[1,8,160,128]{3,2,1,0:T(8,128)S(1)}) custom-call(s32[1]{0:T(128)} %constant.1.clone.1.order, bf16[128,1,32768]{2,1,0:T(2,128)(2,1)} %bitcast.34, f32[1,8,160,128]{3,2,1,0:T(8,128)S(1)} %collective-permute-done.12.refs_0_, f32[1,8,160,128]{3,2,1,0:T(8,128)S(1)} %collective-permute-done.13.refs_1_, ...), custom_call_target="tpu_custom_call" | custom-call | bytes 1600 | tf_op jit(solution)/shard_map/here0/pallas_call | solution.py:147
  55.8 3.1 %collective-permute-start.18 = (f32[1,8,160,128]{3,2,1,0:T(8,128)S(1)}, f32[1,8,160,128]{3,2,1,0:T(8,128)S(1)}, u32[]{:S(2)}, u32[]{:S(2)}) collective-permute-start(f32[1,8,160,128]{3,2,1,0:T(8,128)S(1)} %get-tuple-element.75), channel_id=1, source_target_pairs={{0,64},{8,72},{16,80},{24,88},{32,96},{40,104},{48,112},{56,120},{... | collective-permute-start | bytes 1966088 | tf_op jit(solution)/shard_map/swap_0/ppermute | solution.py:388
  59.7 4.0 %collective-permute-done.17.refs_2_ = f32[2,8,96,128]{3,2,1,0:T(8,128)S(1)} collective-permute-done((f32[2,8,96,128]{3,2,1,0:T(8,128)S(1)}, f32[2,8,96,128]{3,2,1,0:T(8,128)S(1)}, u32[]{:S(2)}, u32[]{:S(2)}) %collective-permute-start.17) | collective-permute-done | bytes 786464 | tf_op jit(solution)/shard_map/far_1/ppermute | solution.py:388
  63.7 2.1 %ahead1.1 = f32[2,8,96,128]{3,2,1,0:T(8,128)} custom-call(s32[1]{0:T(128)} %constant.1.clone.1.order, bf16[128,1,32768]{2,1,0:T(2,128)(2,1)} %bitcast.35, f32[1,8,96,128]{3,2,1,0:T(8,128)S(1)} %collective-permute-done.15.refs_0_, f32[1,8,96,128]{3,2,1,0:T(8,128)S(1)} %collective-permute-done.16.refs_1_, f32[2,8,96,128]{3,2,1,0:T(8,128)S(1)} %collective-permute-done.17.refs_2_), custom_call_target="tpu_custom_call" | custom-call | bytes 768 | tf_op jit(solution)/shard_map/ahead1/pallas_call | solution.py:147
  65.8 1.3 %collective-permute-start.21 = (f32[2,8,96,128]{3,2,1,0:T(8,128)}, f32[2,8,96,128]{3,2,1,0:T(8,128)}, u32[]{:S(2)}, u32[]{:S(2)}) collective-permute-start(f32[2,8,96,128]{3,2,1,0:T(8,128)} %ahead1.1), channel_id=1, source_target_pairs={{0,16},{8,56},{16,32},{24,8},{32,48},{40,24},{48,0},{56,40},{64,80... | collective-permute-start | bytes 2359304 | tf_op jit(solution)/shard_map/ahead_1/ppermute | solution.py:388
  67.5 6.8 %collective-permute-done.18.refs_1_ = f32[1,8,160,128]{3,2,1,0:T(8,128)S(1)} collective-permute-done((f32[1,8,160,128]{3,2,1,0:T(8,128)S(1)}, f32[1,8,160,128]{3,2,1,0:T(8,128)S(1)}, u32[]{:S(2)}, u32[]{:S(2)}) %collective-permute-start.18) | collective-permute-done | bytes 655392 | tf_op jit(solution)/shard_map/swap_0/ppermute | solution.py:388
  74.4 1.5 %finish.2.ordered = f32[8,160,128]{2,1,0:T(8,128)} custom-call(s32[8]{0:T(128)S(1)} %bitcast.22, f32[1,8,160,128]{3,2,1,0:T(8,128)S(1)} %get-tuple-element.70.refs_0_, f32[1,8,160,128]{3,2,1,0:T(8,128)S(1)} %collective-permute-done.18.refs_1_), custom_call_target="tpu_custom_call" | custom-call | bytes 640 | tf_op jit(solution)/shard_map/finish/pallas_call | solution.py:218
  75.9 6.0 %all-to-all-start = ((f32[8,160,128]{2,1,0:T(8,128)}), f32[8,160,128]{2,1,0:T(8,128)}, u32[]{:S(2)}, u32[]{:S(2)}) async-start(f32[8,160,128]{2,1,0:T(8,128)} %finish.2.ordered), calls=%async_computation | async-start | bytes 1310720 | tf_op jit(solution)/shard_map/all_to_all | solution.py:470
  81.9 2.0 %here1.1 = (f32[1,8,96,128]{3,2,1,0:T(8,128)S(1)}, f32[1,8,96,128]{3,2,1,0:T(8,128)S(1)}) custom-call(s32[1]{0:T(128)} %constant.1.clone.1.order, bf16[128,1,32768]{2,1,0:T(2,128)(2,1)} %bitcast.36, f32[1,8,96,128]{3,2,1,0:T(8,128)} %collective-permute-done.19.refs_0_, f32[1,8,96,128]{3,2,1,0:T(8,128)} %collective-permute-done.20.refs_1_, ...), custom_call_target="tpu_custom_call" | custom-call | bytes 960 | tf_op jit(solution)/shard_map/here1/pallas_call | solution.py:147
  83.9 2.8 %collective-permute-start.23 = (f32[1,8,96,128]{3,2,1,0:T(8,128)S(1)}, f32[1,8,96,128]{3,2,1,0:T(8,128)S(1)}, u32[]{:S(2)}, u32[]{:S(2)}) collective-permute-start(f32[1,8,96,128]{3,2,1,0:T(8,128)S(1)} %get-tuple-element.83), channel_id=1, source_target_pairs={{0,64},{8,72},{16,80},{24,88},{32,96},{40,104},{48,112},{56,120},{... | collective-permute-start | bytes 1179656 | tf_op jit(solution)/shard_map/swap_1/ppermute | solution.py:388
  86.7 3.6 %adam.2 = (f32[8,256,128]{2,1,0:T(8,128)}, f32[8,256,128]{2,1,0:T(8,128)}, f32[8,256,128]{2,1,0:T(8,128)}) custom-call(s32[8]{0:T(128)S(1)} %bitcast.23, f32[8,160,128]{2,1,0:T(8,128)} %finish.2.ordered, f32[8,256,128]{2,1,0:T(8,128)} %bitcast.12, f32[8,256,128]{2,1,0:T(8,128)} %bitcast.15, f32[8,256,128]{2,1,0:T(8,128)} %bitcast.18), custom_call_target="tpu_custom_call" | custom-call | bytes 1120 | tf_op jit(solution)/shard_map/adam/pallas_call | solution.py:281
  90.3 9.7 %collective-permute-done.23.refs_1_ = f32[1,8,96,128]{3,2,1,0:T(8,128)S(1)} collective-permute-done((f32[1,8,96,128]{3,2,1,0:T(8,128)S(1)}, f32[1,8,96,128]{3,2,1,0:T(8,128)S(1)}, u32[]{:S(2)}, u32[]{:S(2)}) %collective-permute-start.23) | collective-permute-done | bytes 393248 | tf_op jit(solution)/shard_map/swap_1/ppermute | solution.py:388
  100.0 1.4 %finish.3.ordered = f32[8,96,128]{2,1,0:T(8,128)} custom-call(s32[8]{0:T(128)S(1)} %bitcast.24, f32[1,8,96,128]{3,2,1,0:T(8,128)S(1)} %get-tuple-element.79.refs_0_, f32[1,8,96,128]{3,2,1,0:T(8,128)S(1)} %collective-permute-done.23.refs_1_), custom_call_target="tpu_custom_call" | custom-call | bytes 384 | tf_op jit(solution)/shard_map/finish/pallas_call | solution.py:218
  101.4 4.8 %all-to-all-start.2 = ((f32[8,96,128]{2,1,0:T(8,128)}), f32[8,96,128]{2,1,0:T(8,128)S(1)}, u32[]{:S(2)}, u32[]{:S(2)}) async-start(f32[8,96,128]{2,1,0:T(8,128)} %finish.3.ordered), calls=%async_computation.2 | async-start | bytes 786432 | tf_op jit(solution)/shard_map/all_to_all | solution.py:470
  106.4 3.3 %parity.2.refs_0_ = f32[3,256,2,128]{3,2,1,0:T(2,128)} custom-call(f32[2,8]{1,0:T(2,128)S(1)} %add_divide_fusion.coeff, f32[8,160,128]{2,1,0:T(8,128)} %all-to-all-done.sums, f32[8,3,256,128]{3,2,1,0:T(8,128)S(1)} %all-to-all-done.1.old), custom_call_target="tpu_custom_call" | custom-call | bytes 640 | tf_op jit(solution)/shard_map/parity/pallas_call | solution.py:343
  109.7 3.1 %adam.3 = (f32[8,256,128]{2,1,0:T(8,128)}, f32[8,256,128]{2,1,0:T(8,128)}, f32[8,256,128]{2,1,0:T(8,128)}) custom-call(s32[8]{0:T(128)S(1)} %bitcast.25, f32[8,96,128]{2,1,0:T(8,128)} %finish.3.ordered, f32[8,256,128]{2,1,0:T(8,128)} %bitcast.13, f32[8,256,128]{2,1,0:T(8,128)} %bitcast.16, ...), custom_call_target="tpu_custom_call", output_to_operand_aliasing={{0}: (5, {}), {1}: (6, {}), {2}: (7, {})} | custom-call | bytes 672 | tf_op jit(solution)/shard_map/adam/pallas_call | solution.py:281
  112.9 1.3 %all-to-all-done.2.sums = f32[8,96,128]{2,1,0:T(8,128)S(1)} async-done(((f32[8,96,128]{2,1,0:T(8,128)}), f32[8,96,128]{2,1,0:T(8,128)S(1)}, u32[]{:S(2)}, u32[]{:S(2)}) %all-to-all-start.2) | async-done | bytes 393248 | tf_op jit(solution)/shard_map/all_to_all | solution.py:470
  114.2 2.0 %parity.3 = f32[3,256,2,128]{3,2,1,0:T(2,128)} custom-call(f32[2,8]{1,0:T(2,128)S(1)} %add_divide_fusion.coeff, f32[8,96,128]{2,1,0:T(8,128)S(1)} %all-to-all-done.2.sums, f32[8,3,256,128]{3,2,1,0:T(8,128)S(1)} %all-to-all-done.1.old, f32[3,256,2,128]{3,2,1,0:T(2,128)} %parity.2.refs_0_), custom_call_target="tpu_custom_call", output_to_operand_aliasing={{}: (3, {})} | custom-call | bytes 384 | tf_op jit(solution)/shard_map/parity/pallas_call | solution.py:343
  (53 shorter events, 5.9 us)
Async XLA Ops:
  2.0 3.6 %collective-permute-start.1 = (f32[1,8,160,128]{3,2,1,0:T(8,128)S(1)}, f32[1,8,160,128]{3,2,1,0:T(8,128)S(1)}, u32[]{:S(2)}, u32[]{:S(2)}) collective-permute-start(f32[1,8,160,128]{3,2,1,0:T(8,128)S(1)} %get-tuple-element.52), channel_id=1, source_target_pairs={{0,8},{8,0},{16,24},{24,16},{32,40},{40,32},{48,56},{56,48},{64,72... | collective-permute-start | bytes 1966088 | tf_op jit(solution)/shard_map/core_0/ppermute | solution.py:388
  2.1 3.5 %collective-permute-start = (f32[1,8,160,128]{3,2,1,0:T(8,128)S(1)}, f32[1,8,160,128]{3,2,1,0:T(8,128)S(1)}, u32[]{:S(2)}, u32[]{:S(2)}) collective-permute-start(f32[1,8,160,128]{3,2,1,0:T(8,128)S(1)} %get-tuple-element.48), channel_id=1, source_target_pairs={{0,8},{8,0},{16,24},{24,16},{32,40},{40,32},{48,56},{56,48},{64,72... | collective-permute-start | bytes 1966088 | tf_op jit(solution)/shard_map/core_0/ppermute | solution.py:388
  5.0 12.4 %collective-permute-start.3 = (f32[1,8,160,128]{3,2,1,0:T(8,128)}, f32[1,8,160,128]{3,2,1,0:T(8,128)}, u32[]{:S(2)}, u32[]{:S(2)}) collective-permute-start(f32[1,8,160,128]{3,2,1,0:T(8,128)} %get-tuple-element.55), channel_id=1, source_target_pairs={{0,8},{8,0},{16,24},{24,16},{32,40},{40,32},{48,56},{56,48},{64,72... | collective-permute-start | bytes 1966088 | tf_op jit(solution)/shard_map/core_0/ppermute | solution.py:388
  5.1 3.4 %copy-start = (f32[1,262144]{1,0:T(1,128)S(1)}, f32[1,262144]{1,0:T(1,128)}, u32[]{:S(2)}) copy-start(f32[1,262144]{1,0:T(1,128)} %param.7) | copy-start | bytes 3145732
  5.1 3.4 %copy-start.1 = (f32[1,262144]{1,0:T(1,128)S(1)}, f32[1,262144]{1,0:T(1,128)}, u32[]{:S(2)}) copy-start(f32[1,262144]{1,0:T(1,128)} %param.8) | copy-start | bytes 3145732
  5.1 3.4 %copy-start.2 = (f32[1,262144]{1,0:T(1,128)S(1)}, f32[1,262144]{1,0:T(1,128)}, u32[]{:S(2)}) copy-start(f32[1,262144]{1,0:T(1,128)} %param.9) | copy-start | bytes 3145732
  5.1 3.4 %copy-start.3 = (s32[1,8]{1,0:T(1,128)S(1)}, s32[1,8]{1,0:T(1,128)}, u32[]{:S(2)}) copy-start(s32[1,8]{1,0:T(1,128)} %param.11) | copy-start | bytes 100
  5.1 12.2 %collective-permute-start.2 = (f32[1,8,160,128]{3,2,1,0:T(8,128)}, f32[1,8,160,128]{3,2,1,0:T(8,128)}, u32[]{:S(2)}, u32[]{:S(2)}) collective-permute-start(f32[1,8,160,128]{3,2,1,0:T(8,128)} %get-tuple-element.50), channel_id=1, source_target_pairs={{0,8},{8,0},{16,24},{24,16},{32,40},{40,32},{48,56},{56,48},{64,72... | collective-permute-start | bytes 1966088 | tf_op jit(solution)/shard_map/core_0/ppermute | solution.py:388
  8.4 20.7 %collective-permute-start.6 = (f32[2,8,160,128]{3,2,1,0:T(8,128)}, f32[2,8,160,128]{3,2,1,0:T(8,128)}, u32[]{:S(2)}, u32[]{:S(2)}) collective-permute-start(f32[2,8,160,128]{3,2,1,0:T(8,128)} %far0.1), channel_id=1, source_target_pairs={{0,16},{8,56},{16,32},{24,8},{32,48},{40,24},{48,0},{56,40},{64,80... | collective-permute-start | bytes 3932168 | tf_op jit(solution)/shard_map/far_0/ppermute | solution.py:388
  11.0 64.9 %all-to-all-start.1 = ((f32[8,3,256,128]{3,2,1,0:T(8,128)}), f32[8,3,256,128]{3,2,1,0:T(8,128)S(1)}, u32[]{:S(2)}, u32[]{:S(2)}) async-start(f32[8,3,256,128]{3,2,1,0:T(8,128)} %order.1), calls=%async_computation.1 | async-start | bytes 6291456 | tf_op jit(solution)/shard_map/all_to_all | solution.py:491
  20.8 26.2 %collective-permute-start.7 = (f32[2,8,160,128]{3,2,1,0:T(8,128)S(1)}, f32[2,8,160,128]{3,2,1,0:T(8,128)S(1)}, u32[]{:S(2)}, u32[]{:S(2)}) collective-permute-start(f32[2,8,160,128]{3,2,1,0:T(8,128)S(1)} %get-tuple-element.56), channel_id=1, source_target_pairs={{0,48},{8,24},{16,0},{24,40},{32,16},{40,56},{48,32},{56,8},{64,11... | collective-permute-start | bytes 3932168 | tf_op jit(solution)/shard_map/near_0/ppermute | solution.py:388
  22.7 3.6 %collective-permute-start.4 = (f32[1,8,160,128]{3,2,1,0:T(8,128)S(1)}, f32[1,8,160,128]{3,2,1,0:T(8,128)S(1)}, u32[]{:S(2)}, u32[]{:S(2)}) collective-permute-start(f32[1,8,160,128]{3,2,1,0:T(8,128)S(1)} %get-tuple-element.60), channel_id=1, source_target_pairs={{0,8},{8,0},{16,24},{24,16},{32,40},{40,32},{48,56},{56,48},{64,72... | collective-permute-start | bytes 1966088 | tf_op jit(solution)/shard_map/core_0/ppermute | solution.py:388
  23.1 3.2 %collective-permute-start.5 = (f32[1,8,160,128]{3,2,1,0:T(8,128)S(1)}, f32[1,8,160,128]{3,2,1,0:T(8,128)S(1)}, u32[]{:S(2)}, u32[]{:S(2)}) collective-permute-start(f32[1,8,160,128]{3,2,1,0:T(8,128)S(1)} %get-tuple-element.61), channel_id=1, source_target_pairs={{0,8},{8,0},{16,24},{24,16},{32,40},{40,32},{48,56},{56,48},{64,72... | collective-permute-start | bytes 1966088 | tf_op jit(solution)/shard_map/core_0/ppermute | solution.py:388
  25.9 6.6 %collective-permute-start.9 = (f32[1,8,96,128]{3,2,1,0:T(8,128)S(1)}, f32[1,8,96,128]{3,2,1,0:T(8,128)S(1)}, u32[]{:S(2)}, u32[]{:S(2)}) collective-permute-start(f32[1,8,96,128]{3,2,1,0:T(8,128)S(1)} %get-tuple-element.63), channel_id=1, source_target_pairs={{0,8},{8,0},{16,24},{24,16},{32,40},{40,32},{48,56},{56,48},{64,72... | collective-permute-start | bytes 1179656 | tf_op jit(solution)/shard_map/core_1/ppermute | solution.py:388
  31.8 22.5 %collective-permute-start.14 = (f32[2,8,160,128]{3,2,1,0:T(8,128)S(1)}, f32[2,8,160,128]{3,2,1,0:T(8,128)S(1)}, u32[]{:S(2)}, u32[]{:S(2)}) collective-permute-start(f32[2,8,160,128]{3,2,1,0:T(8,128)S(1)} %ahead0.1), channel_id=1, source_target_pairs={{0,16},{8,56},{16,32},{24,8},{32,48},{40,24},{48,0},{56,40},{64,80... | collective-permute-start | bytes 3932168 | tf_op jit(solution)/shard_map/ahead_0/ppermute | solution.py:388
  31.9 15.1 %collective-permute-start.8 = (f32[1,8,96,128]{3,2,1,0:T(8,128)S(1)}, f32[1,8,96,128]{3,2,1,0:T(8,128)S(1)}, u32[]{:S(2)}, u32[]{:S(2)}) collective-permute-start(f32[1,8,96,128]{3,2,1,0:T(8,128)S(1)} %get-tuple-element.58), channel_id=1, source_target_pairs={{0,8},{8,0},{16,24},{24,16},{32,40},{40,32},{48,56},{56,48},{64,72... | collective-permute-start | bytes 1179656 | tf_op jit(solution)/shard_map/core_1/ppermute | solution.py:388
  32.0 16.3 %collective-permute-start.10 = (f32[1,8,96,128]{3,2,1,0:T(8,128)S(1)}, f32[1,8,96,128]{3,2,1,0:T(8,128)S(1)}, u32[]{:S(2)}, u32[]{:S(2)}) collective-permute-start(f32[1,8,96,128]{3,2,1,0:T(8,128)S(1)} %get-tuple-element.65), channel_id=1, source_target_pairs={{0,8},{8,0},{16,24},{24,16},{32,40},{40,32},{48,56},{56,48},{64,72... | collective-permute-start | bytes 1179656 | tf_op jit(solution)/shard_map/core_1/ppermute | solution.py:388
  32.5 16.6 %collective-permute-start.12 = (f32[1,8,160,128]{3,2,1,0:T(8,128)S(1)}, f32[1,8,160,128]{3,2,1,0:T(8,128)S(1)}, u32[]{:S(2)}, u32[]{:S(2)}) collective-permute-start(f32[1,8,160,128]{3,2,1,0:T(8,128)S(1)} %get-tuple-element.68), channel_id=1, source_target_pairs={{0,8},{8,0},{16,24},{24,16},{32,40},{40,32},{48,56},{56,48},{64,72... | collective-permute-start | bytes 1966088 | tf_op jit(solution)/shard_map/core_0/ppermute | solution.py:388
  47.0 2.0 %collective-permute-start.11 = (f32[1,8,96,128]{3,2,1,0:T(8,128)S(1)}, f32[1,8,96,128]{3,2,1,0:T(8,128)S(1)}, u32[]{:S(2)}, u32[]{:S(2)}) collective-permute-start(f32[1,8,96,128]{3,2,1,0:T(8,128)S(1)} %get-tuple-element.66), channel_id=1, source_target_pairs={{0,8},{8,0},{16,24},{24,16},{32,40},{40,32},{48,56},{56,48},{64,72... | collective-permute-start | bytes 1179656 | tf_op jit(solution)/shard_map/core_1/ppermute | solution.py:388
  48.2 15.4 %collective-permute-start.17 = (f32[2,8,96,128]{3,2,1,0:T(8,128)S(1)}, f32[2,8,96,128]{3,2,1,0:T(8,128)S(1)}, u32[]{:S(2)}, u32[]{:S(2)}) collective-permute-start(f32[2,8,96,128]{3,2,1,0:T(8,128)S(1)} %far1.1), channel_id=1, source_target_pairs={{0,16},{8,56},{16,32},{24,8},{32,48},{40,24},{48,0},{56,40},{64,80... | collective-permute-start | bytes 2359304 | tf_op jit(solution)/shard_map/far_1/ppermute | solution.py:388
  48.3 3.3 %collective-permute-start.13 = (f32[1,8,160,128]{3,2,1,0:T(8,128)S(1)}, f32[1,8,160,128]{3,2,1,0:T(8,128)S(1)}, u32[]{:S(2)}, u32[]{:S(2)}) collective-permute-start(f32[1,8,160,128]{3,2,1,0:T(8,128)S(1)} %get-tuple-element.69), channel_id=1, source_target_pairs={{0,8},{8,0},{16,24},{24,16},{32,40},{40,32},{48,56},{56,48},{64,72... | collective-permute-start | bytes 1966088 | tf_op jit(solution)/shard_map/core_0/ppermute | solution.py:388
  49.1 10.6 %collective-permute-start.15 = (f32[1,8,96,128]{3,2,1,0:T(8,128)S(1)}, f32[1,8,96,128]{3,2,1,0:T(8,128)S(1)}, u32[]{:S(2)}, u32[]{:S(2)}) collective-permute-start(f32[1,8,96,128]{3,2,1,0:T(8,128)S(1)} %get-tuple-element.72), channel_id=1, source_target_pairs={{0,8},{8,0},{16,24},{24,16},{32,40},{40,32},{48,56},{56,48},{64,72... | collective-permute-start | bytes 1179656 | tf_op jit(solution)/shard_map/core_1/ppermute | solution.py:388
  49.2 10.5 %collective-permute-start.16 = (f32[1,8,96,128]{3,2,1,0:T(8,128)S(1)}, f32[1,8,96,128]{3,2,1,0:T(8,128)S(1)}, u32[]{:S(2)}, u32[]{:S(2)}) collective-permute-start(f32[1,8,96,128]{3,2,1,0:T(8,128)S(1)} %get-tuple-element.73), channel_id=1, source_target_pairs={{0,8},{8,0},{16,24},{24,16},{32,40},{40,32},{48,56},{56,48},{64,72... | collective-permute-start | bytes 1179656 | tf_op jit(solution)/shard_map/core_1/ppermute | solution.py:388
  55.8 18.6 %collective-permute-start.18 = (f32[1,8,160,128]{3,2,1,0:T(8,128)S(1)}, f32[1,8,160,128]{3,2,1,0:T(8,128)S(1)}, u32[]{:S(2)}, u32[]{:S(2)}) collective-permute-start(f32[1,8,160,128]{3,2,1,0:T(8,128)S(1)} %get-tuple-element.75), channel_id=1, source_target_pairs={{0,64},{8,72},{16,80},{24,88},{32,96},{40,104},{48,112},{56,120},{... | collective-permute-start | bytes 1966088 | tf_op jit(solution)/shard_map/swap_0/ppermute | solution.py:388
  58.9 23.0 %collective-permute-start.22 = (f32[2,8,96,128]{3,2,1,0:T(8,128)}, f32[2,8,96,128]{3,2,1,0:T(8,128)}, u32[]{:S(2)}, u32[]{:S(2)}) collective-permute-start(f32[2,8,96,128]{3,2,1,0:T(8,128)} %near1.1), channel_id=1, source_target_pairs={{0,48},{8,24},{16,0},{24,40},{32,16},{40,56},{48,32},{56,8},{64,11... | collective-permute-start | bytes 2359304 | tf_op jit(solution)/shard_map/near_1/ppermute | solution.py:388
  65.8 16.1 %collective-permute-start.21 = (f32[2,8,96,128]{3,2,1,0:T(8,128)}, f32[2,8,96,128]{3,2,1,0:T(8,128)}, u32[]{:S(2)}, u32[]{:S(2)}) collective-permute-start(f32[2,8,96,128]{3,2,1,0:T(8,128)} %ahead1.1), channel_id=1, source_target_pairs={{0,16},{8,56},{16,32},{24,8},{32,48},{40,24},{48,0},{56,40},{64,80... | collective-permute-start | bytes 2359304 | tf_op jit(solution)/shard_map/ahead_1/ppermute | solution.py:388
  67.0 14.8 %collective-permute-start.19 = (f32[1,8,96,128]{3,2,1,0:T(8,128)}, f32[1,8,96,128]{3,2,1,0:T(8,128)}, u32[]{:S(2)}, u32[]{:S(2)}) collective-permute-start(f32[1,8,96,128]{3,2,1,0:T(8,128)} %get-tuple-element.77), channel_id=1, source_target_pairs={{0,8},{8,0},{16,24},{24,16},{32,40},{40,32},{48,56},{56,48},{64,72... | collective-permute-start | bytes 1179656 | tf_op jit(solution)/shard_map/core_1/ppermute | solution.py:388
  67.0 14.8 %collective-permute-start.20 = (f32[1,8,96,128]{3,2,1,0:T(8,128)S(1)}, f32[1,8,96,128]{3,2,1,0:T(8,128)}, u32[]{:S(2)}, u32[]{:S(2)}) collective-permute-start(f32[1,8,96,128]{3,2,1,0:T(8,128)S(1)} %get-tuple-element.78), channel_id=1, source_target_pairs={{0,8},{8,0},{16,24},{24,16},{32,40},{40,32},{48,56},{56,48},{64,72... | collective-permute-start | bytes 1179656 | tf_op jit(solution)/shard_map/core_1/ppermute | solution.py:388
  75.9 25.5 %all-to-all-start = ((f32[8,160,128]{2,1,0:T(8,128)}), f32[8,160,128]{2,1,0:T(8,128)}, u32[]{:S(2)}, u32[]{:S(2)}) async-start(f32[8,160,128]{2,1,0:T(8,128)} %finish.2.ordered), calls=%async_computation | async-start | bytes 1310720 | tf_op jit(solution)/shard_map/all_to_all | solution.py:470
  83.9 16.1 %collective-permute-start.23 = (f32[1,8,96,128]{3,2,1,0:T(8,128)S(1)}, f32[1,8,96,128]{3,2,1,0:T(8,128)S(1)}, u32[]{:S(2)}, u32[]{:S(2)}) collective-permute-start(f32[1,8,96,128]{3,2,1,0:T(8,128)S(1)} %get-tuple-element.83), channel_id=1, source_target_pairs={{0,64},{8,72},{16,80},{24,88},{32,96},{40,104},{48,112},{56,120},{... | collective-permute-start | bytes 1179656 | tf_op jit(solution)/shard_map/swap_1/ppermute | solution.py:388
  90.3 15.9 %copy-start.4 = (s32[10]{0:T(128)S(1)}, s32[10]{0:T(128)}, u32[]{:S(2)}) copy-start(s32[10]{0:T(128)} %param.10) | copy-start | bytes 124
  101.4 12.8 %all-to-all-start.2 = ((f32[8,96,128]{2,1,0:T(8,128)}), f32[8,96,128]{2,1,0:T(8,128)S(1)}, u32[]{:S(2)}, u32[]{:S(2)}) async-start(f32[8,96,128]{2,1,0:T(8,128)} %finish.3.ordered), calls=%async_computation.2 | async-start | bytes 786432 | tf_op jit(solution)/shard_map/all_to_all | solution.py:470

commit v7 on v6

--- a/solution.py
+++ b/solution.py
@@ -2,7 +2,6 @@
 
 import jax
 import jax.numpy as jnp
-import numpy as np
 from jax import lax
 from jax.experimental import pallas as pl
 from jax.experimental.pallas import tpu as pltpu
@@ -14,7 +13,7 @@
 ROWS = 256
 LANES = 128
 SHARD = G * ROWS * LANES
-CHUNKS = ((0, 160, False), (160, 96, False))
+CHUNKS = ((0, 160), (160, 96))
 GROUPS = ((0,), (1,))
 VMEM = 8 * 2**20
 
@@ -73,7 +72,7 @@
 
 def combine_kernel(tasks, order, grad, *refs):
     del order
-    arrays = sum(len(term["rows"]) for task in tasks for term in task["terms"])
+    arrays = sum(len(task["offsets"]) for task in tasks)
     pieces = sum(len(task["splits"]) for task in tasks)
     given, outs, scratch = refs[:arrays], refs[arrays : arrays + pieces], refs[arrays + pieces :]
     work = []
@@ -95,19 +94,17 @@
             for i in range(count)
         ]
         terms = []
-        for term in task["terms"]:
-            mine, given = given[: len(term["rows"])], given[len(term["rows"]) :]
-            blocks = [i for i in range(count) if 0 <= term["offset"] + i < mine[0].shape[0]]
+        for offset in task["offsets"]:
+            mine, given = given[0], given[1:]
+            blocks = [i for i in range(count) if 0 <= offset + i < mine.shape[0]]
             if task["far"]:
                 (near, near_sems), scratch = scratch[:2], scratch[2:]
                 for i in blocks:
-                    copy = pltpu.make_async_copy(
-                        mine[0].at[term["offset"] + i], near.at[i], near_sems.at[i]
-                    )
-                    copies[i].append(copy)
-                terms.append({i: ((near, i),) for i in blocks})
+                    source = mine.at[offset + i]
+                    copies[i].append(pltpu.make_async_copy(source, near.at[i], near_sems.at[i]))
+                terms.append({i: (near, i) for i in blocks})
             else:
-                terms.append({i: tuple((a, term["offset"] + i) for a in mine) for i in blocks})
+                terms.append({i: (mine, offset + i) for i in blocks})
         for block in copies:
             for copy in block:
                 copy.start()
@@ -122,8 +119,8 @@
                 total = held[i * G + j].reshape(task["rows"], LANES).astype(jnp.float32)
                 for term in terms:
                     if i in term:
-                        parts = [a[b, j] for a, b in term[i]]
-                        total = total + (parts[0] if len(parts) == 1 else jnp.concatenate(parts))
+                        held_term, place = term[i]
+                        total = total + held_term[place, j]
                 out[at, j] = total
 
 
@@ -134,14 +131,12 @@
         scratch.append(pltpu.VMEM((count * G, 1, rows * LANES), jnp.bfloat16))
         scratch.append(pltpu.SemaphoreType.DMA((count,)))
         for held, _ in task["terms"]:
-            for a in held:
-                arrays.append(in_hbm(a) if task["far"] else in_vmem(a))
-                places.append(pl.BlockSpec(memory_space=pl.ANY if task["far"] else pltpu.VMEM))
+            arrays.append(in_hbm(held) if task["far"] else in_vmem(held))
+            places.append(pl.BlockSpec(memory_space=pl.ANY if task["far"] else pltpu.VMEM))
             if task["far"]:
                 scratch.append(pltpu.VMEM((count, G, rows, LANES), jnp.float32))
                 scratch.append(pltpu.SemaphoreType.DMA((count,)))
-        terms = [dict(rows=[a.shape[2] for a in held], offset=o) for held, o in task["terms"]]
-        static.append({**task, "terms": terms})
+        static.append({**task, "offsets": [offset for _, offset in task["terms"]]})
     shapes = [(n, task["rows"]) for task in tasks for n in task["splits"]]
     size = sum(n * G * rows * LANES * 8 for n, rows in shapes) + sum(a.size * 4 for a in arrays)
     outs = pl.pallas_call(
@@ -303,9 +298,11 @@
 
 
 def parity_kernel(start, rows, coeff, sums, old, *refs):
-    out, near_sums, near_old, fresh, in_sems, out_sems = refs[-6:]
+    out, near_coeff, near_sums, near_old, fresh, coeff_sem, in_sems, out_sems = refs[-8:]
     size = rows // 2
     loads, stores = [], []
+    coeff_load = pltpu.make_async_copy(coeff, near_coeff, coeff_sem)
+    coeff_load.start()
     for n in range(2):
         mine, whole = pl.ds(n * size, size), pl.ds(start + n * size, size)
         loads.append(
@@ -318,6 +315,7 @@
         )
         for load in loads[n]:
             load.start()
+    coeff_load.wait()
     for n in range(2):
         mine, whole = pl.ds(n * size, size), pl.ds(start + n * size, size)
         for load in loads[n]:
@@ -327,7 +325,7 @@
             values = adam_step(near_sums[g, mine], *[near_old[g, s, mine] for s in range(3)])
             for s, value in enumerate(values):
                 for k in range(2):
-                    term = coeff[k, g] * value
+                    term = near_coeff[pl.ds(k * G + g, 1)] * value
                     totals[s][k] = term if g == 0 else totals[s][k] + term
         for s in range(3):
             for k in range(2):
@@ -343,14 +341,16 @@
     return pl.pallas_call(
         functools.partial(parity_kernel, start, rows),
         grid_spec=pltpu.PrefetchScalarGridSpec(
-            num_scalar_prefetch=1,
+            num_scalar_prefetch=0,
             grid=(),
-            in_specs=[pl.BlockSpec(memory_space=pl.ANY)] * (2 + len(held)),
+            in_specs=[pl.BlockSpec(memory_space=pl.ANY)] * (3 + len(held)),
             out_specs=pl.BlockSpec(memory_space=pl.ANY),
             scratch_shapes=[
+                pltpu.VMEM((2 * G, LANES), jnp.float32),
                 pltpu.VMEM((G, rows, LANES), jnp.float32),
                 pltpu.VMEM((G, 3, rows, LANES), jnp.float32),
                 pltpu.VMEM((3, rows, 2, LANES), jnp.float32),
+                pltpu.SemaphoreType.DMA,
                 pltpu.SemaphoreType.DMA((2, 2)),
                 pltpu.SemaphoreType.DMA((2,)),
             ],
@@ -370,17 +370,15 @@
     state = [a.reshape(G, ROWS, LANES) for a in (master_weights, first_moment, second_moment)]
     points = cauchy_points.astype(jnp.float32)
     coeff = 1.0 / (points[:2][:, None] + points[2:][None, :])
-
+    coeff = jnp.broadcast_to(coeff.reshape(2 * G, 1), (2 * G, LANES))
     grad = grad_parts.reshape(X * Y * C * G, 1, ROWS * LANES)
-    blocks = jnp.zeros((1,), jnp.int32)
+    nothing = jnp.zeros((1,), jnp.int32)
     half = X * Y // 2
-    got, across, hop, totals, ordered, sums = {}, {}, {}, {}, {}, {}
+    got, hop, totals, ordered, sums = {}, {}, {}, {}, {}
     olds, done, shards, token = None, None, None, ()
 
-    def task(n, own, first, splits, terms, part=None, far=False):
-        start, rows, _ = CHUNKS[n]
-        if part:
-            start, rows = start + part[0], part[1]
+    def task(n, own, first, splits, terms, far=False):
+        start, rows = CHUNKS[n]
         return dict(own=own, first=first, start=start, rows=rows, splits=splits, terms=terms, far=far)
 
     def send(value, name, n, pairs):
@@ -389,7 +387,7 @@
 
     def run(*jobs, wait=()):
         nonlocal token
-        order = after(blocks, *token, *wait)
+        order = after(nothing, *token, *wait)
         name = "_".join(f"{job[2]}{job[3]}" for job in jobs)
         results = combine(grad, order, [job[0] for job in jobs], name)
         token = (results[0][0],)
@@ -400,59 +398,43 @@
         nonlocal token
         token = values
 
-    def swap_core(n, first, splits, part=None):
+    def swap_core(n, first, splits):
         def use(*sent):
             at = first
             for a in sent:
-                got.setdefault((n, part), []).append((at, send(a, "core", n, CORE_SWAP)))
+                got.setdefault(n, []).append((at, send(a, "core", n, CORE_SWAP)))
                 at += a.shape[0]
 
-        return task(n, False, first, splits, [], part), use, "core", n
-
-    def terms_at(n, first, count, part=None):
-        held = got[n, part] + (across[n] if CHUNKS[n][2] else [])
-        return [((a,), first - at) for at, a in held if first < at + a.shape[0] and at < first + count]
-
-    def x_sum(n):
-        def use(*sent):
-            across[n] = [(half + 2 * i, send(a, "cross", n, X_SWAP)) for i, a in enumerate(sent)]
-
-        terms = [((a,), -at) for at, a in got[n, None] if at < half]
-        return task(n, True, 0, (2, 2), terms), use, "cross", n
-
-    def far(n, part=None):
-        first, size = (half, 1) if CHUNKS[n][2] else (0, X)
-
+        return task(n, False, first, splits, []), use, "core", n
+
+    def terms_at(n, first, count):
+        return [(a, first - at) for at, a in got[n] if first < at + a.shape[0] and at < first + count]
+
+    def far(n):
         def use(block):
-            hop[n, 0] = hop.get((n, 0), ()) + (send(block, "far", n, Y_ON),)
-
-        return task(n, True, first, (size,), terms_at(n, first, size, part), part), use, "far", n
+            hop[n, 0] = send(block, "far", n, Y_ON)
+
+        return task(n, True, 0, (X,), terms_at(n, 0, X)), use, "far", n
 
     def near(n):
-        first, size = (half + 1, 1) if CHUNKS[n][2] else (X, X)
-
         def use(block):
-            hop[n, 1] = (send(block, "near", n, Y_BACK),)
-
-        return task(n, True, first, (size,), terms_at(n, first, size)), use, "near", n
+            hop[n, 1] = send(block, "near", n, Y_BACK)
+
+        return task(n, True, X, (X,), terms_at(n, X, X)), use, "near", n
 
     def ahead(n):
-        first, size = (half + 2, 1) if CHUNKS[n][2] else (half, X)
-
         def use(block):
-            hop[n, 2] = (send(block, "ahead", n, Y_ON),)
-
-        terms = terms_at(n, first, size) + [(hop[n, 0], 0)]
-        return task(n, True, first, (size,), terms), use, "ahead", n
+            hop[n, 2] = send(block, "ahead", n, Y_ON)
+
+        terms = terms_at(n, half, X) + [(hop[n, 0], 0)]
+        return task(n, True, half, (X,), terms), use, "ahead", n
 
     def here(n, from_hbm=False):
-        first, splits = (half + 3, (1,)) if CHUNKS[n][2] else (half + X, (1, 1))
-
-        def use(own, *block):
-            totals[n] = [own] + [send(b, "swap", n, X_SWAP) for b in block]
-
-        terms = terms_at(n, first, len(splits)) + [(hop[n, 2], 0), (hop[n, 1], 0)]
-        return task(n, True, first, splits, terms, far=from_hbm), use, "here", n
+        def use(own, block):
+            totals[n] = [own, send(block, "swap", n, X_SWAP)]
+
+        terms = terms_at(n, half + X, X) + [(hop[n, 2], 0), (hop[n, 1], 0)]
+        return task(n, True, half + X, (1, 1), terms, far=from_hbm), use, "here", n
 
     def place(n):
         (group,) = [g for g in GROUPS if n in g]
@@ -472,7 +454,7 @@
     def update(n):
         nonlocal done
         group, first, _ = place(n)
-        start, rows, _ = CHUNKS[n]
+        start, rows = CHUNKS[n]
         done = adam(ordered[group], state, done, after(holder, *token), first, start, rows)
         then(done[0])
 
@@ -492,7 +474,7 @@
     run(near(0), swap_core(0, 4, (1, 1, 1, 1)))
     run(swap_core(1, 0, (1, 1, 1, 1)), swap_core(1, 4, (1, 1, 1, 1)))
     run(ahead(0))
-    run(far(1), wait=hop[0, 1])
+    run(far(1), wait=(hop[0, 1],))
     run(near(1))
     run(here(0))
     run(ahead(1))

time: 117 us -> 117 us (level)
  transfers between devices with their start and end apart: 27 -> 27, of which waited for: 7 -> 7; matrix products, arithmetic and copies ran while one was open for 0% -> 0% of each run, Pallas kernels for 33% -> 32%
where the time goes in v7:
time: 117 us; the launch traced here: 116 us
  waiting for transfers between devices  42.1 us (36%)
  Pallas kernels  40.4 us (35%)
  starting transfers between devices  32 us (27%)
    ppermute x24, waiting for transfers between devices, send(): return lax.ppermute(value, 'dp', pairs)  40.4 us
    pallas_call x11, Pallas kernels, combine(): pl.pallas_call(functools.partial(combine_kernel, static), grid_spec=pltpu...  24.1 us
    ppermute x24, starting transfers between devices, send(): return lax.ppermute(value, 'dp', pairs)  14.9 us
    all_to_all x2, starting transfers between devices, to_holders(): sums[group] = lax.all_to_all(ordered[group], 'group', 0, 0)  10.8 us
    pallas_call x2, Pallas kernels, adam(): pl.pallas_call(functools.partial(adam_kernel, first, rows, start), grid_s...  6.78 us
    all_to_all x1, starting transfers between devices, per_device(): olds = lax.all_to_all(old, 'group', 0, 0)  6.34 us
    pallas_call x2, Pallas kernels, parity(): pl.pallas_call(functools.partial(parity_kernel, start, rows), grid_spec=p...  4.3 us
    pallas_call x2, Pallas kernels, finish(): pl.pallas_call(functools.partial(finish_kernel, len(parts), first, rows),...  2.89 us
  transfers between devices with their start and end apart: 27, of which 7 were waited for; matrix products, arithmetic and copies ran while one was open for 0% of the time, Pallas kernels for 32%

profile of v7, /device:TPU:24, one launch (start us, length us, event | category | flops | bytes accessed | tf_op | source)
XLA Modules:
  0.0 115.9 jit_solution(585940159096896054)
XLA Ops:
  0.6 1.4 %core0.2 = (f32[1,8,160,128]{3,2,1,0:T(8,128)S(1)}, f32[1,8,160,128]{3,2,1,0:T(8,128)S(1)}) custom-call(s32[1]{0:T(128)} %constant.1.clone.1.order, bf16[128,1,32768]{2,1,0:T(2,128)(2,1)} %bitcast.26), custom_call_target="tpu_custom_call" | custom-call | bytes 640 | tf_op jit(solution)/shard_map/core0/pallas_call | solution.py:142
  2.6 2.4 %core0.3 = (f32[1,8,160,128]{3,2,1,0:T(8,128)}, f32[1,8,160,128]{3,2,1,0:T(8,128)}) custom-call(s32[1]{0:T(128)} %constant.1.clone.1.order, bf16[128,1,32768]{2,1,0:T(2,128)(2,1)} %bitcast.27), custom_call_target="tpu_custom_call" | custom-call | bytes 640 | tf_op jit(solution)/shard_map/core0/pallas_call | solution.py:142
  5.6 2.7 %far0.1 = f32[2,8,160,128]{3,2,1,0:T(8,128)} custom-call(s32[1]{0:T(128)} %constant.1.clone.1.order, bf16[128,1,32768]{2,1,0:T(2,128)(2,1)} %bitcast.28, f32[1,8,160,128]{3,2,1,0:T(8,128)S(1)} %collective-permute-done.refs_0_, f32[1,8,160,128]{3,2,1,0:T(8,128)S(1)} %collective-permute-done.1.refs_1_), custom_call_target="tpu_custom_call" | custom-call | bytes 960 | tf_op jit(solution)/shard_map/far0/pallas_call | solution.py:142
  8.6 2.4 %order.1 = f32[8,3,256,128]{3,2,1,0:T(8,128)} custom-call(s32[8]{0:T(128)S(1)} %bitcast.21, f32[8,256,128]{2,1,0:T(8,128)S(1)} %bitcast.14, f32[8,256,128]{2,1,0:T(8,128)S(1)} %bitcast.17, f32[8,256,128]{2,1,0:T(8,128)S(1)} %bitcast.20), custom_call_target="tpu_custom_call" | custom-call | bytes 1536 | tf_op jit(solution)/shard_map/order/pallas_call | solution.py:177
  11.0 6.3 %all-to-all-start.1 = ((f32[8,3,256,128]{3,2,1,0:T(8,128)}), f32[8,3,256,128]{3,2,1,0:T(8,128)S(1)}, u32[]{:S(2)}, u32[]{:S(2)}) async-start(f32[8,3,256,128]{3,2,1,0:T(8,128)} %order.1), calls=%async_computation.1 | async-start | bytes 6291456 | tf_op jit(solution)/shard_map/all_to_all | solution.py:473
  17.3 3.5 %near0_core0.1 = (f32[2,8,160,128]{3,2,1,0:T(8,128)S(1)}, f32[1,8,160,128]{3,2,1,0:T(8,128)S(1)}, f32[1,8,160,128]{3,2,1,0:T(8,128)S(1)}, f32[1,8,160,128]{3,2,1,0:T(8,128)S(1)}, f32[1,8,160,128]{3,2,1,0:T(8,128)S(1)}) custom-call(s32[1]{0:T(128)} %constant.1.clone.1.order, bf16[128,1,32768]{2,1,0:T(2,128)(2,1)} %bitcast.29, ...), custom_call_target="tpu_custom_call" | custom-call | bytes 2240 | tf_op jit(solution)/shard_map/near0_core0/pallas_call | solution.py:142
  20.8 1.9 %collective-permute-start.7 = (f32[2,8,160,128]{3,2,1,0:T(8,128)S(1)}, f32[2,8,160,128]{3,2,1,0:T(8,128)S(1)}, u32[]{:S(2)}, u32[]{:S(2)}) collective-permute-start(f32[2,8,160,128]{3,2,1,0:T(8,128)S(1)} %get-tuple-element.56), channel_id=1, source_target_pairs={{0,48},{8,24},{16,0},{24,40},{32,16},{40,56},{48,32},{56,8},{64,11... | collective-permute-start | bytes 3932168 | tf_op jit(solution)/shard_map/near_0/ppermute | solution.py:386
  23.2 2.6 %core1_core1.1 = (f32[1,8,96,128]{3,2,1,0:T(8,128)S(1)}, f32[1,8,96,128]{3,2,1,0:T(8,128)S(1)}, f32[1,8,96,128]{3,2,1,0:T(8,128)S(1)}, f32[1,8,96,128]{3,2,1,0:T...) custom-call(s32[1]{0:T(128)} %constant.1.clone.1.order, ...), custom_call_target="tpu_custom_call" | custom-call | bytes 1536 | tf_op jit(solution)/shard_map/core1_core1/pallas_call | solution.py:142
  26.4 2.7 %collective-permute-done.6.refs_2_ = f32[2,8,160,128]{3,2,1,0:T(8,128)} collective-permute-done((f32[2,8,160,128]{3,2,1,0:T(8,128)}, f32[2,8,160,128]{3,2,1,0:T(8,128)}, u32[]{:S(2)}, u32[]{:S(2)}) %collective-permute-start.6) | collective-permute-done | bytes 1310752 | tf_op jit(solution)/shard_map/far_0/ppermute | solution.py:386
  29.0 2.8 %ahead0.1 = f32[2,8,160,128]{3,2,1,0:T(8,128)S(1)} custom-call(s32[1]{0:T(128)} %constant.1.clone.1.order, bf16[128,1,32768]{2,1,0:T(2,128)(2,1)} %bitcast.31, f32[1,8,160,128]{3,2,1,0:T(8,128)S(1)} %collective-permute-done.4.refs_0_, f32[1,8,160,128]{3,2,1,0:T(8,128)S(1)} %collective-permute-done.5.refs_1_, f32[2,8,160,128]{3,2,1,0:T(8,128)} %collective-permute-done.6.refs_2_), custom_call_target="tpu_custom_call" | custom-call | bytes 1280 | tf_op jit(solution)/shard_map/ahead0/pallas_call | solution.py:142
  32.6 14.4 %collective-permute-done.7.refs_3_ = f32[2,8,160,128]{3,2,1,0:T(8,128)S(1)} collective-permute-done((f32[2,8,160,128]{3,2,1,0:T(8,128)S(1)}, f32[2,8,160,128]{3,2,1,0:T(8,128)S(1)}, u32[]{:S(2)}, u32[]{:S(2)}) %collective-permute-start.7) | collective-permute-done | bytes 1310752 | tf_op jit(solution)/shard_map/near_0/ppermute | solution.py:386
  47.0 1.2 %far1.1 = f32[2,8,96,128]{3,2,1,0:T(8,128)S(1)} custom-call(s32[1]{0:T(128)} %constant.1.clone.1.order, bf16[128,1,32768]{2,1,0:T(2,128)(2,1)} %bitcast.32, f32[1,8,96,128]{3,2,1,0:T(8,128)S(1)} %collective-permute-done.8.refs_0_, f32[1,8,96,128]{3,2,1,0:T(8,128)S(1)} %collective-permute-done.9.refs_1_), custom_call_target="tpu_custom_call" | custom-call | bytes 576 | tf_op jit(solution)/shard_map/far1/pallas_call | solution.py:142
  49.6 2.1 %near1.1 = f32[2,8,96,128]{3,2,1,0:T(8,128)} custom-call(s32[1]{0:T(128)} %constant.1.clone.1.order, bf16[128,1,32768]{2,1,0:T(2,128)(2,1)} %bitcast.33, f32[1,8,96,128]{3,2,1,0:T(8,128)S(1)} %collective-permute-done.10.refs_0_, f32[1,8,96,128]{3,2,1,0:T(8,128)S(1)} %collective-permute-done.11.refs_1_), custom_call_target="tpu_custom_call" | custom-call | bytes 576 | tf_op jit(solution)/shard_map/near1/pallas_call | solution.py:142
  51.6 2.7 %collective-permute-done.14.refs_2_ = f32[2,8,160,128]{3,2,1,0:T(8,128)S(1)} collective-permute-done((f32[2,8,160,128]{3,2,1,0:T(8,128)S(1)}, f32[2,8,160,128]{3,2,1,0:T(8,128)S(1)}, u32[]{:S(2)}, u32[]{:S(2)}) %collective-permute-start.14) | collective-permute-done | bytes 1310752 | tf_op jit(solution)/shard_map/ahead_0/ppermute | solution.py:386
  54.3 1.5 %here0.1 = (f32[1,8,160,128]{3,2,1,0:T(8,128)S(1)}, f32[1,8,160,128]{3,2,1,0:T(8,128)S(1)}) custom-call(s32[1]{0:T(128)} %constant.1.clone.1.order, bf16[128,1,32768]{2,1,0:T(2,128)(2,1)} %bitcast.34, f32[1,8,160,128]{3,2,1,0:T(8,128)S(1)} %collective-permute-done.12.refs_0_, f32[1,8,160,128]{3,2,1,0:T(8,128)S(1)} %collective-permute-done.13.refs_1_, ...), custom_call_target="tpu_custom_call" | custom-call | bytes 1600 | tf_op jit(solution)/shard_map/here0/pallas_call | solution.py:142
  55.8 3.1 %collective-permute-start.18 = (f32[1,8,160,128]{3,2,1,0:T(8,128)S(1)}, f32[1,8,160,128]{3,2,1,0:T(8,128)S(1)}, u32[]{:S(2)}, u32[]{:S(2)}) collective-permute-start(f32[1,8,160,128]{3,2,1,0:T(8,128)S(1)} %get-tuple-element.75), channel_id=1, source_target_pairs={{0,64},{8,72},{16,80},{24,88},{32,96},{40,104},{48,112},{56,120},{... | collective-permute-start | bytes 1966088 | tf_op jit(solution)/shard_map/swap_0/ppermute | solution.py:386
  59.7 4.0 %collective-permute-done.17.refs_2_ = f32[2,8,96,128]{3,2,1,0:T(8,128)S(1)} collective-permute-done((f32[2,8,96,128]{3,2,1,0:T(8,128)S(1)}, f32[2,8,96,128]{3,2,1,0:T(8,128)S(1)}, u32[]{:S(2)}, u32[]{:S(2)}) %collective-permute-start.17) | collective-permute-done | bytes 786464 | tf_op jit(solution)/shard_map/far_1/ppermute | solution.py:386
  63.7 2.1 %ahead1.1 = f32[2,8,96,128]{3,2,1,0:T(8,128)} custom-call(s32[1]{0:T(128)} %constant.1.clone.1.order, bf16[128,1,32768]{2,1,0:T(2,128)(2,1)} %bitcast.35, f32[1,8,96,128]{3,2,1,0:T(8,128)S(1)} %collective-permute-done.15.refs_0_, f32[1,8,96,128]{3,2,1,0:T(8,128)S(1)} %collective-permute-done.16.refs_1_, f32[2,8,96,128]{3,2,1,0:T(8,128)S(1)} %collective-permute-done.17.refs_2_), custom_call_target="tpu_custom_call" | custom-call | bytes 768 | tf_op jit(solution)/shard_map/ahead1/pallas_call | solution.py:142
  65.8 1.3 %collective-permute-start.21 = (f32[2,8,96,128]{3,2,1,0:T(8,128)}, f32[2,8,96,128]{3,2,1,0:T(8,128)}, u32[]{:S(2)}, u32[]{:S(2)}) collective-permute-start(f32[2,8,96,128]{3,2,1,0:T(8,128)} %ahead1.1), channel_id=1, source_target_pairs={{0,16},{8,56},{16,32},{24,8},{32,48},{40,24},{48,0},{56,40},{64,80... | collective-permute-start | bytes 2359304 | tf_op jit(solution)/shard_map/ahead_1/ppermute | solution.py:386
  67.5 6.8 %collective-permute-done.18.refs_1_ = f32[1,8,160,128]{3,2,1,0:T(8,128)S(1)} collective-permute-done((f32[1,8,160,128]{3,2,1,0:T(8,128)S(1)}, f32[1,8,160,128]{3,2,1,0:T(8,128)S(1)}, u32[]{:S(2)}, u32[]{:S(2)}) %collective-permute-start.18) | collective-permute-done | bytes 655392 | tf_op jit(solution)/shard_map/swap_0/ppermute | solution.py:386
  74.4 1.5 %finish.2.ordered = f32[8,160,128]{2,1,0:T(8,128)} custom-call(s32[8]{0:T(128)S(1)} %bitcast.22, f32[1,8,160,128]{3,2,1,0:T(8,128)S(1)} %get-tuple-element.70.refs_0_, f32[1,8,160,128]{3,2,1,0:T(8,128)S(1)} %collective-permute-done.18.refs_1_), custom_call_target="tpu_custom_call" | custom-call | bytes 640 | tf_op jit(solution)/shard_map/finish/pallas_call | solution.py:213
  75.9 6.0 %all-to-all-start = ((f32[8,160,128]{2,1,0:T(8,128)}), f32[8,160,128]{2,1,0:T(8,128)}, u32[]{:S(2)}, u32[]{:S(2)}) async-start(f32[8,160,128]{2,1,0:T(8,128)} %finish.2.ordered), calls=%async_computation | async-start | bytes 1310720 | tf_op jit(solution)/shard_map/all_to_all | solution.py:452
  81.9 2.0 %here1.1 = (f32[1,8,96,128]{3,2,1,0:T(8,128)S(1)}, f32[1,8,96,128]{3,2,1,0:T(8,128)S(1)}) custom-call(s32[1]{0:T(128)} %constant.1.clone.1.order, bf16[128,1,32768]{2,1,0:T(2,128)(2,1)} %bitcast.36, f32[1,8,96,128]{3,2,1,0:T(8,128)} %collective-permute-done.19.refs_0_, f32[1,8,96,128]{3,2,1,0:T(8,128)} %collective-permute-done.20.refs_1_, ...), custom_call_target="tpu_custom_call" | custom-call | bytes 960 | tf_op jit(solution)/shard_map/here1/pallas_call | solution.py:142
  83.9 2.8 %collective-permute-start.23 = (f32[1,8,96,128]{3,2,1,0:T(8,128)S(1)}, f32[1,8,96,128]{3,2,1,0:T(8,128)S(1)}, u32[]{:S(2)}, u32[]{:S(2)}) collective-permute-start(f32[1,8,96,128]{3,2,1,0:T(8,128)S(1)} %get-tuple-element.83), channel_id=1, source_target_pairs={{0,64},{8,72},{16,80},{24,88},{32,96},{40,104},{48,112},{56,120},{... | collective-permute-start | bytes 1179656 | tf_op jit(solution)/shard_map/swap_1/ppermute | solution.py:386
  86.7 3.6 %adam.2 = (f32[8,256,128]{2,1,0:T(8,128)}, f32[8,256,128]{2,1,0:T(8,128)}, f32[8,256,128]{2,1,0:T(8,128)}) custom-call(s32[8]{0:T(128)S(1)} %bitcast.23, f32[8,160,128]{2,1,0:T(8,128)} %finish.2.ordered, f32[8,256,128]{2,1,0:T(8,128)} %bitcast.12, f32[8,256,128]{2,1,0:T(8,128)} %bitcast.15, f32[8,256,128]{2,1,0:T(8,128)} %bitcast.18), custom_call_target="tpu_custom_call" | custom-call | bytes 1120 | tf_op jit(solution)/shard_map/adam/pallas_call | solution.py:276
  90.4 9.7 %collective-permute-done.23.refs_1_ = f32[1,8,96,128]{3,2,1,0:T(8,128)S(1)} collective-permute-done((f32[1,8,96,128]{3,2,1,0:T(8,128)S(1)}, f32[1,8,96,128]{3,2,1,0:T(8,128)S(1)}, u32[]{:S(2)}, u32[]{:S(2)}) %collective-permute-start.23) | collective-permute-done | bytes 393248 | tf_op jit(solution)/shard_map/swap_1/ppermute | solution.py:386
  100.1 1.4 %finish.3.ordered = f32[8,96,128]{2,1,0:T(8,128)} custom-call(s32[8]{0:T(128)S(1)} %bitcast.24, f32[1,8,96,128]{3,2,1,0:T(8,128)S(1)} %get-tuple-element.79.refs_0_, f32[1,8,96,128]{3,2,1,0:T(8,128)S(1)} %collective-permute-done.23.refs_1_), custom_call_target="tpu_custom_call" | custom-call | bytes 384 | tf_op jit(solution)/shard_map/finish/pallas_call | solution.py:213
  101.5 4.8 %all-to-all-start.2 = ((f32[8,96,128]{2,1,0:T(8,128)}), f32[8,96,128]{2,1,0:T(8,128)S(1)}, u32[]{:S(2)}, u32[]{:S(2)}) async-start(f32[8,96,128]{2,1,0:T(8,128)} %finish.3.ordered), calls=%async_computation.2 | async-start | bytes 786432 | tf_op jit(solution)/shard_map/all_to_all | solution.py:452
  106.6 2.8 %parity.2.refs_0_ = f32[3,256,2,128]{3,2,1,0:T(2,128)} custom-call(f32[16,128]{1,0:T(8,128)S(1)} %broadcast_in_dim.2.coeff, f32[8,160,128]{2,1,0:T(8,128)} %all-to-all-done.sums, f32[8,3,256,128]{3,2,1,0:T(8,128)S(1)} %all-to-all-done.1.old), custom_call_target="tpu_custom_call" | custom-call | bytes 640 | tf_op jit(solution)/shard_map/parity/pallas_call | solution.py:341
  109.4 3.1 %adam.3 = (f32[8,256,128]{2,1,0:T(8,128)}, f32[8,256,128]{2,1,0:T(8,128)}, f32[8,256,128]{2,1,0:T(8,128)}) custom-call(s32[8]{0:T(128)S(1)} %bitcast.25, f32[8,96,128]{2,1,0:T(8,128)} %finish.3.ordered, f32[8,256,128]{2,1,0:T(8,128)} %bitcast.13, f32[8,256,128]{2,1,0:T(8,128)} %bitcast.16, ...), custom_call_target="tpu_custom_call", output_to_operand_aliasing={{0}: (5, {}), {1}: (6, {}), {2}: (7, {})} | custom-call | bytes 672 | tf_op jit(solution)/shard_map/adam/pallas_call | solution.py:276
  112.6 1.7 %all-to-all-done.2.sums = f32[8,96,128]{2,1,0:T(8,128)S(1)} async-done(((f32[8,96,128]{2,1,0:T(8,128)}), f32[8,96,128]{2,1,0:T(8,128)S(1)}, u32[]{:S(2)}, u32[]{:S(2)}) %all-to-all-start.2) | async-done | bytes 393248 | tf_op jit(solution)/shard_map/all_to_all | solution.py:452
  114.3 1.5 %parity.3 = f32[3,256,2,128]{3,2,1,0:T(2,128)} custom-call(f32[16,128]{1,0:T(8,128)S(1)} %broadcast_in_dim.2.coeff, f32[8,96,128]{2,1,0:T(8,128)S(1)} %all-to-all-done.2.sums, f32[8,3,256,128]{3,2,1,0:T(8,128)S(1)} %all-to-all-done.1.old, f32[3,256,2,128]{3,2,1,0:T(2,128)} %parity.2.refs_0_), custom_call_target="tpu_custom_call", output_to_operand_aliasing={{}: (3, {})} | custom-call | bytes 384 | tf_op jit(solution)/shard_map/parity/pallas_call | solution.py:341
  (55 shorter events, 6.1 us)
Async XLA Ops:
  2.0 3.6 %collective-permute-start.1 = (f32[1,8,160,128]{3,2,1,0:T(8,128)S(1)}, f32[1,8,160,128]{3,2,1,0:T(8,128)S(1)}, u32[]{:S(2)}, u32[]{:S(2)}) collective-permute-start(f32[1,8,160,128]{3,2,1,0:T(8,128)S(1)} %get-tuple-element.52), channel_id=1, source_target_pairs={{0,8},{8,0},{16,24},{24,16},{32,40},{40,32},{48,56},{56,48},{64,72... | collective-permute-start | bytes 1966088 | tf_op jit(solution)/shard_map/core_0/ppermute | solution.py:386
  2.1 3.5 %collective-permute-start = (f32[1,8,160,128]{3,2,1,0:T(8,128)S(1)}, f32[1,8,160,128]{3,2,1,0:T(8,128)S(1)}, u32[]{:S(2)}, u32[]{:S(2)}) collective-permute-start(f32[1,8,160,128]{3,2,1,0:T(8,128)S(1)} %get-tuple-element.48), channel_id=1, source_target_pairs={{0,8},{8,0},{16,24},{24,16},{32,40},{40,32},{48,56},{56,48},{64,72... | collective-permute-start | bytes 1966088 | tf_op jit(solution)/shard_map/core_0/ppermute | solution.py:386
  5.0 12.4 %collective-permute-start.3 = (f32[1,8,160,128]{3,2,1,0:T(8,128)}, f32[1,8,160,128]{3,2,1,0:T(8,128)}, u32[]{:S(2)}, u32[]{:S(2)}) collective-permute-start(f32[1,8,160,128]{3,2,1,0:T(8,128)} %get-tuple-element.55), channel_id=1, source_target_pairs={{0,8},{8,0},{16,24},{24,16},{32,40},{40,32},{48,56},{56,48},{64,72... | collective-permute-start | bytes 1966088 | tf_op jit(solution)/shard_map/core_0/ppermute | solution.py:386
  5.1 3.4 %copy-start = (f32[1,262144]{1,0:T(1,128)S(1)}, f32[1,262144]{1,0:T(1,128)}, u32[]{:S(2)}) copy-start(f32[1,262144]{1,0:T(1,128)} %param.7) | copy-start | bytes 3145732
  5.1 3.4 %copy-start.1 = (f32[1,262144]{1,0:T(1,128)S(1)}, f32[1,262144]{1,0:T(1,128)}, u32[]{:S(2)}) copy-start(f32[1,262144]{1,0:T(1,128)} %param.8) | copy-start | bytes 3145732
  5.1 3.4 %copy-start.2 = (f32[1,262144]{1,0:T(1,128)S(1)}, f32[1,262144]{1,0:T(1,128)}, u32[]{:S(2)}) copy-start(f32[1,262144]{1,0:T(1,128)} %param.9) | copy-start | bytes 3145732
  5.1 3.4 %copy-start.3 = (s32[1,8]{1,0:T(1,128)S(1)}, s32[1,8]{1,0:T(1,128)}, u32[]{:S(2)}) copy-start(s32[1,8]{1,0:T(1,128)} %param.11) | copy-start | bytes 100
  5.1 12.2 %collective-permute-start.2 = (f32[1,8,160,128]{3,2,1,0:T(8,128)}, f32[1,8,160,128]{3,2,1,0:T(8,128)}, u32[]{:S(2)}, u32[]{:S(2)}) collective-permute-start(f32[1,8,160,128]{3,2,1,0:T(8,128)} %get-tuple-element.50), channel_id=1, source_target_pairs={{0,8},{8,0},{16,24},{24,16},{32,40},{40,32},{48,56},{56,48},{64,72... | collective-permute-start | bytes 1966088 | tf_op jit(solution)/shard_map/core_0/ppermute | solution.py:386
  8.4 20.7 %collective-permute-start.6 = (f32[2,8,160,128]{3,2,1,0:T(8,128)}, f32[2,8,160,128]{3,2,1,0:T(8,128)}, u32[]{:S(2)}, u32[]{:S(2)}) collective-permute-start(f32[2,8,160,128]{3,2,1,0:T(8,128)} %far0.1), channel_id=1, source_target_pairs={{0,16},{8,56},{16,32},{24,8},{32,48},{40,24},{48,0},{56,40},{64,80... | collective-permute-start | bytes 3932168 | tf_op jit(solution)/shard_map/far_0/ppermute | solution.py:386
  11.0 64.9 %all-to-all-start.1 = ((f32[8,3,256,128]{3,2,1,0:T(8,128)}), f32[8,3,256,128]{3,2,1,0:T(8,128)S(1)}, u32[]{:S(2)}, u32[]{:S(2)}) async-start(f32[8,3,256,128]{3,2,1,0:T(8,128)} %order.1), calls=%async_computation.1 | async-start | bytes 6291456 | tf_op jit(solution)/shard_map/all_to_all | solution.py:473
  20.8 26.2 %collective-permute-start.7 = (f32[2,8,160,128]{3,2,1,0:T(8,128)S(1)}, f32[2,8,160,128]{3,2,1,0:T(8,128)S(1)}, u32[]{:S(2)}, u32[]{:S(2)}) collective-permute-start(f32[2,8,160,128]{3,2,1,0:T(8,128)S(1)} %get-tuple-element.56), channel_id=1, source_target_pairs={{0,48},{8,24},{16,0},{24,40},{32,16},{40,56},{48,32},{56,8},{64,11... | collective-permute-start | bytes 3932168 | tf_op jit(solution)/shard_map/near_0/ppermute | solution.py:386
  22.7 3.6 %collective-permute-start.4 = (f32[1,8,160,128]{3,2,1,0:T(8,128)S(1)}, f32[1,8,160,128]{3,2,1,0:T(8,128)S(1)}, u32[]{:S(2)}, u32[]{:S(2)}) collective-permute-start(f32[1,8,160,128]{3,2,1,0:T(8,128)S(1)} %get-tuple-element.60), channel_id=1, source_target_pairs={{0,8},{8,0},{16,24},{24,16},{32,40},{40,32},{48,56},{56,48},{64,72... | collective-permute-start | bytes 1966088 | tf_op jit(solution)/shard_map/core_0/ppermute | solution.py:386
  23.1 3.2 %collective-permute-start.5 = (f32[1,8,160,128]{3,2,1,0:T(8,128)S(1)}, f32[1,8,160,128]{3,2,1,0:T(8,128)S(1)}, u32[]{:S(2)}, u32[]{:S(2)}) collective-permute-start(f32[1,8,160,128]{3,2,1,0:T(8,128)S(1)} %get-tuple-element.61), channel_id=1, source_target_pairs={{0,8},{8,0},{16,24},{24,16},{32,40},{40,32},{48,56},{56,48},{64,72... | collective-permute-start | bytes 1966088 | tf_op jit(solution)/shard_map/core_0/ppermute | solution.py:386
  25.9 6.6 %collective-permute-start.9 = (f32[1,8,96,128]{3,2,1,0:T(8,128)S(1)}, f32[1,8,96,128]{3,2,1,0:T(8,128)S(1)}, u32[]{:S(2)}, u32[]{:S(2)}) collective-permute-start(f32[1,8,96,128]{3,2,1,0:T(8,128)S(1)} %get-tuple-element.63), channel_id=1, source_target_pairs={{0,8},{8,0},{16,24},{24,16},{32,40},{40,32},{48,56},{56,48},{64,72... | collective-permute-start | bytes 1179656 | tf_op jit(solution)/shard_map/core_1/ppermute | solution.py:386
  31.8 22.5 %collective-permute-start.14 = (f32[2,8,160,128]{3,2,1,0:T(8,128)S(1)}, f32[2,8,160,128]{3,2,1,0:T(8,128)S(1)}, u32[]{:S(2)}, u32[]{:S(2)}) collective-permute-start(f32[2,8,160,128]{3,2,1,0:T(8,128)S(1)} %ahead0.1), channel_id=1, source_target_pairs={{0,16},{8,56},{16,32},{24,8},{32,48},{40,24},{48,0},{56,40},{64,80... | collective-permute-start | bytes 3932168 | tf_op jit(solution)/shard_map/ahead_0/ppermute | solution.py:386
  31.9 15.1 %collective-permute-start.8 = (f32[1,8,96,128]{3,2,1,0:T(8,128)S(1)}, f32[1,8,96,128]{3,2,1,0:T(8,128)S(1)}, u32[]{:S(2)}, u32[]{:S(2)}) collective-permute-start(f32[1,8,96,128]{3,2,1,0:T(8,128)S(1)} %get-tuple-element.58), channel_id=1, source_target_pairs={{0,8},{8,0},{16,24},{24,16},{32,40},{40,32},{48,56},{56,48},{64,72... | collective-permute-start | bytes 1179656 | tf_op jit(solution)/shard_map/core_1/ppermute | solution.py:386
  32.0 16.3 %collective-permute-start.10 = (f32[1,8,96,128]{3,2,1,0:T(8,128)S(1)}, f32[1,8,96,128]{3,2,1,0:T(8,128)S(1)}, u32[]{:S(2)}, u32[]{:S(2)}) collective-permute-start(f32[1,8,96,128]{3,2,1,0:T(8,128)S(1)} %get-tuple-element.65), channel_id=1, source_target_pairs={{0,8},{8,0},{16,24},{24,16},{32,40},{40,32},{48,56},{56,48},{64,72... | collective-permute-start | bytes 1179656 | tf_op jit(solution)/shard_map/core_1/ppermute | solution.py:386
  32.5 16.6 %collective-permute-start.12 = (f32[1,8,160,128]{3,2,1,0:T(8,128)S(1)}, f32[1,8,160,128]{3,2,1,0:T(8,128)S(1)}, u32[]{:S(2)}, u32[]{:S(2)}) collective-permute-start(f32[1,8,160,128]{3,2,1,0:T(8,128)S(1)} %get-tuple-element.68), channel_id=1, source_target_pairs={{0,8},{8,0},{16,24},{24,16},{32,40},{40,32},{48,56},{56,48},{64,72... | collective-permute-start | bytes 1966088 | tf_op jit(solution)/shard_map/core_0/ppermute | solution.py:386
  47.0 2.0 %collective-permute-start.11 = (f32[1,8,96,128]{3,2,1,0:T(8,128)S(1)}, f32[1,8,96,128]{3,2,1,0:T(8,128)S(1)}, u32[]{:S(2)}, u32[]{:S(2)}) collective-permute-start(f32[1,8,96,128]{3,2,1,0:T(8,128)S(1)} %get-tuple-element.66), channel_id=1, source_target_pairs={{0,8},{8,0},{16,24},{24,16},{32,40},{40,32},{48,56},{56,48},{64,72... | collective-permute-start | bytes 1179656 | tf_op jit(solution)/shard_map/core_1/ppermute | solution.py:386
  48.2 15.5 %collective-permute-start.17 = (f32[2,8,96,128]{3,2,1,0:T(8,128)S(1)}, f32[2,8,96,128]{3,2,1,0:T(8,128)S(1)}, u32[]{:S(2)}, u32[]{:S(2)}) collective-permute-start(f32[2,8,96,128]{3,2,1,0:T(8,128)S(1)} %far1.1), channel_id=1, source_target_pairs={{0,16},{8,56},{16,32},{24,8},{32,48},{40,24},{48,0},{56,40},{64,80... | collective-permute-start | bytes 2359304 | tf_op jit(solution)/shard_map/far_1/ppermute | solution.py:386
  48.3 3.3 %collective-permute-start.13 = (f32[1,8,160,128]{3,2,1,0:T(8,128)S(1)}, f32[1,8,160,128]{3,2,1,0:T(8,128)S(1)}, u32[]{:S(2)}, u32[]{:S(2)}) collective-permute-start(f32[1,8,160,128]{3,2,1,0:T(8,128)S(1)} %get-tuple-element.69), channel_id=1, source_target_pairs={{0,8},{8,0},{16,24},{24,16},{32,40},{40,32},{48,56},{56,48},{64,72... | collective-permute-start | bytes 1966088 | tf_op jit(solution)/shard_map/core_0/ppermute | solution.py:386
  49.0 10.6 %collective-permute-start.15 = (f32[1,8,96,128]{3,2,1,0:T(8,128)S(1)}, f32[1,8,96,128]{3,2,1,0:T(8,128)S(1)}, u32[]{:S(2)}, u32[]{:S(2)}) collective-permute-start(f32[1,8,96,128]{3,2,1,0:T(8,128)S(1)} %get-tuple-element.72), channel_id=1, source_target_pairs={{0,8},{8,0},{16,24},{24,16},{32,40},{40,32},{48,56},{56,48},{64,72... | collective-permute-start | bytes 1179656 | tf_op jit(solution)/shard_map/core_1/ppermute | solution.py:386
  49.1 10.5 %collective-permute-start.16 = (f32[1,8,96,128]{3,2,1,0:T(8,128)S(1)}, f32[1,8,96,128]{3,2,1,0:T(8,128)S(1)}, u32[]{:S(2)}, u32[]{:S(2)}) collective-permute-start(f32[1,8,96,128]{3,2,1,0:T(8,128)S(1)} %get-tuple-element.73), channel_id=1, source_target_pairs={{0,8},{8,0},{16,24},{24,16},{32,40},{40,32},{48,56},{56,48},{64,72... | collective-permute-start | bytes 1179656 | tf_op jit(solution)/shard_map/core_1/ppermute | solution.py:386
  55.8 18.6 %collective-permute-start.18 = (f32[1,8,160,128]{3,2,1,0:T(8,128)S(1)}, f32[1,8,160,128]{3,2,1,0:T(8,128)S(1)}, u32[]{:S(2)}, u32[]{:S(2)}) collective-permute-start(f32[1,8,160,128]{3,2,1,0:T(8,128)S(1)} %get-tuple-element.75), channel_id=1, source_target_pairs={{0,64},{8,72},{16,80},{24,88},{32,96},{40,104},{48,112},{56,120},{... | collective-permute-start | bytes 1966088 | tf_op jit(solution)/shard_map/swap_0/ppermute | solution.py:386
  58.9 22.9 %collective-permute-start.22 = (f32[2,8,96,128]{3,2,1,0:T(8,128)}, f32[2,8,96,128]{3,2,1,0:T(8,128)}, u32[]{:S(2)}, u32[]{:S(2)}) collective-permute-start(f32[2,8,96,128]{3,2,1,0:T(8,128)} %near1.1), channel_id=1, source_target_pairs={{0,48},{8,24},{16,0},{24,40},{32,16},{40,56},{48,32},{56,8},{64,11... | collective-permute-start | bytes 2359304 | tf_op jit(solution)/shard_map/near_1/ppermute | solution.py:386
  65.8 16.1 %collective-permute-start.21 = (f32[2,8,96,128]{3,2,1,0:T(8,128)}, f32[2,8,96,128]{3,2,1,0:T(8,128)}, u32[]{:S(2)}, u32[]{:S(2)}) collective-permute-start(f32[2,8,96,128]{3,2,1,0:T(8,128)} %ahead1.1), channel_id=1, source_target_pairs={{0,16},{8,56},{16,32},{24,8},{32,48},{40,24},{48,0},{56,40},{64,80... | collective-permute-start | bytes 2359304 | tf_op jit(solution)/shard_map/ahead_1/ppermute | solution.py:386
  67.0 14.8 %collective-permute-start.19 = (f32[1,8,96,128]{3,2,1,0:T(8,128)}, f32[1,8,96,128]{3,2,1,0:T(8,128)}, u32[]{:S(2)}, u32[]{:S(2)}) collective-permute-start(f32[1,8,96,128]{3,2,1,0:T(8,128)} %get-tuple-element.77), channel_id=1, source_target_pairs={{0,8},{8,0},{16,24},{24,16},{32,40},{40,32},{48,56},{56,48},{64,72... | collective-permute-start | bytes 1179656 | tf_op jit(solution)/shard_map/core_1/ppermute | solution.py:386
  67.0 14.8 %collective-permute-start.20 = (f32[1,8,96,128]{3,2,1,0:T(8,128)S(1)}, f32[1,8,96,128]{3,2,1,0:T(8,128)}, u32[]{:S(2)}, u32[]{:S(2)}) collective-permute-start(f32[1,8,96,128]{3,2,1,0:T(8,128)S(1)} %get-tuple-element.78), channel_id=1, source_target_pairs={{0,8},{8,0},{16,24},{24,16},{32,40},{40,32},{48,56},{56,48},{64,72... | collective-permute-start | bytes 1179656 | tf_op jit(solution)/shard_map/core_1/ppermute | solution.py:386
  75.9 25.6 %all-to-all-start = ((f32[8,160,128]{2,1,0:T(8,128)}), f32[8,160,128]{2,1,0:T(8,128)}, u32[]{:S(2)}, u32[]{:S(2)}) async-start(f32[8,160,128]{2,1,0:T(8,128)} %finish.2.ordered), calls=%async_computation | async-start | bytes 1310720 | tf_op jit(solution)/shard_map/all_to_all | solution.py:452
  83.9 16.2 %collective-permute-start.23 = (f32[1,8,96,128]{3,2,1,0:T(8,128)S(1)}, f32[1,8,96,128]{3,2,1,0:T(8,128)S(1)}, u32[]{:S(2)}, u32[]{:S(2)}) collective-permute-start(f32[1,8,96,128]{3,2,1,0:T(8,128)S(1)} %get-tuple-element.83), channel_id=1, source_target_pairs={{0,64},{8,72},{16,80},{24,88},{32,96},{40,104},{48,112},{56,120},{... | collective-permute-start | bytes 1179656 | tf_op jit(solution)/shard_map/swap_1/ppermute | solution.py:386
  90.4 15.9 %copy-start.4 = (s32[10]{0:T(128)S(1)}, s32[10]{0:T(128)}, u32[]{:S(2)}) copy-start(s32[10]{0:T(128)} %param.10) | copy-start | bytes 124
  101.5 12.8 %all-to-all-start.2 = ((f32[8,96,128]{2,1,0:T(8,128)}), f32[8,96,128]{2,1,0:T(8,128)S(1)}, u32[]{:S(2)}, u32[]{:S(2)}) async-start(f32[8,96,128]{2,1,0:T(8,128)} %finish.3.ordered), calls=%async_computation.2 | async-start | bytes 786432 | tf_op jit(solution)/shard_map/all_to_all | solution.py:452

commit v8 on v7

--- a/solution.py
+++ b/solution.py
@@ -472,8 +472,8 @@
     then(old)
     olds = lax.all_to_all(old, 'group', 0, 0)
     run(near(0), swap_core(0, 4, (1, 1, 1, 1)))
+    run(ahead(0))
     run(swap_core(1, 0, (1, 1, 1, 1)), swap_core(1, 4, (1, 1, 1, 1)))
-    run(ahead(0))
     run(far(1), wait=(hop[0, 1],))
     run(near(1))
     run(here(0))

time: 117 us -> 117 us (level)
  transfers between devices with their start and end apart: 27 -> 27, of which waited for: 7 -> 9; matrix products, arithmetic and copies ran while one was open for 0% -> 0% of each run, Pallas kernels for 32% -> 32%
where the time goes in v8:
time: 117 us; the launch traced here: 116 us
  waiting for transfers between devices  42 us (36%)
  Pallas kernels  40.5 us (35%)
  starting transfers between devices  32 us (27%)
    ppermute x24, waiting for transfers between devices, send(): return lax.ppermute(value, 'dp', pairs)  40.3 us
    pallas_call x11, Pallas kernels, combine(): pl.pallas_call(functools.partial(combine_kernel, static), grid_spec=pltpu...  24.1 us
    ppermute x24, starting transfers between devices, send(): return lax.ppermute(value, 'dp', pairs)  14.9 us
    all_to_all x2, starting transfers between devices, to_holders(): sums[group] = lax.all_to_all(ordered[group], 'group', 0, 0)  10.8 us
    pallas_call x2, Pallas kernels, adam(): pl.pallas_call(functools.partial(adam_kernel, first, rows, start), grid_s...  6.78 us
    all_to_all x1, starting transfers between devices, per_device(): olds = lax.all_to_all(old, 'group', 0, 0)  6.34 us
    pallas_call x2, Pallas kernels, parity(): pl.pallas_call(functools.partial(parity_kernel, start, rows), grid_spec=p...  4.3 us
    pallas_call x2, Pallas kernels, finish(): pl.pallas_call(functools.partial(finish_kernel, len(parts), first, rows),...  2.89 us
  transfers between devices with their start and end apart: 27, of which 9 were waited for; matrix products, arithmetic and copies ran while one was open for 0% of the time, Pallas kernels for 32%

profile of v8, /device:TPU:24, one launch (start us, length us, event | category | flops | bytes accessed | tf_op | source)
XLA Modules:
  0.0 115.9 jit_solution(12433884237546655289)
XLA Ops:
  0.6 1.4 %core0.2 = (f32[1,8,160,128]{3,2,1,0:T(8,128)S(1)}, f32[1,8,160,128]{3,2,1,0:T(8,128)S(1)}) custom-call(s32[1]{0:T(128)} %constant.1.clone.1.order, bf16[128,1,32768]{2,1,0:T(2,128)(2,1)} %bitcast.26), custom_call_target="tpu_custom_call" | custom-call | bytes 640 | tf_op jit(solution)/shard_map/core0/pallas_call | solution.py:142
  2.6 2.4 %core0.3 = (f32[1,8,160,128]{3,2,1,0:T(8,128)}, f32[1,8,160,128]{3,2,1,0:T(8,128)}) custom-call(s32[1]{0:T(128)} %constant.1.clone.1.order, bf16[128,1,32768]{2,1,0:T(2,128)(2,1)} %bitcast.27), custom_call_target="tpu_custom_call" | custom-call | bytes 640 | tf_op jit(solution)/shard_map/core0/pallas_call | solution.py:142
  5.6 2.7 %far0.1 = f32[2,8,160,128]{3,2,1,0:T(8,128)} custom-call(s32[1]{0:T(128)} %constant.1.clone.1.order, bf16[128,1,32768]{2,1,0:T(2,128)(2,1)} %bitcast.28, f32[1,8,160,128]{3,2,1,0:T(8,128)S(1)} %collective-permute-done.refs_0_, f32[1,8,160,128]{3,2,1,0:T(8,128)S(1)} %collective-permute-done.1.refs_1_), custom_call_target="tpu_custom_call" | custom-call | bytes 960 | tf_op jit(solution)/shard_map/far0/pallas_call | solution.py:142
  8.6 2.4 %order.1 = f32[8,3,256,128]{3,2,1,0:T(8,128)} custom-call(s32[8]{0:T(128)S(1)} %bitcast.21, f32[8,256,128]{2,1,0:T(8,128)S(1)} %bitcast.14, f32[8,256,128]{2,1,0:T(8,128)S(1)} %bitcast.17, f32[8,256,128]{2,1,0:T(8,128)S(1)} %bitcast.20), custom_call_target="tpu_custom_call" | custom-call | bytes 1536 | tf_op jit(solution)/shard_map/order/pallas_call | solution.py:177
  11.0 6.3 %all-to-all-start.1 = ((f32[8,3,256,128]{3,2,1,0:T(8,128)}), f32[8,3,256,128]{3,2,1,0:T(8,128)S(1)}, u32[]{:S(2)}, u32[]{:S(2)}) async-start(f32[8,3,256,128]{3,2,1,0:T(8,128)} %order.1), calls=%async_computation.1 | async-start | bytes 6291456 | tf_op jit(solution)/shard_map/all_to_all | solution.py:473
  17.4 3.5 %near0_core0.1 = (f32[2,8,160,128]{3,2,1,0:T(8,128)S(1)}, f32[1,8,160,128]{3,2,1,0:T(8,128)S(1)}, f32[1,8,160,128]{3,2,1,0:T(8,128)S(1)}, f32[1,8,160,128]{3,2,1,0:T(8,128)S(1)}, f32[1,8,160,128]{3,2,1,0:T(8,128)S(1)}) custom-call(s32[1]{0:T(128)} %constant.1.clone.1.order, bf16[128,1,32768]{2,1,0:T(2,128)(2,1)} %bitcast.29, ...), custom_call_target="tpu_custom_call" | custom-call | bytes 2240 | tf_op jit(solution)/shard_map/near0_core0/pallas_call | solution.py:142
  20.9 1.9 %collective-permute-start.7 = (f32[2,8,160,128]{3,2,1,0:T(8,128)S(1)}, f32[2,8,160,128]{3,2,1,0:T(8,128)S(1)}, u32[]{:S(2)}, u32[]{:S(2)}) collective-permute-start(f32[2,8,160,128]{3,2,1,0:T(8,128)S(1)} %get-tuple-element.56), channel_id=1, source_target_pairs={{0,48},{8,24},{16,0},{24,40},{32,16},{40,56},{48,32},{56,8},{64,11... | collective-permute-start | bytes 3932168 | tf_op jit(solution)/shard_map/near_0/ppermute | solution.py:386
  23.6 1.2 %collective-permute-done.4.refs_0_ = f32[1,8,160,128]{3,2,1,0:T(8,128)S(1)} collective-permute-done((f32[1,8,160,128]{3,2,1,0:T(8,128)S(1)}, f32[1,8,160,128]{3,2,1,0:T(8,128)S(1)}, u32[]{:S(2)}, u32[]{:S(2)}) %collective-permute-start.4) | collective-permute-done | bytes 655392 | tf_op jit(solution)/shard_map/core_0/ppermute | solution.py:386
  25.8 3.3 %collective-permute-done.6.refs_2_ = f32[2,8,160,128]{3,2,1,0:T(8,128)} collective-permute-done((f32[2,8,160,128]{3,2,1,0:T(8,128)}, f32[2,8,160,128]{3,2,1,0:T(8,128)}, u32[]{:S(2)}, u32[]{:S(2)}) %collective-permute-start.6) | collective-permute-done | bytes 1310752 | tf_op jit(solution)/shard_map/far_0/ppermute | solution.py:386
  29.1 2.8 %ahead0.1 = f32[2,8,160,128]{3,2,1,0:T(8,128)S(1)} custom-call(s32[1]{0:T(128)} %constant.1.clone.1.order, bf16[128,1,32768]{2,1,0:T(2,128)(2,1)} %bitcast.30, f32[1,8,160,128]{3,2,1,0:T(8,128)S(1)} %collective-permute-done.4.refs_0_, f32[1,8,160,128]{3,2,1,0:T(8,128)S(1)} %collective-permute-done.5.refs_1_, f32[2,8,160,128]{3,2,1,0:T(8,128)} %collective-permute-done.6.refs_2_), custom_call_target="tpu_custom_call" | custom-call | bytes 1280 | tf_op jit(solution)/shard_map/ahead0/pallas_call | solution.py:142
  32.0 2.7 %core1_core1.1 = (f32[1,8,96,128]{3,2,1,0:T(8,128)S(1)}, f32[1,8,96,128]{3,2,1,0:T(8,128)S(1)}, f32[1,8,96,128]{3,2,1,0:T(8,128)S(1)}, f32[1,8,96,128]{3,2,1,0:T...) custom-call(s32[1]{0:T(128)} %constant.1.clone.1.order, ...), custom_call_target="tpu_custom_call" | custom-call | bytes 1536 | tf_op jit(solution)/shard_map/core1_core1/pallas_call | solution.py:142
  35.2 11.8 %collective-permute-done.7.refs_3_ = f32[2,8,160,128]{3,2,1,0:T(8,128)S(1)} collective-permute-done((f32[2,8,160,128]{3,2,1,0:T(8,128)S(1)}, f32[2,8,160,128]{3,2,1,0:T(8,128)S(1)}, u32[]{:S(2)}, u32[]{:S(2)}) %collective-permute-start.7) | collective-permute-done | bytes 1310752 | tf_op jit(solution)/shard_map/near_0/ppermute | solution.py:386
  49.9 2.1 %near1.1 = f32[2,8,96,128]{3,2,1,0:T(8,128)} custom-call(s32[1]{0:T(128)} %constant.1.clone.1.order, bf16[128,1,32768]{2,1,0:T(2,128)(2,1)} %bitcast.33, f32[1,8,96,128]{3,2,1,0:T(8,128)S(1)} %collective-permute-done.10.refs_0_, f32[1,8,96,128]{3,2,1,0:T(8,128)S(1)} %collective-permute-done.11.refs_1_), custom_call_target="tpu_custom_call" | custom-call | bytes 576 | tf_op jit(solution)/shard_map/near1/pallas_call | solution.py:142
  51.9 2.4 %collective-permute-done.14.refs_2_ = f32[2,8,160,128]{3,2,1,0:T(8,128)S(1)} collective-permute-done((f32[2,8,160,128]{3,2,1,0:T(8,128)S(1)}, f32[2,8,160,128]{3,2,1,0:T(8,128)S(1)}, u32[]{:S(2)}, u32[]{:S(2)}) %collective-permute-start.14) | collective-permute-done | bytes 1310752 | tf_op jit(solution)/shard_map/ahead_0/ppermute | solution.py:386
  54.3 1.5 %here0.1 = (f32[1,8,160,128]{3,2,1,0:T(8,128)S(1)}, f32[1,8,160,128]{3,2,1,0:T(8,128)S(1)}) custom-call(s32[1]{0:T(128)} %constant.1.clone.1.order, bf16[128,1,32768]{2,1,0:T(2,128)(2,1)} %bitcast.34, f32[1,8,160,128]{3,2,1,0:T(8,128)S(1)} %collective-permute-done.12.refs_0_, f32[1,8,160,128]{3,2,1,0:T(8,128)S(1)} %collective-permute-done.13.refs_1_, ...), custom_call_target="tpu_custom_call" | custom-call | bytes 1600 | tf_op jit(solution)/shard_map/here0/pallas_call | solution.py:142
  55.8 3.1 %collective-permute-start.18 = (f32[1,8,160,128]{3,2,1,0:T(8,128)S(1)}, f32[1,8,160,128]{3,2,1,0:T(8,128)S(1)}, u32[]{:S(2)}, u32[]{:S(2)}) collective-permute-start(f32[1,8,160,128]{3,2,1,0:T(8,128)S(1)} %get-tuple-element.75), channel_id=1, source_target_pairs={{0,64},{8,72},{16,80},{24,88},{32,96},{40,104},{48,112},{56,120},{... | collective-permute-start | bytes 1966088 | tf_op jit(solution)/shard_map/swap_0/ppermute | solution.py:386
  59.7 4.0 %collective-permute-done.17.refs_2_ = f32[2,8,96,128]{3,2,1,0:T(8,128)S(1)} collective-permute-done((f32[2,8,96,128]{3,2,1,0:T(8,128)S(1)}, f32[2,8,96,128]{3,2,1,0:T(8,128)S(1)}, u32[]{:S(2)}, u32[]{:S(2)}) %collective-permute-start.17) | collective-permute-done | bytes 786464 | tf_op jit(solution)/shard_map/far_1/ppermute | solution.py:386
  63.7 2.1 %ahead1.1 = f32[2,8,96,128]{3,2,1,0:T(8,128)} custom-call(s32[1]{0:T(128)} %constant.1.clone.1.order, bf16[128,1,32768]{2,1,0:T(2,128)(2,1)} %bitcast.35, f32[1,8,96,128]{3,2,1,0:T(8,128)S(1)} %collective-permute-done.15.refs_0_, f32[1,8,96,128]{3,2,1,0:T(8,128)S(1)} %collective-permute-done.16.refs_1_, f32[2,8,96,128]{3,2,1,0:T(8,128)S(1)} %collective-permute-done.17.refs_2_), custom_call_target="tpu_custom_call" | custom-call | bytes 768 | tf_op jit(solution)/shard_map/ahead1/pallas_call | solution.py:142
  65.8 1.3 %collective-permute-start.21 = (f32[2,8,96,128]{3,2,1,0:T(8,128)}, f32[2,8,96,128]{3,2,1,0:T(8,128)}, u32[]{:S(2)}, u32[]{:S(2)}) collective-permute-start(f32[2,8,96,128]{3,2,1,0:T(8,128)} %ahead1.1), channel_id=1, source_target_pairs={{0,16},{8,56},{16,32},{24,8},{32,48},{40,24},{48,0},{56,40},{64,80... | collective-permute-start | bytes 2359304 | tf_op jit(solution)/shard_map/ahead_1/ppermute | solution.py:386
  67.5 6.8 %collective-permute-done.18.refs_1_ = f32[1,8,160,128]{3,2,1,0:T(8,128)S(1)} collective-permute-done((f32[1,8,160,128]{3,2,1,0:T(8,128)S(1)}, f32[1,8,160,128]{3,2,1,0:T(8,128)S(1)}, u32[]{:S(2)}, u32[]{:S(2)}) %collective-permute-start.18) | collective-permute-done | bytes 655392 | tf_op jit(solution)/shard_map/swap_0/ppermute | solution.py:386
  74.4 1.5 %finish.2.ordered = f32[8,160,128]{2,1,0:T(8,128)} custom-call(s32[8]{0:T(128)S(1)} %bitcast.22, f32[1,8,160,128]{3,2,1,0:T(8,128)S(1)} %get-tuple-element.70.refs_0_, f32[1,8,160,128]{3,2,1,0:T(8,128)S(1)} %collective-permute-done.18.refs_1_), custom_call_target="tpu_custom_call" | custom-call | bytes 640 | tf_op jit(solution)/shard_map/finish/pallas_call | solution.py:213
  75.9 6.0 %all-to-all-start = ((f32[8,160,128]{2,1,0:T(8,128)}), f32[8,160,128]{2,1,0:T(8,128)}, u32[]{:S(2)}, u32[]{:S(2)}) async-start(f32[8,160,128]{2,1,0:T(8,128)} %finish.2.ordered), calls=%async_computation | async-start | bytes 1310720 | tf_op jit(solution)/shard_map/all_to_all | solution.py:452
  81.9 2.0 %here1.1 = (f32[1,8,96,128]{3,2,1,0:T(8,128)S(1)}, f32[1,8,96,128]{3,2,1,0:T(8,128)S(1)}) custom-call(s32[1]{0:T(128)} %constant.1.clone.1.order, bf16[128,1,32768]{2,1,0:T(2,128)(2,1)} %bitcast.36, f32[1,8,96,128]{3,2,1,0:T(8,128)} %collective-permute-done.19.refs_0_, f32[1,8,96,128]{3,2,1,0:T(8,128)} %collective-permute-done.20.refs_1_, ...), custom_call_target="tpu_custom_call" | custom-call | bytes 960 | tf_op jit(solution)/shard_map/here1/pallas_call | solution.py:142
  83.9 2.8 %collective-permute-start.23 = (f32[1,8,96,128]{3,2,1,0:T(8,128)S(1)}, f32[1,8,96,128]{3,2,1,0:T(8,128)S(1)}, u32[]{:S(2)}, u32[]{:S(2)}) collective-permute-start(f32[1,8,96,128]{3,2,1,0:T(8,128)S(1)} %get-tuple-element.83), channel_id=1, source_target_pairs={{0,64},{8,72},{16,80},{24,88},{32,96},{40,104},{48,112},{56,120},{... | collective-permute-start | bytes 1179656 | tf_op jit(solution)/shard_map/swap_1/ppermute | solution.py:386
  86.7 3.6 %adam.2 = (f32[8,256,128]{2,1,0:T(8,128)}, f32[8,256,128]{2,1,0:T(8,128)}, f32[8,256,128]{2,1,0:T(8,128)}) custom-call(s32[8]{0:T(128)S(1)} %bitcast.23, f32[8,160,128]{2,1,0:T(8,128)} %finish.2.ordered, f32[8,256,128]{2,1,0:T(8,128)} %bitcast.12, f32[8,256,128]{2,1,0:T(8,128)} %bitcast.15, f32[8,256,128]{2,1,0:T(8,128)} %bitcast.18), custom_call_target="tpu_custom_call" | custom-call | bytes 1120 | tf_op jit(solution)/shard_map/adam/pallas_call | solution.py:276
  90.4 9.7 %collective-permute-done.23.refs_1_ = f32[1,8,96,128]{3,2,1,0:T(8,128)S(1)} collective-permute-done((f32[1,8,96,128]{3,2,1,0:T(8,128)S(1)}, f32[1,8,96,128]{3,2,1,0:T(8,128)S(1)}, u32[]{:S(2)}, u32[]{:S(2)}) %collective-permute-start.23) | collective-permute-done | bytes 393248 | tf_op jit(solution)/shard_map/swap_1/ppermute | solution.py:386
  100.0 1.4 %finish.3.ordered = f32[8,96,128]{2,1,0:T(8,128)} custom-call(s32[8]{0:T(128)S(1)} %bitcast.24, f32[1,8,96,128]{3,2,1,0:T(8,128)S(1)} %get-tuple-element.79.refs_0_, f32[1,8,96,128]{3,2,1,0:T(8,128)S(1)} %collective-permute-done.23.refs_1_), custom_call_target="tpu_custom_call" | custom-call | bytes 384 | tf_op jit(solution)/shard_map/finish/pallas_call | solution.py:213
  101.5 4.8 %all-to-all-start.2 = ((f32[8,96,128]{2,1,0:T(8,128)}), f32[8,96,128]{2,1,0:T(8,128)S(1)}, u32[]{:S(2)}, u32[]{:S(2)}) async-start(f32[8,96,128]{2,1,0:T(8,128)} %finish.3.ordered), calls=%async_computation.2 | async-start | bytes 786432 | tf_op jit(solution)/shard_map/all_to_all | solution.py:452
  106.6 2.8 %parity.2.refs_0_ = f32[3,256,2,128]{3,2,1,0:T(2,128)} custom-call(f32[16,128]{1,0:T(8,128)S(1)} %broadcast_in_dim.2.coeff, f32[8,160,128]{2,1,0:T(8,128)} %all-to-all-done.sums, f32[8,3,256,128]{3,2,1,0:T(8,128)S(1)} %all-to-all-done.1.old), custom_call_target="tpu_custom_call" | custom-call | bytes 640 | tf_op jit(solution)/shard_map/parity/pallas_call | solution.py:341
  109.4 3.1 %adam.3 = (f32[8,256,128]{2,1,0:T(8,128)}, f32[8,256,128]{2,1,0:T(8,128)}, f32[8,256,128]{2,1,0:T(8,128)}) custom-call(s32[8]{0:T(128)S(1)} %bitcast.25, f32[8,96,128]{2,1,0:T(8,128)} %finish.3.ordered, f32[8,256,128]{2,1,0:T(8,128)} %bitcast.13, f32[8,256,128]{2,1,0:T(8,128)} %bitcast.16, ...), custom_call_target="tpu_custom_call", output_to_operand_aliasing={{0}: (5, {}), {1}: (6, {}), {2}: (7, {})} | custom-call | bytes 672 | tf_op jit(solution)/shard_map/adam/pallas_call | solution.py:276
  112.6 1.7 %all-to-all-done.2.sums = f32[8,96,128]{2,1,0:T(8,128)S(1)} async-done(((f32[8,96,128]{2,1,0:T(8,128)}), f32[8,96,128]{2,1,0:T(8,128)S(1)}, u32[]{:S(2)}, u32[]{:S(2)}) %all-to-all-start.2) | async-done | bytes 393248 | tf_op jit(solution)/shard_map/all_to_all | solution.py:452
  114.3 1.5 %parity.3 = f32[3,256,2,128]{3,2,1,0:T(2,128)} custom-call(f32[16,128]{1,0:T(8,128)S(1)} %broadcast_in_dim.2.coeff, f32[8,96,128]{2,1,0:T(8,128)S(1)} %all-to-all-done.2.sums, f32[8,3,256,128]{3,2,1,0:T(8,128)S(1)} %all-to-all-done.1.old, f32[3,256,2,128]{3,2,1,0:T(2,128)} %parity.2.refs_0_), custom_call_target="tpu_custom_call", output_to_operand_aliasing={{}: (3, {})} | custom-call | bytes 384 | tf_op jit(solution)/shard_map/parity/pallas_call | solution.py:341
  (55 shorter events, 8.3 us)
Async XLA Ops:
  2.0 3.6 %collective-permute-start.1 = (f32[1,8,160,128]{3,2,1,0:T(8,128)S(1)}, f32[1,8,160,128]{3,2,1,0:T(8,128)S(1)}, u32[]{:S(2)}, u32[]{:S(2)}) collective-permute-start(f32[1,8,160,128]{3,2,1,0:T(8,128)S(1)} %get-tuple-element.52), channel_id=1, source_target_pairs={{0,8},{8,0},{16,24},{24,16},{32,40},{40,32},{48,56},{56,48},{64,72... | collective-permute-start | bytes 1966088 | tf_op jit(solution)/shard_map/core_0/ppermute | solution.py:386
  2.1 3.5 %collective-permute-start = (f32[1,8,160,128]{3,2,1,0:T(8,128)S(1)}, f32[1,8,160,128]{3,2,1,0:T(8,128)S(1)}, u32[]{:S(2)}, u32[]{:S(2)}) collective-permute-start(f32[1,8,160,128]{3,2,1,0:T(8,128)S(1)} %get-tuple-element.48), channel_id=1, source_target_pairs={{0,8},{8,0},{16,24},{24,16},{32,40},{40,32},{48,56},{56,48},{64,72... | collective-permute-start | bytes 1966088 | tf_op jit(solution)/shard_map/core_0/ppermute | solution.py:386
  5.0 12.4 %collective-permute-start.3 = (f32[1,8,160,128]{3,2,1,0:T(8,128)}, f32[1,8,160,128]{3,2,1,0:T(8,128)}, u32[]{:S(2)}, u32[]{:S(2)}) collective-permute-start(f32[1,8,160,128]{3,2,1,0:T(8,128)} %get-tuple-element.55), channel_id=1, source_target_pairs={{0,8},{8,0},{16,24},{24,16},{32,40},{40,32},{48,56},{56,48},{64,72... | collective-permute-start | bytes 1966088 | tf_op jit(solution)/shard_map/core_0/ppermute | solution.py:386
  5.1 3.4 %copy-start = (f32[1,262144]{1,0:T(1,128)S(1)}, f32[1,262144]{1,0:T(1,128)}, u32[]{:S(2)}) copy-start(f32[1,262144]{1,0:T(1,128)} %param.7) | copy-start | bytes 3145732
  5.1 3.4 %copy-start.1 = (f32[1,262144]{1,0:T(1,128)S(1)}, f32[1,262144]{1,0:T(1,128)}, u32[]{:S(2)}) copy-start(f32[1,262144]{1,0:T(1,128)} %param.8) | copy-start | bytes 3145732
  5.1 3.4 %copy-start.2 = (f32[1,262144]{1,0:T(1,128)S(1)}, f32[1,262144]{1,0:T(1,128)}, u32[]{:S(2)}) copy-start(f32[1,262144]{1,0:T(1,128)} %param.9) | copy-start | bytes 3145732
  5.1 3.4 %copy-start.3 = (s32[1,8]{1,0:T(1,128)S(1)}, s32[1,8]{1,0:T(1,128)}, u32[]{:S(2)}) copy-start(s32[1,8]{1,0:T(1,128)} %param.11) | copy-start | bytes 100
  5.1 12.2 %collective-permute-start.2 = (f32[1,8,160,128]{3,2,1,0:T(8,128)}, f32[1,8,160,128]{3,2,1,0:T(8,128)}, u32[]{:S(2)}, u32[]{:S(2)}) collective-permute-start(f32[1,8,160,128]{3,2,1,0:T(8,128)} %get-tuple-element.50), channel_id=1, source_target_pairs={{0,8},{8,0},{16,24},{24,16},{32,40},{40,32},{48,56},{56,48},{64,72... | collective-permute-start | bytes 1966088 | tf_op jit(solution)/shard_map/core_0/ppermute | solution.py:386
  8.4 20.7 %collective-permute-start.6 = (f32[2,8,160,128]{3,2,1,0:T(8,128)}, f32[2,8,160,128]{3,2,1,0:T(8,128)}, u32[]{:S(2)}, u32[]{:S(2)}) collective-permute-start(f32[2,8,160,128]{3,2,1,0:T(8,128)} %far0.1), channel_id=1, source_target_pairs={{0,16},{8,56},{16,32},{24,8},{32,48},{40,24},{48,0},{56,40},{64,80... | collective-permute-start | bytes 3932168 | tf_op jit(solution)/shard_map/far_0/ppermute | solution.py:386
  11.0 64.8 %all-to-all-start.1 = ((f32[8,3,256,128]{3,2,1,0:T(8,128)}), f32[8,3,256,128]{3,2,1,0:T(8,128)S(1)}, u32[]{:S(2)}, u32[]{:S(2)}) async-start(f32[8,3,256,128]{3,2,1,0:T(8,128)} %order.1), calls=%async_computation.1 | async-start | bytes 6291456 | tf_op jit(solution)/shard_map/all_to_all | solution.py:473
  20.9 26.2 %collective-permute-start.7 = (f32[2,8,160,128]{3,2,1,0:T(8,128)S(1)}, f32[2,8,160,128]{3,2,1,0:T(8,128)S(1)}, u32[]{:S(2)}, u32[]{:S(2)}) collective-permute-start(f32[2,8,160,128]{3,2,1,0:T(8,128)S(1)} %get-tuple-element.56), channel_id=1, source_target_pairs={{0,48},{8,24},{16,0},{24,40},{32,16},{40,56},{48,32},{56,8},{64,11... | collective-permute-start | bytes 3932168 | tf_op jit(solution)/shard_map/near_0/ppermute | solution.py:386
  22.7 2.1 %collective-permute-start.4 = (f32[1,8,160,128]{3,2,1,0:T(8,128)S(1)}, f32[1,8,160,128]{3,2,1,0:T(8,128)S(1)}, u32[]{:S(2)}, u32[]{:S(2)}) collective-permute-start(f32[1,8,160,128]{3,2,1,0:T(8,128)S(1)} %get-tuple-element.58), channel_id=1, source_target_pairs={{0,8},{8,0},{16,24},{24,16},{32,40},{40,32},{48,56},{56,48},{64,72... | collective-permute-start | bytes 1966088 | tf_op jit(solution)/shard_map/core_0/ppermute | solution.py:386
  23.1 2.7 %collective-permute-start.5 = (f32[1,8,160,128]{3,2,1,0:T(8,128)S(1)}, f32[1,8,160,128]{3,2,1,0:T(8,128)S(1)}, u32[]{:S(2)}, u32[]{:S(2)}) collective-permute-start(f32[1,8,160,128]{3,2,1,0:T(8,128)S(1)} %get-tuple-element.59), channel_id=1, source_target_pairs={{0,8},{8,0},{16,24},{24,16},{32,40},{40,32},{48,56},{56,48},{64,72... | collective-permute-start | bytes 1966088 | tf_op jit(solution)/shard_map/core_0/ppermute | solution.py:386
  23.2 26.0 %collective-permute-start.12 = (f32[1,8,160,128]{3,2,1,0:T(8,128)S(1)}, f32[1,8,160,128]{3,2,1,0:T(8,128)S(1)}, u32[]{:S(2)}, u32[]{:S(2)}) collective-permute-start(f32[1,8,160,128]{3,2,1,0:T(8,128)S(1)} %get-tuple-element.68), channel_id=1, source_target_pairs={{0,8},{8,0},{16,24},{24,16},{32,40},{40,32},{48,56},{56,48},{64,72... | collective-permute-start | bytes 1966088 | tf_op jit(solution)/shard_map/core_0/ppermute | solution.py:386
  31.9 22.5 %collective-permute-start.14 = (f32[2,8,160,128]{3,2,1,0:T(8,128)S(1)}, f32[2,8,160,128]{3,2,1,0:T(8,128)S(1)}, u32[]{:S(2)}, u32[]{:S(2)}) collective-permute-start(f32[2,8,160,128]{3,2,1,0:T(8,128)S(1)} %ahead0.1), channel_id=1, source_target_pairs={{0,16},{8,56},{16,32},{24,8},{32,48},{40,24},{48,0},{56,40},{64,80... | collective-permute-start | bytes 3932168 | tf_op jit(solution)/shard_map/ahead_0/ppermute | solution.py:386
  34.6 12.4 %collective-permute-start.9 = (f32[1,8,96,128]{3,2,1,0:T(8,128)S(1)}, f32[1,8,96,128]{3,2,1,0:T(8,128)S(1)}, u32[]{:S(2)}, u32[]{:S(2)}) collective-permute-start(f32[1,8,96,128]{3,2,1,0:T(8,128)S(1)} %get-tuple-element.63), channel_id=1, source_target_pairs={{0,8},{8,0},{16,24},{24,16},{32,40},{40,32},{48,56},{56,48},{64,72... | collective-permute-start | bytes 1179656 | tf_op jit(solution)/shard_map/core_1/ppermute | solution.py:386
  34.7 12.8 %collective-permute-start.8 = (f32[1,8,96,128]{3,2,1,0:T(8,128)S(1)}, f32[1,8,96,128]{3,2,1,0:T(8,128)S(1)}, u32[]{:S(2)}, u32[]{:S(2)}) collective-permute-start(f32[1,8,96,128]{3,2,1,0:T(8,128)S(1)} %get-tuple-element.61), channel_id=1, source_target_pairs={{0,8},{8,0},{16,24},{24,16},{32,40},{40,32},{48,56},{56,48},{64,72... | collective-permute-start | bytes 1179656 | tf_op jit(solution)/shard_map/core_1/ppermute | solution.py:386
  47.1 2.2 %collective-permute-start.10 = (f32[1,8,96,128]{3,2,1,0:T(8,128)S(1)}, f32[1,8,96,128]{3,2,1,0:T(8,128)S(1)}, u32[]{:S(2)}, u32[]{:S(2)}) collective-permute-start(f32[1,8,96,128]{3,2,1,0:T(8,128)S(1)} %get-tuple-element.65), channel_id=1, source_target_pairs={{0,8},{8,0},{16,24},{24,16},{32,40},{40,32},{48,56},{56,48},{64,72... | collective-permute-start | bytes 1179656 | tf_op jit(solution)/shard_map/core_1/ppermute | solution.py:386
  47.1 2.7 %collective-permute-start.11 = (f32[1,8,96,128]{3,2,1,0:T(8,128)S(1)}, f32[1,8,96,128]{3,2,1,0:T(8,128)S(1)}, u32[]{:S(2)}, u32[]{:S(2)}) collective-permute-start(f32[1,8,96,128]{3,2,1,0:T(8,128)S(1)} %get-tuple-element.66), channel_id=1, source_target_pairs={{0,8},{8,0},{16,24},{24,16},{32,40},{40,32},{48,56},{56,48},{64,72... | collective-permute-start | bytes 1179656 | tf_op jit(solution)/shard_map/core_1/ppermute | solution.py:386
  48.8 14.9 %collective-permute-start.17 = (f32[2,8,96,128]{3,2,1,0:T(8,128)S(1)}, f32[2,8,96,128]{3,2,1,0:T(8,128)S(1)}, u32[]{:S(2)}, u32[]{:S(2)}) collective-permute-start(f32[2,8,96,128]{3,2,1,0:T(8,128)S(1)} %far1.1), channel_id=1, source_target_pairs={{0,16},{8,56},{16,32},{24,8},{32,48},{40,24},{48,0},{56,40},{64,80... | collective-permute-start | bytes 2359304 | tf_op jit(solution)/shard_map/far_1/ppermute | solution.py:386
  49.3 2.7 %collective-permute-start.13 = (f32[1,8,160,128]{3,2,1,0:T(8,128)S(1)}, f32[1,8,160,128]{3,2,1,0:T(8,128)S(1)}, u32[]{:S(2)}, u32[]{:S(2)}) collective-permute-start(f32[1,8,160,128]{3,2,1,0:T(8,128)S(1)} %get-tuple-element.69), channel_id=1, source_target_pairs={{0,8},{8,0},{16,24},{24,16},{32,40},{40,32},{48,56},{56,48},{64,72... | collective-permute-start | bytes 1966088 | tf_op jit(solution)/shard_map/core_0/ppermute | solution.py:386
  49.3 10.4 %collective-permute-start.15 = (f32[1,8,96,128]{3,2,1,0:T(8,128)S(1)}, f32[1,8,96,128]{3,2,1,0:T(8,128)S(1)}, u32[]{:S(2)}, u32[]{:S(2)}) collective-permute-start(f32[1,8,96,128]{3,2,1,0:T(8,128)S(1)} %get-tuple-element.72), channel_id=1, source_target_pairs={{0,8},{8,0},{16,24},{24,16},{32,40},{40,32},{48,56},{56,48},{64,72... | collective-permute-start | bytes 1179656 | tf_op jit(solution)/shard_map/core_1/ppermute | solution.py:386
  49.8 9.9 %collective-permute-start.16 = (f32[1,8,96,128]{3,2,1,0:T(8,128)S(1)}, f32[1,8,96,128]{3,2,1,0:T(8,128)S(1)}, u32[]{:S(2)}, u32[]{:S(2)}) collective-permute-start(f32[1,8,96,128]{3,2,1,0:T(8,128)S(1)} %get-tuple-element.73), channel_id=1, source_target_pairs={{0,8},{8,0},{16,24},{24,16},{32,40},{40,32},{48,56},{56,48},{64,72... | collective-permute-start | bytes 1179656 | tf_op jit(solution)/shard_map/core_1/ppermute | solution.py:386
  55.8 18.6 %collective-permute-start.18 = (f32[1,8,160,128]{3,2,1,0:T(8,128)S(1)}, f32[1,8,160,128]{3,2,1,0:T(8,128)S(1)}, u32[]{:S(2)}, u32[]{:S(2)}) collective-permute-start(f32[1,8,160,128]{3,2,1,0:T(8,128)S(1)} %get-tuple-element.75), channel_id=1, source_target_pairs={{0,64},{8,72},{16,80},{24,88},{32,96},{40,104},{48,112},{56,120},{... | collective-permute-start | bytes 1966088 | tf_op jit(solution)/shard_map/swap_0/ppermute | solution.py:386
  58.9 22.9 %collective-permute-start.22 = (f32[2,8,96,128]{3,2,1,0:T(8,128)}, f32[2,8,96,128]{3,2,1,0:T(8,128)}, u32[]{:S(2)}, u32[]{:S(2)}) collective-permute-start(f32[2,8,96,128]{3,2,1,0:T(8,128)} %near1.1), channel_id=1, source_target_pairs={{0,48},{8,24},{16,0},{24,40},{32,16},{40,56},{48,32},{56,8},{64,11... | collective-permute-start | bytes 2359304 | tf_op jit(solution)/shard_map/near_1/ppermute | solution.py:386
  65.8 16.1 %collective-permute-start.21 = (f32[2,8,96,128]{3,2,1,0:T(8,128)}, f32[2,8,96,128]{3,2,1,0:T(8,128)}, u32[]{:S(2)}, u32[]{:S(2)}) collective-permute-start(f32[2,8,96,128]{3,2,1,0:T(8,128)} %ahead1.1), channel_id=1, source_target_pairs={{0,16},{8,56},{16,32},{24,8},{32,48},{40,24},{48,0},{56,40},{64,80... | collective-permute-start | bytes 2359304 | tf_op jit(solution)/shard_map/ahead_1/ppermute | solution.py:386
  67.0 14.8 %collective-permute-start.19 = (f32[1,8,96,128]{3,2,1,0:T(8,128)}, f32[1,8,96,128]{3,2,1,0:T(8,128)}, u32[]{:S(2)}, u32[]{:S(2)}) collective-permute-start(f32[1,8,96,128]{3,2,1,0:T(8,128)} %get-tuple-element.77), channel_id=1, source_target_pairs={{0,8},{8,0},{16,24},{24,16},{32,40},{40,32},{48,56},{56,48},{64,72... | collective-permute-start | bytes 1179656 | tf_op jit(solution)/shard_map/core_1/ppermute | solution.py:386
  67.0 14.8 %collective-permute-start.20 = (f32[1,8,96,128]{3,2,1,0:T(8,128)S(1)}, f32[1,8,96,128]{3,2,1,0:T(8,128)}, u32[]{:S(2)}, u32[]{:S(2)}) collective-permute-start(f32[1,8,96,128]{3,2,1,0:T(8,128)S(1)} %get-tuple-element.78), channel_id=1, source_target_pairs={{0,8},{8,0},{16,24},{24,16},{32,40},{40,32},{48,56},{56,48},{64,72... | collective-permute-start | bytes 1179656 | tf_op jit(solution)/shard_map/core_1/ppermute | solution.py:386
  75.9 25.6 %all-to-all-start = ((f32[8,160,128]{2,1,0:T(8,128)}), f32[8,160,128]{2,1,0:T(8,128)}, u32[]{:S(2)}, u32[]{:S(2)}) async-start(f32[8,160,128]{2,1,0:T(8,128)} %finish.2.ordered), calls=%async_computation | async-start | bytes 1310720 | tf_op jit(solution)/shard_map/all_to_all | solution.py:452
  83.9 16.2 %collective-permute-start.23 = (f32[1,8,96,128]{3,2,1,0:T(8,128)S(1)}, f32[1,8,96,128]{3,2,1,0:T(8,128)S(1)}, u32[]{:S(2)}, u32[]{:S(2)}) collective-permute-start(f32[1,8,96,128]{3,2,1,0:T(8,128)S(1)} %get-tuple-element.83), channel_id=1, source_target_pairs={{0,64},{8,72},{16,80},{24,88},{32,96},{40,104},{48,112},{56,120},{... | collective-permute-start | bytes 1179656 | tf_op jit(solution)/shard_map/swap_1/ppermute | solution.py:386
  90.3 15.9 %copy-start.4 = (s32[10]{0:T(128)S(1)}, s32[10]{0:T(128)}, u32[]{:S(2)}) copy-start(s32[10]{0:T(128)} %param.10) | copy-start | bytes 124
  101.5 12.8 %all-to-all-start.2 = ((f32[8,96,128]{2,1,0:T(8,128)}), f32[8,96,128]{2,1,0:T(8,128)S(1)}, u32[]{:S(2)}, u32[]{:S(2)}) async-start(f32[8,96,128]{2,1,0:T(8,128)} %finish.3.ordered), calls=%async_computation.2 | async-start | bytes 786432 | tf_op jit(solution)/shard_map/all_to_all | solution.py:452
